TPU v7x, 32 devices: a whole 2x2x4 slice. The times are simulated.
32 devices in a mesh: stack: 8 (over z, y), azimuth: 2 (over x), range: 2 (over core).
Axes of the slice: x: 2, y: 2, z: 4, core: 2. Of those that a mesh axis runs over, the one named last changes fastest.
Arguments:
- phases: bfloat16 [1152, 4, 2048], P('stack', 'azimuth', 'range'), may hold values from -6 to 6
- ifg_pairs: int32 [1152, 2], replicated, may hold values from 0 to 599, as said below
- preconditioner: float32 [600, 600], replicated, as said below
- coherence: int32 [4, 2048], P('azimuth', ('range', 'stack')), may hold values 0 or 1
- geo_tiles: int32 [4, 2048], P('azimuth', ('range', 'stack')), may hold values from 0 to 15, as said below
Outputs:
- deramped: float32 [600, 4, 2048], P(None, 'azimuth', ('range', 'stack'))
Inputs may be any that keep to these rules, and one draw needn't show every extreme that they name: `ifg_pairs`: each row names an earlier date first and a later date second. `preconditioner`: a symmetric matrix. geo_tiles[r, c] = min(max(floor((c + shift_r) / 128), 0), 15) with one integer shift_r per slab row, -32 <= shift_r <= 32; some row has shift -32 and another +32.
All inputs are finite; a program needn't handle non-finite values. No bound on the sum of `coherence` on one device may be relied on, other than what follows from the above.
Results may differ from a plain program's by a relative error of at most 0.002.
Values may be sent and summed in bfloat16 or wider, within the bound.
No kernel may reach another device: no remote copies, remote signals or barrier semaphores. Data moves between devices by JAX's collectives and lax.ppermute only.
A program may use at most 64 MiB of HBM per device.

v0:
```python
import jax
import jax.numpy as jnp
from jax import lax
from jax.sharding import PartitionSpec as P

REWEIGHTS = 2
SKEW = 32


def from_behind(value, axis, steps):
    count = lax.axis_size(axis)
    pairs = [(source, (source + steps) % count) for source in range(count)]
    return lax.ppermute(value, axis, pairs)


def shifted_2(block, axis, distance):
    devices = range(lax.axis_size(axis))
    route = [(i - distance, i) for i in devices if i - distance in devices]
    return lax.ppermute(block, axis, route)


def plane_solve(gram_matrix, right_side):

    def entry(row_pos, col_pos):
        return gram_matrix[row_pos % 3, col_pos % 3]

    cofactors = [
        [
            entry(row_pos + 1, col_pos + 1) * entry(row_pos + 2, col_pos + 2)
            - entry(row_pos + 1, col_pos + 2) * entry(row_pos + 2, col_pos + 1)
            for col_pos in range(3)
        ]
        for row_pos in range(3)
    ]
    determinant = (
        entry(0, 0) * cofactors[0][0]
        + entry(0, 1) * cofactors[0][1]
        + entry(0, 2) * cofactors[0][2]
    )
    solution = [
        (
            cofactors[0][col_pos] * right_side[0]
            + cofactors[1][col_pos] * right_side[1]
            + cofactors[2][col_pos] * right_side[2]
        )
        / determinant
        for col_pos in range(3)
    ]
    return jnp.stack(solution)


def invert_pixels(stack_data, coherence_row, incidence, incidence_half, preconditioner):
    normal_rhs = lax.dot_general(
        incidence_half, stack_data, (((0,), (0,)), ((), ())), preferred_element_type=jnp.float32
    )
    series = jnp.dot(
        preconditioner,
        normal_rhs,
        precision=lax.Precision.HIGHEST,
        preferred_element_type=jnp.float32,
    )
    values = stack_data.astype(jnp.float32)
    for sweep in range(REWEIGHTS):
        predicted = jnp.dot(
            incidence, series, precision=lax.Precision.HIGHEST, preferred_element_type=jnp.float32
        )
        residual = values - predicted
        square = residual * residual
        robust_scale = jnp.mean(square, axis=0) + 1e-06
        shifted = square + robust_scale
        weight = coherence_row * (robust_scale * robust_scale) / (shifted * shifted)
        update = lax.dot_general(
            incidence,
            weight * residual,
            (((0,), (0,)), ((), ())),
            precision=lax.Precision.HIGHEST,
            preferred_element_type=jnp.float32,
        )
        series = series + jnp.dot(
            preconditioner,
            update,
            precision=lax.Precision.HIGHEST,
            preferred_element_type=jnp.float32,
        )
    return series


def tile_moments(series_part, weight, coord_u, coord_v):
    date_total = series_part.shape[0]
    basis = jnp.stack([jnp.ones_like(coord_u), coord_u, coord_v]).reshape(3, -1)
    weighted_basis = basis * weight.reshape(1, -1)
    moments = lax.dot_general(
        weighted_basis,
        series_part.reshape(date_total, -1),
        (((1,), (1,)), ((), ())),
        precision=lax.Precision.HIGHEST,
        preferred_element_type=jnp.float32,
    )
    gram_matrix = lax.dot_general(
        weighted_basis,
        basis,
        (((1,), (1,)), ((), ())),
        precision=lax.Precision.HIGHEST,
        preferred_element_type=jnp.float32,
    )
    return (moments, gram_matrix)


def plane_at(plane_coefs, coord_u, coord_v):
    return (
        plane_coefs[0][:, None, None]
        + plane_coefs[1][:, None, None] * coord_u[None]
        + plane_coefs[2][:, None, None] * coord_v[None]
    )


def pixel_from_lower(values, stack_pos):
    wrapped = from_behind(values, "stack", 1)
    across = shifted_2(wrapped.astype(jnp.bfloat16), "range", 1).astype(wrapped.dtype)
    return jnp.where(stack_pos == 0, across, wrapped)


def pixel_from_upper(values, stack_pos, last_pos):
    wrapped = from_behind(values, "stack", -1)
    across = shifted_2(wrapped.astype(jnp.bfloat16), "range", -1).astype(wrapped.dtype)
    return jnp.where(stack_pos == last_pos, across, wrapped)


def local(phases, ifg_pairs, preconditioner, coherence, geo_tiles):
    stacked = lax.all_to_all(phases, "stack", split_axis=2, concat_axis=0, tiled=True)
    ifg_total, row_local, col_local = stacked.shape
    pixel_count = row_local * col_local
    stack_data = stacked.reshape(ifg_total, pixel_count)
    date_total = preconditioner.shape[0]
    stack_size = lax.axis_size("stack")
    range_size = lax.axis_size("range")
    azimuth_size = lax.axis_size("azimuth")
    edge = SKEW
    earlier_date = ifg_pairs[:, 0]
    later_date = ifg_pairs[:, 1]
    date_ids = jnp.arange(date_total, dtype=jnp.int32)
    incidence = (later_date[:, None] == date_ids).astype(jnp.float32) - (
        earlier_date[:, None] == date_ids
    ).astype(jnp.float32)
    incidence_half = incidence.astype(jnp.bfloat16)
    coherence_f = coherence.astype(jnp.float32)
    series = invert_pixels(
        stack_data, coherence_f.reshape(-1), incidence, incidence_half, preconditioner
    )
    series3 = series.reshape(date_total, row_local, col_local)
    stack_pos = lax.axis_index("stack")
    last_pos = stack_size - 1
    block_index = lax.axis_index("range") * stack_size + stack_pos
    row_ids = lax.axis_index("azimuth") * row_local + jnp.arange(row_local, dtype=jnp.int32)
    row_coord = (row_ids.astype(jnp.float32) + 0.5) / (row_local * azimuth_size) - 0.5

    def coords(first_col, width):
        col_ids = first_col + jnp.arange(width, dtype=jnp.int32)
        col_coord = (col_ids.astype(jnp.float32) + 0.5) / (
            col_local * stack_size * range_size
        ) - 0.5
        return (
            jnp.broadcast_to(row_coord[:, None], (row_local, width)),
            jnp.broadcast_to(col_coord[None, :], (row_local, width)),
        )

    own_u, own_v = coords(block_index * col_local, col_local)
    lower_member = (geo_tiles == block_index - 1).astype(jnp.float32)
    upper_member = (geo_tiles == block_index + 1).astype(jnp.float32)
    own_weight = coherence_f * (geo_tiles == block_index).astype(jnp.float32)
    own_moments, own_gram = tile_moments(series3, own_weight, own_u, own_v)
    identity = jnp.eye(3, dtype=jnp.float32)
    left_member = lower_member[:, :edge]
    right_member = upper_member[:, col_local - edge :]
    left_send = jnp.concatenate(
        [series3[:, :, :edge], (coherence_f[:, :edge] * left_member)[None]], axis=0
    )
    right_send = jnp.concatenate(
        [
            series3[:, :, col_local - edge :],
            (coherence_f[:, col_local - edge :] * right_member)[None],
        ],
        axis=0,
    )
    from_upper = pixel_from_upper(left_send, stack_pos, last_pos)
    from_lower = pixel_from_lower(right_send, stack_pos)
    upper_u, upper_v = coords((block_index + 1) * col_local, edge)
    lower_u, lower_v = coords(block_index * col_local - edge, edge)
    upper_moments, upper_gram = tile_moments(
        from_upper[:date_total], from_upper[date_total], upper_u, upper_v
    )
    lower_moments, lower_gram = tile_moments(
        from_lower[:date_total], from_lower[date_total], lower_u, lower_v
    )
    moments = own_moments + upper_moments + lower_moments
    gram_matrix = own_gram + upper_gram + lower_gram
    moments, gram_matrix = lax.psum((moments, gram_matrix), "azimuth")
    plane_coefs = plane_solve(gram_matrix + identity, moments)
    own_flat = series3 - plane_at(plane_coefs, own_u, own_v)
    upper_flat = from_upper[:date_total] - plane_at(plane_coefs, upper_u, upper_v)
    lower_flat = from_lower[:date_total] - plane_at(plane_coefs, lower_u, lower_v)
    back_right = pixel_from_upper(lower_flat, stack_pos, last_pos)
    back_left = pixel_from_lower(upper_flat, stack_pos)
    left_final = jnp.where(left_member[None] > 0.5, back_left, own_flat[:, :, :edge])
    right_final = jnp.where(
        right_member[None] > 0.5, back_right, own_flat[:, :, col_local - edge :]
    )
    result = jnp.concatenate(
        [left_final, own_flat[:, :, edge : col_local - edge], right_final], axis=2
    )
    return result


def solution(mesh):
    return jax.shard_map(
        local,
        mesh=mesh,
        in_specs=(
            P("stack", "azimuth", "range"),
            P(),
            P(),
            P("azimuth", ("range", "stack")),
            P("azimuth", ("range", "stack")),
        ),
        out_specs=P(None, "azimuth", ("range", "stack")),
        check_vma=False,
    )
```

profile of v0, /device:TPU:0, one launch (start us, length us, event | category | flops | bytes accessed | tf_op | source)
XLA Modules:
  0.0 127.6 jit_solution(12451960636428274054)
XLA Ops:
  0.0 4.8 %copy.28 = bf16[144,2,1024]{0,1,2:T(2,128)(2,1)} copy(bf16[144,2,1024]{2,1,0:T(2,128)(2,1)} %param.5) | data formatting | bytes 1179648 | tf_op args[0]
  4.8 7.3 %all-to-all-start = ((bf16[144,2,1024]{0,1,2:T(2,128)(2,1)}), bf16[144,2,1024]{0,1,2:T(2,128)(2,1)S(1)}, u32[]{:S(2)}, u32[]{:S(2)}) async-start(bf16[144,2,1024]{0,1,2:T(2,128)(2,1)} %copy.28), calls=%async_computation | async-start | bytes 2097152 | tf_op jit(solution)/shard_map/all_to_all | solution.py:130
  12.4 25.5 %all-to-all-done = bf16[144,2,1024]{0,1,2:T(2,128)(2,1)S(1)} async-done(((bf16[144,2,1024]{0,1,2:T(2,128)(2,1)}), bf16[144,2,1024]{0,1,2:T(2,128)(2,1)S(1)}, u32[]{:S(2)}, u32[]{:S(2)}) %all-to-all-start) | async-done | bytes 589856 | tf_op jit(solution)/shard_map/all_to_all | solution.py:130
  37.8 3.3 %copy.29 = bf16[144,2,8,128]{3,1,0,2:T(2,128)(2,1)S(1)} copy(bf16[144,2,8,128]{0,1,3,2:T(2,128)(2,1)S(1)} %bitcast.63) | data formatting | bytes 1179648 | tf_op jit(solution)/shard_map/all_to_all | solution.py:130
  41.1 1.2 fusion.7
  42.3 1.6 %fusion.77 = f32[256,600]{0,1:T(8,128)S(1)} fusion(f32[600,256]{1,0:T(8,128)S(1)} %fusion.7, f32[600,600]{1,0:T(8,128)S(1)} %copy-done), kind=kOutput, calls=%fused_computation.123 | convolution fusion | flops 1105920000 | bytes 2668800 | tf_op jit(solution)/shard_map/dot_general | solution.py:56
  43.9 3.6 %multiply_reduce_fusion.1 = (f32[256]{0:T(256)S(1)}, f32[1152,256]{1,0:T(8,128)S(1)}) fusion(f32[256,600]{0,1:T(8,128)S(1)} %fusion.77, s32[1152]{0:T(1024)S(1)} %get-tuple-element.9, s32[1152]{0:T(1024)S(1)} %get-tuple-element.8, bf16[144,8,2,128]{3,2,1,0:T(2,128)(2,1)S(1)} %bitcast.67), kind=kOutput, calls=%fused_computation.34 | convolution fusion | flops 2128001792 | bytes 2394112 | tf_op jit(solution)/shard_map/dot_general | solution.py:64
  47.6 5.4 %fusion.2 = f32[600,256]{1,0:T(8,128)S(1)} fusion(s32[1152]{0:T(1024)S(1)} %get-tuple-element.9, s32[1152]{0:T(1024)S(1)} %get-tuple-element.8, f32[1152,256]{1,0:T(8,128)S(1)} %get-tuple-element.36, f32[256]{0:T(256)S(1)} %get-tuple-element.34, f32[256]{0:T(256)S(1)} %get-tuple-element.33), kind=kOutput, calls=%fused_computation.4 | convolution fusion | flops 2128296960 | bytes 1805312 | tf_op jit(solution)/shard_map/dot_general | solution.py:72
  52.9 1.9 %convolution_add_fusion.1 = f32[256,600]{0,1:T(8,128)S(1)} fusion(f32[256,600]{0,1:T(8,128)S(1)} %fusion.77, f32[600,256]{1,0:T(8,128)S(1)} %fusion.2, f32[600,600]{1,0:T(8,128)S(1)} %copy-done), kind=kOutput, calls=%fused_computation.22 | convolution fusion | flops 1106073600 | bytes 3283200 | tf_op jit(solution)/shard_map/dot_general | solution.py:79
  54.8 3.7 %multiply_reduce_fusion = (f32[256]{0:T(256)S(1)}, f32[1152,256]{1,0:T(8,128)S(1)}) fusion(f32[256,600]{0,1:T(8,128)S(1)} %convolution_add_fusion.1, s32[1152]{0:T(1024)S(1)} %get-tuple-element.9, s32[1152]{0:T(1024)S(1)} %get-tuple-element.8, bf16[144,8,2,128]{3,2,1,0:T(2,128)(2,1)S(1)} %bitcast.68), kind=kOutput, calls=%fused_computation.32 | convolution fusion | flops 2128001792 | bytes 2394112 | tf_op jit(solution)/shard_map/dot_general | solution.py:64
  58.5 5.4 %fusion = f32[600,256]{1,0:T(8,128)S(1)} fusion(s32[1152]{0:T(1024)S(1)} %get-tuple-element.9, s32[1152]{0:T(1024)S(1)} %get-tuple-element.8, f32[1152,256]{1,0:T(8,128)S(1)} %get-tuple-element.38, f32[256]{0:T(256)S(1)} %get-tuple-element.32, f32[256]{0:T(256)S(1)} %get-tuple-element.31), kind=kOutput, calls=%fused_computation.2 | convolution fusion | flops 2128296960 | bytes 1805312 | tf_op jit(solution)/shard_map/dot_general | solution.py:72
  63.9 1.7 %convolution_add_fusion = f32[256,600]{0,1:T(8,128)S(1)} fusion(f32[256,600]{0,1:T(8,128)S(1)} %convolution_add_fusion.1, f32[600,256]{1,0:T(8,128)S(1)} %fusion, f32[600,600]{1,0:T(8,128)S(1)} %copy-done), kind=kOutput, calls=%fused_computation.21 | convolution fusion | flops 1106073600 | bytes 3283200 | tf_op jit(solution)/shard_map/dot_general | solution.py:79
  65.5 0.4 copy.36
  66.1 2.3 %collective-permute-start = (f32[601,2,32]{0,2,1:T(8,128)S(1)}, f32[601,2,32]{0,2,1:T(8,128)S(1)}, u32[]{:S(2)}, u32[]{:S(2)}) collective-permute-start(f32[601,2,32]{0,2,1:T(8,128)S(1)} %pad_maximum_fusion.1), channel_id=1, source_target_pairs={{0,28},{4,0},{8,4},{12,8},{16,12},{20,16},{24,20},{28,24},{1,29},{... | collective-permute-start | bytes 461576 | tf_op jit(solution)/shard_map/ppermute | solution.py:13
  68.6 3.4 %collective-permute-done = f32[601,2,32]{0,2,1:T(8,128)S(1)} collective-permute-done((f32[601,2,32]{0,2,1:T(8,128)S(1)}, f32[601,2,32]{0,2,1:T(8,128)S(1)}, u32[]{:S(2)}, u32[]{:S(2)}) %collective-permute-start) | collective-permute-done | bytes 153888 | tf_op jit(solution)/shard_map/ppermute | solution.py:13
  72.1 1.3 %collective-permute-start.1 = (bf16[601,2,32]{0,2,1:T(8,128)(2,1)S(1)}, bf16[601,2,32]{0,2,1:T(8,128)(2,1)S(1)}, u32[]{:S(2)}, u32[]{:S(2)}) collective-permute-start(bf16[601,2,32]{0,2,1:T(8,128)(2,1)S(1)} %convert_element_type.62), channel_id=1, source_target_pairs={{1,0},{3,2},{5,4},{7,6},{9,8},{11,10},{13,12},{15,14},{17,16},{19,... | collective-permute-start | bytes 230792 | tf_op jit(solution)/shard_map/ppermute | solution.py:19
  73.4 0.6 fusion.48
  74.0 3.1 %collective-permute-done.2 = f32[601,2,32]{0,2,1:T(8,128)S(1)} collective-permute-done((f32[601,2,32]{0,2,1:T(8,128)S(1)}, f32[601,2,32]{0,2,1:T(8,128)S(1)}, u32[]{:S(2)}, u32[]{:S(2)}) %collective-permute-start.2) | collective-permute-done | bytes 153888 | tf_op jit(solution)/shard_map/ppermute | solution.py:13
  77.2 1.3 %collective-permute-start.3 = (bf16[601,2,32]{0,2,1:T(8,128)(2,1)S(1)}, bf16[601,2,32]{0,2,1:T(8,128)(2,1)S(1)}, u32[]{:S(2)}, u32[]{:S(2)}) collective-permute-start(bf16[601,2,32]{0,2,1:T(8,128)(2,1)S(1)} %convert_element_type.68), channel_id=1, source_target_pairs={{0,1},{2,3},{4,5},{6,7},{8,9},{10,11},{12,13},{14,15},{16,17},{18,... | collective-permute-start | bytes 230792 | tf_op jit(solution)/shard_map/ppermute | solution.py:19
  78.7 0.3 fusion.30
  79.5 0.2 convolution_bitcast_fusion.2
  79.7 0.3 fusion.29
  80.1 0.2 fusion.32
  80.3 8.1 %all-reduce = (f32[3,3]{1,0:T(4,128)S(1)}, f32[3,600]{1,0:T(4,128)S(1)}) all-reduce(f32[3,3]{1,0:T(4,128)S(1)} %fusion.32, f32[3,600]{1,0:T(4,128)S(1)} %fusion.29), channel_id=1, replica_groups=mesh['stack'=8,'azimuth'=2,'range'=2] {'azimuth'}, use_global_device_ids=true, to_apply=%region_2.3 | all-reduce | flops 1809 | bytes 14472 | tf_op jit(solution)/shard_map/psum | solution.py:197
  88.4 0.7 fusion.76
  113.7 0.5 collective-permute-start.4
  114.2 4.2 %collective-permute-start.6 = (f32[600,2,32]{0,2,1:T(8,128)S(1)}, f32[600,2,32]{0,2,1:T(8,128)S(1)}, u32[]{:S(2)}, u32[]{:S(2)}) collective-permute-start(f32[600,2,32]{0,2,1:T(8,128)S(1)} %get-tuple-element.17), channel_id=1, source_target_pairs={{0,28},{4,0},{8,4},{12,8},{16,12},{20,16},{24,20},{28,24},{1,29},{... | collective-permute-start | bytes 460808 | tf_op jit(solution)/shard_map/ppermute | solution.py:13
  118.5 3.3 %collective-permute-done.4 = f32[600,2,32]{0,2,1:T(8,128)S(1)} collective-permute-done((f32[600,2,32]{0,2,1:T(8,128)S(1)}, f32[600,2,32]{0,2,1:T(8,128)S(1)}, u32[]{:S(2)}, u32[]{:S(2)}) %collective-permute-start.4) | collective-permute-done | bytes 153632 | tf_op jit(solution)/shard_map/ppermute | solution.py:13
  121.9 1.3 %collective-permute-start.5 = (bf16[600,2,32]{0,2,1:T(8,128)(2,1)S(1)}, bf16[600,2,32]{0,2,1:T(8,128)(2,1)S(1)}, u32[]{:S(2)}, u32[]{:S(2)}) collective-permute-start(bf16[600,2,32]{0,2,1:T(8,128)(2,1)S(1)} %convert_element_type.71), channel_id=1, source_target_pairs={{0,1},{2,3},{4,5},{6,7},{8,9},{10,11},{12,13},{14,15},{16,17},{18,... | collective-permute-start | bytes 230408 | tf_op jit(solution)/shard_map/ppermute | solution.py:19
  123.2 1.3 %collective-permute-start.7 = (bf16[600,2,32]{0,2,1:T(8,128)(2,1)S(1)}, bf16[600,2,32]{0,2,1:T(8,128)(2,1)S(1)}, u32[]{:S(2)}, u32[]{:S(2)}) collective-permute-start(bf16[600,2,32]{0,2,1:T(8,128)(2,1)S(1)} %convert_element_type.73), channel_id=1, source_target_pairs={{1,0},{3,2},{5,4},{7,6},{9,8},{11,10},{13,12},{15,14},{17,16},{19,... | collective-permute-start | bytes 230408 | tf_op jit(solution)/shard_map/ppermute | solution.py:19
  124.7 1.7 %collective-permute-done.7 = bf16[600,2,32]{0,2,1:T(8,128)(2,1)S(1)} collective-permute-done((bf16[600,2,32]{0,2,1:T(8,128)(2,1)S(1)}, bf16[600,2,32]{0,2,1:T(8,128)(2,1)S(1)}, u32[]{:S(2)}, u32[]{:S(2)}) %collective-permute-start.7) | collective-permute-done | bytes 76832 | tf_op jit(solution)/shard_map/ppermute | solution.py:19
  126.5 1.1 copy.35
  (51 shorter events, 1.9 us)
Async XLA Ops:
  0.0 42.3 %copy-start = (f32[600,600]{1,0:T(8,128)S(1)}, f32[600,600]{1,0:T(8,128)}, u32[]{:S(2)}) copy-start(f32[600,600]{1,0:T(8,128)} %param.7) | copy-start | bytes 4320004
  0.0 12.1 %copy-start.1 = (s32[2,128]{1,0:T(2,128)S(1)}, s32[2,128]{1,0:T(2,128)}, u32[]{:S(2)}) copy-start(s32[2,128]{1,0:T(2,128)} %param.8) | copy-start | bytes 3076
  0.0 12.1 %copy-start.3 = (s32[2,128]{1,0:T(2,128)S(1)}, s32[2,128]{1,0:T(2,128)}, u32[]{:S(2)}) copy-start(s32[2,128]{1,0:T(2,128)} %param.9) | copy-start | bytes 3076
  0.0 12.3 %copy-start.2 = (s32[1152,2]{0,1:T(2,128)S(1)}, s32[1152,2]{0,1:T(2,128)}, u32[]{:S(2)}) copy-start(s32[1152,2]{0,1:T(2,128)} %param.6) | copy-start | bytes 27652
  4.8 33.1 %all-to-all-start = ((bf16[144,2,1024]{0,1,2:T(2,128)(2,1)}), bf16[144,2,1024]{0,1,2:T(2,128)(2,1)S(1)}, u32[]{:S(2)}, u32[]{:S(2)}) async-start(bf16[144,2,1024]{0,1,2:T(2,128)(2,1)} %copy.28), calls=%async_computation | async-start | bytes 2097152 | tf_op jit(solution)/shard_map/all_to_all | solution.py:130
  66.1 5.9 %collective-permute-start = (f32[601,2,32]{0,2,1:T(8,128)S(1)}, f32[601,2,32]{0,2,1:T(8,128)S(1)}, u32[]{:S(2)}, u32[]{:S(2)}) collective-permute-start(f32[601,2,32]{0,2,1:T(8,128)S(1)} %pad_maximum_fusion.1), channel_id=1, source_target_pairs={{0,28},{4,0},{8,4},{12,8},{16,12},{20,16},{24,20},{28,24},{1,29},{... | collective-permute-start | bytes 461576 | tf_op jit(solution)/shard_map/ppermute | solution.py:13
  68.6 8.5 %collective-permute-start.2 = (f32[601,2,32]{0,2,1:T(8,128)S(1)}, f32[601,2,32]{0,2,1:T(8,128)S(1)}, u32[]{:S(2)}, u32[]{:S(2)}) collective-permute-start(f32[601,2,32]{0,2,1:T(8,128)S(1)} %pad_maximum_fusion.2), channel_id=1, source_target_pairs={{0,4},{4,8},{8,12},{12,16},{16,20},{20,24},{24,28},{28,0},{1,5},{5... | collective-permute-start | bytes 461576 | tf_op jit(solution)/shard_map/ppermute | solution.py:13
  72.1 6.4 %collective-permute-start.1 = (bf16[601,2,32]{0,2,1:T(8,128)(2,1)S(1)}, bf16[601,2,32]{0,2,1:T(8,128)(2,1)S(1)}, u32[]{:S(2)}, u32[]{:S(2)}) collective-permute-start(bf16[601,2,32]{0,2,1:T(8,128)(2,1)S(1)} %convert_element_type.62), channel_id=1, source_target_pairs={{1,0},{3,2},{5,4},{7,6},{9,8},{11,10},{13,12},{15,14},{17,16},{19,... | collective-permute-start | bytes 230792 | tf_op jit(solution)/shard_map/ppermute | solution.py:19
  77.2 2.2 %collective-permute-start.3 = (bf16[601,2,32]{0,2,1:T(8,128)(2,1)S(1)}, bf16[601,2,32]{0,2,1:T(8,128)(2,1)S(1)}, u32[]{:S(2)}, u32[]{:S(2)}) collective-permute-start(bf16[601,2,32]{0,2,1:T(8,128)(2,1)S(1)} %convert_element_type.68), channel_id=1, source_target_pairs={{0,1},{2,3},{4,5},{6,7},{8,9},{10,11},{12,13},{14,15},{16,17},{18,... | collective-permute-start | bytes 230792 | tf_op jit(solution)/shard_map/ppermute | solution.py:19
  113.7 8.2 %collective-permute-start.4 = (f32[600,2,32]{0,2,1:T(8,128)S(1)}, f32[600,2,32]{0,2,1:T(8,128)S(1)}, u32[]{:S(2)}, u32[]{:S(2)}) collective-permute-start(f32[600,2,32]{0,2,1:T(8,128)S(1)} %get-tuple-element.16), channel_id=1, source_target_pairs={{0,4},{4,8},{8,12},{12,16},{16,20},{20,24},{24,28},{28,0},{1,5},{5... | collective-permute-start | bytes 460808 | tf_op jit(solution)/shard_map/ppermute | solution.py:13
  114.2 9.0 %collective-permute-start.6 = (f32[600,2,32]{0,2,1:T(8,128)S(1)}, f32[600,2,32]{0,2,1:T(8,128)S(1)}, u32[]{:S(2)}, u32[]{:S(2)}) collective-permute-start(f32[600,2,32]{0,2,1:T(8,128)S(1)} %get-tuple-element.17), channel_id=1, source_target_pairs={{0,28},{4,0},{8,4},{12,8},{16,12},{20,16},{24,20},{28,24},{1,29},{... | collective-permute-start | bytes 460808 | tf_op jit(solution)/shard_map/ppermute | solution.py:13
  121.9 2.8 %collective-permute-start.5 = (bf16[600,2,32]{0,2,1:T(8,128)(2,1)S(1)}, bf16[600,2,32]{0,2,1:T(8,128)(2,1)S(1)}, u32[]{:S(2)}, u32[]{:S(2)}) collective-permute-start(bf16[600,2,32]{0,2,1:T(8,128)(2,1)S(1)} %convert_element_type.71), channel_id=1, source_target_pairs={{0,1},{2,3},{4,5},{6,7},{8,9},{10,11},{12,13},{14,15},{16,17},{18,... | collective-permute-start | bytes 230408 | tf_op jit(solution)/shard_map/ppermute | solution.py:19
  123.2 3.2 %collective-permute-start.7 = (bf16[600,2,32]{0,2,1:T(8,128)(2,1)S(1)}, bf16[600,2,32]{0,2,1:T(8,128)(2,1)S(1)}, u32[]{:S(2)}, u32[]{:S(2)}) collective-permute-start(bf16[600,2,32]{0,2,1:T(8,128)(2,1)S(1)} %convert_element_type.73), channel_id=1, source_target_pairs={{1,0},{3,2},{5,4},{7,6},{9,8},{11,10},{13,12},{15,14},{17,16},{19,... | collective-permute-start | bytes 230408 | tf_op jit(solution)/shard_map/ppermute | solution.py:19
where the time goes:
time: 128 us
  waiting for transfers between devices  37.1 us (29%)
  matrix products  26.2 us (20%)
  between operations  24.8 us (19%)
  starting transfers between devices  19.6 us (15%)
  local copies, waits for them, and re-layouts  11 us (9%)
  blocking collectives  8.1 us (6%)
    all_to_all x1, waiting for transfers between devices, local(): lax.all_to_all(phases, 'stack', split_axis=2, concat_axis=0, tiled=True)  25.5 us
    dot_general x2, matrix products, invert_pixels(): lax.dot_general(incidence, weight * residual, (((0,), (0,)), ((), ())), p...  10.7 us
    ppermute x4, waiting for transfers between devices, from_behind(): return lax.ppermute(value, axis, pairs)  9.88 us
    psum x1, blocking collectives, local(): moments, gram_matrix = lax.psum((moments, gram_matrix), 'azimuth')  8.1 us
    dot_general x2, matrix products, invert_pixels(): jnp.dot(incidence, series, precision=lax.Precision.HIGHEST, preferred_ele...  7.31 us
    all_to_all x1, starting transfers between devices, local(): lax.all_to_all(phases, 'stack', split_axis=2, concat_axis=0, tiled=True)  7.29 us
    ppermute x4, starting transfers between devices, from_behind(): return lax.ppermute(value, axis, pairs)  7.09 us
    ppermute x4, starting transfers between devices, shifted_2(): return lax.ppermute(block, axis, route)  5.17 us
  transfers between devices with their start and end apart: 9, of which 6 were waited for; matrix products, arithmetic and copies ran while one was open for 2% of the time, Pallas kernels for 0%

commit v1 on v0

v1 whole, which is shorter than its diff:
```python
import functools

import jax
import jax.numpy as jnp
from jax import lax
from jax.experimental import pallas as pl
from jax.experimental.pallas import tpu as pltpu
from jax.sharding import PartitionSpec as P

REWEIGHTS = 2
LANES = 128
VMEM_LIMIT = 48 * 1024 * 1024
ROWS_A = 384
ROWS_B = 128


def halves(value):
    top = value.astype(jnp.bfloat16)
    return top, (value - top.astype(jnp.float32)).astype(jnp.bfloat16)


def product(left, right, dims=(((1,), (0,)), ((), ()))):
    return lax.dot_general(left, right, dims, preferred_element_type=jnp.float32)


def prepare_kernel(pairs_ref, prec_ref, hat_top, hat_low, gain_top, gain_low, *, date_pad):
    ifg_total = pairs_ref.shape[1]
    date_total = prec_ref.shape[0]
    pairs = pairs_ref[...]
    date_ids = lax.broadcasted_iota(jnp.int32, (date_total, ifg_total), 0)
    incidence_t = (
        jnp.where(date_ids == pairs[1:2], 1.0, 0.0) - jnp.where(date_ids == pairs[0:1], 1.0, 0.0)
    ).astype(jnp.bfloat16)
    prec = prec_ref[...]
    top, rest = halves(prec)
    middle, low = halves(prec - top.astype(jnp.float32))
    gain = product(top, incidence_t) + (product(middle, incidence_t) + product(low, incidence_t))
    gain_a, gain_b = halves(gain)
    gain_top[pl.ds(0, date_total), :] = gain_a
    gain_low[pl.ds(0, date_total), :] = gain_b
    zeros = jnp.zeros((date_pad - date_total, ifg_total), jnp.bfloat16)
    gain_top[pl.ds(date_total, date_pad - date_total), :] = zeros
    gain_low[pl.ds(date_total, date_pad - date_total), :] = zeros
    incidence = incidence_t.T
    for start in range(0, ifg_total, ROWS_A):
        rows = incidence[start : start + ROWS_A]
        hat = product(rows, gain_a) + product(rows, gain_b)
        hat_a, hat_b = halves(hat)
        hat_top[pl.ds(start, ROWS_A), :] = hat_a
        hat_low[pl.ds(start, ROWS_A), :] = hat_b


def prepare(pairs_t, preconditioner, date_pad):
    ifg_total = pairs_t.shape[1]
    shapes = [(ifg_total, ifg_total)] * 2 + [(date_pad, ifg_total)] * 2
    return pl.pallas_call(
        functools.partial(prepare_kernel, date_pad=date_pad),
        out_shape=[jax.ShapeDtypeStruct(shape, jnp.bfloat16) for shape in shapes],
        compiler_params=pltpu.CompilerParams(vmem_limit_bytes=VMEM_LIMIT),
        name="prepare",
    )(pairs_t, preconditioner)


def invert_kernel(
    data_ref, hat_top, hat_low, gain_top, gain_low, coherence_ref, weighted_ref, basis_ref,
    series_ref, moments_ref, wide, data, residual, moved, *, row_local, date_total,
):
    ifg_total, pixel_count = data.shape
    date_pad = gain_top.shape[0]
    col_local = pixel_count // row_local
    wide[...] = data_ref[...].astype(jnp.float32)
    for row in range(row_local):
        part = wide[pl.ds(row, ifg_total, stride=row_local), :]
        data[:, row * col_local : (row + 1) * col_local] = part.astype(jnp.bfloat16)
    coherence = coherence_ref[...]

    def folded(square):
        return jnp.sum(square.reshape(-1, 8, pixel_count), axis=0)

    def robust(total):
        return jnp.sum(total, axis=0, keepdims=True) / ifg_total + 1e-06

    total = jnp.zeros((8, pixel_count), jnp.float32)
    for start in range(0, ifg_total, ROWS_A):
        rows = pl.ds(start, ROWS_A)
        fit = product(hat_top[rows, :], data[...]) + product(hat_low[rows, :], data[...])
        left = data[rows, :].astype(jnp.float32) - fit
        residual[rows, :] = left
        total = total + folded(left * left)
    for sweep in range(REWEIGHTS):
        scale = robust(total)
        for start in range(0, ifg_total, ROWS_B):
            rows = pl.ds(start, ROWS_B)
            left = residual[rows, :]
            ratio = scale / (left * left + scale)
            moved[rows, :] = (coherence * (ratio * ratio) * left).astype(jnp.bfloat16)
        source = data if sweep == 0 else None
        for start in range(0, date_pad, ROWS_B):
            rows = pl.ds(start, ROWS_B)
            part = product(gain_top[rows, :], moved[...]) + product(gain_low[rows, :], moved[...])
            if sweep == 0:
                part = part + (
                    product(gain_top[rows, :], data[...]) + product(gain_low[rows, :], data[...])
                )
            else:
                part = part + series_ref[rows, :]
            series_ref[rows, :] = part
        if sweep + 1 < REWEIGHTS:
            total = jnp.zeros((8, pixel_count), jnp.float32)
            for start in range(0, ifg_total, ROWS_A):
                rows = pl.ds(start, ROWS_A)
                left = residual[rows, :] - product(hat_top[rows, :], moved[...])
                residual[rows, :] = left
                total = total + folded(left * left)
    series_ref[pl.ds(date_total, 8), :] = basis_ref[...]
    series_top, series_low = halves(series_ref[...])
    weighted_top, weighted_low = halves(weighted_ref[...])
    across = (((1,), (1,)), ((), ()))
    moments_ref[...] = product(weighted_top, series_top, across) + (
        product(weighted_low, series_top, across) + product(weighted_top, series_low, across)
    )


def invert(data, hats, coherence, weighted, basis, row_local, date_total):
    hat_top, hat_low, gain_top, gain_low = hats
    ifg_total = hat_top.shape[0]
    date_pad = gain_top.shape[0]
    pixel_count = coherence.shape[1]
    return pl.pallas_call(
        functools.partial(invert_kernel, row_local=row_local, date_total=date_total),
        out_shape=[
            jax.ShapeDtypeStruct((date_pad, pixel_count), jnp.float32),
            jax.ShapeDtypeStruct((weighted.shape[0], date_pad), jnp.float32),
        ],
        scratch_shapes=[
            pltpu.VMEM(data.shape, jnp.float32),
            pltpu.VMEM((ifg_total, pixel_count), jnp.bfloat16),
            pltpu.VMEM((ifg_total, pixel_count), jnp.float32),
            pltpu.VMEM((ifg_total, pixel_count), jnp.bfloat16),
        ],
        compiler_params=pltpu.CompilerParams(vmem_limit_bytes=VMEM_LIMIT),
        name="invert",
    )(data, *hats, coherence, weighted, basis)


def plane_solve(gram_matrix, right_side):

    def entry(row_pos, col_pos):
        return gram_matrix[row_pos % 3][col_pos % 3]

    cofactors = [
        [
            entry(row_pos + 1, col_pos + 1) * entry(row_pos + 2, col_pos + 2)
            - entry(row_pos + 1, col_pos + 2) * entry(row_pos + 2, col_pos + 1)
            for col_pos in range(3)
        ]
        for row_pos in range(3)
    ]
    determinant = (
        entry(0, 0) * cofactors[0][0]
        + entry(0, 1) * cofactors[0][1]
        + entry(0, 2) * cofactors[0][2]
    )
    return [
        (
            (cofactors[0][col_pos] / determinant) * right_side[0]
            + (cofactors[1][col_pos] / determinant) * right_side[1]
            + (cofactors[2][col_pos] / determinant) * right_side[2]
        )
        for col_pos in range(3)
    ]


def deramp_kernel(first_ref, *refs, row_local, date_total):
    *others, series_ref, member_ref, out_ref = refs
    totals = first_ref[...]
    for other in others:
        totals = totals + other[...]
    planes = []
    for base in (0, 3, 8, 11):
        gram = [
            [
                totals[base + k : base + k + 1, date_total + m : date_total + m + 1]
                + (1.0 if k == m else 0.0)
                for m in range(3)
            ]
            for k in range(3)
        ]
        planes += plane_solve(gram, [totals[base + k : base + k + 1, :] for k in range(3)])
        if base in (3, 11):
            planes += [jnp.zeros_like(planes[0])] * 2
    planes_top, planes_low = halves(jnp.concatenate(planes, axis=0))
    member_top, member_low = halves(member_ref[...])
    ramp = product(
        jnp.concatenate([planes_top, planes_low, planes_top], axis=0),
        jnp.concatenate([member_top, member_top, member_low], axis=0),
        (((0,), (0,)), ((), ())),
    )
    flat = series_ref[pl.ds(0, date_total), :] - ramp[:date_total]
    col_local = flat.shape[1] // row_local
    for row in range(row_local):
        out_ref[pl.ds(row, date_total, stride=row_local), :] = flat[
            :, row * col_local : (row + 1) * col_local
        ]


def deramp(parts, series, member, row_local, date_total):
    col_local = series.shape[1] // row_local
    return pl.pallas_call(
        functools.partial(deramp_kernel, row_local=row_local, date_total=date_total),
        out_shape=jax.ShapeDtypeStruct((date_total * row_local, col_local), jnp.float32),
        compiler_params=pltpu.CompilerParams(vmem_limit_bytes=VMEM_LIMIT),
        name="deramp",
    )(*parts, series, member)


def swap(value, axes, pairs):
    both = [(i, j) for i, j in pairs] + [(j, i) for i, j in pairs]
    return lax.ppermute(value, axes, both)


def local(phases, ifg_pairs, preconditioner, coherence, geo_tiles):
    stack_size = lax.axis_size("stack")
    range_size = lax.axis_size("range")
    azimuth_size = lax.axis_size("azimuth")
    ifg_local, row_local, col_range = phases.shape
    col_local = col_range // stack_size
    pixel_count = row_local * col_local
    date_total = preconditioner.shape[0]
    date_pad = -(-(date_total + 8) // LANES) * LANES
    stack_pos = lax.axis_index("stack")
    block_index = lax.axis_index("range") * stack_size + stack_pos

    blocks = phases.reshape(ifg_local, row_local, stack_size, col_local).transpose(2, 0, 1, 3)
    stacked = lax.all_to_all(blocks, "stack", split_axis=0, concat_axis=0, tiled=True)
    data = stacked.reshape(stack_size * ifg_local * row_local, col_local)

    hats = prepare(ifg_pairs.T, preconditioner, date_pad)

    row_ids = lax.axis_index("azimuth") * row_local + jnp.arange(row_local, dtype=jnp.int32)
    col_ids = block_index * col_local + jnp.arange(col_local, dtype=jnp.int32)
    row_coord = (row_ids.astype(jnp.float32) + 0.5) / (row_local * azimuth_size) - 0.5
    col_coord = (col_ids.astype(jnp.float32) + 0.5) / (col_range * range_size) - 0.5
    shape = (row_local, col_local)
    coord_u = jnp.broadcast_to(row_coord[:, None], shape).reshape(1, pixel_count)
    coord_v = jnp.broadcast_to(col_coord[None, :], shape).reshape(1, pixel_count)
    basis = jnp.concatenate([jnp.ones_like(coord_u), coord_u, coord_v], axis=0)
    coherence_f = coherence.astype(jnp.float32).reshape(1, pixel_count)
    tiles = geo_tiles.reshape(1, pixel_count)

    node = block_index // 2
    even = node % 2 == 0
    first_tile = jnp.where(even, 2 * node + 1, 2 * node - 1)
    second_tile = jnp.where(even, 2 * node - 1, 2 * node + 1)
    spare = jnp.zeros((2, pixel_count), jnp.float32)
    member_rows = []
    for base in (first_tile, second_tile):
        for step in range(2):
            member_rows.append(basis * (tiles == base + step).astype(jnp.float32))
        member_rows.append(spare)
    member = jnp.concatenate(member_rows, axis=0)
    weighted = member * coherence_f
    basis8 = jnp.concatenate([basis, jnp.zeros((5, pixel_count), jnp.float32)], axis=0)

    series, moments = invert(
        data, hats, coherence_f, weighted, basis8, row_local, date_total
    )

    def place(block):
        return (block % stack_size) * range_size + block // stack_size

    block_count = stack_size * range_size
    inner = [
        (place(block), place(block + 2)) for block in range(block_count - 2) if block // 2 % 2 == 0
    ]
    outer = [
        (place(block), place(block + 2)) for block in range(block_count - 2) if block // 2 % 2 == 1
    ]
    axes = ("stack", "range")
    second = swap(moments[8:], axes, outer)
    first = swap(moments[:8], axes, inner)
    moments = moments + jnp.concatenate([first, second], axis=0)
    pairs = [(i, i + 1) for i in range(0, stack_size, 2)]
    crossed = [
        (i * azimuth_size + a, (i + 1) * azimuth_size + (azimuth_size - 1 - a))
        for i in range(0, stack_size, 2)
        for a in range(azimuth_size)
    ]
    parts = [
        moments,
        swap(moments, "azimuth", [(0, 1)]),
        swap(moments, "stack", pairs),
        swap(moments, ("stack", "azimuth"), crossed),
    ]
    flat = deramp(parts, series, member, row_local, date_total)
    return flat.reshape(date_total, row_local, col_local)


def solution(mesh):
    return jax.shard_map(
        local,
        mesh=mesh,
        in_specs=(
            P("stack", "azimuth", "range"),
            P(),
            P(),
            P("azimuth", ("range", "stack")),
            P("azimuth", ("range", "stack")),
        ),
        out_specs=P(None, "azimuth", ("range", "stack")),
        check_vma=False,
    )
```

time: 128 us -> 52.1 us (0.41)
  waiting for transfers between devices: 37.1 us -> 8.57 us
  matrix products: 26.2 us -> 0 us
  between operations: 24.8 us -> 0.08 us
  Pallas kernels: 0 us -> 22.5 us
  blocking collectives: 8.1 us -> 0 us
  starting transfers between devices: 19.6 us -> 12.4 us
  local copies, waits for them, and re-layouts: 11 us -> 7.51 us
    dot_general x14 -> x0, matrix products: 26.2 us -> none  [the longest x2 10.7 us: invert_pixels(): lax.dot_general(incidence, weight * residual, (((0,), (0,)), ((), ())), p...]
    all_to_all x1, waiting for transfers between devices: 25.5 us -> 2.52 us  [local(): lax.all_to_all(blocks, 'stack', split_axis=0, concat_axis=0, tiled=True)]
    pallas_call x0 -> x3, Pallas kernels: none -> 22.5 us  [the longest x1 10.7 us: prepare(): pl.pallas_call(functools.partial(prepare_kernel, date_pad=date_pad), out_...]
    psum x1 -> x0, blocking collectives: 8.1 us -> none  [local(): moments, gram_matrix = lax.psum((moments, gram_matrix), 'azimuth')]
    ppermute x8 -> x5, starting transfers between devices: 12.3 us -> 4.95 us  [swap(): return lax.ppermute(value, axes, both)]
    ppermute x8 -> x5, waiting for transfers between devices: 11.7 us -> 6.05 us  [swap(): return lax.ppermute(value, axes, both)]
    all_to_all x1 -> x0, local copies, waits for them, and re-layouts: 3.28 us -> none  [local(): lax.all_to_all(phases, 'stack', split_axis=2, concat_axis=0, tiled=True)]
    unnamed x9 -> x18, local copies, waits for them, and re-layouts: 4.79 us -> 6.08 us
  transfers between devices with their start and end apart: 9 -> 6, of which waited for: 6 -> 5; matrix products, arithmetic and copies ran while one was open for 2% -> 1% of each run, Pallas kernels for 0% -> 21%
where the time goes in v1:
time: 52.1 us; the launch traced here: 51.1 us
  Pallas kernels  22.5 us (43%)
  starting transfers between devices  12.4 us (24%)
  waiting for transfers between devices  8.57 us (16%)
  local copies, waits for them, and re-layouts  7.51 us (14%)
    pallas_call x1, Pallas kernels, prepare(): pl.pallas_call(functools.partial(prepare_kernel, date_pad=date_pad), out_...  10.7 us
    pallas_call x1, Pallas kernels, invert(): pl.pallas_call(functools.partial(invert_kernel, row_local=row_local, date...  10.2 us
    all_to_all x1, starting transfers between devices, local(): lax.all_to_all(blocks, 'stack', split_axis=0, concat_axis=0, tiled=True)  7.41 us
    unnamed x18, local copies, waits for them, and re-layouts  6.08 us
    ppermute x5, waiting for transfers between devices, swap(): return lax.ppermute(value, axes, both)  6.05 us
    ppermute x5, starting transfers between devices, swap(): return lax.ppermute(value, axes, both)  4.95 us
    all_to_all x1, waiting for transfers between devices, local(): lax.all_to_all(blocks, 'stack', split_axis=0, concat_axis=0, tiled=True)  2.52 us
    pallas_call x1, Pallas kernels, deramp(): pl.pallas_call(functools.partial(deramp_kernel, row_local=row_local, date...  1.56 us
  transfers between devices with their start and end apart: 6, of which 5 were waited for; matrix products, arithmetic and copies ran while one was open for 1% of the time, Pallas kernels for 21%

profile of v1, /device:TPU:0, one launch (start us, length us, event | category | flops | bytes accessed | tf_op | source)
XLA Modules:
  0.0 51.1 jit_solution(13652975364669413995)
XLA Ops:
  0.0 0.0 copy-start
  0.0 0.0 copy-start.7
  0.0 0.0 copy-start.1
  0.0 0.0 copy-start.6
  0.0 1.1 %copy-done = bf16[144,2,1024]{2,1,0:T(2,128)(2,1)S(1)} copy-done((bf16[144,2,1024]{2,1,0:T(2,128)(2,1)S(1)}, bf16[144,2,1024]{2,1,0:T(2,128)(2,1)}, u32[]{:S(2)}) %copy-start) | copy-done | bytes 589848
  1.1 1.2 %bitcast_bitcast_fusion = bf16[8,144,2,128]{3,2,1,0:T(2,128)(2,1)} fusion(bf16[144,2,1024]{2,1,0:T(2,128)(2,1)S(1)} %copy-done), kind=kLoop, calls=%fused_computation | loop fusion | bytes 1179648 | tf_op jit(solution)/shard_map/transpose | solution.py:234
  2.3 7.4 %all-to-all-start = ((bf16[8,144,2,128]{3,2,1,0:T(2,128)(2,1)}), bf16[8,144,2,128]{3,2,1,0:T(2,128)(2,1)S(1)}, u32[]{:S(2)}, u32[]{:S(2)}) async-start(bf16[8,144,2,128]{3,2,1,0:T(2,128)(2,1)} %bitcast_bitcast_fusion), calls=%async_computation | async-start | bytes 1179648 | tf_op jit(solution)/shard_map/all_to_all | solution.py:235
  9.7 0.0 copy-done.7
  9.7 0.1 pad.5.clone
  9.8 0.0 copy-done.1
  9.8 0.0 copy-done.6
  9.8 10.7 %prepare.1 = (bf16[1152,1152]{1,0:T(8,128)(2,1)}, bf16[1152,1152]{1,0:T(8,128)(2,1)}, bf16[640,1152]{1,0:T(8,128)(2,1)S(1)}, bf16[640,1152]{1,0:T(8,128)(2,1)S(1)}) custom-call(s32[2,1152]{1,0:T(2,128)S(1)} %bitcast.24, f32[600,600]{1,0:T(8,128)S(1)} %copy-done.1), custom_call_target="tpu_custom_call" | custom-call | tf_op jit(solution)/shard_map/prepare/pallas_call | solution.py:56
  20.6 1.1 %copy-done.2 = bf16[640,1152]{1,0:T(8,128)(2,1)} copy-done((bf16[640,1152]{1,0:T(8,128)(2,1)}, bf16[640,1152]{1,0:T(8,128)(2,1)S(1)}, u32[]{:S(2)}) %copy-start.2) | copy-done | bytes 1474584
  21.7 1.1 %copy-done.4 = bf16[640,1152]{1,0:T(8,128)(2,1)} copy-done((bf16[640,1152]{1,0:T(8,128)(2,1)}, bf16[640,1152]{1,0:T(8,128)(2,1)S(1)}, u32[]{:S(2)}) %copy-start.4) | copy-done | bytes 1474584
  22.8 0.1 broadcast_in_dim.22
  23.0 0.0 copy-done.8
  23.0 0.1 maximum_maximum_fusion.basis_ref
  23.1 2.5 %all-to-all-done = bf16[8,144,2,128]{3,2,1,0:T(2,128)(2,1)S(1)} async-done(((bf16[8,144,2,128]{3,2,1,0:T(2,128)(2,1)}), bf16[8,144,2,128]{3,2,1,0:T(2,128)(2,1)S(1)}, u32[]{:S(2)}, u32[]{:S(2)}) %all-to-all-start) | async-done | bytes 589856 | tf_op jit(solution)/shard_map/all_to_all | solution.py:235
  25.6 1.4 %copy-done.3 = bf16[640,1152]{1,0:T(8,128)(2,1)S(1)} copy-done((bf16[640,1152]{1,0:T(8,128)(2,1)S(1)}, bf16[640,1152]{1,0:T(8,128)(2,1)}, u32[]{:S(2)}) %copy-start.3) | copy-done | bytes 1474584
  27.0 1.4 %copy-done.5 = bf16[640,1152]{1,0:T(8,128)(2,1)S(1)} copy-done((bf16[640,1152]{1,0:T(8,128)(2,1)S(1)}, bf16[640,1152]{1,0:T(8,128)(2,1)}, u32[]{:S(2)}) %copy-start.5) | copy-done | bytes 1474584
  28.3 10.2 %invert.1 = (f32[640,256]{1,0:T(8,128)S(1)}, f32[16,640]{1,0:T(8,128)S(1)}) custom-call(bf16[2304,128]{1,0:T(8,128)(2,1)S(1)} %bitcast.23, bf16[1152,1152]{1,0:T(8,128)(2,1)} %get-tuple-element.11.hat_top, bf16[1152,1152]{1,0:T(8,128)(2,1)} %get-tuple-element.12.hat_low, bf16[640,1152]{1,0:T(8,128)(2,1)S(1)} %copy-done.3, bf16[640,1152]{1,0:T(8,128)(2,1)S(1)} %copy-done.5, ...), custom_call_target="tpu_custom_call" | custom-call | tf_op jit(solution)/shard_map/invert/pallas_call | solution.py:129
  38.5 0.7 %collective-permute-start = (f32[8,640]{1,0:T(8,128)S(1)}, f32[8,640]{1,0:T(8,128)S(1)}, u32[]{:S(2)}, u32[]{:S(2)}) collective-permute-start(f32[8,640]{1,0:T(8,128)S(1)} %get-tuple-element.17), channel_id=1, source_target_pairs={{0,8},{4,12},{16,24},{20,28},{1,9},{5,13},{17,25},{21,29},{8,0},{1... | collective-permute-start | bytes 61448 | tf_op jit(solution)/shard_map/ppermute | solution.py:219
  39.3 0.7 %collective-permute-start.1 = (f32[8,640]{1,0:T(8,128)S(1)}, f32[8,640]{1,0:T(8,128)S(1)}, u32[]{:S(2)}, u32[]{:S(2)}) collective-permute-start(f32[8,640]{1,0:T(8,128)S(1)} %get-tuple-element.18), channel_id=1, source_target_pairs={{8,16},{12,20},{24,1},{28,5},{9,17},{13,21},{16,8},{20,12},{1,24},... | collective-permute-start | bytes 61448 | tf_op jit(solution)/shard_map/ppermute | solution.py:219
  39.9 2.4 %collective-permute-done = f32[8,640]{1,0:T(8,128)S(1)} collective-permute-done((f32[8,640]{1,0:T(8,128)S(1)}, f32[8,640]{1,0:T(8,128)S(1)}, u32[]{:S(2)}, u32[]{:S(2)}) %collective-permute-start) | collective-permute-done | bytes 20512 | tf_op jit(solution)/shard_map/ppermute | solution.py:219
  42.4 0.0 collective-permute-done.1
  42.4 2.5 %collective-permute-start.4 = (f32[16,640]{1,0:T(8,128)S(1)}, f32[16,640]{1,0:T(8,128)S(1)}, u32[]{:S(2)}, u32[]{:S(2)}) collective-permute-start(f32[16,640]{1,0:T(8,128)S(1)} %maximum_add_fusion.first_ref), channel_id=1, source_target_pairs={{0,6},{2,4},{8,14},{10,12},{16,22},{18,20},{24,30},{26,28},{6,0},{... | collective-permute-start | bytes 122888 | tf_op jit(solution)/shard_map/ppermute | solution.py:219
  44.8 0.5 %collective-permute-start.3 = (f32[16,640]{1,0:T(8,128)S(1)}, f32[16,640]{1,0:T(8,128)S(1)}, u32[]{:S(2)}, u32[]{:S(2)}) collective-permute-start(f32[16,640]{1,0:T(8,128)S(1)} %maximum_add_fusion.first_ref), channel_id=1, source_target_pairs={{0,4},{8,12},{16,20},{24,28},{4,0},{12,8},{20,16},{28,24},{1,5},{9... | collective-permute-start | bytes 122888 | tf_op jit(solution)/shard_map/ppermute | solution.py:219
  45.4 0.5 %collective-permute-start.2 = (f32[16,640]{1,0:T(8,128)S(1)}, f32[16,640]{1,0:T(8,128)S(1)}, u32[]{:S(2)}, u32[]{:S(2)}) collective-permute-start(f32[16,640]{1,0:T(8,128)S(1)} %maximum_add_fusion.first_ref), channel_id=1, source_target_pairs={{0,2},{2,0},{1,3},{3,1},{4,6},{6,4},{5,7},{7,5},{8,10},{10,8},{9,1... | collective-permute-start | bytes 122888 | tf_op jit(solution)/shard_map/ppermute | solution.py:219
  45.9 1.4 %collective-permute-done.4.refs_2_ = f32[16,640]{1,0:T(8,128)S(1)} collective-permute-done((f32[16,640]{1,0:T(8,128)S(1)}, f32[16,640]{1,0:T(8,128)S(1)}, u32[]{:S(2)}, u32[]{:S(2)}) %collective-permute-start.4) | collective-permute-done | bytes 40992 | tf_op jit(solution)/shard_map/ppermute | solution.py:219
  47.3 1.5 %collective-permute-done.3.refs_1_ = f32[16,640]{1,0:T(8,128)S(1)} collective-permute-done((f32[16,640]{1,0:T(8,128)S(1)}, f32[16,640]{1,0:T(8,128)S(1)}, u32[]{:S(2)}, u32[]{:S(2)}) %collective-permute-start.3) | collective-permute-done | bytes 40992 | tf_op jit(solution)/shard_map/ppermute | solution.py:219
  48.9 0.7 %collective-permute-done.2.refs_0_ = f32[16,640]{1,0:T(8,128)S(1)} collective-permute-done((f32[16,640]{1,0:T(8,128)S(1)}, f32[16,640]{1,0:T(8,128)S(1)}, u32[]{:S(2)}, u32[]{:S(2)}) %collective-permute-start.2) | collective-permute-done | bytes 40992 | tf_op jit(solution)/shard_map/ppermute | solution.py:219
  49.5 1.6 %deramp.1 = f32[1200,128]{1,0:T(8,128)} custom-call(f32[16,640]{1,0:T(8,128)S(1)} %maximum_add_fusion.first_ref, f32[16,640]{1,0:T(8,128)S(1)} %collective-permute-done.2.refs_0_, f32[16,640]{1,0:T(8,128)S(1)} %collective-permute-done.3.refs_1_, f32[16,640]{1,0:T(8,128)S(1)} %collective-permute-done.4.refs_2_, f32[640,256]{1,0:T(8,128)S(1)} %get-tuple-element.16.refs_3_, ...), custom_call_target="tpu_custom_call" | custom-call | tf_op jit(solution)/shard_map/deramp/pallas_call | solution.py:209
  (18 shorter events, 0.1 us)
Async XLA Ops:
  0.0 1.1 %copy-start = (bf16[144,2,1024]{2,1,0:T(2,128)(2,1)S(1)}, bf16[144,2,1024]{2,1,0:T(2,128)(2,1)}, u32[]{:S(2)}) copy-start(bf16[144,2,1024]{2,1,0:T(2,128)(2,1)} %param.5) | copy-start | bytes 1769476
  0.0 9.7 %copy-start.7 = (s32[2,128]{1,0:T(2,128)S(1)}, s32[2,128]{1,0:T(2,128)}, u32[]{:S(2)}) copy-start(s32[2,128]{1,0:T(2,128)} %param.9) | copy-start | bytes 3076
  0.0 9.8 %copy-start.1 = (f32[600,600]{1,0:T(8,128)S(1)}, f32[600,600]{1,0:T(8,128)}, u32[]{:S(2)}) copy-start(f32[600,600]{1,0:T(8,128)} %prec_ref.1) | copy-start | bytes 4320004
  0.0 9.8 %copy-start.6 = (s32[1152,2]{0,1:T(2,128)S(1)}, s32[1152,2]{0,1:T(2,128)}, u32[]{:S(2)}) copy-start(s32[1152,2]{0,1:T(2,128)} %param.6) | copy-start | bytes 27652
  2.3 20.7 %copy-start.8 = (s32[2,128]{1,0:T(2,128)S(1)}, s32[2,128]{1,0:T(2,128)}, u32[]{:S(2)}) copy-start(s32[2,128]{1,0:T(2,128)} %param.8) | copy-start | bytes 3076
  2.3 23.3 %all-to-all-start = ((bf16[8,144,2,128]{3,2,1,0:T(2,128)(2,1)}), bf16[8,144,2,128]{3,2,1,0:T(2,128)(2,1)S(1)}, u32[]{:S(2)}, u32[]{:S(2)}) async-start(bf16[8,144,2,128]{3,2,1,0:T(2,128)(2,1)} %bitcast_bitcast_fusion), calls=%async_computation | async-start | bytes 1179648 | tf_op jit(solution)/shard_map/all_to_all | solution.py:235
  20.6 1.1 %copy-start.2 = (bf16[640,1152]{1,0:T(8,128)(2,1)}, bf16[640,1152]{1,0:T(8,128)(2,1)S(1)}, u32[]{:S(2)}) copy-start(bf16[640,1152]{1,0:T(8,128)(2,1)S(1)} %get-tuple-element.13.gain_top) | copy-start | bytes 4423684
  21.7 1.1 %copy-start.4 = (bf16[640,1152]{1,0:T(8,128)(2,1)}, bf16[640,1152]{1,0:T(8,128)(2,1)S(1)}, u32[]{:S(2)}) copy-start(bf16[640,1152]{1,0:T(8,128)(2,1)S(1)} %get-tuple-element.14.gain_low) | copy-start | bytes 4423684
  25.6 1.4 %copy-start.3 = (bf16[640,1152]{1,0:T(8,128)(2,1)S(1)}, bf16[640,1152]{1,0:T(8,128)(2,1)}, u32[]{:S(2)}) copy-start(bf16[640,1152]{1,0:T(8,128)(2,1)} %copy-done.2) | copy-start | bytes 4423684
  27.0 1.4 %copy-start.5 = (bf16[640,1152]{1,0:T(8,128)(2,1)S(1)}, bf16[640,1152]{1,0:T(8,128)(2,1)}, u32[]{:S(2)}) copy-start(bf16[640,1152]{1,0:T(8,128)(2,1)} %copy-done.4) | copy-start | bytes 4423684
  38.5 3.8 %collective-permute-start = (f32[8,640]{1,0:T(8,128)S(1)}, f32[8,640]{1,0:T(8,128)S(1)}, u32[]{:S(2)}, u32[]{:S(2)}) collective-permute-start(f32[8,640]{1,0:T(8,128)S(1)} %get-tuple-element.17), channel_id=1, source_target_pairs={{0,8},{4,12},{16,24},{20,28},{1,9},{5,13},{17,25},{21,29},{8,0},{1... | collective-permute-start | bytes 61448 | tf_op jit(solution)/shard_map/ppermute | solution.py:219
  39.3 3.1 %collective-permute-start.1 = (f32[8,640]{1,0:T(8,128)S(1)}, f32[8,640]{1,0:T(8,128)S(1)}, u32[]{:S(2)}, u32[]{:S(2)}) collective-permute-start(f32[8,640]{1,0:T(8,128)S(1)} %get-tuple-element.18), channel_id=1, source_target_pairs={{8,16},{12,20},{24,1},{28,5},{9,17},{13,21},{16,8},{20,12},{1,24},... | collective-permute-start | bytes 61448 | tf_op jit(solution)/shard_map/ppermute | solution.py:219
  42.4 5.0 %collective-permute-start.4 = (f32[16,640]{1,0:T(8,128)S(1)}, f32[16,640]{1,0:T(8,128)S(1)}, u32[]{:S(2)}, u32[]{:S(2)}) collective-permute-start(f32[16,640]{1,0:T(8,128)S(1)} %maximum_add_fusion.first_ref), channel_id=1, source_target_pairs={{0,6},{2,4},{8,14},{10,12},{16,22},{18,20},{24,30},{26,28},{6,0},{... | collective-permute-start | bytes 122888 | tf_op jit(solution)/shard_map/ppermute | solution.py:219
  44.8 4.0 %collective-permute-start.3 = (f32[16,640]{1,0:T(8,128)S(1)}, f32[16,640]{1,0:T(8,128)S(1)}, u32[]{:S(2)}, u32[]{:S(2)}) collective-permute-start(f32[16,640]{1,0:T(8,128)S(1)} %maximum_add_fusion.first_ref), channel_id=1, source_target_pairs={{0,4},{8,12},{16,20},{24,28},{4,0},{12,8},{20,16},{28,24},{1,5},{9... | collective-permute-start | bytes 122888 | tf_op jit(solution)/shard_map/ppermute | solution.py:219
  45.4 4.1 %collective-permute-start.2 = (f32[16,640]{1,0:T(8,128)S(1)}, f32[16,640]{1,0:T(8,128)S(1)}, u32[]{:S(2)}, u32[]{:S(2)}) collective-permute-start(f32[16,640]{1,0:T(8,128)S(1)} %maximum_add_fusion.first_ref), channel_id=1, source_target_pairs={{0,2},{2,0},{1,3},{3,1},{4,6},{6,4},{5,7},{7,5},{8,10},{10,8},{9,1... | collective-permute-start | bytes 122888 | tf_op jit(solution)/shard_map/ppermute | solution.py:219

commit v2 on v1

--- a/solution.py
+++ b/solution.py
@@ -9,9 +9,11 @@
 
 REWEIGHTS = 2
 LANES = 128
-VMEM_LIMIT = 48 * 1024 * 1024
-ROWS_A = 384
+VMEM_LIMIT = 24 * 1024 * 1024
+ROWS_A = 128
 ROWS_B = 128
+ARRIVAL = (0, 1, 4, 5, 2, 6, 7, 3)
+EARLY = 6
 
 
 def halves(value):
@@ -23,95 +25,155 @@
     return lax.dot_general(left, right, dims, preferred_element_type=jnp.float32)
 
 
-def prepare_kernel(pairs_ref, prec_ref, hat_top, hat_low, gain_top, gain_low, *, date_pad):
-    ifg_total = pairs_ref.shape[1]
+def prepare_kernel(place_ref, pairs_ref, prec_ref, incidence_ref, gain_top, gain_low, pairs, *, order):
+    chunk = pairs_ref.shape[2]
     date_total = prec_ref.shape[0]
-    pairs = pairs_ref[...]
-    date_ids = lax.broadcasted_iota(jnp.int32, (date_total, ifg_total), 0)
+    date_pad, ifg_total = gain_top.shape
+    place = place_ref[0]
+    for position, mask in enumerate(order):
+        pairs[:, position * chunk : (position + 1) * chunk] = pairs_ref[place ^ mask]
+    date_ids = lax.broadcasted_iota(jnp.int32, (date_pad, ifg_total), 0)
     incidence_t = (
-        jnp.where(date_ids == pairs[1:2], 1.0, 0.0) - jnp.where(date_ids == pairs[0:1], 1.0, 0.0)
+        jnp.where(date_ids == pairs[1:2, :], 1.0, 0.0)
+        - jnp.where(date_ids == pairs[0:1, :], 1.0, 0.0)
     ).astype(jnp.bfloat16)
+    incidence_ref[...] = incidence_t.T
     prec = prec_ref[...]
     top, rest = halves(prec)
     middle, low = halves(prec - top.astype(jnp.float32))
-    gain = product(top, incidence_t) + (product(middle, incidence_t) + product(low, incidence_t))
+    used = incidence_t[:date_total]
+    gain = product(top, used) + (product(middle, used) + product(low, used))
     gain_a, gain_b = halves(gain)
-    gain_top[pl.ds(0, date_total), :] = gain_a
-    gain_low[pl.ds(0, date_total), :] = gain_b
     zeros = jnp.zeros((date_pad - date_total, ifg_total), jnp.bfloat16)
-    gain_top[pl.ds(date_total, date_pad - date_total), :] = zeros
-    gain_low[pl.ds(date_total, date_pad - date_total), :] = zeros
-    incidence = incidence_t.T
-    for start in range(0, ifg_total, ROWS_A):
-        rows = incidence[start : start + ROWS_A]
-        hat = product(rows, gain_a) + product(rows, gain_b)
-        hat_a, hat_b = halves(hat)
-        hat_top[pl.ds(start, ROWS_A), :] = hat_a
-        hat_low[pl.ds(start, ROWS_A), :] = hat_b
-
-
-def prepare(pairs_t, preconditioner, date_pad):
-    ifg_total = pairs_t.shape[1]
-    shapes = [(ifg_total, ifg_total)] * 2 + [(date_pad, ifg_total)] * 2
+    gain_top[...] = jnp.concatenate([gain_a, zeros], axis=0)
+    gain_low[...] = jnp.concatenate([gain_b, zeros], axis=0)
+
+
+def prepare(place, pairs, preconditioner, date_pad, order):
+    ifg_total = pairs.shape[0] * pairs.shape[2]
+    shapes = [(ifg_total, date_pad)] + [(date_pad, ifg_total)] * 2
+    whole = pl.BlockSpec(memory_space=pltpu.VMEM)
     return pl.pallas_call(
-        functools.partial(prepare_kernel, date_pad=date_pad),
+        functools.partial(prepare_kernel, order=order),
         out_shape=[jax.ShapeDtypeStruct(shape, jnp.bfloat16) for shape in shapes],
+        in_specs=[pl.BlockSpec(memory_space=pltpu.SMEM), whole, whole],
+        out_specs=[whole] * 3,
+        scratch_shapes=[pltpu.VMEM((2, ifg_total), jnp.int32)],
         compiler_params=pltpu.CompilerParams(vmem_limit_bytes=VMEM_LIMIT),
         name="prepare",
-    )(pairs_t, preconditioner)
-
-
-def invert_kernel(
-    data_ref, hat_top, hat_low, gain_top, gain_low, coherence_ref, weighted_ref, basis_ref,
-    series_ref, moments_ref, wide, data, residual, moved, *, row_local, date_total,
-):
+    )(place, pairs, preconditioner)
+
+
+def unpack(chunk_refs, wide, data, row_local):
+    start = 0
+    col_local = chunk_refs[0].shape[1]
+    for ref in chunk_refs:
+        count = ref.shape[0] // row_local
+        wide[pl.ds(0, ref.shape[0]), :] = ref[...].astype(jnp.float32)
+        for row in range(row_local):
+            data[pl.ds(start, count), row * col_local : (row + 1) * col_local] = wide[
+                pl.ds(row, count, stride=row_local), :
+            ].astype(jnp.bfloat16)
+        start += count
+
+
+def gained(gain_top, gain_low, rows, columns, value):
+    part = product(gain_top[rows, columns], value)
+    if gain_low is not None:
+        part = part + product(gain_low[rows, columns], value)
+    return part
+
+
+def early_kernel(*refs, row_local):
+    *chunk_refs, gain_top, gain_low, data_ref, series_ref, wide = refs
+    unpack(chunk_refs, wide, data_ref, row_local)
+    columns = pl.ds(0, data_ref.shape[0] // 256 * 256)
+    for start in range(0, series_ref.shape[0], ROWS_B):
+        rows = pl.ds(start, ROWS_B)
+        series_ref[rows, :] = gained(gain_top, gain_low, rows, columns, data_ref[columns, :])
+
+
+def early_fit(chunks, gains, row_local):
+    count = sum(chunk.shape[0] for chunk in chunks) // row_local
+    pixel_count = chunks[0].shape[1] * row_local
+    return pl.pallas_call(
+        functools.partial(early_kernel, row_local=row_local),
+        out_shape=[
+            jax.ShapeDtypeStruct((count, pixel_count), jnp.bfloat16),
+            jax.ShapeDtypeStruct((gains[0].shape[0], pixel_count), jnp.float32),
+        ],
+        scratch_shapes=[pltpu.VMEM(chunks[0].shape, jnp.float32)],
+        compiler_params=pltpu.CompilerParams(vmem_limit_bytes=VMEM_LIMIT),
+        name="early_fit",
+    )(*chunks, *gains)
+
+
+def invert_kernel(*refs, row_local, date_total, late):
+    (
+        *chunk_refs, incidence, gain_top, gain_low, coherence_ref, weighted_ref, basis_ref,
+        series_ref, moments_ref, wide, data, residual, moved,
+    ) = refs
     ifg_total, pixel_count = data.shape
     date_pad = gain_top.shape[0]
-    col_local = pixel_count // row_local
-    wide[...] = data_ref[...].astype(jnp.float32)
-    for row in range(row_local):
-        part = wide[pl.ds(row, ifg_total, stride=row_local), :]
-        data[:, row * col_local : (row + 1) * col_local] = part.astype(jnp.bfloat16)
+    late_refs, early_refs = chunk_refs[:late], chunk_refs[late:]
+    done = 0
+    if early_refs:
+        early_data, early_series = early_refs
+        held = early_data.shape[0]
+        done = held // 256 * 256
+        data[pl.ds(0, held), :] = early_data[...]
+        unpack(late_refs, wide, data.at[pl.ds(held, ifg_total - held)], row_local)
+    else:
+        unpack(late_refs, wide, data, row_local)
     coherence = coherence_ref[...]
+    date_tiles = [pl.ds(start, ROWS_B) for start in range(0, date_pad, ROWS_B)]
+    ifg_tiles = [pl.ds(start, ROWS_A) for start in range(0, ifg_total, ROWS_A)]
+    everything = slice(None)
 
     def folded(square):
         return jnp.sum(square.reshape(-1, 8, pixel_count), axis=0)
 
-    def robust(total):
-        return jnp.sum(total, axis=0, keepdims=True) / ifg_total + 1e-06
-
+    def reweighted(total):
+        scale = jnp.sum(total, axis=0, keepdims=True) / ifg_total + 1e-06
+        for rows in ifg_tiles:
+            left = residual[rows, :]
+            ratio = scale / (left * left + scale)
+            moved[rows, :] = (coherence * (ratio * ratio) * left).astype(jnp.bfloat16)
+
+    left_columns = pl.ds(done, ifg_total - done)
+    tops, lows = [], []
+    for rows in date_tiles:
+        part = gained(gain_top, gain_low, rows, left_columns, data[left_columns, :])
+        if early_refs:
+            part = part + early_series[rows, :]
+        series_ref[rows, :] = part
+        top, low = halves(part)
+        tops.append(top)
+        lows.append(low)
+    top, low = jnp.concatenate(tops, axis=0), jnp.concatenate(lows, axis=0)
     total = jnp.zeros((8, pixel_count), jnp.float32)
-    for start in range(0, ifg_total, ROWS_A):
-        rows = pl.ds(start, ROWS_A)
-        fit = product(hat_top[rows, :], data[...]) + product(hat_low[rows, :], data[...])
+    for rows in ifg_tiles:
+        fit = product(incidence[rows, :], top) + product(incidence[rows, :], low)
         left = data[rows, :].astype(jnp.float32) - fit
         residual[rows, :] = left
         total = total + folded(left * left)
-    for sweep in range(REWEIGHTS):
-        scale = robust(total)
-        for start in range(0, ifg_total, ROWS_B):
-            rows = pl.ds(start, ROWS_B)
-            left = residual[rows, :]
-            ratio = scale / (left * left + scale)
-            moved[rows, :] = (coherence * (ratio * ratio) * left).astype(jnp.bfloat16)
-        source = data if sweep == 0 else None
-        for start in range(0, date_pad, ROWS_B):
-            rows = pl.ds(start, ROWS_B)
-            part = product(gain_top[rows, :], moved[...]) + product(gain_low[rows, :], moved[...])
-            if sweep == 0:
-                part = part + (
-                    product(gain_top[rows, :], data[...]) + product(gain_low[rows, :], data[...])
-                )
-            else:
-                part = part + series_ref[rows, :]
-            series_ref[rows, :] = part
-        if sweep + 1 < REWEIGHTS:
-            total = jnp.zeros((8, pixel_count), jnp.float32)
-            for start in range(0, ifg_total, ROWS_A):
-                rows = pl.ds(start, ROWS_A)
-                left = residual[rows, :] - product(hat_top[rows, :], moved[...])
-                residual[rows, :] = left
-                total = total + folded(left * left)
+    reweighted(total)
+    for sweep in range(1, REWEIGHTS):
+        steps = []
+        for rows in date_tiles:
+            part = gained(gain_top, gain_low, rows, everything, moved[...])
+            steps.append(part.astype(jnp.bfloat16))
+            series_ref[rows, :] = series_ref[rows, :] + part
+        step = jnp.concatenate(steps, axis=0)
+        total = jnp.zeros((8, pixel_count), jnp.float32)
+        for rows in ifg_tiles:
+            left = residual[rows, :] - product(incidence[rows, :], step)
+            residual[rows, :] = left
+            total = total + folded(left * left)
+        reweighted(total)
+    for rows in date_tiles:
+        part = gained(gain_top, None, rows, everything, moved[...])
+        series_ref[rows, :] = series_ref[rows, :] + part
     series_ref[pl.ds(date_total, 8), :] = basis_ref[...]
     series_top, series_low = halves(series_ref[...])
     weighted_top, weighted_low = halves(weighted_ref[...])
@@ -121,26 +183,51 @@
     )
 
 
-def invert(data, hats, coherence, weighted, basis, row_local, date_total):
-    hat_top, hat_low, gain_top, gain_low = hats
-    ifg_total = hat_top.shape[0]
-    date_pad = gain_top.shape[0]
+def invert(late_chunks, early, incidence, gains, coherence, weighted, basis, row_local, date_total):
+    ifg_total = incidence.shape[0]
+    date_pad = gains[0].shape[0]
     pixel_count = coherence.shape[1]
     return pl.pallas_call(
-        functools.partial(invert_kernel, row_local=row_local, date_total=date_total),
+        functools.partial(
+            invert_kernel, row_local=row_local, date_total=date_total, late=len(late_chunks)
+        ),
         out_shape=[
             jax.ShapeDtypeStruct((date_pad, pixel_count), jnp.float32),
             jax.ShapeDtypeStruct((weighted.shape[0], date_pad), jnp.float32),
         ],
         scratch_shapes=[
-            pltpu.VMEM(data.shape, jnp.float32),
+            pltpu.VMEM(late_chunks[0].shape, jnp.float32),
             pltpu.VMEM((ifg_total, pixel_count), jnp.bfloat16),
             pltpu.VMEM((ifg_total, pixel_count), jnp.float32),
             pltpu.VMEM((ifg_total, pixel_count), jnp.bfloat16),
         ],
         compiler_params=pltpu.CompilerParams(vmem_limit_bytes=VMEM_LIMIT),
         name="invert",
-    )(data, *hats, coherence, weighted, basis)
+    )(*late_chunks, *early, incidence, *gains, coherence, weighted, basis)
+
+
+def exchange(phases, stack_pos, stack_size):
+    ifg_local, row_local, col_range = phases.shape
+    col_local = col_range // stack_size
+    if stack_size != 8:
+        blocks = phases.reshape(ifg_local, row_local, stack_size, col_local).transpose(2, 0, 1, 3)
+        stacked = lax.all_to_all(blocks, "stack", split_axis=0, concat_axis=0, tiled=True)
+        return [stacked.reshape(-1, col_local)], []
+    blocks = [
+        lax.dynamic_slice_in_dim(phases, (stack_pos ^ mask) * col_local, col_local, axis=2)
+        for mask in range(stack_size)
+    ]
+    found = {0: blocks[0]}
+
+    def send(mask, after=None):
+        block = blocks[mask]
+        if after is not None:
+            block, found[after] = lax.optimization_barrier((block, found[after]))
+        found[mask] = lax.ppermute(block, "stack", [(i, i ^ mask) for i in range(stack_size)])
+
+    for mask, after in ((4, None), (5, None), (1, None), (6, None), (2, None), (7, 1), (3, 2)):
+        send(mask, after)
+    return [found[mask].reshape(-1, col_local) for mask in ARRIVAL], ARRIVAL
 
 
 def plane_solve(gram_matrix, right_side):
@@ -231,11 +318,19 @@
     stack_pos = lax.axis_index("stack")
     block_index = lax.axis_index("range") * stack_size + stack_pos
 
-    blocks = phases.reshape(ifg_local, row_local, stack_size, col_local).transpose(2, 0, 1, 3)
-    stacked = lax.all_to_all(blocks, "stack", split_axis=0, concat_axis=0, tiled=True)
-    data = stacked.reshape(stack_size * ifg_local * row_local, col_local)
-
-    hats = prepare(ifg_pairs.T, preconditioner, date_pad)
+    chunks, order = exchange(phases, stack_pos, stack_size)
+    pairs = ifg_pairs.T.reshape(2, stack_size, ifg_local).transpose(1, 0, 2)
+    place = stack_pos
+    if not order:
+        pairs = ifg_pairs.T[None]
+        place, order = jnp.int32(0), [0]
+    incidence, *gains = prepare(
+        place.astype(jnp.int32).reshape(1), pairs, preconditioner, date_pad, order
+    )
+    early = []
+    if len(chunks) > EARLY:
+        early = early_fit(chunks[:EARLY], gains, row_local)
+        chunks = chunks[EARLY:]
 
     row_ids = lax.axis_index("azimuth") * row_local + jnp.arange(row_local, dtype=jnp.int32)
     col_ids = block_index * col_local + jnp.arange(col_local, dtype=jnp.int32)
@@ -263,7 +358,7 @@
     basis8 = jnp.concatenate([basis, jnp.zeros((5, pixel_count), jnp.float32)], axis=0)
 
     series, moments = invert(
-        data, hats, coherence_f, weighted, basis8, row_local, date_total
+        chunks, early, incidence, gains, coherence_f, weighted, basis8, row_local, date_total
     )
 
     def place(block):

time: 52.1 us -> 41.3 us (0.79)
  the two profiles are of different devices: /device:TPU:0 before, /device:TPU:8 now
where the time goes in v2:
time: 41.3 us; the launch traced here: 41.1 us
  starting transfers between devices  19.8 us (48%)
  Pallas kernels  11.8 us (29%)
  waiting for transfers between devices  5.93 us (14%)
  local copies, waits for them, and re-layouts  1.96 us (5%)
  other arithmetic  1.48 us (4%)
    ppermute x7, starting transfers between devices, send(): lax.ppermute(block, 'stack', [(i, i ^ mask) for i in range(stack_size)])  10.3 us
    ppermute x5, starting transfers between devices, swap(): return lax.ppermute(value, axes, both)  9.48 us
    ppermute x5, waiting for transfers between devices, swap(): return lax.ppermute(value, axes, both)  5.91 us
    pallas_call x1, Pallas kernels, invert(): pl.pallas_call(functools.partial(invert_kernel, row_local=row_local, date...  5.03 us
    pallas_call x1, Pallas kernels, prepare(): pl.pallas_call(functools.partial(prepare_kernel, order=order), out_shape=...  4.43 us
    dynamic_slice x1, local copies, waits for them, and re-layouts, exchange(): lax.dynamic_slice_in_dim(phases, (stack_pos ^ mask) * col_local, col_loca...  1.66 us
    pallas_call x1, Pallas kernels, deramp(): pl.pallas_call(functools.partial(deramp_kernel, row_local=row_local, date...  1.57 us
  transfers between devices with their start and end apart: 12, of which 4 were waited for; matrix products, arithmetic and copies ran while one was open for 4% of the time, Pallas kernels for 13%

profile of v2, /device:TPU:8, one launch (start us, length us, event | category | flops | bytes accessed | tf_op | source)
XLA Modules:
  0.0 41.1 jit_solution(12762976483096758718)
XLA Ops:
  0.0 1.7 %constant_dynamic-slice_fusion = (bf16[144,2,128]{2,1,0:T(2,128)(2,1)S(1)}, bf16[144,2,128]{2,1,0:T(2,128)(2,1)S(1)}, bf16[144,2,128]{2,1,0:T(2,128)(2,1)S(1)}, ...) fusion(bf16[144,2,1024]{2,1,0:T(2,128)(2,1)} %param.5, ...), kind=kLoop, calls=%fused_computation.9 | loop fusion | bytes 1179680 | tf_op jit(solution)/shard_map/dynamic_slice | solution.py:217
  1.7 1.6 %collective-permute-start.6 = (bf16[144,2,128]{2,1,0:T(2,128)(2,1)S(1)}, bf16[144,2,128]{2,1,0:T(2,128)(2,1)S(1)}, u32[]{:S(2)}, u32[]{:S(2)}) collective-permute-start(bf16[144,2,128]{2,1,0:T(2,128)(2,1)S(1)} %get-tuple-element.27), channel_id=1, source_target_pairs={{0,24},{4,28},{8,16},{12,20},{16,8},{20,12},{24,0},{28,4},{1,25},{... | collective-permute-start | bytes 221192 | tf_op jit(solution)/shard_map/ppermute | solution.py:226
  3.3 1.1 %collective-permute-start.4 = (bf16[144,2,128]{2,1,0:T(2,128)(2,1)S(1)}, bf16[144,2,128]{2,1,0:T(2,128)(2,1)S(1)}, u32[]{:S(2)}, u32[]{:S(2)}) collective-permute-start(bf16[144,2,128]{2,1,0:T(2,128)(2,1)S(1)} %get-tuple-element.28), channel_id=1, source_target_pairs={{0,16},{4,20},{8,24},{12,28},{16,0},{20,4},{24,8},{28,12},{1,17},{... | collective-permute-start | bytes 221192 | tf_op jit(solution)/shard_map/ppermute | solution.py:226
  4.4 1.4 %collective-permute-start.2 = (bf16[144,2,128]{2,1,0:T(2,128)(2,1)S(1)}, bf16[144,2,128]{2,1,0:T(2,128)(2,1)S(1)}, u32[]{:S(2)}, u32[]{:S(2)}) collective-permute-start(bf16[144,2,128]{2,1,0:T(2,128)(2,1)S(1)} %get-tuple-element.30), channel_id=1, source_target_pairs={{0,8},{4,12},{8,0},{12,4},{16,24},{20,28},{24,16},{28,20},{1,9},{5... | collective-permute-start | bytes 221192 | tf_op jit(solution)/shard_map/ppermute | solution.py:226
  5.8 1.5 %collective-permute-start = (bf16[144,2,128]{2,1,0:T(2,128)(2,1)S(1)}, bf16[144,2,128]{2,1,0:T(2,128)(2,1)S(1)}, u32[]{:S(2)}, u32[]{:S(2)}) collective-permute-start(bf16[144,2,128]{2,1,0:T(2,128)(2,1)S(1)} %get-tuple-element.32), channel_id=1, source_target_pairs={{0,4},{4,0},{8,12},{12,8},{16,20},{20,16},{24,28},{28,24},{1,5},{5... | collective-permute-start | bytes 221192 | tf_op jit(solution)/shard_map/ppermute | solution.py:226
  7.3 2.9 %collective-permute-start.5 = (bf16[144,2,128]{2,1,0:T(2,128)(2,1)S(1)}, bf16[144,2,128]{2,1,0:T(2,128)(2,1)S(1)}, u32[]{:S(2)}, u32[]{:S(2)}) collective-permute-start(bf16[144,2,128]{2,1,0:T(2,128)(2,1)S(1)} %get-tuple-element.34), channel_id=1, source_target_pairs={{0,20},{4,16},{8,28},{12,24},{16,4},{20,0},{24,12},{28,8},{1,21},{... | collective-permute-start | bytes 221192 | tf_op jit(solution)/shard_map/ppermute | solution.py:226
  10.2 0.7 %convert_bitcast_fusion = (f32[256]{0:T(256)S(1)}, f32[2,128]{1,0:T(2,128)S(1)}) fusion(s32[2,128]{1,0:T(2,128)} %param.8), kind=kLoop, calls=%fused_computation.27 | loop fusion | flops 256 | bytes 3072 | tf_op jit(solution)/shard_map/mul | solution.py:357
  10.9 0.7 %fusion.3 = (f32[256]{0:T(256)S(1)}, f32[256]{0:T(256)S(1)}, f32[256]{0:T(256)S(1)}, f32[256]{0:T(256)S(1)}) fusion(s32[2,128]{1,0:T(2,128)} %param.9, s32[]{:T(128)S(6)} %add.108, s32[]{:T(128)S(6)} %add.107, s32[]{:T(128)S(6)} %select_n.51, s32[]{:T(128)S(6)} %select_n.52), kind=kLoop, calls=%fused_computation.24 | loop fusion | flops 2048 | bytes 5136 | tf_op jit(solution)/shard_map/convert_element_type | solution.py:354
  11.6 0.1 broadcast_in_dim.22
  11.7 0.1 pad.5.clone
  11.8 1.0 %collective-permute-start.3 = (bf16[144,2,128]{2,1,0:T(2,128)(2,1)S(1)}, bf16[144,2,128]{2,1,0:T(2,128)(2,1)S(1)}, u32[]{:S(2)}, u32[]{:S(2)}) collective-permute-start(bf16[144,2,128]{2,1,0:T(2,128)(2,1)S(1)} %get-tuple-element.17), channel_id=1, source_target_pairs={{0,12},{4,8},{8,4},{12,0},{16,28},{20,24},{24,20},{28,16},{1,13},{... | collective-permute-start | bytes 221192 | tf_op jit(solution)/shard_map/ppermute | solution.py:226
  12.8 0.0 collective-permute-done
  12.8 0.9 %collective-permute-start.1 = (bf16[144,2,128]{2,1,0:T(2,128)(2,1)S(1)}, bf16[144,2,128]{2,1,0:T(2,128)(2,1)S(1)}, u32[]{:S(2)}, u32[]{:S(2)}) collective-permute-start(bf16[144,2,128]{2,1,0:T(2,128)(2,1)S(1)} %get-tuple-element.16), channel_id=1, source_target_pairs={{0,28},{4,24},{8,20},{12,16},{16,12},{20,8},{24,4},{28,0},{1,29},{... | collective-permute-start | bytes 221192 | tf_op jit(solution)/shard_map/ppermute | solution.py:226
  13.6 0.1 maximum_maximum_fusion.refs_9_
  13.7 0.1 reshape.121
  13.8 4.4 %prepare.1 = (bf16[1152,640]{1,0:T(8,128)(2,1)S(1)}, bf16[640,1152]{1,0:T(8,128)(2,1)S(1)}, bf16[640,1152]{1,0:T(8,128)(2,1)S(1)}) custom-call(s32[1]{0:T(128)} %bitcast.8.place_ref, s32[8,2,144]{2,1,0:T(2,128)S(1)} %bitcast.35, f32[600,600]{1,0:T(8,128)S(1)} %copy-done), custom_call_target="tpu_custom_call" | custom-call | tf_op jit(solution)/shard_map/prepare/pallas_call | solution.py:56
  18.2 0.0 collective-permute-done.6
  18.3 0.0 collective-permute-done.4
  18.3 0.8 %early_fit.1 = (bf16[864,256]{1,0:T(8,128)(2,1)S(1)}, f32[640,256]{1,0:T(8,128)S(1)}) custom-call(bf16[288,128]{1,0:T(8,128)(2,1)S(1)} %bitcast.27, bf16[288,128]{1,0:T(8,128)(2,1)S(1)} %bitcast.31, bf16[288,128]{1,0:T(8,128)(2,1)S(1)} %bitcast.29, bf16[288,128]{1,0:T(8,128)(2,1)S(1)} %bitcast.32, bf16[288,128]{1,0:T(8,128)(2,1)S(1)} %bitcast.30, ...), custom_call_target="tpu_custom_call" | custom-call | tf_op jit(solution)/shard_map/early_fit/pallas_call | solution.py:99
  19.1 0.0 collective-permute-done.3
  19.1 0.0 collective-permute-done.1
  19.1 5.0 %invert.1 = (f32[640,256]{1,0:T(8,128)S(1)}, f32[16,640]{1,0:T(8,128)S(1)}) custom-call(bf16[288,128]{1,0:T(8,128)(2,1)S(1)} %bitcast.34, bf16[288,128]{1,0:T(8,128)(2,1)S(1)} %bitcast.33, bf16[864,256]{1,0:T(8,128)(2,1)S(1)} %get-tuple-element.22.refs_2_, f32[640,256]{1,0:T(8,128)S(1)} %get-tuple-element.23.refs_3_, ...), custom_call_target="tpu_custom_call" | custom-call | tf_op jit(solution)/shard_map/invert/pallas_call | solution.py:190
  24.1 2.8 %collective-permute-start.7 = (f32[8,640]{1,0:T(8,128)S(1)}, f32[8,640]{1,0:T(8,128)S(1)}, u32[]{:S(2)}, u32[]{:S(2)}) collective-permute-start(f32[8,640]{1,0:T(8,128)S(1)} %get-tuple-element.35), channel_id=1, source_target_pairs={{0,8},{4,12},{16,24},{20,28},{1,9},{5,13},{17,25},{21,29},{8,0},{1... | collective-permute-start | bytes 61448 | tf_op jit(solution)/shard_map/ppermute | solution.py:306
  26.9 3.2 %collective-permute-start.8 = (f32[8,640]{1,0:T(8,128)S(1)}, f32[8,640]{1,0:T(8,128)S(1)}, u32[]{:S(2)}, u32[]{:S(2)}) collective-permute-start(f32[8,640]{1,0:T(8,128)S(1)} %get-tuple-element.36), channel_id=1, source_target_pairs={{8,16},{12,20},{24,1},{28,5},{9,17},{13,21},{16,8},{20,12},{1,24},... | collective-permute-start | bytes 61448 | tf_op jit(solution)/shard_map/ppermute | solution.py:306
  30.1 2.4 %collective-permute-done.8 = f32[8,640]{1,0:T(8,128)S(1)} collective-permute-done((f32[8,640]{1,0:T(8,128)S(1)}, f32[8,640]{1,0:T(8,128)S(1)}, u32[]{:S(2)}, u32[]{:S(2)}) %collective-permute-start.8) | collective-permute-done | bytes 20512 | tf_op jit(solution)/shard_map/ppermute | solution.py:306
  32.6 1.8 %collective-permute-start.11 = (f32[16,640]{1,0:T(8,128)S(1)}, f32[16,640]{1,0:T(8,128)S(1)}, u32[]{:S(2)}, u32[]{:S(2)}) collective-permute-start(f32[16,640]{1,0:T(8,128)S(1)} %maximum_add_fusion.first_ref), channel_id=1, source_target_pairs={{0,6},{2,4},{8,14},{10,12},{16,22},{18,20},{24,30},{26,28},{6,0},{... | collective-permute-start | bytes 122888 | tf_op jit(solution)/shard_map/ppermute | solution.py:306
  34.4 1.2 %collective-permute-start.10 = (f32[16,640]{1,0:T(8,128)S(1)}, f32[16,640]{1,0:T(8,128)S(1)}, u32[]{:S(2)}, u32[]{:S(2)}) collective-permute-start(f32[16,640]{1,0:T(8,128)S(1)} %maximum_add_fusion.first_ref), channel_id=1, source_target_pairs={{0,4},{8,12},{16,20},{24,28},{4,0},{12,8},{20,16},{28,24},{1,5},{9... | collective-permute-start | bytes 122888 | tf_op jit(solution)/shard_map/ppermute | solution.py:306
  35.5 0.5 %collective-permute-start.9 = (f32[16,640]{1,0:T(8,128)S(1)}, f32[16,640]{1,0:T(8,128)S(1)}, u32[]{:S(2)}, u32[]{:S(2)}) collective-permute-start(f32[16,640]{1,0:T(8,128)S(1)} %maximum_add_fusion.first_ref), channel_id=1, source_target_pairs={{0,2},{2,0},{1,3},{3,1},{4,6},{6,4},{5,7},{7,5},{8,10},{10,8},{9,1... | collective-permute-start | bytes 122888 | tf_op jit(solution)/shard_map/ppermute | solution.py:306
  36.1 1.4 %collective-permute-done.11.refs_2_ = f32[16,640]{1,0:T(8,128)S(1)} collective-permute-done((f32[16,640]{1,0:T(8,128)S(1)}, f32[16,640]{1,0:T(8,128)S(1)}, u32[]{:S(2)}, u32[]{:S(2)}) %collective-permute-start.11) | collective-permute-done | bytes 40992 | tf_op jit(solution)/shard_map/ppermute | solution.py:306
  37.5 0.9 %collective-permute-done.10.refs_1_ = f32[16,640]{1,0:T(8,128)S(1)} collective-permute-done((f32[16,640]{1,0:T(8,128)S(1)}, f32[16,640]{1,0:T(8,128)S(1)}, u32[]{:S(2)}, u32[]{:S(2)}) %collective-permute-start.10) | collective-permute-done | bytes 40992 | tf_op jit(solution)/shard_map/ppermute | solution.py:306
  38.4 1.2 %collective-permute-done.9.refs_0_ = f32[16,640]{1,0:T(8,128)S(1)} collective-permute-done((f32[16,640]{1,0:T(8,128)S(1)}, f32[16,640]{1,0:T(8,128)S(1)}, u32[]{:S(2)}, u32[]{:S(2)}) %collective-permute-start.9) | collective-permute-done | bytes 40992 | tf_op jit(solution)/shard_map/ppermute | solution.py:306
  39.5 1.6 %deramp.1 = f32[1200,128]{1,0:T(8,128)} custom-call(f32[16,640]{1,0:T(8,128)S(1)} %maximum_add_fusion.first_ref, f32[16,640]{1,0:T(8,128)S(1)} %collective-permute-done.9.refs_0_, f32[16,640]{1,0:T(8,128)S(1)} %collective-permute-done.10.refs_1_, f32[16,640]{1,0:T(8,128)S(1)} %collective-permute-done.11.refs_2_, f32[640,256]{1,0:T(8,128)S(1)} %get-tuple-element.26.refs_3_, ...), custom_call_target="tpu_custom_call" | custom-call | tf_op jit(solution)/shard_map/deramp/pallas_call | solution.py:296
  (19 shorter events, 0.1 us)
Async XLA Ops:
  0.0 13.7 %copy-start.1 = (s32[1152,2]{0,1:T(2,128)S(1)}, s32[1152,2]{0,1:T(2,128)}, u32[]{:S(2)}) copy-start(s32[1152,2]{0,1:T(2,128)} %param.6) | copy-start | bytes 27652
  0.0 13.8 %copy-start = (f32[600,600]{1,0:T(8,128)S(1)}, f32[600,600]{1,0:T(8,128)}, u32[]{:S(2)}) copy-start(f32[600,600]{1,0:T(8,128)} %prec_ref.1) | copy-start | bytes 4320004
  1.7 16.6 %collective-permute-start.6 = (bf16[144,2,128]{2,1,0:T(2,128)(2,1)S(1)}, bf16[144,2,128]{2,1,0:T(2,128)(2,1)S(1)}, u32[]{:S(2)}, u32[]{:S(2)}) collective-permute-start(bf16[144,2,128]{2,1,0:T(2,128)(2,1)S(1)} %get-tuple-element.27), channel_id=1, source_target_pairs={{0,24},{4,28},{8,16},{12,20},{16,8},{20,12},{24,0},{28,4},{1,25},{... | collective-permute-start | bytes 221192 | tf_op jit(solution)/shard_map/ppermute | solution.py:226
  3.3 15.0 %collective-permute-start.4 = (bf16[144,2,128]{2,1,0:T(2,128)(2,1)S(1)}, bf16[144,2,128]{2,1,0:T(2,128)(2,1)S(1)}, u32[]{:S(2)}, u32[]{:S(2)}) collective-permute-start(bf16[144,2,128]{2,1,0:T(2,128)(2,1)S(1)} %get-tuple-element.28), channel_id=1, source_target_pairs={{0,16},{4,20},{8,24},{12,28},{16,0},{20,4},{24,8},{28,12},{1,17},{... | collective-permute-start | bytes 221192 | tf_op jit(solution)/shard_map/ppermute | solution.py:226
  4.4 7.4 %collective-permute-start.2 = (bf16[144,2,128]{2,1,0:T(2,128)(2,1)S(1)}, bf16[144,2,128]{2,1,0:T(2,128)(2,1)S(1)}, u32[]{:S(2)}, u32[]{:S(2)}) collective-permute-start(bf16[144,2,128]{2,1,0:T(2,128)(2,1)S(1)} %get-tuple-element.30), channel_id=1, source_target_pairs={{0,8},{4,12},{8,0},{12,4},{16,24},{20,28},{24,16},{28,20},{1,9},{5... | collective-permute-start | bytes 221192 | tf_op jit(solution)/shard_map/ppermute | solution.py:226
  5.8 7.0 %collective-permute-start = (bf16[144,2,128]{2,1,0:T(2,128)(2,1)S(1)}, bf16[144,2,128]{2,1,0:T(2,128)(2,1)S(1)}, u32[]{:S(2)}, u32[]{:S(2)}) collective-permute-start(bf16[144,2,128]{2,1,0:T(2,128)(2,1)S(1)} %get-tuple-element.32), channel_id=1, source_target_pairs={{0,4},{4,0},{8,12},{12,8},{16,20},{20,16},{24,28},{28,24},{1,5},{5... | collective-permute-start | bytes 221192 | tf_op jit(solution)/shard_map/ppermute | solution.py:226
  7.3 11.0 %collective-permute-start.5 = (bf16[144,2,128]{2,1,0:T(2,128)(2,1)S(1)}, bf16[144,2,128]{2,1,0:T(2,128)(2,1)S(1)}, u32[]{:S(2)}, u32[]{:S(2)}) collective-permute-start(bf16[144,2,128]{2,1,0:T(2,128)(2,1)S(1)} %get-tuple-element.34), channel_id=1, source_target_pairs={{0,20},{4,16},{8,28},{12,24},{16,4},{20,0},{24,12},{28,8},{1,21},{... | collective-permute-start | bytes 221192 | tf_op jit(solution)/shard_map/ppermute | solution.py:226
  11.8 7.3 %collective-permute-start.3 = (bf16[144,2,128]{2,1,0:T(2,128)(2,1)S(1)}, bf16[144,2,128]{2,1,0:T(2,128)(2,1)S(1)}, u32[]{:S(2)}, u32[]{:S(2)}) collective-permute-start(bf16[144,2,128]{2,1,0:T(2,128)(2,1)S(1)} %get-tuple-element.17), channel_id=1, source_target_pairs={{0,12},{4,8},{8,4},{12,0},{16,28},{20,24},{24,20},{28,16},{1,13},{... | collective-permute-start | bytes 221192 | tf_op jit(solution)/shard_map/ppermute | solution.py:226
  12.8 6.3 %collective-permute-start.1 = (bf16[144,2,128]{2,1,0:T(2,128)(2,1)S(1)}, bf16[144,2,128]{2,1,0:T(2,128)(2,1)S(1)}, u32[]{:S(2)}, u32[]{:S(2)}) collective-permute-start(bf16[144,2,128]{2,1,0:T(2,128)(2,1)S(1)} %get-tuple-element.16), channel_id=1, source_target_pairs={{0,28},{4,24},{8,20},{12,16},{16,12},{20,8},{24,4},{28,0},{1,29},{... | collective-permute-start | bytes 221192 | tf_op jit(solution)/shard_map/ppermute | solution.py:226
  24.1 6.0 %collective-permute-start.7 = (f32[8,640]{1,0:T(8,128)S(1)}, f32[8,640]{1,0:T(8,128)S(1)}, u32[]{:S(2)}, u32[]{:S(2)}) collective-permute-start(f32[8,640]{1,0:T(8,128)S(1)} %get-tuple-element.35), channel_id=1, source_target_pairs={{0,8},{4,12},{16,24},{20,28},{1,9},{5,13},{17,25},{21,29},{8,0},{1... | collective-permute-start | bytes 61448 | tf_op jit(solution)/shard_map/ppermute | solution.py:306
  26.9 5.7 %collective-permute-start.8 = (f32[8,640]{1,0:T(8,128)S(1)}, f32[8,640]{1,0:T(8,128)S(1)}, u32[]{:S(2)}, u32[]{:S(2)}) collective-permute-start(f32[8,640]{1,0:T(8,128)S(1)} %get-tuple-element.36), channel_id=1, source_target_pairs={{8,16},{12,20},{24,1},{28,5},{9,17},{13,21},{16,8},{20,12},{1,24},... | collective-permute-start | bytes 61448 | tf_op jit(solution)/shard_map/ppermute | solution.py:306
  32.6 4.9 %collective-permute-start.11 = (f32[16,640]{1,0:T(8,128)S(1)}, f32[16,640]{1,0:T(8,128)S(1)}, u32[]{:S(2)}, u32[]{:S(2)}) collective-permute-start(f32[16,640]{1,0:T(8,128)S(1)} %maximum_add_fusion.first_ref), channel_id=1, source_target_pairs={{0,6},{2,4},{8,14},{10,12},{16,22},{18,20},{24,30},{26,28},{6,0},{... | collective-permute-start | bytes 122888 | tf_op jit(solution)/shard_map/ppermute | solution.py:306
  34.4 4.0 %collective-permute-start.10 = (f32[16,640]{1,0:T(8,128)S(1)}, f32[16,640]{1,0:T(8,128)S(1)}, u32[]{:S(2)}, u32[]{:S(2)}) collective-permute-start(f32[16,640]{1,0:T(8,128)S(1)} %maximum_add_fusion.first_ref), channel_id=1, source_target_pairs={{0,4},{8,12},{16,20},{24,28},{4,0},{12,8},{20,16},{28,24},{1,5},{9... | collective-permute-start | bytes 122888 | tf_op jit(solution)/shard_map/ppermute | solution.py:306
  35.5 4.0 %collective-permute-start.9 = (f32[16,640]{1,0:T(8,128)S(1)}, f32[16,640]{1,0:T(8,128)S(1)}, u32[]{:S(2)}, u32[]{:S(2)}) collective-permute-start(f32[16,640]{1,0:T(8,128)S(1)} %maximum_add_fusion.first_ref), channel_id=1, source_target_pairs={{0,2},{2,0},{1,3},{3,1},{4,6},{6,4},{5,7},{7,5},{8,10},{10,8},{9,1... | collective-permute-start | bytes 122888 | tf_op jit(solution)/shard_map/ppermute | solution.py:306

commit v3 on v2

--- a/solution.py
+++ b/solution.py
@@ -11,9 +11,11 @@
 LANES = 128
 VMEM_LIMIT = 24 * 1024 * 1024
 ROWS_A = 128
-ROWS_B = 128
+ROWS_B = 320
+APPROX = False
 ARRIVAL = (0, 1, 4, 5, 2, 6, 7, 3)
 EARLY = 6
+OUT_PARTS = 5
 
 
 def halves(value):
@@ -25,11 +27,14 @@
     return lax.dot_general(left, right, dims, preferred_element_type=jnp.float32)
 
 
-def prepare_kernel(place_ref, pairs_ref, prec_ref, incidence_ref, gain_top, gain_low, pairs, *, order):
+def prepare_kernel(
+    pairs_ref, prec_ref, coherence_ref, tiles_ref, incidence_ref, gain_top, gain_low, member_ref,
+    weighted_ref, basis_ref, pairs, *, order, col_total, row_total,
+):
     chunk = pairs_ref.shape[2]
     date_total = prec_ref.shape[0]
     date_pad, ifg_total = gain_top.shape
-    place = place_ref[0]
+    place = lax.axis_index("stack") if len(order) > 1 else 0
     for position, mask in enumerate(order):
         pairs[:, position * chunk : (position + 1) * chunk] = pairs_ref[place ^ mask]
     date_ids = lax.broadcasted_iota(jnp.int32, (date_pad, ifg_total), 0)
@@ -39,29 +44,62 @@
     ).astype(jnp.bfloat16)
     incidence_ref[...] = incidence_t.T
     prec = prec_ref[...]
-    top, rest = halves(prec)
-    middle, low = halves(prec - top.astype(jnp.float32))
+    prec = prec - jnp.sum(prec, axis=1, keepdims=True) / date_total
+    top, low = halves(prec)
     used = incidence_t[:date_total]
-    gain = product(top, used) + (product(middle, used) + product(low, used))
-    gain_a, gain_b = halves(gain)
+    gain_a, gain_b = halves(product(top, used) + product(low, used))
     zeros = jnp.zeros((date_pad - date_total, ifg_total), jnp.bfloat16)
     gain_top[...] = jnp.concatenate([gain_a, zeros], axis=0)
     gain_low[...] = jnp.concatenate([gain_b, zeros], axis=0)
 
-
-def prepare(place, pairs, preconditioner, date_pad, order):
+    row_local, col_local = coherence_ref.shape
+    pixel_count = row_local * col_local
+    stack_size = lax.axis_size("stack")
+    block = lax.axis_index("range") * stack_size + lax.axis_index("stack")
+    node = block // 2
+    even = node % 2 == 0
+
+    def flat(ref):
+        return jnp.concatenate([ref[row : row + 1, :] for row in range(row_local)], axis=1)
+
+    coherence = flat(coherence_ref).astype(jnp.float32)
+    tiles = flat(tiles_ref)
+    pixel = lax.broadcasted_iota(jnp.int32, (1, pixel_count), 1)
+    row = jnp.zeros_like(pixel)
+    for step in range(1, row_local):
+        row = row + (pixel >= step * col_local).astype(jnp.int32)
+    column = block * col_local + (pixel - row * col_local)
+    row = row + lax.axis_index("azimuth") * row_local
+    coord_u = (row.astype(jnp.float32) + 0.5) / row_total - 0.5
+    coord_v = (column.astype(jnp.float32) + 0.5) / col_total - 0.5
+    basis = jnp.concatenate([jnp.ones_like(coord_u), coord_u, coord_v], axis=0)
+    spare = jnp.zeros((2, pixel_count), jnp.float32)
+    lines = []
+    for base in (jnp.where(even, 2 * node + 1, 2 * node - 1), jnp.where(even, 2 * node - 1, 2 * node + 1)):
+        for step in range(2):
+            lines.append(basis * (tiles == base + step).astype(jnp.float32))
+        lines.append(spare)
+    member = jnp.concatenate(lines, axis=0)
+    member_ref[...] = member
+    weighted_ref[...] = member * coherence
+    basis_ref[...] = jnp.concatenate([basis, coherence, jnp.zeros((4, pixel_count), jnp.float32)], axis=0)
+
+
+def prepare(pairs, preconditioner, coherence, tiles, date_pad, order, col_total, row_total):
     ifg_total = pairs.shape[0] * pairs.shape[2]
-    shapes = [(ifg_total, date_pad)] + [(date_pad, ifg_total)] * 2
+    pixel_count = coherence.size
+    shapes = [((ifg_total, date_pad), jnp.bfloat16)] + [((date_pad, ifg_total), jnp.bfloat16)] * 2
+    shapes += [((rows, pixel_count), jnp.float32) for rows in (16, 16, 8)]
     whole = pl.BlockSpec(memory_space=pltpu.VMEM)
     return pl.pallas_call(
-        functools.partial(prepare_kernel, order=order),
-        out_shape=[jax.ShapeDtypeStruct(shape, jnp.bfloat16) for shape in shapes],
-        in_specs=[pl.BlockSpec(memory_space=pltpu.SMEM), whole, whole],
-        out_specs=[whole] * 3,
+        functools.partial(prepare_kernel, order=order, col_total=col_total, row_total=row_total),
+        out_shape=[jax.ShapeDtypeStruct(shape, dtype) for shape, dtype in shapes],
+        in_specs=[whole] * 4,
+        out_specs=[whole] * 6,
         scratch_shapes=[pltpu.VMEM((2, ifg_total), jnp.int32)],
         compiler_params=pltpu.CompilerParams(vmem_limit_bytes=VMEM_LIMIT),
         name="prepare",
-    )(place, pairs, preconditioner)
+    )(pairs, preconditioner, coherence, tiles)
 
 
 def unpack(chunk_refs, wide, data, row_local):
@@ -110,8 +148,8 @@
 
 def invert_kernel(*refs, row_local, date_total, late):
     (
-        *chunk_refs, incidence, gain_top, gain_low, coherence_ref, weighted_ref, basis_ref,
-        series_ref, moments_ref, wide, data, residual, moved,
+        *chunk_refs, incidence, gain_top, gain_low, weighted_ref, basis_ref, series_ref,
+        moments_ref, wide, data, residual, moved,
     ) = refs
     ifg_total, pixel_count = data.shape
     date_pad = gain_top.shape[0]
@@ -125,7 +163,7 @@
         unpack(late_refs, wide, data.at[pl.ds(held, ifg_total - held)], row_local)
     else:
         unpack(late_refs, wide, data, row_local)
-    coherence = coherence_ref[...]
+    coherence = basis_ref[3:4, :]
     date_tiles = [pl.ds(start, ROWS_B) for start in range(0, date_pad, ROWS_B)]
     ifg_tiles = [pl.ds(start, ROWS_A) for start in range(0, ifg_total, ROWS_A)]
     everything = slice(None)
@@ -135,10 +173,11 @@
 
     def reweighted(total):
         scale = jnp.sum(total, axis=0, keepdims=True) / ifg_total + 1e-06
+        strength = coherence * (scale * scale)
         for rows in ifg_tiles:
             left = residual[rows, :]
-            ratio = scale / (left * left + scale)
-            moved[rows, :] = (coherence * (ratio * ratio) * left).astype(jnp.bfloat16)
+            inverse = pl.reciprocal(left * left + scale, approx=APPROX)
+            moved[rows, :] = ((inverse * left) * (inverse * strength)).astype(jnp.bfloat16)
 
     left_columns = pl.ds(done, ifg_total - done)
     tops, lows = [], []
@@ -183,10 +222,10 @@
     )
 
 
-def invert(late_chunks, early, incidence, gains, coherence, weighted, basis, row_local, date_total):
+def invert(late_chunks, early, incidence, gains, weighted, basis, row_local, date_total):
     ifg_total = incidence.shape[0]
     date_pad = gains[0].shape[0]
-    pixel_count = coherence.shape[1]
+    pixel_count = weighted.shape[1]
     return pl.pallas_call(
         functools.partial(
             invert_kernel, row_local=row_local, date_total=date_total, late=len(late_chunks)
@@ -203,7 +242,7 @@
         ],
         compiler_params=pltpu.CompilerParams(vmem_limit_bytes=VMEM_LIMIT),
         name="invert",
-    )(*late_chunks, *early, incidence, *gains, coherence, weighted, basis)
+    )(*late_chunks, *early, incidence, *gains, weighted, basis)
 
 
 def exchange(phases, stack_pos, stack_size):
@@ -213,10 +252,12 @@
         blocks = phases.reshape(ifg_local, row_local, stack_size, col_local).transpose(2, 0, 1, 3)
         stacked = lax.all_to_all(blocks, "stack", split_axis=0, concat_axis=0, tiled=True)
         return [stacked.reshape(-1, col_local)], []
-    blocks = [
-        lax.dynamic_slice_in_dim(phases, (stack_pos ^ mask) * col_local, col_local, axis=2)
-        for mask in range(stack_size)
-    ]
+    def block_for(array, mask):
+        return lax.dynamic_slice_in_dim(array, (stack_pos ^ mask) * col_local, col_local, axis=2)
+
+    first = block_for(phases, 4)
+    phases, first = lax.optimization_barrier((phases, first))
+    blocks = [first if mask == 4 else block_for(phases, mask) for mask in range(stack_size)]
     found = {0: blocks[0]}
 
     def send(mask, after=None):
@@ -259,7 +300,7 @@
 
 
 def deramp_kernel(first_ref, *refs, row_local, date_total):
-    *others, series_ref, member_ref, out_ref = refs
+    *others, series_ref, member_ref, out_ref, staged, sems = refs
     totals = first_ref[...]
     for other in others:
         totals = totals + other[...]
@@ -283,19 +324,34 @@
         jnp.concatenate([member_top, member_top, member_low], axis=0),
         (((0,), (0,)), ((), ())),
     )
-    flat = series_ref[pl.ds(0, date_total), :] - ramp[:date_total]
-    col_local = flat.shape[1] // row_local
-    for row in range(row_local):
-        out_ref[pl.ds(row, date_total, stride=row_local), :] = flat[
-            :, row * col_local : (row + 1) * col_local
-        ]
+    col_local = series_ref.shape[1] // row_local
+    copies = []
+    step = date_total // OUT_PARTS
+    for part in range(OUT_PARTS):
+        start = part * step
+        flat = series_ref[pl.ds(start, step), :] - ramp[start : start + step]
+        for row in range(row_local):
+            staged[pl.ds(start * row_local + row, step, stride=row_local), :] = flat[
+                :, row * col_local : (row + 1) * col_local
+            ]
+        rows = pl.ds(start * row_local, step * row_local)
+        copy = pltpu.make_async_copy(staged.at[rows], out_ref.at[rows], sems.at[part])
+        copy.start()
+        copies.append(copy)
+    for copy in copies:
+        copy.wait()
 
 
 def deramp(parts, series, member, row_local, date_total):
     col_local = series.shape[1] // row_local
+    shape = (date_total * row_local, col_local)
+    whole = pl.BlockSpec(memory_space=pltpu.VMEM)
     return pl.pallas_call(
         functools.partial(deramp_kernel, row_local=row_local, date_total=date_total),
-        out_shape=jax.ShapeDtypeStruct((date_total * row_local, col_local), jnp.float32),
+        out_shape=jax.ShapeDtypeStruct(shape, jnp.float32),
+        in_specs=[whole] * (len(parts) + 2),
+        out_specs=pl.BlockSpec(memory_space=pl.ANY),
+        scratch_shapes=[pltpu.VMEM(shape, jnp.float32), pltpu.SemaphoreType.DMA((OUT_PARTS,))],
         compiler_params=pltpu.CompilerParams(vmem_limit_bytes=VMEM_LIMIT),
         name="deramp",
     )(*parts, series, member)
@@ -311,54 +367,25 @@
     range_size = lax.axis_size("range")
     azimuth_size = lax.axis_size("azimuth")
     ifg_local, row_local, col_range = phases.shape
-    col_local = col_range // stack_size
-    pixel_count = row_local * col_local
     date_total = preconditioner.shape[0]
     date_pad = -(-(date_total + 8) // LANES) * LANES
     stack_pos = lax.axis_index("stack")
-    block_index = lax.axis_index("range") * stack_size + stack_pos
 
     chunks, order = exchange(phases, stack_pos, stack_size)
     pairs = ifg_pairs.T.reshape(2, stack_size, ifg_local).transpose(1, 0, 2)
-    place = stack_pos
     if not order:
-        pairs = ifg_pairs.T[None]
-        place, order = jnp.int32(0), [0]
-    incidence, *gains = prepare(
-        place.astype(jnp.int32).reshape(1), pairs, preconditioner, date_pad, order
+        pairs, order = ifg_pairs.T[None], (0,)
+    incidence, *gains, member, weighted, basis = prepare(
+        pairs, preconditioner, coherence, geo_tiles, date_pad, order,
+        col_range * range_size, row_local * azimuth_size,
     )
     early = []
     if len(chunks) > EARLY:
         early = early_fit(chunks[:EARLY], gains, row_local)
         chunks = chunks[EARLY:]
 
-    row_ids = lax.axis_index("azimuth") * row_local + jnp.arange(row_local, dtype=jnp.int32)
-    col_ids = block_index * col_local + jnp.arange(col_local, dtype=jnp.int32)
-    row_coord = (row_ids.astype(jnp.float32) + 0.5) / (row_local * azimuth_size) - 0.5
-    col_coord = (col_ids.astype(jnp.float32) + 0.5) / (col_range * range_size) - 0.5
-    shape = (row_local, col_local)
-    coord_u = jnp.broadcast_to(row_coord[:, None], shape).reshape(1, pixel_count)
-    coord_v = jnp.broadcast_to(col_coord[None, :], shape).reshape(1, pixel_count)
-    basis = jnp.concatenate([jnp.ones_like(coord_u), coord_u, coord_v], axis=0)
-    coherence_f = coherence.astype(jnp.float32).reshape(1, pixel_count)
-    tiles = geo_tiles.reshape(1, pixel_count)
-
-    node = block_index // 2
-    even = node % 2 == 0
-    first_tile = jnp.where(even, 2 * node + 1, 2 * node - 1)
-    second_tile = jnp.where(even, 2 * node - 1, 2 * node + 1)
-    spare = jnp.zeros((2, pixel_count), jnp.float32)
-    member_rows = []
-    for base in (first_tile, second_tile):
-        for step in range(2):
-            member_rows.append(basis * (tiles == base + step).astype(jnp.float32))
-        member_rows.append(spare)
-    member = jnp.concatenate(member_rows, axis=0)
-    weighted = member * coherence_f
-    basis8 = jnp.concatenate([basis, jnp.zeros((5, pixel_count), jnp.float32)], axis=0)
-
     series, moments = invert(
-        chunks, early, incidence, gains, coherence_f, weighted, basis8, row_local, date_total
+        chunks, early, incidence, gains, weighted, basis, row_local, date_total
     )
 
     def place(block):
@@ -388,7 +415,7 @@
         swap(moments, ("stack", "azimuth"), crossed),
     ]
     flat = deramp(parts, series, member, row_local, date_total)
-    return flat.reshape(date_total, row_local, col_local)
+    return flat.reshape(date_total, row_local, -1)
 
 
 def solution(mesh):

time: 41.3 us -> 42 us (1.017)
  the two profiles are of different devices: /device:TPU:8 before, /device:TPU:16 now
where the time goes in v3:
time: 42 us; the launch traced here: 41.7 us
  starting transfers between devices  18.2 us (43%)
  Pallas kernels  10.1 us (24%)
  waiting for transfers between devices  7.23 us (17%)
  local copies, waits for them, and re-layouts  5.96 us (14%)
    ppermute x7, starting transfers between devices, send(): lax.ppermute(block, 'stack', [(i, i ^ mask) for i in range(stack_size)])  9.98 us
    ppermute x5, starting transfers between devices, swap(): return lax.ppermute(value, axes, both)  8.23 us
    ppermute x5, waiting for transfers between devices, swap(): return lax.ppermute(value, axes, both)  7.21 us
    pallas_call x1, Pallas kernels, invert(): pl.pallas_call(functools.partial(invert_kernel, row_local=row_local, date...  4.66 us
    pallas_call x1, Pallas kernels, prepare(): pl.pallas_call(functools.partial(prepare_kernel, order=order, col_total=c...  3.19 us
    unnamed x6, local copies, waits for them, and re-layouts  2.75 us
    dynamic_slice x2, local copies, waits for them, and re-layouts, block_for(): lax.dynamic_slice_in_dim(array, (stack_pos ^ mask) * col_local, col_local...  2.41 us
    pallas_call x1, Pallas kernels, deramp(): pl.pallas_call(functools.partial(deramp_kernel, row_local=row_local, date...  1.53 us
  transfers between devices with their start and end apart: 12, of which 4 were waited for; matrix products, arithmetic and copies ran while one was open for 2% of the time, Pallas kernels for 9%

profile of v3, /device:TPU:16, one launch (start us, length us, event | category | flops | bytes accessed | tf_op | source)
XLA Modules:
  0.0 41.7 jit_solution(44936204107151979)
XLA Ops:
  0.0 0.9 %constant_dynamic-slice_fusion.7 = bf16[144,2,128]{2,1,0:T(2,128)(2,1)S(1)} fusion(bf16[144,2,1024]{2,1,0:T(2,128)(2,1)} %param.5, s32[]{:T(128)S(6)} %select_n.24), kind=kLoop, calls=%fused_computation.9 | loop fusion | bytes 147460 | tf_op jit(solution)/shard_map/dynamic_slice | solution.py:256
  1.0 1.5 %constant_dynamic-slice_fusion = (bf16[144,2,128]{2,1,0:T(2,128)(2,1)S(1)}, bf16[144,2,128]{2,1,0:T(2,128)(2,1)S(1)}, bf16[144,2,128]{2,1,0:T(2,128)(2,1)S(1)}, ...) fusion(bf16[144,2,1024]{2,1,0:T(2,128)(2,1)} %param.5, ...), kind=kLoop, calls=%fused_computation.2 | loop fusion | bytes 1032220 | tf_op jit(solution)/shard_map/dynamic_slice | solution.py:256
  2.5 1.6 %collective-permute-start.2 = (bf16[144,2,128]{2,1,0:T(2,128)(2,1)S(1)}, bf16[144,2,128]{2,1,0:T(2,128)(2,1)S(1)}, u32[]{:S(2)}, u32[]{:S(2)}) collective-permute-start(bf16[144,2,128]{2,1,0:T(2,128)(2,1)S(1)} %get-tuple-element.40), channel_id=1, source_target_pairs={{0,8},{4,12},{8,0},{12,4},{16,24},{20,28},{24,16},{28,20},{1,9},{5... | collective-permute-start | bytes 221192 | tf_op jit(solution)/shard_map/ppermute | solution.py:267
  4.1 1.5 %collective-permute-start = (bf16[144,2,128]{2,1,0:T(2,128)(2,1)S(1)}, bf16[144,2,128]{2,1,0:T(2,128)(2,1)S(1)}, u32[]{:S(2)}, u32[]{:S(2)}) collective-permute-start(bf16[144,2,128]{2,1,0:T(2,128)(2,1)S(1)} %get-tuple-element.42), channel_id=1, source_target_pairs={{0,4},{4,0},{8,12},{12,8},{16,20},{20,16},{24,28},{28,24},{1,5},{5... | collective-permute-start | bytes 221192 | tf_op jit(solution)/shard_map/ppermute | solution.py:267
  5.6 0.3 collective-permute-start.4
  5.9 1.6 %collective-permute-start.6 = (bf16[144,2,128]{2,1,0:T(2,128)(2,1)S(1)}, bf16[144,2,128]{2,1,0:T(2,128)(2,1)S(1)}, u32[]{:S(2)}, u32[]{:S(2)}) collective-permute-start(bf16[144,2,128]{2,1,0:T(2,128)(2,1)S(1)} %get-tuple-element.37), channel_id=1, source_target_pairs={{0,24},{4,28},{8,16},{12,20},{16,8},{20,12},{24,0},{28,4},{1,25},{... | collective-permute-start | bytes 221192 | tf_op jit(solution)/shard_map/ppermute | solution.py:267
  7.5 1.0 %collective-permute-start.5 = (bf16[144,2,128]{2,1,0:T(2,128)(2,1)S(1)}, bf16[144,2,128]{2,1,0:T(2,128)(2,1)S(1)}, u32[]{:S(2)}, u32[]{:S(2)}) collective-permute-start(bf16[144,2,128]{2,1,0:T(2,128)(2,1)S(1)} %get-tuple-element.38), channel_id=1, source_target_pairs={{0,20},{4,16},{8,28},{12,24},{16,4},{20,0},{24,12},{28,8},{1,21},{... | collective-permute-start | bytes 221192 | tf_op jit(solution)/shard_map/ppermute | solution.py:267
  8.5 0.0 collective-permute-done.2
  8.5 1.9 %collective-permute-start.3 = (bf16[144,2,128]{2,1,0:T(2,128)(2,1)S(1)}, bf16[144,2,128]{2,1,0:T(2,128)(2,1)S(1)}, u32[]{:S(2)}, u32[]{:S(2)}) collective-permute-start(bf16[144,2,128]{2,1,0:T(2,128)(2,1)S(1)} %get-tuple-element.23), channel_id=1, source_target_pairs={{0,12},{4,8},{8,4},{12,0},{16,28},{20,24},{24,20},{28,16},{1,13},{... | collective-permute-start | bytes 221192 | tf_op jit(solution)/shard_map/ppermute | solution.py:267
  10.3 2.1 %collective-permute-start.1 = (bf16[144,2,128]{2,1,0:T(2,128)(2,1)S(1)}, bf16[144,2,128]{2,1,0:T(2,128)(2,1)S(1)}, u32[]{:S(2)}, u32[]{:S(2)}) collective-permute-start(bf16[144,2,128]{2,1,0:T(2,128)(2,1)S(1)} %get-tuple-element.22), channel_id=1, source_target_pairs={{0,28},{4,24},{8,20},{12,16},{16,12},{20,8},{24,4},{28,0},{1,29},{... | collective-permute-start | bytes 221192 | tf_op jit(solution)/shard_map/ppermute | solution.py:267
  12.4 0.8 %reshape.38 = s32[2,8,144]{2,1,0:T(8,128)S(1)} reshape(s32[2,1152]{1,0:T(2,128)} %bitcast.22) | data formatting | bytes 18432 | tf_op jit(solution)/shard_map/reshape | solution.py:375
  13.2 0.0 copy-start
  13.3 1.4 %copy-done = f32[600,600]{1,0:T(8,128)S(1)} copy-done((f32[600,600]{1,0:T(8,128)S(1)}, f32[600,600]{1,0:T(8,128)}, u32[]{:S(2)}) %copy-start) | copy-done | bytes 1440024
  14.6 0.7 %copy-done.1 = s32[2,128]{1,0:T(2,128)S(1)} copy-done((s32[2,128]{1,0:T(2,128)S(1)}, s32[2,128]{1,0:T(2,128)}, u32[]{:S(2)}) %copy-start.1) | copy-done | bytes 1048
  15.3 0.7 %copy-done.2 = s32[2,128]{1,0:T(2,128)S(1)} copy-done((s32[2,128]{1,0:T(2,128)S(1)}, s32[2,128]{1,0:T(2,128)}, u32[]{:S(2)}) %copy-start.2) | copy-done | bytes 1048
  16.0 3.2 %prepare.1 = (bf16[1152,640]{1,0:T(8,128)(2,1)S(1)}, bf16[640,1152]{1,0:T(8,128)(2,1)S(1)}, bf16[640,1152]{1,0:T(8,128)(2,1)S(1)}, f32[16,256]{1,0:T(8,128)S(1)}...) custom-call(s32[8,2,144]{2,1,0:T(2,128)S(1)} %bitcast.21, f32[600,600]{1,0:T(8,128)S(1)} %copy-done, ...), custom_call_target="tpu_custom_call" | custom-call | tf_op jit(solution)/shard_map/prepare/pallas_call | solution.py:94
  19.2 0.0 collective-permute-done.4
  19.2 0.0 collective-permute-done.6
  19.2 0.7 %early_fit.1 = (bf16[864,256]{1,0:T(8,128)(2,1)S(1)}, f32[640,256]{1,0:T(8,128)S(1)}) custom-call(bf16[288,128]{1,0:T(8,128)(2,1)S(1)} %bitcast.13, bf16[288,128]{1,0:T(8,128)(2,1)S(1)} %bitcast.15, bf16[288,128]{1,0:T(8,128)(2,1)S(1)} %bitcast.16, bf16[288,128]{1,0:T(8,128)(2,1)S(1)} %bitcast.18, bf16[288,128]{1,0:T(8,128)(2,1)S(1)} %bitcast.14, ...), custom_call_target="tpu_custom_call" | custom-call | tf_op jit(solution)/shard_map/early_fit/pallas_call | solution.py:137
  20.0 0.0 collective-permute-done.1
  20.0 4.7 %invert.1 = (f32[640,256]{1,0:T(8,128)S(1)}, f32[16,640]{1,0:T(8,128)S(1)}) custom-call(bf16[288,128]{1,0:T(8,128)(2,1)S(1)} %bitcast.20, bf16[288,128]{1,0:T(8,128)(2,1)S(1)} %bitcast.19, bf16[864,256]{1,0:T(8,128)(2,1)S(1)} %get-tuple-element.29.refs_2_, f32[640,256]{1,0:T(8,128)S(1)} %get-tuple-element.30.refs_3_, ...), custom_call_target="tpu_custom_call" | custom-call | tf_op jit(solution)/shard_map/invert/pallas_call | solution.py:229
  24.7 2.8 %collective-permute-start.7 = (f32[8,640]{1,0:T(8,128)S(1)}, f32[8,640]{1,0:T(8,128)S(1)}, u32[]{:S(2)}, u32[]{:S(2)}) collective-permute-start(f32[8,640]{1,0:T(8,128)S(1)} %get-tuple-element.44), channel_id=1, source_target_pairs={{0,8},{4,12},{16,24},{20,28},{1,9},{5,13},{17,25},{21,29},{8,0},{1... | collective-permute-start | bytes 61448 | tf_op jit(solution)/shard_map/ppermute | solution.py:362
  27.5 1.9 %collective-permute-start.8 = (f32[8,640]{1,0:T(8,128)S(1)}, f32[8,640]{1,0:T(8,128)S(1)}, u32[]{:S(2)}, u32[]{:S(2)}) collective-permute-start(f32[8,640]{1,0:T(8,128)S(1)} %get-tuple-element.45), channel_id=1, source_target_pairs={{8,16},{12,20},{24,1},{28,5},{9,17},{13,21},{16,8},{20,12},{1,24},... | collective-permute-start | bytes 61448 | tf_op jit(solution)/shard_map/ppermute | solution.py:362
  29.4 0.0 collective-permute-done.7
  29.4 3.7 %collective-permute-done.8 = f32[8,640]{1,0:T(8,128)S(1)} collective-permute-done((f32[8,640]{1,0:T(8,128)S(1)}, f32[8,640]{1,0:T(8,128)S(1)}, u32[]{:S(2)}, u32[]{:S(2)}) %collective-permute-start.8) | collective-permute-done | bytes 20512 | tf_op jit(solution)/shard_map/ppermute | solution.py:362
  33.2 2.4 %collective-permute-start.11 = (f32[16,640]{1,0:T(8,128)S(1)}, f32[16,640]{1,0:T(8,128)S(1)}, u32[]{:S(2)}, u32[]{:S(2)}) collective-permute-start(f32[16,640]{1,0:T(8,128)S(1)} %maximum_add_fusion.first_ref), channel_id=1, source_target_pairs={{0,6},{2,4},{8,14},{10,12},{16,22},{18,20},{24,30},{26,28},{6,0},{... | collective-permute-start | bytes 122888 | tf_op jit(solution)/shard_map/ppermute | solution.py:362
  35.6 0.5 %collective-permute-start.10 = (f32[16,640]{1,0:T(8,128)S(1)}, f32[16,640]{1,0:T(8,128)S(1)}, u32[]{:S(2)}, u32[]{:S(2)}) collective-permute-start(f32[16,640]{1,0:T(8,128)S(1)} %maximum_add_fusion.first_ref), channel_id=1, source_target_pairs={{0,4},{8,12},{16,20},{24,28},{4,0},{12,8},{20,16},{28,24},{1,5},{9... | collective-permute-start | bytes 122888 | tf_op jit(solution)/shard_map/ppermute | solution.py:362
  36.1 0.5 %collective-permute-start.9 = (f32[16,640]{1,0:T(8,128)S(1)}, f32[16,640]{1,0:T(8,128)S(1)}, u32[]{:S(2)}, u32[]{:S(2)}) collective-permute-start(f32[16,640]{1,0:T(8,128)S(1)} %maximum_add_fusion.first_ref), channel_id=1, source_target_pairs={{0,2},{2,0},{1,3},{3,1},{4,6},{6,4},{5,7},{7,5},{8,10},{10,8},{9,1... | collective-permute-start | bytes 122888 | tf_op jit(solution)/shard_map/ppermute | solution.py:362
  36.7 1.4 %collective-permute-done.11.refs_2_ = f32[16,640]{1,0:T(8,128)S(1)} collective-permute-done((f32[16,640]{1,0:T(8,128)S(1)}, f32[16,640]{1,0:T(8,128)S(1)}, u32[]{:S(2)}, u32[]{:S(2)}) %collective-permute-start.11) | collective-permute-done | bytes 40992 | tf_op jit(solution)/shard_map/ppermute | solution.py:362
  38.1 1.5 %collective-permute-done.10.refs_1_ = f32[16,640]{1,0:T(8,128)S(1)} collective-permute-done((f32[16,640]{1,0:T(8,128)S(1)}, f32[16,640]{1,0:T(8,128)S(1)}, u32[]{:S(2)}, u32[]{:S(2)}) %collective-permute-start.10) | collective-permute-done | bytes 40992 | tf_op jit(solution)/shard_map/ppermute | solution.py:362
  39.6 0.5 %collective-permute-done.9.refs_0_ = f32[16,640]{1,0:T(8,128)S(1)} collective-permute-done((f32[16,640]{1,0:T(8,128)S(1)}, f32[16,640]{1,0:T(8,128)S(1)}, u32[]{:S(2)}, u32[]{:S(2)}) %collective-permute-start.9) | collective-permute-done | bytes 40992 | tf_op jit(solution)/shard_map/ppermute | solution.py:362
  40.1 1.5 %deramp.1 = f32[1200,128]{1,0:T(8,128)} custom-call(f32[16,640]{1,0:T(8,128)S(1)} %maximum_add_fusion.first_ref, f32[16,640]{1,0:T(8,128)S(1)} %collective-permute-done.9.refs_0_, f32[16,640]{1,0:T(8,128)S(1)} %collective-permute-done.10.refs_1_, f32[16,640]{1,0:T(8,128)S(1)} %collective-permute-done.11.refs_2_, f32[640,256]{1,0:T(8,128)S(1)} %get-tuple-element.35.refs_3_, ...), custom_call_target="tpu_custom_call" | custom-call | tf_op jit(solution)/shard_map/deramp/pallas_call | solution.py:349
  (8 shorter events, 0.0 us)
Async XLA Ops:
  2.5 6.0 %collective-permute-start.2 = (bf16[144,2,128]{2,1,0:T(2,128)(2,1)S(1)}, bf16[144,2,128]{2,1,0:T(2,128)(2,1)S(1)}, u32[]{:S(2)}, u32[]{:S(2)}) collective-permute-start(bf16[144,2,128]{2,1,0:T(2,128)(2,1)S(1)} %get-tuple-element.40), channel_id=1, source_target_pairs={{0,8},{4,12},{8,0},{12,4},{16,24},{20,28},{24,16},{28,20},{1,9},{5... | collective-permute-start | bytes 221192 | tf_op jit(solution)/shard_map/ppermute | solution.py:267
  4.1 6.3 %collective-permute-start = (bf16[144,2,128]{2,1,0:T(2,128)(2,1)S(1)}, bf16[144,2,128]{2,1,0:T(2,128)(2,1)S(1)}, u32[]{:S(2)}, u32[]{:S(2)}) collective-permute-start(bf16[144,2,128]{2,1,0:T(2,128)(2,1)S(1)} %get-tuple-element.42), channel_id=1, source_target_pairs={{0,4},{4,0},{8,12},{12,8},{16,20},{20,16},{24,28},{28,24},{1,5},{5... | collective-permute-start | bytes 221192 | tf_op jit(solution)/shard_map/ppermute | solution.py:267
  5.6 13.6 %collective-permute-start.4 = (bf16[144,2,128]{2,1,0:T(2,128)(2,1)S(1)}, bf16[144,2,128]{2,1,0:T(2,128)(2,1)S(1)}, u32[]{:S(2)}, u32[]{:S(2)}) collective-permute-start(bf16[144,2,128]{2,1,0:T(2,128)(2,1)S(1)} %constant_dynamic-slice_fusion.7), channel_id=1, source_target_pairs={{0,16},{4,20},{8,24},{12,28},{16,0},{20,4},{24,8},{28,12},{1,17},{... | collective-permute-start | bytes 221192 | tf_op jit(solution)/shard_map/ppermute | solution.py:267
  5.9 13.3 %collective-permute-start.6 = (bf16[144,2,128]{2,1,0:T(2,128)(2,1)S(1)}, bf16[144,2,128]{2,1,0:T(2,128)(2,1)S(1)}, u32[]{:S(2)}, u32[]{:S(2)}) collective-permute-start(bf16[144,2,128]{2,1,0:T(2,128)(2,1)S(1)} %get-tuple-element.37), channel_id=1, source_target_pairs={{0,24},{4,28},{8,16},{12,20},{16,8},{20,12},{24,0},{28,4},{1,25},{... | collective-permute-start | bytes 221192 | tf_op jit(solution)/shard_map/ppermute | solution.py:267
  7.5 11.7 %collective-permute-start.5 = (bf16[144,2,128]{2,1,0:T(2,128)(2,1)S(1)}, bf16[144,2,128]{2,1,0:T(2,128)(2,1)S(1)}, u32[]{:S(2)}, u32[]{:S(2)}) collective-permute-start(bf16[144,2,128]{2,1,0:T(2,128)(2,1)S(1)} %get-tuple-element.38), channel_id=1, source_target_pairs={{0,20},{4,16},{8,28},{12,24},{16,4},{20,0},{24,12},{28,8},{1,21},{... | collective-permute-start | bytes 221192 | tf_op jit(solution)/shard_map/ppermute | solution.py:267
  8.5 11.5 %collective-permute-start.3 = (bf16[144,2,128]{2,1,0:T(2,128)(2,1)S(1)}, bf16[144,2,128]{2,1,0:T(2,128)(2,1)S(1)}, u32[]{:S(2)}, u32[]{:S(2)}) collective-permute-start(bf16[144,2,128]{2,1,0:T(2,128)(2,1)S(1)} %get-tuple-element.23), channel_id=1, source_target_pairs={{0,12},{4,8},{8,4},{12,0},{16,28},{20,24},{24,20},{28,16},{1,13},{... | collective-permute-start | bytes 221192 | tf_op jit(solution)/shard_map/ppermute | solution.py:267
  10.3 9.6 %collective-permute-start.1 = (bf16[144,2,128]{2,1,0:T(2,128)(2,1)S(1)}, bf16[144,2,128]{2,1,0:T(2,128)(2,1)S(1)}, u32[]{:S(2)}, u32[]{:S(2)}) collective-permute-start(bf16[144,2,128]{2,1,0:T(2,128)(2,1)S(1)} %get-tuple-element.22), channel_id=1, source_target_pairs={{0,28},{4,24},{8,20},{12,16},{16,12},{20,8},{24,4},{28,0},{1,29},{... | collective-permute-start | bytes 221192 | tf_op jit(solution)/shard_map/ppermute | solution.py:267
  13.2 1.4 %copy-start = (f32[600,600]{1,0:T(8,128)S(1)}, f32[600,600]{1,0:T(8,128)}, u32[]{:S(2)}) copy-start(f32[600,600]{1,0:T(8,128)} %prec_ref.1) | copy-start | bytes 4320004
  14.6 0.7 %copy-start.1 = (s32[2,128]{1,0:T(2,128)S(1)}, s32[2,128]{1,0:T(2,128)}, u32[]{:S(2)}) copy-start(s32[2,128]{1,0:T(2,128)} %coherence_ref.1) | copy-start | bytes 3076
  15.3 0.7 %copy-start.2 = (s32[2,128]{1,0:T(2,128)S(1)}, s32[2,128]{1,0:T(2,128)}, u32[]{:S(2)}) copy-start(s32[2,128]{1,0:T(2,128)} %tiles_ref.1) | copy-start | bytes 3076
  24.7 4.8 %collective-permute-start.7 = (f32[8,640]{1,0:T(8,128)S(1)}, f32[8,640]{1,0:T(8,128)S(1)}, u32[]{:S(2)}, u32[]{:S(2)}) collective-permute-start(f32[8,640]{1,0:T(8,128)S(1)} %get-tuple-element.44), channel_id=1, source_target_pairs={{0,8},{4,12},{16,24},{20,28},{1,9},{5,13},{17,25},{21,29},{8,0},{1... | collective-permute-start | bytes 61448 | tf_op jit(solution)/shard_map/ppermute | solution.py:362
  27.5 5.7 %collective-permute-start.8 = (f32[8,640]{1,0:T(8,128)S(1)}, f32[8,640]{1,0:T(8,128)S(1)}, u32[]{:S(2)}, u32[]{:S(2)}) collective-permute-start(f32[8,640]{1,0:T(8,128)S(1)} %get-tuple-element.45), channel_id=1, source_target_pairs={{8,16},{12,20},{24,1},{28,5},{9,17},{13,21},{16,8},{20,12},{1,24},... | collective-permute-start | bytes 61448 | tf_op jit(solution)/shard_map/ppermute | solution.py:362
  33.2 4.9 %collective-permute-start.11 = (f32[16,640]{1,0:T(8,128)S(1)}, f32[16,640]{1,0:T(8,128)S(1)}, u32[]{:S(2)}, u32[]{:S(2)}) collective-permute-start(f32[16,640]{1,0:T(8,128)S(1)} %maximum_add_fusion.first_ref), channel_id=1, source_target_pairs={{0,6},{2,4},{8,14},{10,12},{16,22},{18,20},{24,30},{26,28},{6,0},{... | collective-permute-start | bytes 122888 | tf_op jit(solution)/shard_map/ppermute | solution.py:362
  35.6 4.0 %collective-permute-start.10 = (f32[16,640]{1,0:T(8,128)S(1)}, f32[16,640]{1,0:T(8,128)S(1)}, u32[]{:S(2)}, u32[]{:S(2)}) collective-permute-start(f32[16,640]{1,0:T(8,128)S(1)} %maximum_add_fusion.first_ref), channel_id=1, source_target_pairs={{0,4},{8,12},{16,20},{24,28},{4,0},{12,8},{20,16},{28,24},{1,5},{9... | collective-permute-start | bytes 122888 | tf_op jit(solution)/shard_map/ppermute | solution.py:362
  36.1 4.0 %collective-permute-start.9 = (f32[16,640]{1,0:T(8,128)S(1)}, f32[16,640]{1,0:T(8,128)S(1)}, u32[]{:S(2)}, u32[]{:S(2)}) collective-permute-start(f32[16,640]{1,0:T(8,128)S(1)} %maximum_add_fusion.first_ref), channel_id=1, source_target_pairs={{0,2},{2,0},{1,3},{3,1},{4,6},{6,4},{5,7},{7,5},{8,10},{10,8},{9,1... | collective-permute-start | bytes 122888 | tf_op jit(solution)/shard_map/ppermute | solution.py:362

commit v4 on v3

--- a/solution.py
+++ b/solution.py
@@ -28,21 +28,41 @@
 
 
 def prepare_kernel(
-    pairs_ref, prec_ref, coherence_ref, tiles_ref, incidence_ref, gain_top, gain_low, member_ref,
-    weighted_ref, basis_ref, pairs, *, order, col_total, row_total,
+    pairs_hbm, prec_hbm, coherence_hbm, tiles_hbm, incidence_ref, gain_top, gain_low, member_ref,
+    weighted_ref, basis_ref, pairs_ref, prec_ref, coherence_ref, tiles_ref, pairs, sems, *, order,
+    col_total, row_total,
 ):
-    chunk = pairs_ref.shape[2]
+    copies = [
+        pltpu.make_async_copy(source, target, sems.at[index])
+        for index, (source, target) in enumerate(
+            (
+                (pairs_hbm, pairs_ref),
+                (prec_hbm, prec_ref),
+                (coherence_hbm, coherence_ref),
+                (tiles_hbm, tiles_ref),
+            )
+        )
+    ]
+    for copy in copies:
+        copy.start()
+    copies[0].wait()
+    chunk = pairs_ref.shape[1] // len(order)
     date_total = prec_ref.shape[0]
     date_pad, ifg_total = gain_top.shape
-    place = lax.axis_index("stack") if len(order) > 1 else 0
     for position, mask in enumerate(order):
-        pairs[:, position * chunk : (position + 1) * chunk] = pairs_ref[place ^ mask]
+        moved = pairs_ref[...]
+        if len(order) > 1:
+            back = (len(order) - (lax.axis_index("stack") ^ mask)) % len(order)
+            moved = pltpu.roll(moved, back * chunk, 1)
+        pairs[:, position * chunk : (position + 1) * chunk] = moved[:, :chunk]
     date_ids = lax.broadcasted_iota(jnp.int32, (date_pad, ifg_total), 0)
     incidence_t = (
         jnp.where(date_ids == pairs[1:2, :], 1.0, 0.0)
         - jnp.where(date_ids == pairs[0:1, :], 1.0, 0.0)
     ).astype(jnp.bfloat16)
     incidence_ref[...] = incidence_t.T
+    for copy in copies[1:]:
+        copy.wait()
     prec = prec_ref[...]
     prec = prec - jnp.sum(prec, axis=1, keepdims=True) / date_total
     top, low = halves(prec)
@@ -86,20 +106,25 @@
 
 
 def prepare(pairs, preconditioner, coherence, tiles, date_pad, order, col_total, row_total):
-    ifg_total = pairs.shape[0] * pairs.shape[2]
+    ifg_total = pairs.shape[1]
     pixel_count = coherence.size
+    arguments = (pairs, preconditioner, coherence, tiles)
     shapes = [((ifg_total, date_pad), jnp.bfloat16)] + [((date_pad, ifg_total), jnp.bfloat16)] * 2
     shapes += [((rows, pixel_count), jnp.float32) for rows in (16, 16, 8)]
     whole = pl.BlockSpec(memory_space=pltpu.VMEM)
     return pl.pallas_call(
         functools.partial(prepare_kernel, order=order, col_total=col_total, row_total=row_total),
         out_shape=[jax.ShapeDtypeStruct(shape, dtype) for shape, dtype in shapes],
-        in_specs=[whole] * 4,
+        in_specs=[pl.BlockSpec(memory_space=pltpu.HBM)] * 4,
         out_specs=[whole] * 6,
-        scratch_shapes=[pltpu.VMEM((2, ifg_total), jnp.int32)],
+        scratch_shapes=[
+            *(pltpu.VMEM(value.shape, value.dtype) for value in arguments),
+            pltpu.VMEM(pairs.shape, jnp.int32),
+            pltpu.SemaphoreType.DMA((4,)),
+        ],
         compiler_params=pltpu.CompilerParams(vmem_limit_bytes=VMEM_LIMIT),
         name="prepare",
-    )(pairs, preconditioner, coherence, tiles)
+    )(*(pltpu.with_memory_space_constraint(value, pltpu.HBM) for value in arguments))
 
 
 def unpack(chunk_refs, wide, data, row_local):
@@ -245,19 +270,43 @@
     )(*late_chunks, *early, incidence, *gains, weighted, basis)
 
 
-def exchange(phases, stack_pos, stack_size):
+def cut_kernel(source, *refs):
+    *targets, sems = refs
+    copies = [
+        pltpu.make_async_copy(
+            source.at[:, lax.axis_index("stack") ^ mask], target, sems.at[mask]
+        )
+        for mask, target in enumerate(targets)
+    ]
+    for copy in copies:
+        copy.start()
+    for copy in copies:
+        copy.wait()
+
+
+def cut(phases, col_local):
+    ifg_local, row_local, col_range = phases.shape
+    count = col_range // col_local
+    view = phases.reshape(ifg_local, row_local, count, col_local).transpose(0, 2, 1, 3)
+    return pl.pallas_call(
+        cut_kernel,
+        out_shape=[jax.ShapeDtypeStruct((ifg_local, row_local, col_local), phases.dtype)] * count,
+        in_specs=[pl.BlockSpec(memory_space=pltpu.HBM)],
+        out_specs=[pl.BlockSpec(memory_space=pltpu.VMEM)] * count,
+        scratch_shapes=[pltpu.SemaphoreType.DMA((count,))],
+        compiler_params=pltpu.CompilerParams(vmem_limit_bytes=8 * 1024 * 1024),
+        name="cut",
+    )(pltpu.with_memory_space_constraint(view, pltpu.HBM))
+
+
+def exchange(phases, stack_size):
     ifg_local, row_local, col_range = phases.shape
     col_local = col_range // stack_size
     if stack_size != 8:
         blocks = phases.reshape(ifg_local, row_local, stack_size, col_local).transpose(2, 0, 1, 3)
         stacked = lax.all_to_all(blocks, "stack", split_axis=0, concat_axis=0, tiled=True)
-        return [stacked.reshape(-1, col_local)], []
-    def block_for(array, mask):
-        return lax.dynamic_slice_in_dim(array, (stack_pos ^ mask) * col_local, col_local, axis=2)
-
-    first = block_for(phases, 4)
-    phases, first = lax.optimization_barrier((phases, first))
-    blocks = [first if mask == 4 else block_for(phases, mask) for mask in range(stack_size)]
+        return [stacked.reshape(-1, col_local)], (0,)
+    blocks = cut(phases, col_local)
     found = {0: blocks[0]}
 
     def send(mask, after=None):
@@ -369,14 +418,10 @@
     ifg_local, row_local, col_range = phases.shape
     date_total = preconditioner.shape[0]
     date_pad = -(-(date_total + 8) // LANES) * LANES
-    stack_pos = lax.axis_index("stack")
-
-    chunks, order = exchange(phases, stack_pos, stack_size)
-    pairs = ifg_pairs.T.reshape(2, stack_size, ifg_local).transpose(1, 0, 2)
-    if not order:
-        pairs, order = ifg_pairs.T[None], (0,)
+
+    chunks, order = exchange(phases, stack_size)
     incidence, *gains, member, weighted, basis = prepare(
-        pairs, preconditioner, coherence, geo_tiles, date_pad, order,
+        ifg_pairs.T, preconditioner, coherence, geo_tiles, date_pad, order,
         col_range * range_size, row_local * azimuth_size,
     )
     early = []

time: 42 us -> 39.7 us (0.945)
  the two profiles are of different devices: /device:TPU:16 before, /device:TPU:24 now
where the time goes in v4:
time: 39.7 us; the launch traced here: 39.5 us
  starting transfers between devices  17.6 us (44%)
  Pallas kernels  12.5 us (31%)
  waiting for transfers between devices  9.31 us (23%)
    ppermute x7, starting transfers between devices, send(): lax.ppermute(block, 'stack', [(i, i ^ mask) for i in range(stack_size)])  9.68 us
    ppermute x5, waiting for transfers between devices, swap(): return lax.ppermute(value, axes, both)  8.03 us
    ppermute x5, starting transfers between devices, swap(): return lax.ppermute(value, axes, both)  7.89 us
    pallas_call x1, Pallas kernels, invert(): pl.pallas_call(functools.partial(invert_kernel, row_local=row_local, date...  4.66 us
    pallas_call x1, Pallas kernels, prepare(): pl.pallas_call(functools.partial(prepare_kernel, order=order, col_total=c...  4.39 us
    pallas_call x1, Pallas kernels, deramp(): pl.pallas_call(functools.partial(deramp_kernel, row_local=row_local, date...  1.54 us
    ppermute x7, waiting for transfers between devices, send(): lax.ppermute(block, 'stack', [(i, i ^ mask) for i in range(stack_size)])  1.29 us
    pallas_call x1, Pallas kernels, cut(): pl.pallas_call(cut_kernel, out_shape=[jax.ShapeDtypeStruct((ifg_local, ro...  1.2 us
  transfers between devices with their start and end apart: 12, of which 5 were waited for; matrix products, arithmetic and copies ran while one was open for 0% of the time, Pallas kernels for 13%

profile of v4, /device:TPU:24, one launch (start us, length us, event | category | flops | bytes accessed | tf_op | source)
XLA Modules:
  0.0 39.5 jit_solution(1013919536069270383)
XLA Ops:
  0.0 1.2 %cut.1 = (bf16[144,2,128]{2,1,0:T(2,128)(2,1)S(1)}, bf16[144,2,128]{2,1,0:T(2,128)(2,1)S(1)}, bf16[144,2,128]{2,1,0:T(2,128)(2,1)S(1)}, bf16[144,2,128]{2,1,0:T(...) custom-call(bf16[144,8,2,128]{3,2,1,0:T(2,128)(2,1)} %bitcast.21), custom_call_target="tpu_custom_call" | custom-call | tf_op jit(solution)/shard_map/cut/pallas_call | solution.py:291
  1.2 1.6 %collective-permute-start = (bf16[144,2,128]{2,1,0:T(2,128)(2,1)S(1)}, bf16[144,2,128]{2,1,0:T(2,128)(2,1)S(1)}, u32[]{:S(2)}, u32[]{:S(2)}) collective-permute-start(bf16[144,2,128]{2,1,0:T(2,128)(2,1)S(1)} %get-tuple-element.28), channel_id=1, source_target_pairs={{0,4},{4,0},{8,12},{12,8},{16,20},{20,16},{24,28},{28,24},{1,5},{5... | collective-permute-start | bytes 221192 | tf_op jit(solution)/shard_map/ppermute | solution.py:316
  2.8 0.4 %collective-permute-start.2 = (bf16[144,2,128]{2,1,0:T(2,128)(2,1)S(1)}, bf16[144,2,128]{2,1,0:T(2,128)(2,1)S(1)}, u32[]{:S(2)}, u32[]{:S(2)}) collective-permute-start(bf16[144,2,128]{2,1,0:T(2,128)(2,1)S(1)} %get-tuple-element.31), channel_id=1, source_target_pairs={{0,8},{4,12},{8,0},{12,4},{16,24},{20,28},{24,16},{28,20},{1,9},{5... | collective-permute-start | bytes 221192 | tf_op jit(solution)/shard_map/ppermute | solution.py:316
  3.2 0.3 collective-permute-start.4
  3.6 2.5 %collective-permute-start.5 = (bf16[144,2,128]{2,1,0:T(2,128)(2,1)S(1)}, bf16[144,2,128]{2,1,0:T(2,128)(2,1)S(1)}, u32[]{:S(2)}, u32[]{:S(2)}) collective-permute-start(bf16[144,2,128]{2,1,0:T(2,128)(2,1)S(1)} %get-tuple-element.36), channel_id=1, source_target_pairs={{0,20},{4,16},{8,28},{12,24},{16,4},{20,0},{24,12},{28,8},{1,21},{... | collective-permute-start | bytes 221192 | tf_op jit(solution)/shard_map/ppermute | solution.py:316
  6.1 1.3 %collective-permute-start.6 = (bf16[144,2,128]{2,1,0:T(2,128)(2,1)S(1)}, bf16[144,2,128]{2,1,0:T(2,128)(2,1)S(1)}, u32[]{:S(2)}, u32[]{:S(2)}) collective-permute-start(bf16[144,2,128]{2,1,0:T(2,128)(2,1)S(1)} %get-tuple-element.38), channel_id=1, source_target_pairs={{0,24},{4,28},{8,16},{12,20},{16,8},{20,12},{24,0},{28,4},{1,25},{... | collective-permute-start | bytes 221192 | tf_op jit(solution)/shard_map/ppermute | solution.py:316
  7.5 0.0 collective-permute-done
  7.5 3.4 %collective-permute-start.1 = (bf16[144,2,128]{2,1,0:T(2,128)(2,1)S(1)}, bf16[144,2,128]{2,1,0:T(2,128)(2,1)S(1)}, u32[]{:S(2)}, u32[]{:S(2)}) collective-permute-start(bf16[144,2,128]{2,1,0:T(2,128)(2,1)S(1)} %get-tuple-element.29), channel_id=1, source_target_pairs={{0,28},{4,24},{8,20},{12,16},{16,12},{20,8},{24,4},{28,0},{1,29},{... | collective-permute-start | bytes 221192 | tf_op jit(solution)/shard_map/ppermute | solution.py:316
  10.9 0.0 collective-permute-done.2
  10.9 0.0 collective-permute-start.3
  10.9 4.4 %prepare.1 = (bf16[1152,640]{1,0:T(8,128)(2,1)S(1)}, bf16[640,1152]{1,0:T(8,128)(2,1)S(1)}, bf16[640,1152]{1,0:T(8,128)(2,1)S(1)}, f32[16,256]{1,0:T(8,128)S(1)}...) custom-call(s32[2,1152]{1,0:T(2,128)} %bitcast.22, f32[600,600]{1,0:T(8,128)} %prec_hbm.1, s32[2,128]{1,0:T(2,128)} %coherence_hbm.1, ...), custom_call_target="tpu_custom_call" | custom-call | tf_op jit(solution)/shard_map/prepare/pallas_call | solution.py:115
  15.3 0.0 collective-permute-done.4
  15.3 1.3 %collective-permute-done.5 = bf16[144,2,128]{2,1,0:T(2,128)(2,1)S(1)} collective-permute-done((bf16[144,2,128]{2,1,0:T(2,128)(2,1)S(1)}, bf16[144,2,128]{2,1,0:T(2,128)(2,1)S(1)}, u32[]{:S(2)}, u32[]{:S(2)}) %collective-permute-start.5) | collective-permute-done | bytes 73760 | tf_op jit(solution)/shard_map/ppermute | solution.py:316
  16.6 0.0 collective-permute-done.6
  16.6 0.7 %early_fit.1 = (bf16[864,256]{1,0:T(8,128)(2,1)S(1)}, f32[640,256]{1,0:T(8,128)S(1)}) custom-call(bf16[288,128]{1,0:T(8,128)(2,1)S(1)} %bitcast.13, bf16[288,128]{1,0:T(8,128)(2,1)S(1)} %bitcast.14, bf16[288,128]{1,0:T(8,128)(2,1)S(1)} %bitcast.16, bf16[288,128]{1,0:T(8,128)(2,1)S(1)} %bitcast.17, bf16[288,128]{1,0:T(8,128)(2,1)S(1)} %bitcast.15, ...), custom_call_target="tpu_custom_call" | custom-call | tf_op jit(solution)/shard_map/early_fit/pallas_call | solution.py:162
  17.3 0.0 collective-permute-done.1
  17.4 0.0 collective-permute-done.3
  17.4 4.7 %invert.1 = (f32[640,256]{1,0:T(8,128)S(1)}, f32[16,640]{1,0:T(8,128)S(1)}) custom-call(bf16[288,128]{1,0:T(8,128)(2,1)S(1)} %bitcast.19, bf16[288,128]{1,0:T(8,128)(2,1)S(1)} %bitcast.20, bf16[864,256]{1,0:T(8,128)(2,1)S(1)} %get-tuple-element.41.refs_2_, f32[640,256]{1,0:T(8,128)S(1)} %get-tuple-element.42.refs_3_, ...), custom_call_target="tpu_custom_call" | custom-call | tf_op jit(solution)/shard_map/invert/pallas_call | solution.py:254
  22.0 2.1 %collective-permute-start.7 = (f32[8,640]{1,0:T(8,128)S(1)}, f32[8,640]{1,0:T(8,128)S(1)}, u32[]{:S(2)}, u32[]{:S(2)}) collective-permute-start(f32[8,640]{1,0:T(8,128)S(1)} %get-tuple-element.49), channel_id=1, source_target_pairs={{0,8},{4,12},{16,24},{20,28},{1,9},{5,13},{17,25},{21,29},{8,0},{1... | collective-permute-start | bytes 61448 | tf_op jit(solution)/shard_map/ppermute | solution.py:411
  24.1 2.3 %collective-permute-start.8 = (f32[8,640]{1,0:T(8,128)S(1)}, f32[8,640]{1,0:T(8,128)S(1)}, u32[]{:S(2)}, u32[]{:S(2)}) collective-permute-start(f32[8,640]{1,0:T(8,128)S(1)} %get-tuple-element.50), channel_id=1, source_target_pairs={{8,16},{12,20},{24,1},{28,5},{9,17},{13,21},{16,8},{20,12},{1,24},... | collective-permute-start | bytes 61448 | tf_op jit(solution)/shard_map/ppermute | solution.py:411
  26.4 0.0 collective-permute-done.7
  26.5 4.6 %collective-permute-done.8 = f32[8,640]{1,0:T(8,128)S(1)} collective-permute-done((f32[8,640]{1,0:T(8,128)S(1)}, f32[8,640]{1,0:T(8,128)S(1)}, u32[]{:S(2)}, u32[]{:S(2)}) %collective-permute-start.8) | collective-permute-done | bytes 20512 | tf_op jit(solution)/shard_map/ppermute | solution.py:411
  31.0 2.2 %collective-permute-start.11 = (f32[16,640]{1,0:T(8,128)S(1)}, f32[16,640]{1,0:T(8,128)S(1)}, u32[]{:S(2)}, u32[]{:S(2)}) collective-permute-start(f32[16,640]{1,0:T(8,128)S(1)} %maximum_add_fusion.first_ref), channel_id=1, source_target_pairs={{0,6},{2,4},{8,14},{10,12},{16,22},{18,20},{24,30},{26,28},{6,0},{... | collective-permute-start | bytes 122888 | tf_op jit(solution)/shard_map/ppermute | solution.py:411
  33.3 0.7 %collective-permute-start.10 = (f32[16,640]{1,0:T(8,128)S(1)}, f32[16,640]{1,0:T(8,128)S(1)}, u32[]{:S(2)}, u32[]{:S(2)}) collective-permute-start(f32[16,640]{1,0:T(8,128)S(1)} %maximum_add_fusion.first_ref), channel_id=1, source_target_pairs={{0,4},{8,12},{16,20},{24,28},{4,0},{12,8},{20,16},{28,24},{1,5},{9... | collective-permute-start | bytes 122888 | tf_op jit(solution)/shard_map/ppermute | solution.py:411
  34.0 0.5 %collective-permute-start.9 = (f32[16,640]{1,0:T(8,128)S(1)}, f32[16,640]{1,0:T(8,128)S(1)}, u32[]{:S(2)}, u32[]{:S(2)}) collective-permute-start(f32[16,640]{1,0:T(8,128)S(1)} %maximum_add_fusion.first_ref), channel_id=1, source_target_pairs={{0,2},{2,0},{1,3},{3,1},{4,6},{6,4},{5,7},{7,5},{8,10},{10,8},{9,1... | collective-permute-start | bytes 122888 | tf_op jit(solution)/shard_map/ppermute | solution.py:411
  34.5 1.4 %collective-permute-done.11.refs_2_ = f32[16,640]{1,0:T(8,128)S(1)} collective-permute-done((f32[16,640]{1,0:T(8,128)S(1)}, f32[16,640]{1,0:T(8,128)S(1)}, u32[]{:S(2)}, u32[]{:S(2)}) %collective-permute-start.11) | collective-permute-done | bytes 40992 | tf_op jit(solution)/shard_map/ppermute | solution.py:411
  35.9 1.3 %collective-permute-done.10.refs_1_ = f32[16,640]{1,0:T(8,128)S(1)} collective-permute-done((f32[16,640]{1,0:T(8,128)S(1)}, f32[16,640]{1,0:T(8,128)S(1)}, u32[]{:S(2)}, u32[]{:S(2)}) %collective-permute-start.10) | collective-permute-done | bytes 40992 | tf_op jit(solution)/shard_map/ppermute | solution.py:411
  37.3 0.7 %collective-permute-done.9.refs_0_ = f32[16,640]{1,0:T(8,128)S(1)} collective-permute-done((f32[16,640]{1,0:T(8,128)S(1)}, f32[16,640]{1,0:T(8,128)S(1)}, u32[]{:S(2)}, u32[]{:S(2)}) %collective-permute-start.9) | collective-permute-done | bytes 40992 | tf_op jit(solution)/shard_map/ppermute | solution.py:411
  38.0 1.5 %deramp.1 = f32[1200,128]{1,0:T(8,128)} custom-call(f32[16,640]{1,0:T(8,128)S(1)} %maximum_add_fusion.first_ref, f32[16,640]{1,0:T(8,128)S(1)} %collective-permute-done.9.refs_0_, f32[16,640]{1,0:T(8,128)S(1)} %collective-permute-done.10.refs_1_, f32[16,640]{1,0:T(8,128)S(1)} %collective-permute-done.11.refs_2_, f32[640,256]{1,0:T(8,128)S(1)} %get-tuple-element.47.refs_3_, ...), custom_call_target="tpu_custom_call" | custom-call | tf_op jit(solution)/shard_map/deramp/pallas_call | solution.py:398
  (2 shorter events, 0.0 us)
Async XLA Ops:
  1.2 6.3 %collective-permute-start = (bf16[144,2,128]{2,1,0:T(2,128)(2,1)S(1)}, bf16[144,2,128]{2,1,0:T(2,128)(2,1)S(1)}, u32[]{:S(2)}, u32[]{:S(2)}) collective-permute-start(bf16[144,2,128]{2,1,0:T(2,128)(2,1)S(1)} %get-tuple-element.28), channel_id=1, source_target_pairs={{0,4},{4,0},{8,12},{12,8},{16,20},{20,16},{24,28},{28,24},{1,5},{5... | collective-permute-start | bytes 221192 | tf_op jit(solution)/shard_map/ppermute | solution.py:316
  2.8 8.1 %collective-permute-start.2 = (bf16[144,2,128]{2,1,0:T(2,128)(2,1)S(1)}, bf16[144,2,128]{2,1,0:T(2,128)(2,1)S(1)}, u32[]{:S(2)}, u32[]{:S(2)}) collective-permute-start(bf16[144,2,128]{2,1,0:T(2,128)(2,1)S(1)} %get-tuple-element.31), channel_id=1, source_target_pairs={{0,8},{4,12},{8,0},{12,4},{16,24},{20,28},{24,16},{28,20},{1,9},{5... | collective-permute-start | bytes 221192 | tf_op jit(solution)/shard_map/ppermute | solution.py:316
  3.2 12.1 %collective-permute-start.4 = (bf16[144,2,128]{2,1,0:T(2,128)(2,1)S(1)}, bf16[144,2,128]{2,1,0:T(2,128)(2,1)S(1)}, u32[]{:S(2)}, u32[]{:S(2)}) collective-permute-start(bf16[144,2,128]{2,1,0:T(2,128)(2,1)S(1)} %get-tuple-element.35), channel_id=1, source_target_pairs={{0,16},{4,20},{8,24},{12,28},{16,0},{20,4},{24,8},{28,12},{1,17},{... | collective-permute-start | bytes 221192 | tf_op jit(solution)/shard_map/ppermute | solution.py:316
  3.6 13.0 %collective-permute-start.5 = (bf16[144,2,128]{2,1,0:T(2,128)(2,1)S(1)}, bf16[144,2,128]{2,1,0:T(2,128)(2,1)S(1)}, u32[]{:S(2)}, u32[]{:S(2)}) collective-permute-start(bf16[144,2,128]{2,1,0:T(2,128)(2,1)S(1)} %get-tuple-element.36), channel_id=1, source_target_pairs={{0,20},{4,16},{8,28},{12,24},{16,4},{20,0},{24,12},{28,8},{1,21},{... | collective-permute-start | bytes 221192 | tf_op jit(solution)/shard_map/ppermute | solution.py:316
  6.1 10.5 %collective-permute-start.6 = (bf16[144,2,128]{2,1,0:T(2,128)(2,1)S(1)}, bf16[144,2,128]{2,1,0:T(2,128)(2,1)S(1)}, u32[]{:S(2)}, u32[]{:S(2)}) collective-permute-start(bf16[144,2,128]{2,1,0:T(2,128)(2,1)S(1)} %get-tuple-element.38), channel_id=1, source_target_pairs={{0,24},{4,28},{8,16},{12,20},{16,8},{20,12},{24,0},{28,4},{1,25},{... | collective-permute-start | bytes 221192 | tf_op jit(solution)/shard_map/ppermute | solution.py:316
  7.5 9.9 %collective-permute-start.1 = (bf16[144,2,128]{2,1,0:T(2,128)(2,1)S(1)}, bf16[144,2,128]{2,1,0:T(2,128)(2,1)S(1)}, u32[]{:S(2)}, u32[]{:S(2)}) collective-permute-start(bf16[144,2,128]{2,1,0:T(2,128)(2,1)S(1)} %get-tuple-element.29), channel_id=1, source_target_pairs={{0,28},{4,24},{8,20},{12,16},{16,12},{20,8},{24,4},{28,0},{1,29},{... | collective-permute-start | bytes 221192 | tf_op jit(solution)/shard_map/ppermute | solution.py:316
  10.9 6.5 %collective-permute-start.3 = (bf16[144,2,128]{2,1,0:T(2,128)(2,1)S(1)}, bf16[144,2,128]{2,1,0:T(2,128)(2,1)S(1)}, u32[]{:S(2)}, u32[]{:S(2)}) collective-permute-start(bf16[144,2,128]{2,1,0:T(2,128)(2,1)S(1)} %get-tuple-element.32), channel_id=1, source_target_pairs={{0,12},{4,8},{8,4},{12,0},{16,28},{20,24},{24,20},{28,16},{1,13},{... | collective-permute-start | bytes 221192 | tf_op jit(solution)/shard_map/ppermute | solution.py:316
  22.0 4.4 %collective-permute-start.7 = (f32[8,640]{1,0:T(8,128)S(1)}, f32[8,640]{1,0:T(8,128)S(1)}, u32[]{:S(2)}, u32[]{:S(2)}) collective-permute-start(f32[8,640]{1,0:T(8,128)S(1)} %get-tuple-element.49), channel_id=1, source_target_pairs={{0,8},{4,12},{16,24},{20,28},{1,9},{5,13},{17,25},{21,29},{8,0},{1... | collective-permute-start | bytes 61448 | tf_op jit(solution)/shard_map/ppermute | solution.py:411
  24.1 6.9 %collective-permute-start.8 = (f32[8,640]{1,0:T(8,128)S(1)}, f32[8,640]{1,0:T(8,128)S(1)}, u32[]{:S(2)}, u32[]{:S(2)}) collective-permute-start(f32[8,640]{1,0:T(8,128)S(1)} %get-tuple-element.50), channel_id=1, source_target_pairs={{8,16},{12,20},{24,1},{28,5},{9,17},{13,21},{16,8},{20,12},{1,24},... | collective-permute-start | bytes 61448 | tf_op jit(solution)/shard_map/ppermute | solution.py:411
  31.0 4.9 %collective-permute-start.11 = (f32[16,640]{1,0:T(8,128)S(1)}, f32[16,640]{1,0:T(8,128)S(1)}, u32[]{:S(2)}, u32[]{:S(2)}) collective-permute-start(f32[16,640]{1,0:T(8,128)S(1)} %maximum_add_fusion.first_ref), channel_id=1, source_target_pairs={{0,6},{2,4},{8,14},{10,12},{16,22},{18,20},{24,30},{26,28},{6,0},{... | collective-permute-start | bytes 122888 | tf_op jit(solution)/shard_map/ppermute | solution.py:411
  33.3 4.0 %collective-permute-start.10 = (f32[16,640]{1,0:T(8,128)S(1)}, f32[16,640]{1,0:T(8,128)S(1)}, u32[]{:S(2)}, u32[]{:S(2)}) collective-permute-start(f32[16,640]{1,0:T(8,128)S(1)} %maximum_add_fusion.first_ref), channel_id=1, source_target_pairs={{0,4},{8,12},{16,20},{24,28},{4,0},{12,8},{20,16},{28,24},{1,5},{9... | collective-permute-start | bytes 122888 | tf_op jit(solution)/shard_map/ppermute | solution.py:411
  34.0 4.0 %collective-permute-start.9 = (f32[16,640]{1,0:T(8,128)S(1)}, f32[16,640]{1,0:T(8,128)S(1)}, u32[]{:S(2)}, u32[]{:S(2)}) collective-permute-start(f32[16,640]{1,0:T(8,128)S(1)} %maximum_add_fusion.first_ref), channel_id=1, source_target_pairs={{0,2},{2,0},{1,3},{3,1},{4,6},{6,4},{5,7},{7,5},{8,10},{10,8},{9,1... | collective-permute-start | bytes 122888 | tf_op jit(solution)/shard_map/ppermute | solution.py:411

commit v5 on v4

--- a/solution.py
+++ b/solution.py
@@ -10,11 +10,11 @@
 REWEIGHTS = 2
 LANES = 128
 VMEM_LIMIT = 24 * 1024 * 1024
-ROWS_A = 128
+ROWS_A = 192
 ROWS_B = 320
 APPROX = False
-ARRIVAL = (0, 1, 4, 5, 2, 6, 7, 3)
-EARLY = 6
+ARRIVAL = (0, 1, 2, 4, 5, 6, 7, 3)
+EARLY = (4, 6)
 OUT_PARTS = 5
 
 
@@ -95,7 +95,7 @@
     basis = jnp.concatenate([jnp.ones_like(coord_u), coord_u, coord_v], axis=0)
     spare = jnp.zeros((2, pixel_count), jnp.float32)
     lines = []
-    for base in (jnp.where(even, 2 * node + 1, 2 * node - 1), jnp.where(even, 2 * node - 1, 2 * node + 1)):
+    for base in (jnp.where(even, 2 * node - 1, 2 * node + 1), jnp.where(even, 2 * node + 1, 2 * node - 1)):
         for step in range(2):
             lines.append(basis * (tiles == base + step).astype(jnp.float32))
         lines.append(spare)
@@ -147,20 +147,30 @@
     return part
 
 
-def early_kernel(*refs, row_local):
+def early_kernel(*refs, row_local, start, end, late):
     *chunk_refs, gain_top, gain_low, data_ref, series_ref, wide = refs
-    unpack(chunk_refs, wide, data_ref, row_local)
-    columns = pl.ds(0, data_ref.shape[0] // 256 * 256)
-    for start in range(0, series_ref.shape[0], ROWS_B):
-        rows = pl.ds(start, ROWS_B)
-        series_ref[rows, :] = gained(gain_top, gain_low, rows, columns, data_ref[columns, :])
-
-
-def early_fit(chunks, gains, row_local):
+    unpack(chunk_refs[:late], wide, data_ref, row_local)
+    before = chunk_refs[late:]
+    columns = pl.ds(start, end - start)
+    value = data_ref[...]
+    if before:
+        held = before[0].shape[0] - start
+        value = jnp.concatenate([before[0][pl.ds(start, held), :], value[: end - start - held]], axis=0)
+    else:
+        value = value[:end]
+    for first in range(0, series_ref.shape[0], ROWS_B):
+        rows = pl.ds(first, ROWS_B)
+        part = gained(gain_top, gain_low, rows, columns, value)
+        series_ref[rows, :] = part + before[1][rows, :] if before else part
+
+
+def early_fit(chunks, before, gains, row_local, start, end):
     count = sum(chunk.shape[0] for chunk in chunks) // row_local
     pixel_count = chunks[0].shape[1] * row_local
     return pl.pallas_call(
-        functools.partial(early_kernel, row_local=row_local),
+        functools.partial(
+            early_kernel, row_local=row_local, start=start, end=end, late=len(chunks)
+        ),
         out_shape=[
             jax.ShapeDtypeStruct((count, pixel_count), jnp.bfloat16),
             jax.ShapeDtypeStruct((gains[0].shape[0], pixel_count), jnp.float32),
@@ -168,7 +178,7 @@
         scratch_shapes=[pltpu.VMEM(chunks[0].shape, jnp.float32)],
         compiler_params=pltpu.CompilerParams(vmem_limit_bytes=VMEM_LIMIT),
         name="early_fit",
-    )(*chunks, *gains)
+    )(*chunks, *before, *gains)
 
 
 def invert_kernel(*refs, row_local, date_total, late):
@@ -176,18 +186,32 @@
         *chunk_refs, incidence, gain_top, gain_low, weighted_ref, basis_ref, series_ref,
         moments_ref, wide, data, residual, moved,
     ) = refs
-    ifg_total, pixel_count = data.shape
+    ifg_total, pixel_count = moved.shape
     date_pad = gain_top.shape[0]
     late_refs, early_refs = chunk_refs[:late], chunk_refs[late:]
     done = 0
+    pieces = []
     if early_refs:
-        early_data, early_series = early_refs
-        held = early_data.shape[0]
-        done = held // 256 * 256
-        data[pl.ds(0, held), :] = early_data[...]
-        unpack(late_refs, wide, data.at[pl.ds(held, ifg_total - held)], row_local)
+        *early_data, early_series = early_refs
+        for ref in early_data:
+            count = ref.shape[0]
+            used = min(count, (done + count) // 128 * 128 - done) if ref is early_data[-1] else count
+            pieces.append((ref, done, used))
+            done += used
+        data[pl.ds(0, count - used), :] = early_data[-1][pl.ds(used, count - used), :]
+        unpack(late_refs, wide, data.at[pl.ds(count - used, ifg_total - done - count + used)], row_local)
     else:
         unpack(late_refs, wide, data, row_local)
+    pieces.append((data, done, ifg_total - done))
+
+    def observed(rows):
+        parts = []
+        for ref, first, count in pieces:
+            low, high = max(rows.start, first), min(rows.start + rows.size, first + count)
+            if low < high:
+                parts.append(ref[pl.ds(low - first, high - low), :])
+        return parts[0] if len(parts) == 1 else jnp.concatenate(parts, axis=0)
+
     coherence = basis_ref[3:4, :]
     date_tiles = [pl.ds(start, ROWS_B) for start in range(0, date_pad, ROWS_B)]
     ifg_tiles = [pl.ds(start, ROWS_A) for start in range(0, ifg_total, ROWS_A)]
@@ -207,7 +231,7 @@
     left_columns = pl.ds(done, ifg_total - done)
     tops, lows = [], []
     for rows in date_tiles:
-        part = gained(gain_top, gain_low, rows, left_columns, data[left_columns, :])
+        part = gained(gain_top, gain_low, rows, left_columns, data[...])
         if early_refs:
             part = part + early_series[rows, :]
         series_ref[rows, :] = part
@@ -218,14 +242,14 @@
     total = jnp.zeros((8, pixel_count), jnp.float32)
     for rows in ifg_tiles:
         fit = product(incidence[rows, :], top) + product(incidence[rows, :], low)
-        left = data[rows, :].astype(jnp.float32) - fit
+        left = observed(rows).astype(jnp.float32) - fit
         residual[rows, :] = left
         total = total + folded(left * left)
     reweighted(total)
     for sweep in range(1, REWEIGHTS):
         steps = []
         for rows in date_tiles:
-            part = gained(gain_top, gain_low, rows, everything, moved[...])
+            part = gained(gain_top, None, rows, everything, moved[...])
             steps.append(part.astype(jnp.bfloat16))
             series_ref[rows, :] = series_ref[rows, :] + part
         step = jnp.concatenate(steps, axis=0)
@@ -234,6 +258,9 @@
             left = residual[rows, :] - product(incidence[rows, :], step)
             residual[rows, :] = left
             total = total + folded(left * left)
+        held = moved[...]
+        for rows in date_tiles:
+            series_ref[rows, :] = series_ref[rows, :] + product(gain_low[rows, :], held)
         reweighted(total)
     for rows in date_tiles:
         part = gained(gain_top, None, rows, everything, moved[...])
@@ -249,6 +276,7 @@
 
 def invert(late_chunks, early, incidence, gains, weighted, basis, row_local, date_total):
     ifg_total = incidence.shape[0]
+    kept = sum(value.shape[0] for value in early[:-1]) // 128 * 128
     date_pad = gains[0].shape[0]
     pixel_count = weighted.shape[1]
     return pl.pallas_call(
@@ -261,7 +289,7 @@
         ],
         scratch_shapes=[
             pltpu.VMEM(late_chunks[0].shape, jnp.float32),
-            pltpu.VMEM((ifg_total, pixel_count), jnp.bfloat16),
+            pltpu.VMEM((ifg_total - kept, pixel_count), jnp.bfloat16),
             pltpu.VMEM((ifg_total, pixel_count), jnp.float32),
             pltpu.VMEM((ifg_total, pixel_count), jnp.bfloat16),
         ],
@@ -425,9 +453,16 @@
         col_range * range_size, row_local * azimuth_size,
     )
     early = []
-    if len(chunks) > EARLY:
-        early = early_fit(chunks[:EARLY], gains, row_local)
-        chunks = chunks[EARLY:]
+    if len(chunks) > 1:
+        first, second = EARLY
+        count = ifg_local * first // 256 * 256
+        data_a, series_a = early_fit(chunks[:first], [], gains, row_local, 0, count)
+        data_b, series_b = early_fit(
+            chunks[first:second], [data_a, series_a], gains, row_local, count,
+            ifg_local * second // 128 * 128,
+        )
+        early = [data_a, data_b, series_b]
+        chunks = chunks[second:]
 
     series, moments = invert(
         chunks, early, incidence, gains, weighted, basis, row_local, date_total
@@ -444,8 +479,8 @@
         (place(block), place(block + 2)) for block in range(block_count - 2) if block // 2 % 2 == 1
     ]
     axes = ("stack", "range")
-    second = swap(moments[8:], axes, outer)
-    first = swap(moments[:8], axes, inner)
+    first = swap(moments[:8], axes, outer)
+    second = swap(moments[8:], axes, inner)
     moments = moments + jnp.concatenate([first, second], axis=0)
     pairs = [(i, i + 1) for i in range(0, stack_size, 2)]
     crossed = [

time: 39.7 us -> 40.5 us (1.020)
  the two profiles are of different devices: /device:TPU:24 before, /device:TPU:0 now
where the time goes in v5:
time: 40.5 us; the launch traced here: 40.3 us
  starting transfers between devices  21.6 us (53%)
  Pallas kernels  12.3 us (30%)
  waiting for transfers between devices  6.18 us (15%)
    ppermute x7, starting transfers between devices, send(): lax.ppermute(block, 'stack', [(i, i ^ mask) for i in range(stack_size)])  12.3 us
    ppermute x5, starting transfers between devices, swap(): return lax.ppermute(value, axes, both)  9.38 us
    ppermute x5, waiting for transfers between devices, swap(): return lax.ppermute(value, axes, both)  5.32 us
    pallas_call x1, Pallas kernels, prepare(): pl.pallas_call(functools.partial(prepare_kernel, order=order, col_total=c...  4.39 us
    pallas_call x1, Pallas kernels, invert(): pl.pallas_call(functools.partial(invert_kernel, row_local=row_local, date...  4.29 us
    pallas_call x1, Pallas kernels, deramp(): pl.pallas_call(functools.partial(deramp_kernel, row_local=row_local, date...  1.54 us
    pallas_call x1, Pallas kernels, cut(): pl.pallas_call(cut_kernel, out_shape=[jax.ShapeDtypeStruct((ifg_local, ro...  1.2 us
    pallas_call x2, Pallas kernels, early_fit(): pl.pallas_call(functools.partial(early_kernel, row_local=row_local, start...  0.92 us
  transfers between devices with their start and end apart: 12, of which 5 were waited for; matrix products, arithmetic and copies ran while one was open for 0% of the time, Pallas kernels for 13%

profile of v5, /device:TPU:0, one launch (start us, length us, event | category | flops | bytes accessed | tf_op | source)
XLA Modules:
  0.0 40.3 jit_solution(10256245036890188655)
XLA Ops:
  0.0 1.2 %cut.1 = (bf16[144,2,128]{2,1,0:T(2,128)(2,1)S(1)}, bf16[144,2,128]{2,1,0:T(2,128)(2,1)S(1)}, bf16[144,2,128]{2,1,0:T(2,128)(2,1)S(1)}, bf16[144,2,128]{2,1,0:T(...) custom-call(bf16[144,8,2,128]{3,2,1,0:T(2,128)(2,1)} %bitcast.21), custom_call_target="tpu_custom_call" | custom-call | tf_op jit(solution)/shard_map/cut/pallas_call | solution.py:319
  1.2 3.0 %collective-permute-start = (bf16[144,2,128]{2,1,0:T(2,128)(2,1)S(1)}, bf16[144,2,128]{2,1,0:T(2,128)(2,1)S(1)}, u32[]{:S(2)}, u32[]{:S(2)}) collective-permute-start(bf16[144,2,128]{2,1,0:T(2,128)(2,1)S(1)} %get-tuple-element.30), channel_id=1, source_target_pairs={{0,4},{4,0},{8,12},{12,8},{16,20},{20,16},{24,28},{28,24},{1,5},{5... | collective-permute-start | bytes 221192 | tf_op jit(solution)/shard_map/ppermute | solution.py:344
  4.2 1.6 %collective-permute-start.2 = (bf16[144,2,128]{2,1,0:T(2,128)(2,1)S(1)}, bf16[144,2,128]{2,1,0:T(2,128)(2,1)S(1)}, u32[]{:S(2)}, u32[]{:S(2)}) collective-permute-start(bf16[144,2,128]{2,1,0:T(2,128)(2,1)S(1)} %get-tuple-element.33), channel_id=1, source_target_pairs={{0,8},{4,12},{8,0},{12,4},{16,24},{20,28},{24,16},{28,20},{1,9},{5... | collective-permute-start | bytes 221192 | tf_op jit(solution)/shard_map/ppermute | solution.py:344
  5.8 2.6 %collective-permute-start.4 = (bf16[144,2,128]{2,1,0:T(2,128)(2,1)S(1)}, bf16[144,2,128]{2,1,0:T(2,128)(2,1)S(1)}, u32[]{:S(2)}, u32[]{:S(2)}) collective-permute-start(bf16[144,2,128]{2,1,0:T(2,128)(2,1)S(1)} %get-tuple-element.38), channel_id=1, source_target_pairs={{0,16},{4,20},{8,24},{12,28},{16,0},{20,4},{24,8},{28,12},{1,17},{... | collective-permute-start | bytes 221192 | tf_op jit(solution)/shard_map/ppermute | solution.py:344
  8.4 0.3 collective-permute-start.5
  8.7 2.5 %collective-permute-start.6 = (bf16[144,2,128]{2,1,0:T(2,128)(2,1)S(1)}, bf16[144,2,128]{2,1,0:T(2,128)(2,1)S(1)}, u32[]{:S(2)}, u32[]{:S(2)}) collective-permute-start(bf16[144,2,128]{2,1,0:T(2,128)(2,1)S(1)} %get-tuple-element.43), channel_id=1, source_target_pairs={{0,24},{4,28},{8,16},{12,20},{16,8},{20,12},{24,0},{28,4},{1,25},{... | collective-permute-start | bytes 221192 | tf_op jit(solution)/shard_map/ppermute | solution.py:344
  11.2 0.0 collective-permute-done
  11.2 2.3 %collective-permute-start.1 = (bf16[144,2,128]{2,1,0:T(2,128)(2,1)S(1)}, bf16[144,2,128]{2,1,0:T(2,128)(2,1)S(1)}, u32[]{:S(2)}, u32[]{:S(2)}) collective-permute-start(bf16[144,2,128]{2,1,0:T(2,128)(2,1)S(1)} %get-tuple-element.31), channel_id=1, source_target_pairs={{0,28},{4,24},{8,20},{12,16},{16,12},{20,8},{24,4},{28,0},{1,29},{... | collective-permute-start | bytes 221192 | tf_op jit(solution)/shard_map/ppermute | solution.py:344
  13.5 0.0 collective-permute-done.2
  13.5 0.0 collective-permute-start.3
  13.5 4.4 %prepare.1 = (bf16[1152,640]{1,0:T(8,128)(2,1)S(1)}, bf16[640,1152]{1,0:T(8,128)(2,1)S(1)}, bf16[640,1152]{1,0:T(8,128)(2,1)S(1)}, f32[16,256]{1,0:T(8,128)S(1)}...) custom-call(s32[2,1152]{1,0:T(2,128)} %bitcast.22, f32[600,600]{1,0:T(8,128)} %prec_hbm.1, s32[2,128]{1,0:T(2,128)} %coherence_hbm.1, ...), custom_call_target="tpu_custom_call" | custom-call | tf_op jit(solution)/shard_map/prepare/pallas_call | solution.py:115
  17.9 0.0 collective-permute-done.4
  17.9 0.6 %early_fit.2 = (bf16[576,256]{1,0:T(8,128)(2,1)S(1)}, f32[640,256]{1,0:T(8,128)S(1)}) custom-call(bf16[288,128]{1,0:T(8,128)(2,1)S(1)} %bitcast.13, bf16[288,128]{1,0:T(8,128)(2,1)S(1)} %bitcast.14, bf16[288,128]{1,0:T(8,128)(2,1)S(1)} %bitcast.15, bf16[288,128]{1,0:T(8,128)(2,1)S(1)} %bitcast.16, bf16[640,1152]{1,0:T(8,128)(2,1)S(1)} %get-tuple-element.39.refs_4_.refs_6_, ...), custom_call_target="tpu_custom_call" | custom-call | tf_op jit(solution)/shard_map/early_fit/pallas_call | solution.py:170
  18.4 0.0 collective-permute-done.5
  18.5 0.0 collective-permute-done.6
  18.5 0.4 early_fit.3
  18.8 0.0 collective-permute-done.1
  18.9 0.8 %collective-permute-done.3 = bf16[144,2,128]{2,1,0:T(2,128)(2,1)S(1)} collective-permute-done((bf16[144,2,128]{2,1,0:T(2,128)(2,1)S(1)}, bf16[144,2,128]{2,1,0:T(2,128)(2,1)S(1)}, u32[]{:S(2)}, u32[]{:S(2)}) %collective-permute-start.3) | collective-permute-done | bytes 73760 | tf_op jit(solution)/shard_map/ppermute | solution.py:344
  19.7 4.3 %invert.1 = (f32[640,256]{1,0:T(8,128)S(1)}, f32[16,640]{1,0:T(8,128)S(1)}) custom-call(bf16[288,128]{1,0:T(8,128)(2,1)S(1)} %bitcast.17, bf16[288,128]{1,0:T(8,128)(2,1)S(1)} %bitcast.20, bf16[576,256]{1,0:T(8,128)(2,1)S(1)} %get-tuple-element.41.refs_2_, bf16[288,256]{1,0:T(8,128)(2,1)S(1)} %get-tuple-element.45.refs_3_, ...), custom_call_target="tpu_custom_call" | custom-call | tf_op jit(solution)/shard_map/invert/pallas_call | solution.py:282
  24.0 0.7 %collective-permute-start.7 = (f32[8,640]{1,0:T(8,128)S(1)}, f32[8,640]{1,0:T(8,128)S(1)}, u32[]{:S(2)}, u32[]{:S(2)}) collective-permute-start(f32[8,640]{1,0:T(8,128)S(1)} %get-tuple-element.53), channel_id=1, source_target_pairs={{8,16},{12,20},{24,1},{28,5},{9,17},{13,21},{16,8},{20,12},{1,24},... | collective-permute-start | bytes 61448 | tf_op jit(solution)/shard_map/ppermute | solution.py:439
  24.7 5.2 %collective-permute-start.8 = (f32[8,640]{1,0:T(8,128)S(1)}, f32[8,640]{1,0:T(8,128)S(1)}, u32[]{:S(2)}, u32[]{:S(2)}) collective-permute-start(f32[8,640]{1,0:T(8,128)S(1)} %get-tuple-element.54), channel_id=1, source_target_pairs={{0,8},{4,12},{16,24},{20,28},{1,9},{5,13},{17,25},{21,29},{8,0},{1... | collective-permute-start | bytes 61448 | tf_op jit(solution)/shard_map/ppermute | solution.py:439
  29.9 0.0 collective-permute-done.7
  29.9 1.8 %collective-permute-done.8 = f32[8,640]{1,0:T(8,128)S(1)} collective-permute-done((f32[8,640]{1,0:T(8,128)S(1)}, f32[8,640]{1,0:T(8,128)S(1)}, u32[]{:S(2)}, u32[]{:S(2)}) %collective-permute-start.8) | collective-permute-done | bytes 20512 | tf_op jit(solution)/shard_map/ppermute | solution.py:439
  31.8 2.3 %collective-permute-start.11 = (f32[16,640]{1,0:T(8,128)S(1)}, f32[16,640]{1,0:T(8,128)S(1)}, u32[]{:S(2)}, u32[]{:S(2)}) collective-permute-start(f32[16,640]{1,0:T(8,128)S(1)} %maximum_add_fusion.first_ref), channel_id=1, source_target_pairs={{0,6},{2,4},{8,14},{10,12},{16,22},{18,20},{24,30},{26,28},{6,0},{... | collective-permute-start | bytes 122888 | tf_op jit(solution)/shard_map/ppermute | solution.py:439
  34.0 0.7 %collective-permute-start.10 = (f32[16,640]{1,0:T(8,128)S(1)}, f32[16,640]{1,0:T(8,128)S(1)}, u32[]{:S(2)}, u32[]{:S(2)}) collective-permute-start(f32[16,640]{1,0:T(8,128)S(1)} %maximum_add_fusion.first_ref), channel_id=1, source_target_pairs={{0,4},{8,12},{16,20},{24,28},{4,0},{12,8},{20,16},{28,24},{1,5},{9... | collective-permute-start | bytes 122888 | tf_op jit(solution)/shard_map/ppermute | solution.py:439
  34.7 0.5 %collective-permute-start.9 = (f32[16,640]{1,0:T(8,128)S(1)}, f32[16,640]{1,0:T(8,128)S(1)}, u32[]{:S(2)}, u32[]{:S(2)}) collective-permute-start(f32[16,640]{1,0:T(8,128)S(1)} %maximum_add_fusion.first_ref), channel_id=1, source_target_pairs={{0,2},{2,0},{1,3},{3,1},{4,6},{6,4},{5,7},{7,5},{8,10},{10,8},{9,1... | collective-permute-start | bytes 122888 | tf_op jit(solution)/shard_map/ppermute | solution.py:439
  35.2 1.4 %collective-permute-done.11.refs_2_ = f32[16,640]{1,0:T(8,128)S(1)} collective-permute-done((f32[16,640]{1,0:T(8,128)S(1)}, f32[16,640]{1,0:T(8,128)S(1)}, u32[]{:S(2)}, u32[]{:S(2)}) %collective-permute-start.11) | collective-permute-done | bytes 40992 | tf_op jit(solution)/shard_map/ppermute | solution.py:439
  36.7 1.3 %collective-permute-done.10.refs_1_ = f32[16,640]{1,0:T(8,128)S(1)} collective-permute-done((f32[16,640]{1,0:T(8,128)S(1)}, f32[16,640]{1,0:T(8,128)S(1)}, u32[]{:S(2)}, u32[]{:S(2)}) %collective-permute-start.10) | collective-permute-done | bytes 40992 | tf_op jit(solution)/shard_map/ppermute | solution.py:439
  38.0 0.7 %collective-permute-done.9.refs_0_ = f32[16,640]{1,0:T(8,128)S(1)} collective-permute-done((f32[16,640]{1,0:T(8,128)S(1)}, f32[16,640]{1,0:T(8,128)S(1)}, u32[]{:S(2)}, u32[]{:S(2)}) %collective-permute-start.9) | collective-permute-done | bytes 40992 | tf_op jit(solution)/shard_map/ppermute | solution.py:439
  38.7 1.5 %deramp.1 = f32[1200,128]{1,0:T(8,128)} custom-call(f32[16,640]{1,0:T(8,128)S(1)} %maximum_add_fusion.first_ref, f32[16,640]{1,0:T(8,128)S(1)} %collective-permute-done.9.refs_0_, f32[16,640]{1,0:T(8,128)S(1)} %collective-permute-done.10.refs_1_, f32[16,640]{1,0:T(8,128)S(1)} %collective-permute-done.11.refs_2_, f32[640,256]{1,0:T(8,128)S(1)} %get-tuple-element.51.refs_3_, ...), custom_call_target="tpu_custom_call" | custom-call | tf_op jit(solution)/shard_map/deramp/pallas_call | solution.py:426
  (2 shorter events, 0.0 us)
Async XLA Ops:
  1.2 10.0 %collective-permute-start = (bf16[144,2,128]{2,1,0:T(2,128)(2,1)S(1)}, bf16[144,2,128]{2,1,0:T(2,128)(2,1)S(1)}, u32[]{:S(2)}, u32[]{:S(2)}) collective-permute-start(bf16[144,2,128]{2,1,0:T(2,128)(2,1)S(1)} %get-tuple-element.30), channel_id=1, source_target_pairs={{0,4},{4,0},{8,12},{12,8},{16,20},{20,16},{24,28},{28,24},{1,5},{5... | collective-permute-start | bytes 221192 | tf_op jit(solution)/shard_map/ppermute | solution.py:344
  4.2 9.2 %collective-permute-start.2 = (bf16[144,2,128]{2,1,0:T(2,128)(2,1)S(1)}, bf16[144,2,128]{2,1,0:T(2,128)(2,1)S(1)}, u32[]{:S(2)}, u32[]{:S(2)}) collective-permute-start(bf16[144,2,128]{2,1,0:T(2,128)(2,1)S(1)} %get-tuple-element.33), channel_id=1, source_target_pairs={{0,8},{4,12},{8,0},{12,4},{16,24},{20,28},{24,16},{28,20},{1,9},{5... | collective-permute-start | bytes 221192 | tf_op jit(solution)/shard_map/ppermute | solution.py:344
  5.8 12.1 %collective-permute-start.4 = (bf16[144,2,128]{2,1,0:T(2,128)(2,1)S(1)}, bf16[144,2,128]{2,1,0:T(2,128)(2,1)S(1)}, u32[]{:S(2)}, u32[]{:S(2)}) collective-permute-start(bf16[144,2,128]{2,1,0:T(2,128)(2,1)S(1)} %get-tuple-element.38), channel_id=1, source_target_pairs={{0,16},{4,20},{8,24},{12,28},{16,0},{20,4},{24,8},{28,12},{1,17},{... | collective-permute-start | bytes 221192 | tf_op jit(solution)/shard_map/ppermute | solution.py:344
  8.4 10.0 %collective-permute-start.5 = (bf16[144,2,128]{2,1,0:T(2,128)(2,1)S(1)}, bf16[144,2,128]{2,1,0:T(2,128)(2,1)S(1)}, u32[]{:S(2)}, u32[]{:S(2)}) collective-permute-start(bf16[144,2,128]{2,1,0:T(2,128)(2,1)S(1)} %get-tuple-element.42), channel_id=1, source_target_pairs={{0,20},{4,16},{8,28},{12,24},{16,4},{20,0},{24,12},{28,8},{1,21},{... | collective-permute-start | bytes 221192 | tf_op jit(solution)/shard_map/ppermute | solution.py:344
  8.7 9.8 %collective-permute-start.6 = (bf16[144,2,128]{2,1,0:T(2,128)(2,1)S(1)}, bf16[144,2,128]{2,1,0:T(2,128)(2,1)S(1)}, u32[]{:S(2)}, u32[]{:S(2)}) collective-permute-start(bf16[144,2,128]{2,1,0:T(2,128)(2,1)S(1)} %get-tuple-element.43), channel_id=1, source_target_pairs={{0,24},{4,28},{8,16},{12,20},{16,8},{20,12},{24,0},{28,4},{1,25},{... | collective-permute-start | bytes 221192 | tf_op jit(solution)/shard_map/ppermute | solution.py:344
  11.2 7.7 %collective-permute-start.1 = (bf16[144,2,128]{2,1,0:T(2,128)(2,1)S(1)}, bf16[144,2,128]{2,1,0:T(2,128)(2,1)S(1)}, u32[]{:S(2)}, u32[]{:S(2)}) collective-permute-start(bf16[144,2,128]{2,1,0:T(2,128)(2,1)S(1)} %get-tuple-element.31), channel_id=1, source_target_pairs={{0,28},{4,24},{8,20},{12,16},{16,12},{20,8},{24,4},{28,0},{1,29},{... | collective-permute-start | bytes 221192 | tf_op jit(solution)/shard_map/ppermute | solution.py:344
  13.5 6.2 %collective-permute-start.3 = (bf16[144,2,128]{2,1,0:T(2,128)(2,1)S(1)}, bf16[144,2,128]{2,1,0:T(2,128)(2,1)S(1)}, u32[]{:S(2)}, u32[]{:S(2)}) collective-permute-start(bf16[144,2,128]{2,1,0:T(2,128)(2,1)S(1)} %get-tuple-element.34), channel_id=1, source_target_pairs={{0,12},{4,8},{8,4},{12,0},{16,28},{20,24},{24,20},{28,16},{1,13},{... | collective-permute-start | bytes 221192 | tf_op jit(solution)/shard_map/ppermute | solution.py:344
  24.0 5.9 %collective-permute-start.7 = (f32[8,640]{1,0:T(8,128)S(1)}, f32[8,640]{1,0:T(8,128)S(1)}, u32[]{:S(2)}, u32[]{:S(2)}) collective-permute-start(f32[8,640]{1,0:T(8,128)S(1)} %get-tuple-element.53), channel_id=1, source_target_pairs={{8,16},{12,20},{24,1},{28,5},{9,17},{13,21},{16,8},{20,12},{1,24},... | collective-permute-start | bytes 61448 | tf_op jit(solution)/shard_map/ppermute | solution.py:439
  24.7 7.1 %collective-permute-start.8 = (f32[8,640]{1,0:T(8,128)S(1)}, f32[8,640]{1,0:T(8,128)S(1)}, u32[]{:S(2)}, u32[]{:S(2)}) collective-permute-start(f32[8,640]{1,0:T(8,128)S(1)} %get-tuple-element.54), channel_id=1, source_target_pairs={{0,8},{4,12},{16,24},{20,28},{1,9},{5,13},{17,25},{21,29},{8,0},{1... | collective-permute-start | bytes 61448 | tf_op jit(solution)/shard_map/ppermute | solution.py:439
  31.8 4.9 %collective-permute-start.11 = (f32[16,640]{1,0:T(8,128)S(1)}, f32[16,640]{1,0:T(8,128)S(1)}, u32[]{:S(2)}, u32[]{:S(2)}) collective-permute-start(f32[16,640]{1,0:T(8,128)S(1)} %maximum_add_fusion.first_ref), channel_id=1, source_target_pairs={{0,6},{2,4},{8,14},{10,12},{16,22},{18,20},{24,30},{26,28},{6,0},{... | collective-permute-start | bytes 122888 | tf_op jit(solution)/shard_map/ppermute | solution.py:439
  34.0 4.0 %collective-permute-start.10 = (f32[16,640]{1,0:T(8,128)S(1)}, f32[16,640]{1,0:T(8,128)S(1)}, u32[]{:S(2)}, u32[]{:S(2)}) collective-permute-start(f32[16,640]{1,0:T(8,128)S(1)} %maximum_add_fusion.first_ref), channel_id=1, source_target_pairs={{0,4},{8,12},{16,20},{24,28},{4,0},{12,8},{20,16},{28,24},{1,5},{9... | collective-permute-start | bytes 122888 | tf_op jit(solution)/shard_map/ppermute | solution.py:439
  34.7 4.0 %collective-permute-start.9 = (f32[16,640]{1,0:T(8,128)S(1)}, f32[16,640]{1,0:T(8,128)S(1)}, u32[]{:S(2)}, u32[]{:S(2)}) collective-permute-start(f32[16,640]{1,0:T(8,128)S(1)} %maximum_add_fusion.first_ref), channel_id=1, source_target_pairs={{0,2},{2,0},{1,3},{3,1},{4,6},{6,4},{5,7},{7,5},{8,10},{10,8},{9,1... | collective-permute-start | bytes 122888 | tf_op jit(solution)/shard_map/ppermute | solution.py:439

commit v6 on v5

--- a/solution.py
+++ b/solution.py
@@ -479,7 +479,10 @@
         (place(block), place(block + 2)) for block in range(block_count - 2) if block // 2 % 2 == 1
     ]
     axes = ("stack", "range")
+    outer += [(place(0), place(1)), (place(block_count - 2), place(block_count - 1))]
     first = swap(moments[:8], axes, outer)
+    node = (lax.axis_index("range") * stack_size + lax.axis_index("stack")) // 2
+    first = jnp.where((node > 0) & (node < block_count // 2 - 1), first, 0.0)
     second = swap(moments[8:], axes, inner)
     moments = moments + jnp.concatenate([first, second], axis=0)
     pairs = [(i, i + 1) for i in range(0, stack_size, 2)]

time: 40.5 us -> 39.4 us (0.973)
  starting transfers between devices: 21.6 us -> 19.7 us
  waiting for transfers between devices: 6.18 us -> 7.04 us
    ppermute x5, starting transfers between devices: 9.38 us -> 7.44 us  [swap(): return lax.ppermute(value, axes, both)]
    ppermute x5, waiting for transfers between devices: 5.32 us -> 6.17 us  [swap(): return lax.ppermute(value, axes, both)]
  transfers between devices with their start and end apart: 12 -> 12, of which waited for: 5 -> 5; matrix products, arithmetic and copies ran while one was open for 0% -> 0% of each run, Pallas kernels for 13% -> 14%
where the time goes in v6:
time: 39.4 us; the launch traced here: 39.2 us
  starting transfers between devices  19.7 us (50%)
  Pallas kernels  12.3 us (31%)
  waiting for transfers between devices  7.04 us (18%)
    ppermute x7, starting transfers between devices, send(): lax.ppermute(block, 'stack', [(i, i ^ mask) for i in range(stack_size)])  12.3 us
    ppermute x5, starting transfers between devices, swap(): return lax.ppermute(value, axes, both)  7.44 us
    ppermute x5, waiting for transfers between devices, swap(): return lax.ppermute(value, axes, both)  6.17 us
    pallas_call x1, Pallas kernels, prepare(): pl.pallas_call(functools.partial(prepare_kernel, order=order, col_total=c...  4.39 us
    pallas_call x1, Pallas kernels, invert(): pl.pallas_call(functools.partial(invert_kernel, row_local=row_local, date...  4.29 us
    pallas_call x1, Pallas kernels, deramp(): pl.pallas_call(functools.partial(deramp_kernel, row_local=row_local, date...  1.54 us
    pallas_call x1, Pallas kernels, cut(): pl.pallas_call(cut_kernel, out_shape=[jax.ShapeDtypeStruct((ifg_local, ro...  1.2 us
    pallas_call x2, Pallas kernels, early_fit(): pl.pallas_call(functools.partial(early_kernel, row_local=row_local, start...  0.92 us
  transfers between devices with their start and end apart: 12, of which 5 were waited for; matrix products, arithmetic and copies ran while one was open for 0% of the time, Pallas kernels for 14%

profile of v6, /device:TPU:0, one launch (start us, length us, event | category | flops | bytes accessed | tf_op | source)
XLA Modules:
  0.0 39.2 jit_solution(1823313724251442982)
XLA Ops:
  0.0 1.2 %cut.1 = (bf16[144,2,128]{2,1,0:T(2,128)(2,1)S(1)}, bf16[144,2,128]{2,1,0:T(2,128)(2,1)S(1)}, bf16[144,2,128]{2,1,0:T(2,128)(2,1)S(1)}, bf16[144,2,128]{2,1,0:T(...) custom-call(bf16[144,8,2,128]{3,2,1,0:T(2,128)(2,1)} %bitcast.21), custom_call_target="tpu_custom_call" | custom-call | tf_op jit(solution)/shard_map/cut/pallas_call | solution.py:319
  1.2 3.0 %collective-permute-start = (bf16[144,2,128]{2,1,0:T(2,128)(2,1)S(1)}, bf16[144,2,128]{2,1,0:T(2,128)(2,1)S(1)}, u32[]{:S(2)}, u32[]{:S(2)}) collective-permute-start(bf16[144,2,128]{2,1,0:T(2,128)(2,1)S(1)} %get-tuple-element.30), channel_id=1, source_target_pairs={{0,4},{4,0},{8,12},{12,8},{16,20},{20,16},{24,28},{28,24},{1,5},{5... | collective-permute-start | bytes 221192 | tf_op jit(solution)/shard_map/ppermute | solution.py:344
  4.2 1.6 %collective-permute-start.2 = (bf16[144,2,128]{2,1,0:T(2,128)(2,1)S(1)}, bf16[144,2,128]{2,1,0:T(2,128)(2,1)S(1)}, u32[]{:S(2)}, u32[]{:S(2)}) collective-permute-start(bf16[144,2,128]{2,1,0:T(2,128)(2,1)S(1)} %get-tuple-element.33), channel_id=1, source_target_pairs={{0,8},{4,12},{8,0},{12,4},{16,24},{20,28},{24,16},{28,20},{1,9},{5... | collective-permute-start | bytes 221192 | tf_op jit(solution)/shard_map/ppermute | solution.py:344
  5.8 2.6 %collective-permute-start.4 = (bf16[144,2,128]{2,1,0:T(2,128)(2,1)S(1)}, bf16[144,2,128]{2,1,0:T(2,128)(2,1)S(1)}, u32[]{:S(2)}, u32[]{:S(2)}) collective-permute-start(bf16[144,2,128]{2,1,0:T(2,128)(2,1)S(1)} %get-tuple-element.38), channel_id=1, source_target_pairs={{0,16},{4,20},{8,24},{12,28},{16,0},{20,4},{24,8},{28,12},{1,17},{... | collective-permute-start | bytes 221192 | tf_op jit(solution)/shard_map/ppermute | solution.py:344
  8.4 0.3 collective-permute-start.5
  8.7 2.5 %collective-permute-start.6 = (bf16[144,2,128]{2,1,0:T(2,128)(2,1)S(1)}, bf16[144,2,128]{2,1,0:T(2,128)(2,1)S(1)}, u32[]{:S(2)}, u32[]{:S(2)}) collective-permute-start(bf16[144,2,128]{2,1,0:T(2,128)(2,1)S(1)} %get-tuple-element.43), channel_id=1, source_target_pairs={{0,24},{4,28},{8,16},{12,20},{16,8},{20,12},{24,0},{28,4},{1,25},{... | collective-permute-start | bytes 221192 | tf_op jit(solution)/shard_map/ppermute | solution.py:344
  11.2 0.0 collective-permute-done
  11.2 2.3 %collective-permute-start.1 = (bf16[144,2,128]{2,1,0:T(2,128)(2,1)S(1)}, bf16[144,2,128]{2,1,0:T(2,128)(2,1)S(1)}, u32[]{:S(2)}, u32[]{:S(2)}) collective-permute-start(bf16[144,2,128]{2,1,0:T(2,128)(2,1)S(1)} %get-tuple-element.31), channel_id=1, source_target_pairs={{0,28},{4,24},{8,20},{12,16},{16,12},{20,8},{24,4},{28,0},{1,29},{... | collective-permute-start | bytes 221192 | tf_op jit(solution)/shard_map/ppermute | solution.py:344
  13.5 0.0 collective-permute-done.2
  13.5 0.0 collective-permute-start.3
  13.5 4.4 %prepare.1 = (bf16[1152,640]{1,0:T(8,128)(2,1)S(1)}, bf16[640,1152]{1,0:T(8,128)(2,1)S(1)}, bf16[640,1152]{1,0:T(8,128)(2,1)S(1)}, f32[16,256]{1,0:T(8,128)S(1)}...) custom-call(s32[2,1152]{1,0:T(2,128)} %bitcast.22, f32[600,600]{1,0:T(8,128)} %prec_hbm.1, s32[2,128]{1,0:T(2,128)} %coherence_hbm.1, ...), custom_call_target="tpu_custom_call" | custom-call | tf_op jit(solution)/shard_map/prepare/pallas_call | solution.py:115
  17.9 0.0 collective-permute-done.4
  17.9 0.6 %early_fit.2 = (bf16[576,256]{1,0:T(8,128)(2,1)S(1)}, f32[640,256]{1,0:T(8,128)S(1)}) custom-call(bf16[288,128]{1,0:T(8,128)(2,1)S(1)} %bitcast.13, bf16[288,128]{1,0:T(8,128)(2,1)S(1)} %bitcast.14, bf16[288,128]{1,0:T(8,128)(2,1)S(1)} %bitcast.15, bf16[288,128]{1,0:T(8,128)(2,1)S(1)} %bitcast.16, bf16[640,1152]{1,0:T(8,128)(2,1)S(1)} %get-tuple-element.39.refs_4_.refs_6_, ...), custom_call_target="tpu_custom_call" | custom-call | tf_op jit(solution)/shard_map/early_fit/pallas_call | solution.py:170
  18.4 0.0 collective-permute-done.5
  18.5 0.0 collective-permute-done.6
  18.5 0.4 early_fit.3
  18.8 0.0 collective-permute-done.1
  18.9 0.8 %collective-permute-done.3 = bf16[144,2,128]{2,1,0:T(2,128)(2,1)S(1)} collective-permute-done((bf16[144,2,128]{2,1,0:T(2,128)(2,1)S(1)}, bf16[144,2,128]{2,1,0:T(2,128)(2,1)S(1)}, u32[]{:S(2)}, u32[]{:S(2)}) %collective-permute-start.3) | collective-permute-done | bytes 73760 | tf_op jit(solution)/shard_map/ppermute | solution.py:344
  19.7 4.3 %invert.1 = (f32[640,256]{1,0:T(8,128)S(1)}, f32[16,640]{1,0:T(8,128)S(1)}) custom-call(bf16[288,128]{1,0:T(8,128)(2,1)S(1)} %bitcast.17, bf16[288,128]{1,0:T(8,128)(2,1)S(1)} %bitcast.20, bf16[576,256]{1,0:T(8,128)(2,1)S(1)} %get-tuple-element.41.refs_2_, bf16[288,256]{1,0:T(8,128)(2,1)S(1)} %get-tuple-element.45.refs_3_, ...), custom_call_target="tpu_custom_call" | custom-call | tf_op jit(solution)/shard_map/invert/pallas_call | solution.py:282
  24.0 1.6 %collective-permute-start.7 = (f32[8,640]{1,0:T(8,128)S(1)}, f32[8,640]{1,0:T(8,128)S(1)}, u32[]{:S(2)}, u32[]{:S(2)}) collective-permute-start(f32[8,640]{1,0:T(8,128)S(1)} %get-tuple-element.53), channel_id=1, source_target_pairs={{8,16},{12,20},{24,1},{28,5},{9,17},{13,21},{0,4},{25,29},{16,8},{... | collective-permute-start | bytes 61448 | tf_op jit(solution)/shard_map/ppermute | solution.py:439
  25.6 2.4 %collective-permute-start.8 = (f32[8,640]{1,0:T(8,128)S(1)}, f32[8,640]{1,0:T(8,128)S(1)}, u32[]{:S(2)}, u32[]{:S(2)}) collective-permute-start(f32[8,640]{1,0:T(8,128)S(1)} %get-tuple-element.54), channel_id=1, source_target_pairs={{0,8},{4,12},{16,24},{20,28},{1,9},{5,13},{17,25},{21,29},{8,0},{1... | collective-permute-start | bytes 61448 | tf_op jit(solution)/shard_map/ppermute | solution.py:439
  28.0 0.0 collective-permute-done.7
  28.0 1.8 %collective-permute-done.8 = f32[8,640]{1,0:T(8,128)S(1)} collective-permute-done((f32[8,640]{1,0:T(8,128)S(1)}, f32[8,640]{1,0:T(8,128)S(1)}, u32[]{:S(2)}, u32[]{:S(2)}) %collective-permute-start.8) | collective-permute-done | bytes 20512 | tf_op jit(solution)/shard_map/ppermute | solution.py:439
  29.8 1.5 %collective-permute-start.9 = (f32[16,640]{1,0:T(8,128)S(1)}, f32[16,640]{1,0:T(8,128)S(1)}, u32[]{:S(2)}, u32[]{:S(2)}) collective-permute-start(f32[16,640]{1,0:T(8,128)S(1)} %maximum_add_fusion.first_ref), channel_id=1, source_target_pairs={{0,2},{2,0},{1,3},{3,1},{4,6},{6,4},{5,7},{7,5},{8,10},{10,8},{9,1... | collective-permute-start | bytes 122888 | tf_op jit(solution)/shard_map/ppermute | solution.py:439
  31.3 1.4 %collective-permute-start.10 = (f32[16,640]{1,0:T(8,128)S(1)}, f32[16,640]{1,0:T(8,128)S(1)}, u32[]{:S(2)}, u32[]{:S(2)}) collective-permute-start(f32[16,640]{1,0:T(8,128)S(1)} %maximum_add_fusion.first_ref), channel_id=1, source_target_pairs={{0,4},{8,12},{16,20},{24,28},{4,0},{12,8},{20,16},{28,24},{1,5},{9... | collective-permute-start | bytes 122888 | tf_op jit(solution)/shard_map/ppermute | solution.py:439
  32.7 0.6 %collective-permute-start.11 = (f32[16,640]{1,0:T(8,128)S(1)}, f32[16,640]{1,0:T(8,128)S(1)}, u32[]{:S(2)}, u32[]{:S(2)}) collective-permute-start(f32[16,640]{1,0:T(8,128)S(1)} %maximum_add_fusion.first_ref), channel_id=1, source_target_pairs={{0,6},{2,4},{8,14},{10,12},{16,22},{18,20},{24,30},{26,28},{6,0},{... | collective-permute-start | bytes 122888 | tf_op jit(solution)/shard_map/ppermute | solution.py:439
  33.3 0.5 %collective-permute-done.9.refs_0_ = f32[16,640]{1,0:T(8,128)S(1)} collective-permute-done((f32[16,640]{1,0:T(8,128)S(1)}, f32[16,640]{1,0:T(8,128)S(1)}, u32[]{:S(2)}, u32[]{:S(2)}) %collective-permute-start.9) | collective-permute-done | bytes 40992 | tf_op jit(solution)/shard_map/ppermute | solution.py:439
  33.8 1.5 %collective-permute-done.10.refs_1_ = f32[16,640]{1,0:T(8,128)S(1)} collective-permute-done((f32[16,640]{1,0:T(8,128)S(1)}, f32[16,640]{1,0:T(8,128)S(1)}, u32[]{:S(2)}, u32[]{:S(2)}) %collective-permute-start.10) | collective-permute-done | bytes 40992 | tf_op jit(solution)/shard_map/ppermute | solution.py:439
  35.3 2.3 %collective-permute-done.11.refs_2_ = f32[16,640]{1,0:T(8,128)S(1)} collective-permute-done((f32[16,640]{1,0:T(8,128)S(1)}, f32[16,640]{1,0:T(8,128)S(1)}, u32[]{:S(2)}, u32[]{:S(2)}) %collective-permute-start.11) | collective-permute-done | bytes 40992 | tf_op jit(solution)/shard_map/ppermute | solution.py:439
  37.6 1.5 %deramp.1 = f32[1200,128]{1,0:T(8,128)} custom-call(f32[16,640]{1,0:T(8,128)S(1)} %maximum_add_fusion.first_ref, f32[16,640]{1,0:T(8,128)S(1)} %collective-permute-done.9.refs_0_, f32[16,640]{1,0:T(8,128)S(1)} %collective-permute-done.10.refs_1_, f32[16,640]{1,0:T(8,128)S(1)} %collective-permute-done.11.refs_2_, f32[640,256]{1,0:T(8,128)S(1)} %get-tuple-element.51.refs_3_, ...), custom_call_target="tpu_custom_call" | custom-call | tf_op jit(solution)/shard_map/deramp/pallas_call | solution.py:426
  (3 shorter events, 0.0 us)
Async XLA Ops:
  1.2 10.0 %collective-permute-start = (bf16[144,2,128]{2,1,0:T(2,128)(2,1)S(1)}, bf16[144,2,128]{2,1,0:T(2,128)(2,1)S(1)}, u32[]{:S(2)}, u32[]{:S(2)}) collective-permute-start(bf16[144,2,128]{2,1,0:T(2,128)(2,1)S(1)} %get-tuple-element.30), channel_id=1, source_target_pairs={{0,4},{4,0},{8,12},{12,8},{16,20},{20,16},{24,28},{28,24},{1,5},{5... | collective-permute-start | bytes 221192 | tf_op jit(solution)/shard_map/ppermute | solution.py:344
  4.2 9.2 %collective-permute-start.2 = (bf16[144,2,128]{2,1,0:T(2,128)(2,1)S(1)}, bf16[144,2,128]{2,1,0:T(2,128)(2,1)S(1)}, u32[]{:S(2)}, u32[]{:S(2)}) collective-permute-start(bf16[144,2,128]{2,1,0:T(2,128)(2,1)S(1)} %get-tuple-element.33), channel_id=1, source_target_pairs={{0,8},{4,12},{8,0},{12,4},{16,24},{20,28},{24,16},{28,20},{1,9},{5... | collective-permute-start | bytes 221192 | tf_op jit(solution)/shard_map/ppermute | solution.py:344
  5.8 12.1 %collective-permute-start.4 = (bf16[144,2,128]{2,1,0:T(2,128)(2,1)S(1)}, bf16[144,2,128]{2,1,0:T(2,128)(2,1)S(1)}, u32[]{:S(2)}, u32[]{:S(2)}) collective-permute-start(bf16[144,2,128]{2,1,0:T(2,128)(2,1)S(1)} %get-tuple-element.38), channel_id=1, source_target_pairs={{0,16},{4,20},{8,24},{12,28},{16,0},{20,4},{24,8},{28,12},{1,17},{... | collective-permute-start | bytes 221192 | tf_op jit(solution)/shard_map/ppermute | solution.py:344
  8.4 10.0 %collective-permute-start.5 = (bf16[144,2,128]{2,1,0:T(2,128)(2,1)S(1)}, bf16[144,2,128]{2,1,0:T(2,128)(2,1)S(1)}, u32[]{:S(2)}, u32[]{:S(2)}) collective-permute-start(bf16[144,2,128]{2,1,0:T(2,128)(2,1)S(1)} %get-tuple-element.42), channel_id=1, source_target_pairs={{0,20},{4,16},{8,28},{12,24},{16,4},{20,0},{24,12},{28,8},{1,21},{... | collective-permute-start | bytes 221192 | tf_op jit(solution)/shard_map/ppermute | solution.py:344
  8.7 9.8 %collective-permute-start.6 = (bf16[144,2,128]{2,1,0:T(2,128)(2,1)S(1)}, bf16[144,2,128]{2,1,0:T(2,128)(2,1)S(1)}, u32[]{:S(2)}, u32[]{:S(2)}) collective-permute-start(bf16[144,2,128]{2,1,0:T(2,128)(2,1)S(1)} %get-tuple-element.43), channel_id=1, source_target_pairs={{0,24},{4,28},{8,16},{12,20},{16,8},{20,12},{24,0},{28,4},{1,25},{... | collective-permute-start | bytes 221192 | tf_op jit(solution)/shard_map/ppermute | solution.py:344
  11.2 7.7 %collective-permute-start.1 = (bf16[144,2,128]{2,1,0:T(2,128)(2,1)S(1)}, bf16[144,2,128]{2,1,0:T(2,128)(2,1)S(1)}, u32[]{:S(2)}, u32[]{:S(2)}) collective-permute-start(bf16[144,2,128]{2,1,0:T(2,128)(2,1)S(1)} %get-tuple-element.31), channel_id=1, source_target_pairs={{0,28},{4,24},{8,20},{12,16},{16,12},{20,8},{24,4},{28,0},{1,29},{... | collective-permute-start | bytes 221192 | tf_op jit(solution)/shard_map/ppermute | solution.py:344
  13.5 6.2 %collective-permute-start.3 = (bf16[144,2,128]{2,1,0:T(2,128)(2,1)S(1)}, bf16[144,2,128]{2,1,0:T(2,128)(2,1)S(1)}, u32[]{:S(2)}, u32[]{:S(2)}) collective-permute-start(bf16[144,2,128]{2,1,0:T(2,128)(2,1)S(1)} %get-tuple-element.34), channel_id=1, source_target_pairs={{0,12},{4,8},{8,4},{12,0},{16,28},{20,24},{24,20},{28,16},{1,13},{... | collective-permute-start | bytes 221192 | tf_op jit(solution)/shard_map/ppermute | solution.py:344
  24.0 4.0 %collective-permute-start.7 = (f32[8,640]{1,0:T(8,128)S(1)}, f32[8,640]{1,0:T(8,128)S(1)}, u32[]{:S(2)}, u32[]{:S(2)}) collective-permute-start(f32[8,640]{1,0:T(8,128)S(1)} %get-tuple-element.53), channel_id=1, source_target_pairs={{8,16},{12,20},{24,1},{28,5},{9,17},{13,21},{0,4},{25,29},{16,8},{... | collective-permute-start | bytes 61448 | tf_op jit(solution)/shard_map/ppermute | solution.py:439
  25.6 4.2 %collective-permute-start.8 = (f32[8,640]{1,0:T(8,128)S(1)}, f32[8,640]{1,0:T(8,128)S(1)}, u32[]{:S(2)}, u32[]{:S(2)}) collective-permute-start(f32[8,640]{1,0:T(8,128)S(1)} %get-tuple-element.54), channel_id=1, source_target_pairs={{0,8},{4,12},{16,24},{20,28},{1,9},{5,13},{17,25},{21,29},{8,0},{1... | collective-permute-start | bytes 61448 | tf_op jit(solution)/shard_map/ppermute | solution.py:439
  29.8 4.0 %collective-permute-start.9 = (f32[16,640]{1,0:T(8,128)S(1)}, f32[16,640]{1,0:T(8,128)S(1)}, u32[]{:S(2)}, u32[]{:S(2)}) collective-permute-start(f32[16,640]{1,0:T(8,128)S(1)} %maximum_add_fusion.first_ref), channel_id=1, source_target_pairs={{0,2},{2,0},{1,3},{3,1},{4,6},{6,4},{5,7},{7,5},{8,10},{10,8},{9,1... | collective-permute-start | bytes 122888 | tf_op jit(solution)/shard_map/ppermute | solution.py:439
  31.3 4.0 %collective-permute-start.10 = (f32[16,640]{1,0:T(8,128)S(1)}, f32[16,640]{1,0:T(8,128)S(1)}, u32[]{:S(2)}, u32[]{:S(2)}) collective-permute-start(f32[16,640]{1,0:T(8,128)S(1)} %maximum_add_fusion.first_ref), channel_id=1, source_target_pairs={{0,4},{8,12},{16,20},{24,28},{4,0},{12,8},{20,16},{28,24},{1,5},{9... | collective-permute-start | bytes 122888 | tf_op jit(solution)/shard_map/ppermute | solution.py:439
  32.7 4.9 %collective-permute-start.11 = (f32[16,640]{1,0:T(8,128)S(1)}, f32[16,640]{1,0:T(8,128)S(1)}, u32[]{:S(2)}, u32[]{:S(2)}) collective-permute-start(f32[16,640]{1,0:T(8,128)S(1)} %maximum_add_fusion.first_ref), channel_id=1, source_target_pairs={{0,6},{2,4},{8,14},{10,12},{16,22},{18,20},{24,30},{26,28},{6,0},{... | collective-permute-start | bytes 122888 | tf_op jit(solution)/shard_map/ppermute | solution.py:439

commit v7 on v6

--- a/solution.py
+++ b/solution.py
@@ -11,7 +11,6 @@
 LANES = 128
 VMEM_LIMIT = 24 * 1024 * 1024
 ROWS_A = 192
-ROWS_B = 320
 APPROX = False
 ARRIVAL = (0, 1, 2, 4, 5, 6, 7, 3)
 EARLY = (4, 6)
@@ -48,7 +47,8 @@
     copies[0].wait()
     chunk = pairs_ref.shape[1] // len(order)
     date_total = prec_ref.shape[0]
-    date_pad, ifg_total = gain_top.shape
+    ifg_total = gain_top.shape[1]
+    date_pad = incidence_ref.shape[1] // 2
     for position, mask in enumerate(order):
         moved = pairs_ref[...]
         if len(order) > 1:
@@ -60,7 +60,9 @@
         jnp.where(date_ids == pairs[1:2, :], 1.0, 0.0)
         - jnp.where(date_ids == pairs[0:1, :], 1.0, 0.0)
     ).astype(jnp.bfloat16)
-    incidence_ref[...] = incidence_t.T
+    incidence = incidence_t.T
+    incidence_ref[:, :date_pad] = incidence
+    incidence_ref[:, date_pad:] = incidence
     for copy in copies[1:]:
         copy.wait()
     prec = prec_ref[...]
@@ -68,7 +70,7 @@
     top, low = halves(prec)
     used = incidence_t[:date_total]
     gain_a, gain_b = halves(product(top, used) + product(low, used))
-    zeros = jnp.zeros((date_pad - date_total, ifg_total), jnp.bfloat16)
+    zeros = jnp.zeros((gain_top.shape[0] - date_total, ifg_total), jnp.bfloat16)
     gain_top[...] = jnp.concatenate([gain_a, zeros], axis=0)
     gain_low[...] = jnp.concatenate([gain_b, zeros], axis=0)
 
@@ -94,22 +96,26 @@
     coord_v = (column.astype(jnp.float32) + 0.5) / col_total - 0.5
     basis = jnp.concatenate([jnp.ones_like(coord_u), coord_u, coord_v], axis=0)
     spare = jnp.zeros((2, pixel_count), jnp.float32)
-    lines = []
+    lines, inside = [], []
     for base in (jnp.where(even, 2 * node - 1, 2 * node + 1), jnp.where(even, 2 * node + 1, 2 * node - 1)):
-        for step in range(2):
-            lines.append(basis * (tiles == base + step).astype(jnp.float32))
+        held = [(tiles == base + step).astype(jnp.float32) for step in range(2)]
+        for line in range(3):
+            lines += [basis[line : line + 1] * each for each in held]
         lines.append(spare)
-    member = jnp.concatenate(lines, axis=0)
-    member_ref[...] = member
-    weighted_ref[...] = member * coherence
+        inside += held
+    weighted_ref[...] = jnp.concatenate(lines, axis=0) * coherence
+    member_ref[...] = jnp.concatenate(
+        [basis[line : line + 1] * each for line in range(3) for each in inside] + [spare, spare], axis=0
+    )
     basis_ref[...] = jnp.concatenate([basis, coherence, jnp.zeros((4, pixel_count), jnp.float32)], axis=0)
 
 
-def prepare(pairs, preconditioner, coherence, tiles, date_pad, order, col_total, row_total):
+def prepare(pairs, preconditioner, coherence, tiles, date_pad, date_rows, order, col_total, row_total):
     ifg_total = pairs.shape[1]
     pixel_count = coherence.size
     arguments = (pairs, preconditioner, coherence, tiles)
-    shapes = [((ifg_total, date_pad), jnp.bfloat16)] + [((date_pad, ifg_total), jnp.bfloat16)] * 2
+    shapes = [((ifg_total, 2 * date_pad), jnp.bfloat16)]
+    shapes += [((date_rows, ifg_total), jnp.bfloat16)] * 2
     shapes += [((rows, pixel_count), jnp.float32) for rows in (16, 16, 8)]
     whole = pl.BlockSpec(memory_space=pltpu.VMEM)
     return pl.pallas_call(
@@ -158,8 +164,9 @@
         value = jnp.concatenate([before[0][pl.ds(start, held), :], value[: end - start - held]], axis=0)
     else:
         value = value[:end]
-    for first in range(0, series_ref.shape[0], ROWS_B):
-        rows = pl.ds(first, ROWS_B)
+    half = series_ref.shape[0] // 2
+    for first in (0, half):
+        rows = pl.ds(first, half)
         part = gained(gain_top, gain_low, rows, columns, value)
         series_ref[rows, :] = part + before[1][rows, :] if before else part
 
@@ -187,7 +194,8 @@
         moments_ref, wide, data, residual, moved,
     ) = refs
     ifg_total, pixel_count = moved.shape
-    date_pad = gain_top.shape[0]
+    date_rows = gain_top.shape[0]
+    date_pad = incidence.shape[1] // 2
     late_refs, early_refs = chunk_refs[:late], chunk_refs[late:]
     done = 0
     pieces = []
@@ -213,7 +221,8 @@
         return parts[0] if len(parts) == 1 else jnp.concatenate(parts, axis=0)
 
     coherence = basis_ref[3:4, :]
-    date_tiles = [pl.ds(start, ROWS_B) for start in range(0, date_pad, ROWS_B)]
+    date_tiles = [pl.ds(start, date_rows // 2) for start in (0, date_rows // 2)]
+    spare = [jnp.zeros((date_pad - date_rows, pixel_count), jnp.bfloat16)]
     ifg_tiles = [pl.ds(start, ROWS_A) for start in range(0, ifg_total, ROWS_A)]
     everything = slice(None)
 
@@ -238,11 +247,10 @@
         top, low = halves(part)
         tops.append(top)
         lows.append(low)
-    top, low = jnp.concatenate(tops, axis=0), jnp.concatenate(lows, axis=0)
+    both = jnp.concatenate(tops + spare + lows + spare, axis=0)
     total = jnp.zeros((8, pixel_count), jnp.float32)
     for rows in ifg_tiles:
-        fit = product(incidence[rows, :], top) + product(incidence[rows, :], low)
-        left = observed(rows).astype(jnp.float32) - fit
+        left = observed(rows).astype(jnp.float32) - product(incidence[rows, :], both)
         residual[rows, :] = left
         total = total + folded(left * left)
     reweighted(total)
@@ -252,10 +260,10 @@
             part = gained(gain_top, None, rows, everything, moved[...])
             steps.append(part.astype(jnp.bfloat16))
             series_ref[rows, :] = series_ref[rows, :] + part
-        step = jnp.concatenate(steps, axis=0)
+        step = jnp.concatenate(steps + spare, axis=0)
         total = jnp.zeros((8, pixel_count), jnp.float32)
         for rows in ifg_tiles:
-            left = residual[rows, :] - product(incidence[rows, :], step)
+            left = residual[rows, :] - product(incidence[rows, :date_pad], step)
             residual[rows, :] = left
             total = total + folded(left * left)
         held = moved[...]
@@ -277,15 +285,15 @@
 def invert(late_chunks, early, incidence, gains, weighted, basis, row_local, date_total):
     ifg_total = incidence.shape[0]
     kept = sum(value.shape[0] for value in early[:-1]) // 128 * 128
-    date_pad = gains[0].shape[0]
+    date_rows = gains[0].shape[0]
     pixel_count = weighted.shape[1]
     return pl.pallas_call(
         functools.partial(
             invert_kernel, row_local=row_local, date_total=date_total, late=len(late_chunks)
         ),
         out_shape=[
-            jax.ShapeDtypeStruct((date_pad, pixel_count), jnp.float32),
-            jax.ShapeDtypeStruct((weighted.shape[0], date_pad), jnp.float32),
+            jax.ShapeDtypeStruct((date_rows, pixel_count), jnp.float32),
+            jax.ShapeDtypeStruct((weighted.shape[0], date_rows), jnp.float32),
         ],
         scratch_shapes=[
             pltpu.VMEM(late_chunks[0].shape, jnp.float32),
@@ -381,19 +389,16 @@
     totals = first_ref[...]
     for other in others:
         totals = totals + other[...]
-    planes = []
-    for base in (0, 3, 8, 11):
-        gram = [
-            [
-                totals[base + k : base + k + 1, date_total + m : date_total + m + 1]
-                + (1.0 if k == m else 0.0)
-                for m in range(3)
-            ]
-            for k in range(3)
-        ]
-        planes += plane_solve(gram, [totals[base + k : base + k + 1, :] for k in range(3)])
-        if base in (3, 11):
-            planes += [jnp.zeros_like(planes[0])] * 2
+    sums = [
+        jnp.concatenate([totals[2 * k : 2 * k + 2], totals[8 + 2 * k : 10 + 2 * k]], axis=0)
+        for k in range(3)
+    ]
+    gram = [
+        [sums[k][:, date_total + m : date_total + m + 1] + (1.0 if k == m else 0.0) for m in range(3)]
+        for k in range(3)
+    ]
+    planes = plane_solve(gram, sums)
+    planes.append(jnp.zeros_like(planes[0]))
     planes_top, planes_low = halves(jnp.concatenate(planes, axis=0))
     member_top, member_low = halves(member_ref[...])
     ramp = product(
@@ -445,11 +450,12 @@
     azimuth_size = lax.axis_size("azimuth")
     ifg_local, row_local, col_range = phases.shape
     date_total = preconditioner.shape[0]
-    date_pad = -(-(date_total + 8) // LANES) * LANES
+    date_rows = -(-(date_total + 8) // 32) * 32
+    date_pad = -(-date_rows // LANES) * LANES
 
     chunks, order = exchange(phases, stack_size)
     incidence, *gains, member, weighted, basis = prepare(
-        ifg_pairs.T, preconditioner, coherence, geo_tiles, date_pad, order,
+        ifg_pairs.T, preconditioner, coherence, geo_tiles, date_pad, date_rows, order,
         col_range * range_size, row_local * azimuth_size,
     )
     early = []

time: 39.4 us -> 39.2 us (level)
  no operation moved by 1% of the time
where the time goes in v7:
time: 39.2 us; the launch traced here: 39 us
  starting transfers between devices  19.7 us (50%)
  Pallas kernels  12.1 us (31%)
  waiting for transfers between devices  7.1 us (18%)
    ppermute x7, starting transfers between devices, send(): lax.ppermute(block, 'stack', [(i, i ^ mask) for i in range(stack_size)])  12.3 us
    ppermute x5, starting transfers between devices, swap(): return lax.ppermute(value, axes, both)  7.48 us
    ppermute x5, waiting for transfers between devices, swap(): return lax.ppermute(value, axes, both)  6.19 us
    pallas_call x1, Pallas kernels, prepare(): pl.pallas_call(functools.partial(prepare_kernel, order=order, col_total=c...  4.38 us
    pallas_call x1, Pallas kernels, invert(): pl.pallas_call(functools.partial(invert_kernel, row_local=row_local, date...  4.11 us
    pallas_call x1, Pallas kernels, deramp(): pl.pallas_call(functools.partial(deramp_kernel, row_local=row_local, date...  1.51 us
    pallas_call x1, Pallas kernels, cut(): pl.pallas_call(cut_kernel, out_shape=[jax.ShapeDtypeStruct((ifg_local, ro...  1.2 us
    ppermute x7, waiting for transfers between devices, send(): lax.ppermute(block, 'stack', [(i, i ^ mask) for i in range(stack_size)])  0.91 us
  transfers between devices with their start and end apart: 12, of which 5 were waited for; matrix products, arithmetic and copies ran while one was open for 0% of the time, Pallas kernels for 14%

profile of v7, /device:TPU:0, one launch (start us, length us, event | category | flops | bytes accessed | tf_op | source)
XLA Modules:
  0.0 39.0 jit_solution(17394424891319489887)
XLA Ops:
  0.0 1.2 %cut.1 = (bf16[144,2,128]{2,1,0:T(2,128)(2,1)S(1)}, bf16[144,2,128]{2,1,0:T(2,128)(2,1)S(1)}, bf16[144,2,128]{2,1,0:T(2,128)(2,1)S(1)}, bf16[144,2,128]{2,1,0:T(...) custom-call(bf16[144,8,2,128]{3,2,1,0:T(2,128)(2,1)} %bitcast.21), custom_call_target="tpu_custom_call" | custom-call | tf_op jit(solution)/shard_map/cut/pallas_call | solution.py:327
  1.2 3.0 %collective-permute-start = (bf16[144,2,128]{2,1,0:T(2,128)(2,1)S(1)}, bf16[144,2,128]{2,1,0:T(2,128)(2,1)S(1)}, u32[]{:S(2)}, u32[]{:S(2)}) collective-permute-start(bf16[144,2,128]{2,1,0:T(2,128)(2,1)S(1)} %get-tuple-element.30), channel_id=1, source_target_pairs={{0,4},{4,0},{8,12},{12,8},{16,20},{20,16},{24,28},{28,24},{1,5},{5... | collective-permute-start | bytes 221192 | tf_op jit(solution)/shard_map/ppermute | solution.py:352
  4.2 1.6 %collective-permute-start.2 = (bf16[144,2,128]{2,1,0:T(2,128)(2,1)S(1)}, bf16[144,2,128]{2,1,0:T(2,128)(2,1)S(1)}, u32[]{:S(2)}, u32[]{:S(2)}) collective-permute-start(bf16[144,2,128]{2,1,0:T(2,128)(2,1)S(1)} %get-tuple-element.33), channel_id=1, source_target_pairs={{0,8},{4,12},{8,0},{12,4},{16,24},{20,28},{24,16},{28,20},{1,9},{5... | collective-permute-start | bytes 221192 | tf_op jit(solution)/shard_map/ppermute | solution.py:352
  5.8 2.6 %collective-permute-start.4 = (bf16[144,2,128]{2,1,0:T(2,128)(2,1)S(1)}, bf16[144,2,128]{2,1,0:T(2,128)(2,1)S(1)}, u32[]{:S(2)}, u32[]{:S(2)}) collective-permute-start(bf16[144,2,128]{2,1,0:T(2,128)(2,1)S(1)} %get-tuple-element.38), channel_id=1, source_target_pairs={{0,16},{4,20},{8,24},{12,28},{16,0},{20,4},{24,8},{28,12},{1,17},{... | collective-permute-start | bytes 221192 | tf_op jit(solution)/shard_map/ppermute | solution.py:352
  8.4 0.3 collective-permute-start.5
  8.7 2.5 %collective-permute-start.6 = (bf16[144,2,128]{2,1,0:T(2,128)(2,1)S(1)}, bf16[144,2,128]{2,1,0:T(2,128)(2,1)S(1)}, u32[]{:S(2)}, u32[]{:S(2)}) collective-permute-start(bf16[144,2,128]{2,1,0:T(2,128)(2,1)S(1)} %get-tuple-element.43), channel_id=1, source_target_pairs={{0,24},{4,28},{8,16},{12,20},{16,8},{20,12},{24,0},{28,4},{1,25},{... | collective-permute-start | bytes 221192 | tf_op jit(solution)/shard_map/ppermute | solution.py:352
  11.2 0.0 collective-permute-done
  11.2 2.3 %collective-permute-start.1 = (bf16[144,2,128]{2,1,0:T(2,128)(2,1)S(1)}, bf16[144,2,128]{2,1,0:T(2,128)(2,1)S(1)}, u32[]{:S(2)}, u32[]{:S(2)}) collective-permute-start(bf16[144,2,128]{2,1,0:T(2,128)(2,1)S(1)} %get-tuple-element.31), channel_id=1, source_target_pairs={{0,28},{4,24},{8,20},{12,16},{16,12},{20,8},{24,4},{28,0},{1,29},{... | collective-permute-start | bytes 221192 | tf_op jit(solution)/shard_map/ppermute | solution.py:352
  13.5 0.0 collective-permute-done.2
  13.5 0.0 collective-permute-start.3
  13.5 4.4 %prepare.1 = (bf16[1152,1280]{1,0:T(8,128)(2,1)S(1)}, bf16[608,1152]{1,0:T(8,128)(2,1)S(1)}, bf16[608,1152]{1,0:T(8,128)(2,1)S(1)}, f32[16,256]{1,0:T(8,128)S(1)...) custom-call(s32[2,1152]{1,0:T(2,128)} %bitcast.22, f32[600,600]{1,0:T(8,128)} %prec_hbm.1, s32[2,128]{1,0:T(2,128)} %coherence_hbm.1, ...), custom_call_target="tpu_custom_call" | custom-call | tf_op jit(solution)/shard_map/prepare/pallas_call | solution.py:121
  17.9 0.0 collective-permute-done.4
  17.9 0.5 %early_fit.2 = (bf16[576,256]{1,0:T(8,128)(2,1)S(1)}, f32[608,256]{1,0:T(8,128)S(1)}) custom-call(bf16[288,128]{1,0:T(8,128)(2,1)S(1)} %bitcast.13, bf16[288,128]{1,0:T(8,128)(2,1)S(1)} %bitcast.14, bf16[288,128]{1,0:T(8,128)(2,1)S(1)} %bitcast.15, bf16[288,128]{1,0:T(8,128)(2,1)S(1)} %bitcast.16, bf16[608,1152]{1,0:T(8,128)(2,1)S(1)} %get-tuple-element.39.refs_4_.refs_6_, ...), custom_call_target="tpu_custom_call" | custom-call | tf_op jit(solution)/shard_map/early_fit/pallas_call | solution.py:177
  18.4 0.0 collective-permute-done.5
  18.4 0.0 collective-permute-done.6
  18.4 0.4 early_fit.3
  18.8 0.0 collective-permute-done.1
  18.8 0.9 %collective-permute-done.3 = bf16[144,2,128]{2,1,0:T(2,128)(2,1)S(1)} collective-permute-done((bf16[144,2,128]{2,1,0:T(2,128)(2,1)S(1)}, bf16[144,2,128]{2,1,0:T(2,128)(2,1)S(1)}, u32[]{:S(2)}, u32[]{:S(2)}) %collective-permute-start.3) | collective-permute-done | bytes 73760 | tf_op jit(solution)/shard_map/ppermute | solution.py:352
  19.7 4.1 %invert.1 = (f32[608,256]{1,0:T(8,128)S(1)}, f32[16,608]{1,0:T(8,128)S(1)}) custom-call(bf16[288,128]{1,0:T(8,128)(2,1)S(1)} %bitcast.17, bf16[288,128]{1,0:T(8,128)(2,1)S(1)} %bitcast.20, bf16[576,256]{1,0:T(8,128)(2,1)S(1)} %get-tuple-element.41.refs_2_, bf16[288,256]{1,0:T(8,128)(2,1)S(1)} %get-tuple-element.45.refs_3_, ...), custom_call_target="tpu_custom_call" | custom-call | tf_op jit(solution)/shard_map/invert/pallas_call | solution.py:290
  23.8 1.6 %collective-permute-start.7 = (f32[8,608]{1,0:T(8,128)S(1)}, f32[8,608]{1,0:T(8,128)S(1)}, u32[]{:S(2)}, u32[]{:S(2)}) collective-permute-start(f32[8,608]{1,0:T(8,128)S(1)} %get-tuple-element.53), channel_id=1, source_target_pairs={{8,16},{12,20},{24,1},{28,5},{9,17},{13,21},{0,4},{25,29},{16,8},{... | collective-permute-start | bytes 58376 | tf_op jit(solution)/shard_map/ppermute | solution.py:444
  25.4 2.3 %collective-permute-start.8 = (f32[8,608]{1,0:T(8,128)S(1)}, f32[8,608]{1,0:T(8,128)S(1)}, u32[]{:S(2)}, u32[]{:S(2)}) collective-permute-start(f32[8,608]{1,0:T(8,128)S(1)} %get-tuple-element.54), channel_id=1, source_target_pairs={{0,8},{4,12},{16,24},{20,28},{1,9},{5,13},{17,25},{21,29},{8,0},{1... | collective-permute-start | bytes 58376 | tf_op jit(solution)/shard_map/ppermute | solution.py:444
  27.8 0.0 collective-permute-done.7
  27.8 1.8 %collective-permute-done.8 = f32[8,608]{1,0:T(8,128)S(1)} collective-permute-done((f32[8,608]{1,0:T(8,128)S(1)}, f32[8,608]{1,0:T(8,128)S(1)}, u32[]{:S(2)}, u32[]{:S(2)}) %collective-permute-start.8) | collective-permute-done | bytes 19488 | tf_op jit(solution)/shard_map/ppermute | solution.py:444
  29.6 1.6 %collective-permute-start.9 = (f32[16,608]{1,0:T(8,128)S(1)}, f32[16,608]{1,0:T(8,128)S(1)}, u32[]{:S(2)}, u32[]{:S(2)}) collective-permute-start(f32[16,608]{1,0:T(8,128)S(1)} %maximum_add_fusion.first_ref), channel_id=1, source_target_pairs={{0,2},{2,0},{1,3},{3,1},{4,6},{6,4},{5,7},{7,5},{8,10},{10,8},{9,1... | collective-permute-start | bytes 116744 | tf_op jit(solution)/shard_map/ppermute | solution.py:444
  31.2 1.4 %collective-permute-start.10 = (f32[16,608]{1,0:T(8,128)S(1)}, f32[16,608]{1,0:T(8,128)S(1)}, u32[]{:S(2)}, u32[]{:S(2)}) collective-permute-start(f32[16,608]{1,0:T(8,128)S(1)} %maximum_add_fusion.first_ref), channel_id=1, source_target_pairs={{0,4},{8,12},{16,20},{24,28},{4,0},{12,8},{20,16},{28,24},{1,5},{9... | collective-permute-start | bytes 116744 | tf_op jit(solution)/shard_map/ppermute | solution.py:444
  32.6 0.6 %collective-permute-start.11 = (f32[16,608]{1,0:T(8,128)S(1)}, f32[16,608]{1,0:T(8,128)S(1)}, u32[]{:S(2)}, u32[]{:S(2)}) collective-permute-start(f32[16,608]{1,0:T(8,128)S(1)} %maximum_add_fusion.first_ref), channel_id=1, source_target_pairs={{0,6},{2,4},{8,14},{10,12},{16,22},{18,20},{24,30},{26,28},{6,0},{... | collective-permute-start | bytes 116744 | tf_op jit(solution)/shard_map/ppermute | solution.py:444
  33.2 0.5 %collective-permute-done.9.refs_0_ = f32[16,608]{1,0:T(8,128)S(1)} collective-permute-done((f32[16,608]{1,0:T(8,128)S(1)}, f32[16,608]{1,0:T(8,128)S(1)}, u32[]{:S(2)}, u32[]{:S(2)}) %collective-permute-start.9) | collective-permute-done | bytes 38944 | tf_op jit(solution)/shard_map/ppermute | solution.py:444
  33.7 1.5 %collective-permute-done.10.refs_1_ = f32[16,608]{1,0:T(8,128)S(1)} collective-permute-done((f32[16,608]{1,0:T(8,128)S(1)}, f32[16,608]{1,0:T(8,128)S(1)}, u32[]{:S(2)}, u32[]{:S(2)}) %collective-permute-start.10) | collective-permute-done | bytes 38944 | tf_op jit(solution)/shard_map/ppermute | solution.py:444
  35.2 2.3 %collective-permute-done.11.refs_2_ = f32[16,608]{1,0:T(8,128)S(1)} collective-permute-done((f32[16,608]{1,0:T(8,128)S(1)}, f32[16,608]{1,0:T(8,128)S(1)}, u32[]{:S(2)}, u32[]{:S(2)}) %collective-permute-start.11) | collective-permute-done | bytes 38944 | tf_op jit(solution)/shard_map/ppermute | solution.py:444
  37.5 1.5 %deramp.1 = f32[1200,128]{1,0:T(8,128)} custom-call(f32[16,608]{1,0:T(8,128)S(1)} %maximum_add_fusion.first_ref, f32[16,608]{1,0:T(8,128)S(1)} %collective-permute-done.9.refs_0_, f32[16,608]{1,0:T(8,128)S(1)} %collective-permute-done.10.refs_1_, f32[16,608]{1,0:T(8,128)S(1)} %collective-permute-done.11.refs_2_, f32[608,256]{1,0:T(8,128)S(1)} %get-tuple-element.51.refs_3_, ...), custom_call_target="tpu_custom_call" | custom-call | tf_op jit(solution)/shard_map/deramp/pallas_call | solution.py:431
  (3 shorter events, 0.0 us)
Async XLA Ops:
  1.2 10.0 %collective-permute-start = (bf16[144,2,128]{2,1,0:T(2,128)(2,1)S(1)}, bf16[144,2,128]{2,1,0:T(2,128)(2,1)S(1)}, u32[]{:S(2)}, u32[]{:S(2)}) collective-permute-start(bf16[144,2,128]{2,1,0:T(2,128)(2,1)S(1)} %get-tuple-element.30), channel_id=1, source_target_pairs={{0,4},{4,0},{8,12},{12,8},{16,20},{20,16},{24,28},{28,24},{1,5},{5... | collective-permute-start | bytes 221192 | tf_op jit(solution)/shard_map/ppermute | solution.py:352
  4.2 9.2 %collective-permute-start.2 = (bf16[144,2,128]{2,1,0:T(2,128)(2,1)S(1)}, bf16[144,2,128]{2,1,0:T(2,128)(2,1)S(1)}, u32[]{:S(2)}, u32[]{:S(2)}) collective-permute-start(bf16[144,2,128]{2,1,0:T(2,128)(2,1)S(1)} %get-tuple-element.33), channel_id=1, source_target_pairs={{0,8},{4,12},{8,0},{12,4},{16,24},{20,28},{24,16},{28,20},{1,9},{5... | collective-permute-start | bytes 221192 | tf_op jit(solution)/shard_map/ppermute | solution.py:352
  5.8 12.1 %collective-permute-start.4 = (bf16[144,2,128]{2,1,0:T(2,128)(2,1)S(1)}, bf16[144,2,128]{2,1,0:T(2,128)(2,1)S(1)}, u32[]{:S(2)}, u32[]{:S(2)}) collective-permute-start(bf16[144,2,128]{2,1,0:T(2,128)(2,1)S(1)} %get-tuple-element.38), channel_id=1, source_target_pairs={{0,16},{4,20},{8,24},{12,28},{16,0},{20,4},{24,8},{28,12},{1,17},{... | collective-permute-start | bytes 221192 | tf_op jit(solution)/shard_map/ppermute | solution.py:352
  8.4 10.0 %collective-permute-start.5 = (bf16[144,2,128]{2,1,0:T(2,128)(2,1)S(1)}, bf16[144,2,128]{2,1,0:T(2,128)(2,1)S(1)}, u32[]{:S(2)}, u32[]{:S(2)}) collective-permute-start(bf16[144,2,128]{2,1,0:T(2,128)(2,1)S(1)} %get-tuple-element.42), channel_id=1, source_target_pairs={{0,20},{4,16},{8,28},{12,24},{16,4},{20,0},{24,12},{28,8},{1,21},{... | collective-permute-start | bytes 221192 | tf_op jit(solution)/shard_map/ppermute | solution.py:352
  8.7 9.8 %collective-permute-start.6 = (bf16[144,2,128]{2,1,0:T(2,128)(2,1)S(1)}, bf16[144,2,128]{2,1,0:T(2,128)(2,1)S(1)}, u32[]{:S(2)}, u32[]{:S(2)}) collective-permute-start(bf16[144,2,128]{2,1,0:T(2,128)(2,1)S(1)} %get-tuple-element.43), channel_id=1, source_target_pairs={{0,24},{4,28},{8,16},{12,20},{16,8},{20,12},{24,0},{28,4},{1,25},{... | collective-permute-start | bytes 221192 | tf_op jit(solution)/shard_map/ppermute | solution.py:352
  11.2 7.6 %collective-permute-start.1 = (bf16[144,2,128]{2,1,0:T(2,128)(2,1)S(1)}, bf16[144,2,128]{2,1,0:T(2,128)(2,1)S(1)}, u32[]{:S(2)}, u32[]{:S(2)}) collective-permute-start(bf16[144,2,128]{2,1,0:T(2,128)(2,1)S(1)} %get-tuple-element.31), channel_id=1, source_target_pairs={{0,28},{4,24},{8,20},{12,16},{16,12},{20,8},{24,4},{28,0},{1,29},{... | collective-permute-start | bytes 221192 | tf_op jit(solution)/shard_map/ppermute | solution.py:352
  13.5 6.2 %collective-permute-start.3 = (bf16[144,2,128]{2,1,0:T(2,128)(2,1)S(1)}, bf16[144,2,128]{2,1,0:T(2,128)(2,1)S(1)}, u32[]{:S(2)}, u32[]{:S(2)}) collective-permute-start(bf16[144,2,128]{2,1,0:T(2,128)(2,1)S(1)} %get-tuple-element.34), channel_id=1, source_target_pairs={{0,12},{4,8},{8,4},{12,0},{16,28},{20,24},{24,20},{28,16},{1,13},{... | collective-permute-start | bytes 221192 | tf_op jit(solution)/shard_map/ppermute | solution.py:352
  23.8 3.9 %collective-permute-start.7 = (f32[8,608]{1,0:T(8,128)S(1)}, f32[8,608]{1,0:T(8,128)S(1)}, u32[]{:S(2)}, u32[]{:S(2)}) collective-permute-start(f32[8,608]{1,0:T(8,128)S(1)} %get-tuple-element.53), channel_id=1, source_target_pairs={{8,16},{12,20},{24,1},{28,5},{9,17},{13,21},{0,4},{25,29},{16,8},{... | collective-permute-start | bytes 58376 | tf_op jit(solution)/shard_map/ppermute | solution.py:444
  25.4 4.2 %collective-permute-start.8 = (f32[8,608]{1,0:T(8,128)S(1)}, f32[8,608]{1,0:T(8,128)S(1)}, u32[]{:S(2)}, u32[]{:S(2)}) collective-permute-start(f32[8,608]{1,0:T(8,128)S(1)} %get-tuple-element.54), channel_id=1, source_target_pairs={{0,8},{4,12},{16,24},{20,28},{1,9},{5,13},{17,25},{21,29},{8,0},{1... | collective-permute-start | bytes 58376 | tf_op jit(solution)/shard_map/ppermute | solution.py:444
  29.6 4.1 %collective-permute-start.9 = (f32[16,608]{1,0:T(8,128)S(1)}, f32[16,608]{1,0:T(8,128)S(1)}, u32[]{:S(2)}, u32[]{:S(2)}) collective-permute-start(f32[16,608]{1,0:T(8,128)S(1)} %maximum_add_fusion.first_ref), channel_id=1, source_target_pairs={{0,2},{2,0},{1,3},{3,1},{4,6},{6,4},{5,7},{7,5},{8,10},{10,8},{9,1... | collective-permute-start | bytes 116744 | tf_op jit(solution)/shard_map/ppermute | solution.py:444
  31.2 4.0 %collective-permute-start.10 = (f32[16,608]{1,0:T(8,128)S(1)}, f32[16,608]{1,0:T(8,128)S(1)}, u32[]{:S(2)}, u32[]{:S(2)}) collective-permute-start(f32[16,608]{1,0:T(8,128)S(1)} %maximum_add_fusion.first_ref), channel_id=1, source_target_pairs={{0,4},{8,12},{16,20},{24,28},{4,0},{12,8},{20,16},{28,24},{1,5},{9... | collective-permute-start | bytes 116744 | tf_op jit(solution)/shard_map/ppermute | solution.py:444
  32.6 4.9 %collective-permute-start.11 = (f32[16,608]{1,0:T(8,128)S(1)}, f32[16,608]{1,0:T(8,128)S(1)}, u32[]{:S(2)}, u32[]{:S(2)}) collective-permute-start(f32[16,608]{1,0:T(8,128)S(1)} %maximum_add_fusion.first_ref), channel_id=1, source_target_pairs={{0,6},{2,4},{8,14},{10,12},{16,22},{18,20},{24,30},{26,28},{6,0},{... | collective-permute-start | bytes 116744 | tf_op jit(solution)/shard_map/ppermute | solution.py:444

commit v8 on v7

--- a/solution.py
+++ b/solution.py
@@ -499,9 +499,9 @@
     ]
     parts = [
         moments,
+        swap(moments, ("stack", "azimuth"), crossed),
+        swap(moments, "stack", pairs),
         swap(moments, "azimuth", [(0, 1)]),
-        swap(moments, "stack", pairs),
-        swap(moments, ("stack", "azimuth"), crossed),
     ]
     flat = deramp(parts, series, member, row_local, date_total)
     return flat.reshape(date_total, row_local, -1)

time: 39.2 us -> 38.4 us (0.980)
  waiting for transfers between devices: 7.1 us -> 6.23 us
    ppermute x5, waiting for transfers between devices: 6.19 us -> 5.32 us  [swap(): return lax.ppermute(value, axes, both)]
where the time goes in v8:
time: 38.4 us; the launch traced here: 38.2 us
  starting transfers between devices  19.7 us (51%)
  Pallas kernels  12.1 us (32%)
  waiting for transfers between devices  6.23 us (16%)
    ppermute x7, starting transfers between devices, send(): lax.ppermute(block, 'stack', [(i, i ^ mask) for i in range(stack_size)])  12.3 us
    ppermute x5, starting transfers between devices, swap(): return lax.ppermute(value, axes, both)  7.48 us
    ppermute x5, waiting for transfers between devices, swap(): return lax.ppermute(value, axes, both)  5.32 us
    pallas_call x1, Pallas kernels, prepare(): pl.pallas_call(functools.partial(prepare_kernel, order=order, col_total=c...  4.38 us
    pallas_call x1, Pallas kernels, invert(): pl.pallas_call(functools.partial(invert_kernel, row_local=row_local, date...  4.11 us
    pallas_call x1, Pallas kernels, deramp(): pl.pallas_call(functools.partial(deramp_kernel, row_local=row_local, date...  1.51 us
    pallas_call x1, Pallas kernels, cut(): pl.pallas_call(cut_kernel, out_shape=[jax.ShapeDtypeStruct((ifg_local, ro...  1.2 us
    ppermute x7, waiting for transfers between devices, send(): lax.ppermute(block, 'stack', [(i, i ^ mask) for i in range(stack_size)])  0.91 us
  transfers between devices with their start and end apart: 12, of which 5 were waited for; matrix products, arithmetic and copies ran while one was open for 0% of the time, Pallas kernels for 14%

profile of v8, /device:TPU:0, one launch (start us, length us, event | category | flops | bytes accessed | tf_op | source)
XLA Modules:
  0.0 38.2 jit_solution(16279564138245175528)
XLA Ops:
  0.0 1.2 %cut.1 = (bf16[144,2,128]{2,1,0:T(2,128)(2,1)S(1)}, bf16[144,2,128]{2,1,0:T(2,128)(2,1)S(1)}, bf16[144,2,128]{2,1,0:T(2,128)(2,1)S(1)}, bf16[144,2,128]{2,1,0:T(...) custom-call(bf16[144,8,2,128]{3,2,1,0:T(2,128)(2,1)} %bitcast.21), custom_call_target="tpu_custom_call" | custom-call | tf_op jit(solution)/shard_map/cut/pallas_call | solution.py:327
  1.2 3.0 %collective-permute-start = (bf16[144,2,128]{2,1,0:T(2,128)(2,1)S(1)}, bf16[144,2,128]{2,1,0:T(2,128)(2,1)S(1)}, u32[]{:S(2)}, u32[]{:S(2)}) collective-permute-start(bf16[144,2,128]{2,1,0:T(2,128)(2,1)S(1)} %get-tuple-element.30), channel_id=1, source_target_pairs={{0,4},{4,0},{8,12},{12,8},{16,20},{20,16},{24,28},{28,24},{1,5},{5... | collective-permute-start | bytes 221192 | tf_op jit(solution)/shard_map/ppermute | solution.py:352
  4.2 1.6 %collective-permute-start.2 = (bf16[144,2,128]{2,1,0:T(2,128)(2,1)S(1)}, bf16[144,2,128]{2,1,0:T(2,128)(2,1)S(1)}, u32[]{:S(2)}, u32[]{:S(2)}) collective-permute-start(bf16[144,2,128]{2,1,0:T(2,128)(2,1)S(1)} %get-tuple-element.33), channel_id=1, source_target_pairs={{0,8},{4,12},{8,0},{12,4},{16,24},{20,28},{24,16},{28,20},{1,9},{5... | collective-permute-start | bytes 221192 | tf_op jit(solution)/shard_map/ppermute | solution.py:352
  5.8 2.6 %collective-permute-start.4 = (bf16[144,2,128]{2,1,0:T(2,128)(2,1)S(1)}, bf16[144,2,128]{2,1,0:T(2,128)(2,1)S(1)}, u32[]{:S(2)}, u32[]{:S(2)}) collective-permute-start(bf16[144,2,128]{2,1,0:T(2,128)(2,1)S(1)} %get-tuple-element.38), channel_id=1, source_target_pairs={{0,16},{4,20},{8,24},{12,28},{16,0},{20,4},{24,8},{28,12},{1,17},{... | collective-permute-start | bytes 221192 | tf_op jit(solution)/shard_map/ppermute | solution.py:352
  8.4 0.3 collective-permute-start.5
  8.7 2.5 %collective-permute-start.6 = (bf16[144,2,128]{2,1,0:T(2,128)(2,1)S(1)}, bf16[144,2,128]{2,1,0:T(2,128)(2,1)S(1)}, u32[]{:S(2)}, u32[]{:S(2)}) collective-permute-start(bf16[144,2,128]{2,1,0:T(2,128)(2,1)S(1)} %get-tuple-element.43), channel_id=1, source_target_pairs={{0,24},{4,28},{8,16},{12,20},{16,8},{20,12},{24,0},{28,4},{1,25},{... | collective-permute-start | bytes 221192 | tf_op jit(solution)/shard_map/ppermute | solution.py:352
  11.2 0.0 collective-permute-done
  11.2 2.3 %collective-permute-start.1 = (bf16[144,2,128]{2,1,0:T(2,128)(2,1)S(1)}, bf16[144,2,128]{2,1,0:T(2,128)(2,1)S(1)}, u32[]{:S(2)}, u32[]{:S(2)}) collective-permute-start(bf16[144,2,128]{2,1,0:T(2,128)(2,1)S(1)} %get-tuple-element.31), channel_id=1, source_target_pairs={{0,28},{4,24},{8,20},{12,16},{16,12},{20,8},{24,4},{28,0},{1,29},{... | collective-permute-start | bytes 221192 | tf_op jit(solution)/shard_map/ppermute | solution.py:352
  13.5 0.0 collective-permute-done.2
  13.5 0.0 collective-permute-start.3
  13.5 4.4 %prepare.1 = (bf16[1152,1280]{1,0:T(8,128)(2,1)S(1)}, bf16[608,1152]{1,0:T(8,128)(2,1)S(1)}, bf16[608,1152]{1,0:T(8,128)(2,1)S(1)}, f32[16,256]{1,0:T(8,128)S(1)...) custom-call(s32[2,1152]{1,0:T(2,128)} %bitcast.22, f32[600,600]{1,0:T(8,128)} %prec_hbm.1, s32[2,128]{1,0:T(2,128)} %coherence_hbm.1, ...), custom_call_target="tpu_custom_call" | custom-call | tf_op jit(solution)/shard_map/prepare/pallas_call | solution.py:121
  17.9 0.0 collective-permute-done.4
  17.9 0.5 %early_fit.2 = (bf16[576,256]{1,0:T(8,128)(2,1)S(1)}, f32[608,256]{1,0:T(8,128)S(1)}) custom-call(bf16[288,128]{1,0:T(8,128)(2,1)S(1)} %bitcast.13, bf16[288,128]{1,0:T(8,128)(2,1)S(1)} %bitcast.14, bf16[288,128]{1,0:T(8,128)(2,1)S(1)} %bitcast.15, bf16[288,128]{1,0:T(8,128)(2,1)S(1)} %bitcast.16, bf16[608,1152]{1,0:T(8,128)(2,1)S(1)} %get-tuple-element.39.refs_4_.refs_6_, ...), custom_call_target="tpu_custom_call" | custom-call | tf_op jit(solution)/shard_map/early_fit/pallas_call | solution.py:177
  18.4 0.0 collective-permute-done.5
  18.4 0.0 collective-permute-done.6
  18.4 0.4 early_fit.3
  18.8 0.0 collective-permute-done.1
  18.8 0.9 %collective-permute-done.3 = bf16[144,2,128]{2,1,0:T(2,128)(2,1)S(1)} collective-permute-done((bf16[144,2,128]{2,1,0:T(2,128)(2,1)S(1)}, bf16[144,2,128]{2,1,0:T(2,128)(2,1)S(1)}, u32[]{:S(2)}, u32[]{:S(2)}) %collective-permute-start.3) | collective-permute-done | bytes 73760 | tf_op jit(solution)/shard_map/ppermute | solution.py:352
  19.7 4.1 %invert.1 = (f32[608,256]{1,0:T(8,128)S(1)}, f32[16,608]{1,0:T(8,128)S(1)}) custom-call(bf16[288,128]{1,0:T(8,128)(2,1)S(1)} %bitcast.17, bf16[288,128]{1,0:T(8,128)(2,1)S(1)} %bitcast.20, bf16[576,256]{1,0:T(8,128)(2,1)S(1)} %get-tuple-element.41.refs_2_, bf16[288,256]{1,0:T(8,128)(2,1)S(1)} %get-tuple-element.45.refs_3_, ...), custom_call_target="tpu_custom_call" | custom-call | tf_op jit(solution)/shard_map/invert/pallas_call | solution.py:290
  23.8 1.6 %collective-permute-start.7 = (f32[8,608]{1,0:T(8,128)S(1)}, f32[8,608]{1,0:T(8,128)S(1)}, u32[]{:S(2)}, u32[]{:S(2)}) collective-permute-start(f32[8,608]{1,0:T(8,128)S(1)} %get-tuple-element.53), channel_id=1, source_target_pairs={{8,16},{12,20},{24,1},{28,5},{9,17},{13,21},{0,4},{25,29},{16,8},{... | collective-permute-start | bytes 58376 | tf_op jit(solution)/shard_map/ppermute | solution.py:444
  25.4 2.3 %collective-permute-start.8 = (f32[8,608]{1,0:T(8,128)S(1)}, f32[8,608]{1,0:T(8,128)S(1)}, u32[]{:S(2)}, u32[]{:S(2)}) collective-permute-start(f32[8,608]{1,0:T(8,128)S(1)} %get-tuple-element.54), channel_id=1, source_target_pairs={{0,8},{4,12},{16,24},{20,28},{1,9},{5,13},{17,25},{21,29},{8,0},{1... | collective-permute-start | bytes 58376 | tf_op jit(solution)/shard_map/ppermute | solution.py:444
  27.8 0.0 collective-permute-done.7
  27.8 1.8 %collective-permute-done.8 = f32[8,608]{1,0:T(8,128)S(1)} collective-permute-done((f32[8,608]{1,0:T(8,128)S(1)}, f32[8,608]{1,0:T(8,128)S(1)}, u32[]{:S(2)}, u32[]{:S(2)}) %collective-permute-start.8) | collective-permute-done | bytes 19488 | tf_op jit(solution)/shard_map/ppermute | solution.py:444
  29.6 2.4 %collective-permute-start.9 = (f32[16,608]{1,0:T(8,128)S(1)}, f32[16,608]{1,0:T(8,128)S(1)}, u32[]{:S(2)}, u32[]{:S(2)}) collective-permute-start(f32[16,608]{1,0:T(8,128)S(1)} %maximum_add_fusion.first_ref), channel_id=1, source_target_pairs={{0,6},{2,4},{8,14},{10,12},{16,22},{18,20},{24,30},{26,28},{6,0},{... | collective-permute-start | bytes 116744 | tf_op jit(solution)/shard_map/ppermute | solution.py:444
  32.0 0.6 %collective-permute-start.10 = (f32[16,608]{1,0:T(8,128)S(1)}, f32[16,608]{1,0:T(8,128)S(1)}, u32[]{:S(2)}, u32[]{:S(2)}) collective-permute-start(f32[16,608]{1,0:T(8,128)S(1)} %maximum_add_fusion.first_ref), channel_id=1, source_target_pairs={{0,4},{8,12},{16,20},{24,28},{4,0},{12,8},{20,16},{28,24},{1,5},{9... | collective-permute-start | bytes 116744 | tf_op jit(solution)/shard_map/ppermute | solution.py:444
  32.6 0.5 %collective-permute-start.11 = (f32[16,608]{1,0:T(8,128)S(1)}, f32[16,608]{1,0:T(8,128)S(1)}, u32[]{:S(2)}, u32[]{:S(2)}) collective-permute-start(f32[16,608]{1,0:T(8,128)S(1)} %maximum_add_fusion.first_ref), channel_id=1, source_target_pairs={{0,2},{2,0},{1,3},{3,1},{4,6},{6,4},{5,7},{7,5},{8,10},{10,8},{9,1... | collective-permute-start | bytes 116744 | tf_op jit(solution)/shard_map/ppermute | solution.py:444
  33.2 1.4 %collective-permute-done.9.refs_0_ = f32[16,608]{1,0:T(8,128)S(1)} collective-permute-done((f32[16,608]{1,0:T(8,128)S(1)}, f32[16,608]{1,0:T(8,128)S(1)}, u32[]{:S(2)}, u32[]{:S(2)}) %collective-permute-start.9) | collective-permute-done | bytes 38944 | tf_op jit(solution)/shard_map/ppermute | solution.py:444
  34.6 1.4 %collective-permute-done.10.refs_1_ = f32[16,608]{1,0:T(8,128)S(1)} collective-permute-done((f32[16,608]{1,0:T(8,128)S(1)}, f32[16,608]{1,0:T(8,128)S(1)}, u32[]{:S(2)}, u32[]{:S(2)}) %collective-permute-start.10) | collective-permute-done | bytes 38944 | tf_op jit(solution)/shard_map/ppermute | solution.py:444
  36.0 0.6 %collective-permute-done.11.refs_2_ = f32[16,608]{1,0:T(8,128)S(1)} collective-permute-done((f32[16,608]{1,0:T(8,128)S(1)}, f32[16,608]{1,0:T(8,128)S(1)}, u32[]{:S(2)}, u32[]{:S(2)}) %collective-permute-start.11) | collective-permute-done | bytes 38944 | tf_op jit(solution)/shard_map/ppermute | solution.py:444
  36.6 1.5 %deramp.1 = f32[1200,128]{1,0:T(8,128)} custom-call(f32[16,608]{1,0:T(8,128)S(1)} %maximum_add_fusion.first_ref, f32[16,608]{1,0:T(8,128)S(1)} %collective-permute-done.9.refs_0_, f32[16,608]{1,0:T(8,128)S(1)} %collective-permute-done.10.refs_1_, f32[16,608]{1,0:T(8,128)S(1)} %collective-permute-done.11.refs_2_, f32[608,256]{1,0:T(8,128)S(1)} %get-tuple-element.51.refs_3_, ...), custom_call_target="tpu_custom_call" | custom-call | tf_op jit(solution)/shard_map/deramp/pallas_call | solution.py:431
  (3 shorter events, 0.0 us)
Async XLA Ops:
  1.2 10.0 %collective-permute-start = (bf16[144,2,128]{2,1,0:T(2,128)(2,1)S(1)}, bf16[144,2,128]{2,1,0:T(2,128)(2,1)S(1)}, u32[]{:S(2)}, u32[]{:S(2)}) collective-permute-start(bf16[144,2,128]{2,1,0:T(2,128)(2,1)S(1)} %get-tuple-element.30), channel_id=1, source_target_pairs={{0,4},{4,0},{8,12},{12,8},{16,20},{20,16},{24,28},{28,24},{1,5},{5... | collective-permute-start | bytes 221192 | tf_op jit(solution)/shard_map/ppermute | solution.py:352
  4.2 9.2 %collective-permute-start.2 = (bf16[144,2,128]{2,1,0:T(2,128)(2,1)S(1)}, bf16[144,2,128]{2,1,0:T(2,128)(2,1)S(1)}, u32[]{:S(2)}, u32[]{:S(2)}) collective-permute-start(bf16[144,2,128]{2,1,0:T(2,128)(2,1)S(1)} %get-tuple-element.33), channel_id=1, source_target_pairs={{0,8},{4,12},{8,0},{12,4},{16,24},{20,28},{24,16},{28,20},{1,9},{5... | collective-permute-start | bytes 221192 | tf_op jit(solution)/shard_map/ppermute | solution.py:352
  5.8 12.1 %collective-permute-start.4 = (bf16[144,2,128]{2,1,0:T(2,128)(2,1)S(1)}, bf16[144,2,128]{2,1,0:T(2,128)(2,1)S(1)}, u32[]{:S(2)}, u32[]{:S(2)}) collective-permute-start(bf16[144,2,128]{2,1,0:T(2,128)(2,1)S(1)} %get-tuple-element.38), channel_id=1, source_target_pairs={{0,16},{4,20},{8,24},{12,28},{16,0},{20,4},{24,8},{28,12},{1,17},{... | collective-permute-start | bytes 221192 | tf_op jit(solution)/shard_map/ppermute | solution.py:352
  8.4 10.0 %collective-permute-start.5 = (bf16[144,2,128]{2,1,0:T(2,128)(2,1)S(1)}, bf16[144,2,128]{2,1,0:T(2,128)(2,1)S(1)}, u32[]{:S(2)}, u32[]{:S(2)}) collective-permute-start(bf16[144,2,128]{2,1,0:T(2,128)(2,1)S(1)} %get-tuple-element.42), channel_id=1, source_target_pairs={{0,20},{4,16},{8,28},{12,24},{16,4},{20,0},{24,12},{28,8},{1,21},{... | collective-permute-start | bytes 221192 | tf_op jit(solution)/shard_map/ppermute | solution.py:352
  8.7 9.8 %collective-permute-start.6 = (bf16[144,2,128]{2,1,0:T(2,128)(2,1)S(1)}, bf16[144,2,128]{2,1,0:T(2,128)(2,1)S(1)}, u32[]{:S(2)}, u32[]{:S(2)}) collective-permute-start(bf16[144,2,128]{2,1,0:T(2,128)(2,1)S(1)} %get-tuple-element.43), channel_id=1, source_target_pairs={{0,24},{4,28},{8,16},{12,20},{16,8},{20,12},{24,0},{28,4},{1,25},{... | collective-permute-start | bytes 221192 | tf_op jit(solution)/shard_map/ppermute | solution.py:352
  11.2 7.6 %collective-permute-start.1 = (bf16[144,2,128]{2,1,0:T(2,128)(2,1)S(1)}, bf16[144,2,128]{2,1,0:T(2,128)(2,1)S(1)}, u32[]{:S(2)}, u32[]{:S(2)}) collective-permute-start(bf16[144,2,128]{2,1,0:T(2,128)(2,1)S(1)} %get-tuple-element.31), channel_id=1, source_target_pairs={{0,28},{4,24},{8,20},{12,16},{16,12},{20,8},{24,4},{28,0},{1,29},{... | collective-permute-start | bytes 221192 | tf_op jit(solution)/shard_map/ppermute | solution.py:352
  13.5 6.2 %collective-permute-start.3 = (bf16[144,2,128]{2,1,0:T(2,128)(2,1)S(1)}, bf16[144,2,128]{2,1,0:T(2,128)(2,1)S(1)}, u32[]{:S(2)}, u32[]{:S(2)}) collective-permute-start(bf16[144,2,128]{2,1,0:T(2,128)(2,1)S(1)} %get-tuple-element.34), channel_id=1, source_target_pairs={{0,12},{4,8},{8,4},{12,0},{16,28},{20,24},{24,20},{28,16},{1,13},{... | collective-permute-start | bytes 221192 | tf_op jit(solution)/shard_map/ppermute | solution.py:352
  23.8 3.9 %collective-permute-start.7 = (f32[8,608]{1,0:T(8,128)S(1)}, f32[8,608]{1,0:T(8,128)S(1)}, u32[]{:S(2)}, u32[]{:S(2)}) collective-permute-start(f32[8,608]{1,0:T(8,128)S(1)} %get-tuple-element.53), channel_id=1, source_target_pairs={{8,16},{12,20},{24,1},{28,5},{9,17},{13,21},{0,4},{25,29},{16,8},{... | collective-permute-start | bytes 58376 | tf_op jit(solution)/shard_map/ppermute | solution.py:444
  25.4 4.2 %collective-permute-start.8 = (f32[8,608]{1,0:T(8,128)S(1)}, f32[8,608]{1,0:T(8,128)S(1)}, u32[]{:S(2)}, u32[]{:S(2)}) collective-permute-start(f32[8,608]{1,0:T(8,128)S(1)} %get-tuple-element.54), channel_id=1, source_target_pairs={{0,8},{4,12},{16,24},{20,28},{1,9},{5,13},{17,25},{21,29},{8,0},{1... | collective-permute-start | bytes 58376 | tf_op jit(solution)/shard_map/ppermute | solution.py:444
  29.6 5.0 %collective-permute-start.9 = (f32[16,608]{1,0:T(8,128)S(1)}, f32[16,608]{1,0:T(8,128)S(1)}, u32[]{:S(2)}, u32[]{:S(2)}) collective-permute-start(f32[16,608]{1,0:T(8,128)S(1)} %maximum_add_fusion.first_ref), channel_id=1, source_target_pairs={{0,6},{2,4},{8,14},{10,12},{16,22},{18,20},{24,30},{26,28},{6,0},{... | collective-permute-start | bytes 116744 | tf_op jit(solution)/shard_map/ppermute | solution.py:444
  32.0 4.0 %collective-permute-start.10 = (f32[16,608]{1,0:T(8,128)S(1)}, f32[16,608]{1,0:T(8,128)S(1)}, u32[]{:S(2)}, u32[]{:S(2)}) collective-permute-start(f32[16,608]{1,0:T(8,128)S(1)} %maximum_add_fusion.first_ref), channel_id=1, source_target_pairs={{0,4},{8,12},{16,20},{24,28},{4,0},{12,8},{20,16},{28,24},{1,5},{9... | collective-permute-start | bytes 116744 | tf_op jit(solution)/shard_map/ppermute | solution.py:444
  32.6 4.0 %collective-permute-start.11 = (f32[16,608]{1,0:T(8,128)S(1)}, f32[16,608]{1,0:T(8,128)S(1)}, u32[]{:S(2)}, u32[]{:S(2)}) collective-permute-start(f32[16,608]{1,0:T(8,128)S(1)} %maximum_add_fusion.first_ref), channel_id=1, source_target_pairs={{0,2},{2,0},{1,3},{3,1},{4,6},{6,4},{5,7},{7,5},{8,10},{10,8},{9,1... | collective-permute-start | bytes 116744 | tf_op jit(solution)/shard_map/ppermute | solution.py:444

commit v9 on v8

--- a/solution.py
+++ b/solution.py
@@ -193,7 +193,7 @@
         *chunk_refs, incidence, gain_top, gain_low, weighted_ref, basis_ref, series_ref,
         moments_ref, wide, data, residual, moved,
     ) = refs
-    ifg_total, pixel_count = moved.shape
+    ifg_total, pixel_count = moved.shape[1:]
     date_rows = gain_top.shape[0]
     date_pad = incidence.shape[1] // 2
     late_refs, early_refs = chunk_refs[:late], chunk_refs[late:]
@@ -229,7 +229,7 @@
     def folded(square):
         return jnp.sum(square.reshape(-1, 8, pixel_count), axis=0)
 
-    def reweighted(total):
+    def reweighted(total, moved):
         scale = jnp.sum(total, axis=0, keepdims=True) / ifg_total + 1e-06
         strength = coherence * (scale * scale)
         for rows in ifg_tiles:
@@ -253,11 +253,11 @@
         left = observed(rows).astype(jnp.float32) - product(incidence[rows, :], both)
         residual[rows, :] = left
         total = total + folded(left * left)
-    reweighted(total)
+    reweighted(total, moved.at[0])
     for sweep in range(1, REWEIGHTS):
         steps = []
         for rows in date_tiles:
-            part = gained(gain_top, None, rows, everything, moved[...])
+            part = gained(gain_top, None, rows, everything, moved[sweep - 1])
             steps.append(part.astype(jnp.bfloat16))
             series_ref[rows, :] = series_ref[rows, :] + part
         step = jnp.concatenate(steps + spare, axis=0)
@@ -266,20 +266,19 @@
             left = residual[rows, :] - product(incidence[rows, :date_pad], step)
             residual[rows, :] = left
             total = total + folded(left * left)
-        held = moved[...]
+        reweighted(total, moved.at[sweep])
         for rows in date_tiles:
-            series_ref[rows, :] = series_ref[rows, :] + product(gain_low[rows, :], held)
-        reweighted(total)
+            series_ref[rows, :] = series_ref[rows, :] + product(gain_low[rows, :], moved[sweep - 1])
     for rows in date_tiles:
-        part = gained(gain_top, None, rows, everything, moved[...])
+        part = gained(gain_top, None, rows, everything, moved[REWEIGHTS - 1])
         series_ref[rows, :] = series_ref[rows, :] + part
     series_ref[pl.ds(date_total, 8), :] = basis_ref[...]
     series_top, series_low = halves(series_ref[...])
     weighted_top, weighted_low = halves(weighted_ref[...])
+    count = weighted_top.shape[0]
     across = (((1,), (1,)), ((), ()))
-    moments_ref[...] = product(weighted_top, series_top, across) + (
-        product(weighted_low, series_top, across) + product(weighted_top, series_low, across)
-    )
+    first = product(jnp.concatenate([weighted_top, weighted_low], axis=0), series_top, across)
+    moments_ref[...] = first[:count] + (first[count:] + product(weighted_top, series_low, across))
 
 
 def invert(late_chunks, early, incidence, gains, weighted, basis, row_local, date_total):
@@ -299,7 +298,7 @@
             pltpu.VMEM(late_chunks[0].shape, jnp.float32),
             pltpu.VMEM((ifg_total - kept, pixel_count), jnp.bfloat16),
             pltpu.VMEM((ifg_total, pixel_count), jnp.float32),
-            pltpu.VMEM((ifg_total, pixel_count), jnp.bfloat16),
+            pltpu.VMEM((REWEIGHTS, ifg_total, pixel_count), jnp.bfloat16),
         ],
         compiler_params=pltpu.CompilerParams(vmem_limit_bytes=VMEM_LIMIT),
         name="invert",
@@ -356,8 +355,7 @@
     return [found[mask].reshape(-1, col_local) for mask in ARRIVAL], ARRIVAL
 
 
-def plane_solve(gram_matrix, right_side):
-
+def plane_weights(gram_matrix, basis):
     def entry(row_pos, col_pos):
         return gram_matrix[row_pos % 3][col_pos % 3]
 
@@ -369,18 +367,16 @@
         ]
         for row_pos in range(3)
     ]
-    determinant = (
+    inverse = 1.0 / (
         entry(0, 0) * cofactors[0][0]
         + entry(0, 1) * cofactors[0][1]
         + entry(0, 2) * cofactors[0][2]
     )
     return [
-        (
-            (cofactors[0][col_pos] / determinant) * right_side[0]
-            + (cofactors[1][col_pos] / determinant) * right_side[1]
-            + (cofactors[2][col_pos] / determinant) * right_side[2]
-        )
-        for col_pos in range(3)
+        (cofactors[row_pos][0] * inverse) * basis[0]
+        + (cofactors[row_pos][1] * inverse) * basis[1]
+        + (cofactors[row_pos][2] * inverse) * basis[2]
+        for row_pos in range(3)
     ]
 
 
@@ -393,17 +389,26 @@
         jnp.concatenate([totals[2 * k : 2 * k + 2], totals[8 + 2 * k : 10 + 2 * k]], axis=0)
         for k in range(3)
     ]
+    wide = (sums[0].shape[0], member_ref.shape[1])
     gram = [
-        [sums[k][:, date_total + m : date_total + m + 1] + (1.0 if k == m else 0.0) for m in range(3)]
+        [
+            jnp.broadcast_to(sums[k][:, date_total + m : date_total + m + 1], wide)
+            + (1.0 if k == m else 0.0)
+            for m in range(3)
+        ]
         for k in range(3)
     ]
-    planes = plane_solve(gram, sums)
-    planes.append(jnp.zeros_like(planes[0]))
-    planes_top, planes_low = halves(jnp.concatenate(planes, axis=0))
-    member_top, member_low = halves(member_ref[...])
+    weights = plane_weights(gram, [member_ref[4 * k : 4 * k + 4, :] for k in range(3)])
+    spare = 4
+    weights_top, weights_low = halves(
+        jnp.concatenate(weights + [jnp.zeros((spare, weights[0].shape[1]), jnp.float32)], axis=0)
+    )
+    sums_top, sums_low = halves(
+        jnp.concatenate(sums + [jnp.zeros((spare, sums[0].shape[1]), jnp.float32)], axis=0)
+    )
     ramp = product(
-        jnp.concatenate([planes_top, planes_low, planes_top], axis=0),
-        jnp.concatenate([member_top, member_top, member_low], axis=0),
+        jnp.concatenate([sums_top, sums_low, sums_top], axis=0),
+        jnp.concatenate([weights_top, weights_top, weights_low], axis=0),
         (((0,), (0,)), ((), ())),
     )
     col_local = series_ref.shape[1] // row_local

time: 38.4 us -> 37.7 us (0.982)
  Pallas kernels: 12.1 us -> 11.4 us
    pallas_call x1, Pallas kernels: 1.51 us -> 1.11 us  [deramp(): pl.pallas_call(functools.partial(deramp_kernel, row_local=row_local, date...]
where the time goes in v9:
time: 37.7 us; the launch traced here: 37.5 us
  starting transfers between devices  19.7 us (52%)
  Pallas kernels  11.4 us (30%)
  waiting for transfers between devices  6.23 us (17%)
    ppermute x7, starting transfers between devices, send(): lax.ppermute(block, 'stack', [(i, i ^ mask) for i in range(stack_size)])  12.3 us
    ppermute x5, starting transfers between devices, swap(): return lax.ppermute(value, axes, both)  7.49 us
    ppermute x5, waiting for transfers between devices, swap(): return lax.ppermute(value, axes, both)  5.32 us
    pallas_call x1, Pallas kernels, prepare(): pl.pallas_call(functools.partial(prepare_kernel, order=order, col_total=c...  4.38 us
    pallas_call x1, Pallas kernels, invert(): pl.pallas_call(functools.partial(invert_kernel, row_local=row_local, date...  3.84 us
    pallas_call x1, Pallas kernels, cut(): pl.pallas_call(cut_kernel, out_shape=[jax.ShapeDtypeStruct((ifg_local, ro...  1.2 us
    pallas_call x1, Pallas kernels, deramp(): pl.pallas_call(functools.partial(deramp_kernel, row_local=row_local, date...  1.11 us
    ppermute x7, waiting for transfers between devices, send(): lax.ppermute(block, 'stack', [(i, i ^ mask) for i in range(stack_size)])  0.91 us
  transfers between devices with their start and end apart: 12, of which 5 were waited for; matrix products, arithmetic and copies ran while one was open for 0% of the time, Pallas kernels for 14%

profile of v9, /device:TPU:0, one launch (start us, length us, event | category | flops | bytes accessed | tf_op | source)
XLA Modules:
  0.0 37.5 jit_solution(5212151580728228538)
XLA Ops:
  0.0 1.2 %cut.1 = (bf16[144,2,128]{2,1,0:T(2,128)(2,1)S(1)}, bf16[144,2,128]{2,1,0:T(2,128)(2,1)S(1)}, bf16[144,2,128]{2,1,0:T(2,128)(2,1)S(1)}, bf16[144,2,128]{2,1,0:T(...) custom-call(bf16[144,8,2,128]{3,2,1,0:T(2,128)(2,1)} %bitcast.21), custom_call_target="tpu_custom_call" | custom-call | tf_op jit(solution)/shard_map/cut/pallas_call | solution.py:326
  1.2 3.0 %collective-permute-start = (bf16[144,2,128]{2,1,0:T(2,128)(2,1)S(1)}, bf16[144,2,128]{2,1,0:T(2,128)(2,1)S(1)}, u32[]{:S(2)}, u32[]{:S(2)}) collective-permute-start(bf16[144,2,128]{2,1,0:T(2,128)(2,1)S(1)} %get-tuple-element.30), channel_id=1, source_target_pairs={{0,4},{4,0},{8,12},{12,8},{16,20},{20,16},{24,28},{28,24},{1,5},{5... | collective-permute-start | bytes 221192 | tf_op jit(solution)/shard_map/ppermute | solution.py:351
  4.2 1.6 %collective-permute-start.2 = (bf16[144,2,128]{2,1,0:T(2,128)(2,1)S(1)}, bf16[144,2,128]{2,1,0:T(2,128)(2,1)S(1)}, u32[]{:S(2)}, u32[]{:S(2)}) collective-permute-start(bf16[144,2,128]{2,1,0:T(2,128)(2,1)S(1)} %get-tuple-element.33), channel_id=1, source_target_pairs={{0,8},{4,12},{8,0},{12,4},{16,24},{20,28},{24,16},{28,20},{1,9},{5... | collective-permute-start | bytes 221192 | tf_op jit(solution)/shard_map/ppermute | solution.py:351
  5.8 2.6 %collective-permute-start.4 = (bf16[144,2,128]{2,1,0:T(2,128)(2,1)S(1)}, bf16[144,2,128]{2,1,0:T(2,128)(2,1)S(1)}, u32[]{:S(2)}, u32[]{:S(2)}) collective-permute-start(bf16[144,2,128]{2,1,0:T(2,128)(2,1)S(1)} %get-tuple-element.38), channel_id=1, source_target_pairs={{0,16},{4,20},{8,24},{12,28},{16,0},{20,4},{24,8},{28,12},{1,17},{... | collective-permute-start | bytes 221192 | tf_op jit(solution)/shard_map/ppermute | solution.py:351
  8.4 0.3 collective-permute-start.5
  8.7 2.5 %collective-permute-start.6 = (bf16[144,2,128]{2,1,0:T(2,128)(2,1)S(1)}, bf16[144,2,128]{2,1,0:T(2,128)(2,1)S(1)}, u32[]{:S(2)}, u32[]{:S(2)}) collective-permute-start(bf16[144,2,128]{2,1,0:T(2,128)(2,1)S(1)} %get-tuple-element.43), channel_id=1, source_target_pairs={{0,24},{4,28},{8,16},{12,20},{16,8},{20,12},{24,0},{28,4},{1,25},{... | collective-permute-start | bytes 221192 | tf_op jit(solution)/shard_map/ppermute | solution.py:351
  11.2 0.0 collective-permute-done
  11.2 2.3 %collective-permute-start.1 = (bf16[144,2,128]{2,1,0:T(2,128)(2,1)S(1)}, bf16[144,2,128]{2,1,0:T(2,128)(2,1)S(1)}, u32[]{:S(2)}, u32[]{:S(2)}) collective-permute-start(bf16[144,2,128]{2,1,0:T(2,128)(2,1)S(1)} %get-tuple-element.31), channel_id=1, source_target_pairs={{0,28},{4,24},{8,20},{12,16},{16,12},{20,8},{24,4},{28,0},{1,29},{... | collective-permute-start | bytes 221192 | tf_op jit(solution)/shard_map/ppermute | solution.py:351
  13.5 0.0 collective-permute-done.2
  13.5 0.0 collective-permute-start.3
  13.5 4.4 %prepare.1 = (bf16[1152,1280]{1,0:T(8,128)(2,1)S(1)}, bf16[608,1152]{1,0:T(8,128)(2,1)S(1)}, bf16[608,1152]{1,0:T(8,128)(2,1)S(1)}, f32[16,256]{1,0:T(8,128)S(1)...) custom-call(s32[2,1152]{1,0:T(2,128)} %bitcast.22, f32[600,600]{1,0:T(8,128)} %prec_hbm.1, s32[2,128]{1,0:T(2,128)} %coherence_hbm.1, ...), custom_call_target="tpu_custom_call" | custom-call | tf_op jit(solution)/shard_map/prepare/pallas_call | solution.py:121
  17.9 0.0 collective-permute-done.4
  17.9 0.5 %early_fit.2 = (bf16[576,256]{1,0:T(8,128)(2,1)S(1)}, f32[608,256]{1,0:T(8,128)S(1)}) custom-call(bf16[288,128]{1,0:T(8,128)(2,1)S(1)} %bitcast.13, bf16[288,128]{1,0:T(8,128)(2,1)S(1)} %bitcast.14, bf16[288,128]{1,0:T(8,128)(2,1)S(1)} %bitcast.15, bf16[288,128]{1,0:T(8,128)(2,1)S(1)} %bitcast.16, bf16[608,1152]{1,0:T(8,128)(2,1)S(1)} %get-tuple-element.39.refs_4_.refs_6_, ...), custom_call_target="tpu_custom_call" | custom-call | tf_op jit(solution)/shard_map/early_fit/pallas_call | solution.py:177
  18.4 0.0 collective-permute-done.5
  18.4 0.0 collective-permute-done.6
  18.4 0.4 early_fit.3
  18.8 0.0 collective-permute-done.1
  18.8 0.9 %collective-permute-done.3 = bf16[144,2,128]{2,1,0:T(2,128)(2,1)S(1)} collective-permute-done((bf16[144,2,128]{2,1,0:T(2,128)(2,1)S(1)}, bf16[144,2,128]{2,1,0:T(2,128)(2,1)S(1)}, u32[]{:S(2)}, u32[]{:S(2)}) %collective-permute-start.3) | collective-permute-done | bytes 73760 | tf_op jit(solution)/shard_map/ppermute | solution.py:351
  19.7 3.8 %invert.1 = (f32[608,256]{1,0:T(8,128)S(1)}, f32[16,608]{1,0:T(8,128)S(1)}) custom-call(bf16[288,128]{1,0:T(8,128)(2,1)S(1)} %bitcast.17, bf16[288,128]{1,0:T(8,128)(2,1)S(1)} %bitcast.20, bf16[576,256]{1,0:T(8,128)(2,1)S(1)} %get-tuple-element.41.refs_2_, bf16[288,256]{1,0:T(8,128)(2,1)S(1)} %get-tuple-element.45.refs_3_, ...), custom_call_target="tpu_custom_call" | custom-call | tf_op jit(solution)/shard_map/invert/pallas_call | solution.py:289
  23.6 1.6 %collective-permute-start.7 = (f32[8,608]{1,0:T(8,128)S(1)}, f32[8,608]{1,0:T(8,128)S(1)}, u32[]{:S(2)}, u32[]{:S(2)}) collective-permute-start(f32[8,608]{1,0:T(8,128)S(1)} %get-tuple-element.53), channel_id=1, source_target_pairs={{8,16},{12,20},{24,1},{28,5},{9,17},{13,21},{0,4},{25,29},{16,8},{... | collective-permute-start | bytes 58376 | tf_op jit(solution)/shard_map/ppermute | solution.py:449
  25.1 2.4 %collective-permute-start.8 = (f32[8,608]{1,0:T(8,128)S(1)}, f32[8,608]{1,0:T(8,128)S(1)}, u32[]{:S(2)}, u32[]{:S(2)}) collective-permute-start(f32[8,608]{1,0:T(8,128)S(1)} %get-tuple-element.54), channel_id=1, source_target_pairs={{0,8},{4,12},{16,24},{20,28},{1,9},{5,13},{17,25},{21,29},{8,0},{1... | collective-permute-start | bytes 58376 | tf_op jit(solution)/shard_map/ppermute | solution.py:449
  27.5 0.0 collective-permute-done.7
  27.5 1.8 %collective-permute-done.8 = f32[8,608]{1,0:T(8,128)S(1)} collective-permute-done((f32[8,608]{1,0:T(8,128)S(1)}, f32[8,608]{1,0:T(8,128)S(1)}, u32[]{:S(2)}, u32[]{:S(2)}) %collective-permute-start.8) | collective-permute-done | bytes 19488 | tf_op jit(solution)/shard_map/ppermute | solution.py:449
  29.4 2.4 %collective-permute-start.9 = (f32[16,608]{1,0:T(8,128)S(1)}, f32[16,608]{1,0:T(8,128)S(1)}, u32[]{:S(2)}, u32[]{:S(2)}) collective-permute-start(f32[16,608]{1,0:T(8,128)S(1)} %maximum_add_fusion.first_ref), channel_id=1, source_target_pairs={{0,6},{2,4},{8,14},{10,12},{16,22},{18,20},{24,30},{26,28},{6,0},{... | collective-permute-start | bytes 116744 | tf_op jit(solution)/shard_map/ppermute | solution.py:449
  31.8 0.6 %collective-permute-start.10 = (f32[16,608]{1,0:T(8,128)S(1)}, f32[16,608]{1,0:T(8,128)S(1)}, u32[]{:S(2)}, u32[]{:S(2)}) collective-permute-start(f32[16,608]{1,0:T(8,128)S(1)} %maximum_add_fusion.first_ref), channel_id=1, source_target_pairs={{0,4},{8,12},{16,20},{24,28},{4,0},{12,8},{20,16},{28,24},{1,5},{9... | collective-permute-start | bytes 116744 | tf_op jit(solution)/shard_map/ppermute | solution.py:449
  32.4 0.5 %collective-permute-start.11 = (f32[16,608]{1,0:T(8,128)S(1)}, f32[16,608]{1,0:T(8,128)S(1)}, u32[]{:S(2)}, u32[]{:S(2)}) collective-permute-start(f32[16,608]{1,0:T(8,128)S(1)} %maximum_add_fusion.first_ref), channel_id=1, source_target_pairs={{0,2},{2,0},{1,3},{3,1},{4,6},{6,4},{5,7},{7,5},{8,10},{10,8},{9,1... | collective-permute-start | bytes 116744 | tf_op jit(solution)/shard_map/ppermute | solution.py:449
  32.9 1.4 %collective-permute-done.9.refs_0_ = f32[16,608]{1,0:T(8,128)S(1)} collective-permute-done((f32[16,608]{1,0:T(8,128)S(1)}, f32[16,608]{1,0:T(8,128)S(1)}, u32[]{:S(2)}, u32[]{:S(2)}) %collective-permute-start.9) | collective-permute-done | bytes 38944 | tf_op jit(solution)/shard_map/ppermute | solution.py:449
  34.3 1.4 %collective-permute-done.10.refs_1_ = f32[16,608]{1,0:T(8,128)S(1)} collective-permute-done((f32[16,608]{1,0:T(8,128)S(1)}, f32[16,608]{1,0:T(8,128)S(1)}, u32[]{:S(2)}, u32[]{:S(2)}) %collective-permute-start.10) | collective-permute-done | bytes 38944 | tf_op jit(solution)/shard_map/ppermute | solution.py:449
  35.8 0.6 %collective-permute-done.11.refs_2_ = f32[16,608]{1,0:T(8,128)S(1)} collective-permute-done((f32[16,608]{1,0:T(8,128)S(1)}, f32[16,608]{1,0:T(8,128)S(1)}, u32[]{:S(2)}, u32[]{:S(2)}) %collective-permute-start.11) | collective-permute-done | bytes 38944 | tf_op jit(solution)/shard_map/ppermute | solution.py:449
  36.4 1.1 %deramp.1 = f32[1200,128]{1,0:T(8,128)} custom-call(f32[16,608]{1,0:T(8,128)S(1)} %maximum_add_fusion.first_ref, f32[16,608]{1,0:T(8,128)S(1)} %collective-permute-done.9.refs_0_, f32[16,608]{1,0:T(8,128)S(1)} %collective-permute-done.10.refs_1_, f32[16,608]{1,0:T(8,128)S(1)} %collective-permute-done.11.refs_2_, f32[608,256]{1,0:T(8,128)S(1)} %get-tuple-element.51.refs_3_, ...), custom_call_target="tpu_custom_call" | custom-call | tf_op jit(solution)/shard_map/deramp/pallas_call | solution.py:436
  (3 shorter events, 0.0 us)
Async XLA Ops:
  1.2 10.0 %collective-permute-start = (bf16[144,2,128]{2,1,0:T(2,128)(2,1)S(1)}, bf16[144,2,128]{2,1,0:T(2,128)(2,1)S(1)}, u32[]{:S(2)}, u32[]{:S(2)}) collective-permute-start(bf16[144,2,128]{2,1,0:T(2,128)(2,1)S(1)} %get-tuple-element.30), channel_id=1, source_target_pairs={{0,4},{4,0},{8,12},{12,8},{16,20},{20,16},{24,28},{28,24},{1,5},{5... | collective-permute-start | bytes 221192 | tf_op jit(solution)/shard_map/ppermute | solution.py:351
  4.2 9.2 %collective-permute-start.2 = (bf16[144,2,128]{2,1,0:T(2,128)(2,1)S(1)}, bf16[144,2,128]{2,1,0:T(2,128)(2,1)S(1)}, u32[]{:S(2)}, u32[]{:S(2)}) collective-permute-start(bf16[144,2,128]{2,1,0:T(2,128)(2,1)S(1)} %get-tuple-element.33), channel_id=1, source_target_pairs={{0,8},{4,12},{8,0},{12,4},{16,24},{20,28},{24,16},{28,20},{1,9},{5... | collective-permute-start | bytes 221192 | tf_op jit(solution)/shard_map/ppermute | solution.py:351
  5.8 12.1 %collective-permute-start.4 = (bf16[144,2,128]{2,1,0:T(2,128)(2,1)S(1)}, bf16[144,2,128]{2,1,0:T(2,128)(2,1)S(1)}, u32[]{:S(2)}, u32[]{:S(2)}) collective-permute-start(bf16[144,2,128]{2,1,0:T(2,128)(2,1)S(1)} %get-tuple-element.38), channel_id=1, source_target_pairs={{0,16},{4,20},{8,24},{12,28},{16,0},{20,4},{24,8},{28,12},{1,17},{... | collective-permute-start | bytes 221192 | tf_op jit(solution)/shard_map/ppermute | solution.py:351
  8.4 10.0 %collective-permute-start.5 = (bf16[144,2,128]{2,1,0:T(2,128)(2,1)S(1)}, bf16[144,2,128]{2,1,0:T(2,128)(2,1)S(1)}, u32[]{:S(2)}, u32[]{:S(2)}) collective-permute-start(bf16[144,2,128]{2,1,0:T(2,128)(2,1)S(1)} %get-tuple-element.42), channel_id=1, source_target_pairs={{0,20},{4,16},{8,28},{12,24},{16,4},{20,0},{24,12},{28,8},{1,21},{... | collective-permute-start | bytes 221192 | tf_op jit(solution)/shard_map/ppermute | solution.py:351
  8.7 9.8 %collective-permute-start.6 = (bf16[144,2,128]{2,1,0:T(2,128)(2,1)S(1)}, bf16[144,2,128]{2,1,0:T(2,128)(2,1)S(1)}, u32[]{:S(2)}, u32[]{:S(2)}) collective-permute-start(bf16[144,2,128]{2,1,0:T(2,128)(2,1)S(1)} %get-tuple-element.43), channel_id=1, source_target_pairs={{0,24},{4,28},{8,16},{12,20},{16,8},{20,12},{24,0},{28,4},{1,25},{... | collective-permute-start | bytes 221192 | tf_op jit(solution)/shard_map/ppermute | solution.py:351
  11.2 7.6 %collective-permute-start.1 = (bf16[144,2,128]{2,1,0:T(2,128)(2,1)S(1)}, bf16[144,2,128]{2,1,0:T(2,128)(2,1)S(1)}, u32[]{:S(2)}, u32[]{:S(2)}) collective-permute-start(bf16[144,2,128]{2,1,0:T(2,128)(2,1)S(1)} %get-tuple-element.31), channel_id=1, source_target_pairs={{0,28},{4,24},{8,20},{12,16},{16,12},{20,8},{24,4},{28,0},{1,29},{... | collective-permute-start | bytes 221192 | tf_op jit(solution)/shard_map/ppermute | solution.py:351
  13.5 6.2 %collective-permute-start.3 = (bf16[144,2,128]{2,1,0:T(2,128)(2,1)S(1)}, bf16[144,2,128]{2,1,0:T(2,128)(2,1)S(1)}, u32[]{:S(2)}, u32[]{:S(2)}) collective-permute-start(bf16[144,2,128]{2,1,0:T(2,128)(2,1)S(1)} %get-tuple-element.34), channel_id=1, source_target_pairs={{0,12},{4,8},{8,4},{12,0},{16,28},{20,24},{24,20},{28,16},{1,13},{... | collective-permute-start | bytes 221192 | tf_op jit(solution)/shard_map/ppermute | solution.py:351
  23.6 3.9 %collective-permute-start.7 = (f32[8,608]{1,0:T(8,128)S(1)}, f32[8,608]{1,0:T(8,128)S(1)}, u32[]{:S(2)}, u32[]{:S(2)}) collective-permute-start(f32[8,608]{1,0:T(8,128)S(1)} %get-tuple-element.53), channel_id=1, source_target_pairs={{8,16},{12,20},{24,1},{28,5},{9,17},{13,21},{0,4},{25,29},{16,8},{... | collective-permute-start | bytes 58376 | tf_op jit(solution)/shard_map/ppermute | solution.py:449
  25.1 4.2 %collective-permute-start.8 = (f32[8,608]{1,0:T(8,128)S(1)}, f32[8,608]{1,0:T(8,128)S(1)}, u32[]{:S(2)}, u32[]{:S(2)}) collective-permute-start(f32[8,608]{1,0:T(8,128)S(1)} %get-tuple-element.54), channel_id=1, source_target_pairs={{0,8},{4,12},{16,24},{20,28},{1,9},{5,13},{17,25},{21,29},{8,0},{1... | collective-permute-start | bytes 58376 | tf_op jit(solution)/shard_map/ppermute | solution.py:449
  29.4 5.0 %collective-permute-start.9 = (f32[16,608]{1,0:T(8,128)S(1)}, f32[16,608]{1,0:T(8,128)S(1)}, u32[]{:S(2)}, u32[]{:S(2)}) collective-permute-start(f32[16,608]{1,0:T(8,128)S(1)} %maximum_add_fusion.first_ref), channel_id=1, source_target_pairs={{0,6},{2,4},{8,14},{10,12},{16,22},{18,20},{24,30},{26,28},{6,0},{... | collective-permute-start | bytes 116744 | tf_op jit(solution)/shard_map/ppermute | solution.py:449
  31.8 4.0 %collective-permute-start.10 = (f32[16,608]{1,0:T(8,128)S(1)}, f32[16,608]{1,0:T(8,128)S(1)}, u32[]{:S(2)}, u32[]{:S(2)}) collective-permute-start(f32[16,608]{1,0:T(8,128)S(1)} %maximum_add_fusion.first_ref), channel_id=1, source_target_pairs={{0,4},{8,12},{16,20},{24,28},{4,0},{12,8},{20,16},{28,24},{1,5},{9... | collective-permute-start | bytes 116744 | tf_op jit(solution)/shard_map/ppermute | solution.py:449
  32.4 4.0 %collective-permute-start.11 = (f32[16,608]{1,0:T(8,128)S(1)}, f32[16,608]{1,0:T(8,128)S(1)}, u32[]{:S(2)}, u32[]{:S(2)}) collective-permute-start(f32[16,608]{1,0:T(8,128)S(1)} %maximum_add_fusion.first_ref), channel_id=1, source_target_pairs={{0,2},{2,0},{1,3},{3,1},{4,6},{6,4},{5,7},{7,5},{8,10},{10,8},{9,1... | collective-permute-start | bytes 116744 | tf_op jit(solution)/shard_map/ppermute | solution.py:449

commit v10 on v9

--- a/solution.py
+++ b/solution.py
@@ -12,7 +12,7 @@
 VMEM_LIMIT = 24 * 1024 * 1024
 ROWS_A = 192
 APPROX = False
-ARRIVAL = (0, 1, 2, 4, 5, 6, 7, 3)
+ARRIVAL = (0, 7, 1, 6, 2, 5, 3, 4)
 EARLY = (4, 6)
 OUT_PARTS = 5
 
@@ -27,24 +27,11 @@
 
 
 def prepare_kernel(
-    pairs_hbm, prec_hbm, coherence_hbm, tiles_hbm, incidence_ref, gain_top, gain_low, member_ref,
-    weighted_ref, basis_ref, pairs_ref, prec_ref, coherence_ref, tiles_ref, pairs, sems, *, order,
-    col_total, row_total,
+    prec_hbm, pairs_ref, coherence_ref, tiles_ref, incidence_ref, gain_top, gain_low, member_ref,
+    weighted_ref, basis_ref, prec_ref, pairs, sem, *, order, col_total, row_total,
 ):
-    copies = [
-        pltpu.make_async_copy(source, target, sems.at[index])
-        for index, (source, target) in enumerate(
-            (
-                (pairs_hbm, pairs_ref),
-                (prec_hbm, prec_ref),
-                (coherence_hbm, coherence_ref),
-                (tiles_hbm, tiles_ref),
-            )
-        )
-    ]
-    for copy in copies:
-        copy.start()
-    copies[0].wait()
+    copy = pltpu.make_async_copy(prec_hbm, prec_ref, sem)
+    copy.start()
     chunk = pairs_ref.shape[1] // len(order)
     date_total = prec_ref.shape[0]
     ifg_total = gain_top.shape[1]
@@ -60,11 +47,10 @@
         jnp.where(date_ids == pairs[1:2, :], 1.0, 0.0)
         - jnp.where(date_ids == pairs[0:1, :], 1.0, 0.0)
     ).astype(jnp.bfloat16)
+    copy.wait()
     incidence = incidence_t.T
     incidence_ref[:, :date_pad] = incidence
     incidence_ref[:, date_pad:] = incidence
-    for copy in copies[1:]:
-        copy.wait()
     prec = prec_ref[...]
     prec = prec - jnp.sum(prec, axis=1, keepdims=True) / date_total
     top, low = halves(prec)
@@ -110,10 +96,10 @@
     basis_ref[...] = jnp.concatenate([basis, coherence, jnp.zeros((4, pixel_count), jnp.float32)], axis=0)
 
 
-def prepare(pairs, preconditioner, coherence, tiles, date_pad, date_rows, order, col_total, row_total):
+def prepare(preconditioner, small, date_pad, date_rows, order, col_total, row_total):
+    pairs, coherence, tiles = small
     ifg_total = pairs.shape[1]
     pixel_count = coherence.size
-    arguments = (pairs, preconditioner, coherence, tiles)
     shapes = [((ifg_total, 2 * date_pad), jnp.bfloat16)]
     shapes += [((date_rows, ifg_total), jnp.bfloat16)] * 2
     shapes += [((rows, pixel_count), jnp.float32) for rows in (16, 16, 8)]
@@ -121,16 +107,16 @@
     return pl.pallas_call(
         functools.partial(prepare_kernel, order=order, col_total=col_total, row_total=row_total),
         out_shape=[jax.ShapeDtypeStruct(shape, dtype) for shape, dtype in shapes],
-        in_specs=[pl.BlockSpec(memory_space=pltpu.HBM)] * 4,
+        in_specs=[pl.BlockSpec(memory_space=pltpu.HBM)] + [whole] * 3,
         out_specs=[whole] * 6,
         scratch_shapes=[
-            *(pltpu.VMEM(value.shape, value.dtype) for value in arguments),
+            pltpu.VMEM(preconditioner.shape, jnp.float32),
             pltpu.VMEM(pairs.shape, jnp.int32),
-            pltpu.SemaphoreType.DMA((4,)),
+            pltpu.SemaphoreType.DMA,
         ],
         compiler_params=pltpu.CompilerParams(vmem_limit_bytes=VMEM_LIMIT),
         name="prepare",
-    )(*(pltpu.with_memory_space_constraint(value, pltpu.HBM) for value in arguments))
+    )(pltpu.with_memory_space_constraint(preconditioner, pltpu.HBM), *small)
 
 
 def unpack(chunk_refs, wide, data, row_local):
@@ -306,12 +292,18 @@
 
 
 def cut_kernel(source, *refs):
-    *targets, sems = refs
+    sems = refs[-1]
+    extra = len(refs) - 1 - source.shape[1]
+    extra //= 2
+    small, targets, fetched = refs[:extra], refs[extra:-1 - extra], refs[-1 - extra : -1]
+    place = lax.axis_index("stack")
     copies = [
-        pltpu.make_async_copy(
-            source.at[:, lax.axis_index("stack") ^ mask], target, sems.at[mask]
-        )
+        pltpu.make_async_copy(source.at[:, place ^ mask], target, sems.at[mask])
         for mask, target in enumerate(targets)
+    ]
+    copies += [
+        pltpu.make_async_copy(value, target, sems.at[len(targets) + index])
+        for index, (value, target) in enumerate(zip(small, fetched))
     ]
     for copy in copies:
         copy.start()
@@ -319,40 +311,39 @@
         copy.wait()
 
 
-def cut(phases, col_local):
+def cut(phases, col_local, small):
     ifg_local, row_local, col_range = phases.shape
     count = col_range // col_local
     view = phases.reshape(ifg_local, row_local, count, col_local).transpose(0, 2, 1, 3)
-    return pl.pallas_call(
+    shapes = [jax.ShapeDtypeStruct((ifg_local, row_local, col_local), phases.dtype)] * count
+    shapes += [jax.ShapeDtypeStruct(value.shape, value.dtype) for value in small]
+    arguments = (view, *small)
+    results = pl.pallas_call(
         cut_kernel,
-        out_shape=[jax.ShapeDtypeStruct((ifg_local, row_local, col_local), phases.dtype)] * count,
-        in_specs=[pl.BlockSpec(memory_space=pltpu.HBM)],
-        out_specs=[pl.BlockSpec(memory_space=pltpu.VMEM)] * count,
-        scratch_shapes=[pltpu.SemaphoreType.DMA((count,))],
+        out_shape=shapes,
+        in_specs=[pl.BlockSpec(memory_space=pltpu.HBM)] * len(arguments),
+        out_specs=[pl.BlockSpec(memory_space=pltpu.VMEM)] * len(shapes),
+        scratch_shapes=[pltpu.SemaphoreType.DMA((len(shapes),))],
         compiler_params=pltpu.CompilerParams(vmem_limit_bytes=8 * 1024 * 1024),
         name="cut",
-    )(pltpu.with_memory_space_constraint(view, pltpu.HBM))
-
-
-def exchange(phases, stack_size):
+    )(*(pltpu.with_memory_space_constraint(value, pltpu.HBM) for value in arguments))
+    return results[:count], results[count:]
+
+
+def exchange(phases, small, stack_size):
     ifg_local, row_local, col_range = phases.shape
     col_local = col_range // stack_size
     if stack_size != 8:
         blocks = phases.reshape(ifg_local, row_local, stack_size, col_local).transpose(2, 0, 1, 3)
         stacked = lax.all_to_all(blocks, "stack", split_axis=0, concat_axis=0, tiled=True)
-        return [stacked.reshape(-1, col_local)], (0,)
-    blocks = cut(phases, col_local)
+        return [stacked.reshape(-1, col_local)], small, (0,)
+    blocks, small = cut(phases, col_local, small)
     found = {0: blocks[0]}
 
-    def send(mask, after=None):
-        block = blocks[mask]
-        if after is not None:
-            block, found[after] = lax.optimization_barrier((block, found[after]))
-        found[mask] = lax.ppermute(block, "stack", [(i, i ^ mask) for i in range(stack_size)])
-
-    for mask, after in ((4, None), (5, None), (1, None), (6, None), (2, None), (7, 1), (3, 2)):
-        send(mask, after)
-    return [found[mask].reshape(-1, col_local) for mask in ARRIVAL], ARRIVAL
+    for mask in ARRIVAL[1:]:
+        pairs = [(i, i ^ mask) for i in range(stack_size)]
+        found[mask] = lax.ppermute(blocks[mask], "stack", pairs)
+    return [found[mask].reshape(-1, col_local) for mask in ARRIVAL], small, ARRIVAL
 
 
 def plane_weights(gram_matrix, basis):
@@ -458,9 +449,10 @@
     date_rows = -(-(date_total + 8) // 32) * 32
     date_pad = -(-date_rows // LANES) * LANES
 
-    chunks, order = exchange(phases, stack_size)
+    small = (ifg_pairs.T, coherence, geo_tiles)
+    chunks, small, order = exchange(phases, small, stack_size)
     incidence, *gains, member, weighted, basis = prepare(
-        ifg_pairs.T, preconditioner, coherence, geo_tiles, date_pad, date_rows, order,
+        preconditioner, small, date_pad, date_rows, order,
         col_range * range_size, row_local * azimuth_size,
     )
     early = []

time: 37.7 us -> 37.3 us (0.989)
  starting transfers between devices: 19.7 us -> 19.1 us
  waiting for transfers between devices: 6.23 us -> 6.64 us
    ppermute x5, starting transfers between devices: 7.49 us -> 4.62 us  [swap(): return lax.ppermute(value, axes, both)]
    ppermute x7, starting transfers between devices: 12.3 us -> 14.5 us  [exchange(): found[mask] = lax.ppermute(blocks[mask], 'stack', pairs)]
    ppermute x5, waiting for transfers between devices: 5.32 us -> 6.62 us  [swap(): return lax.ppermute(value, axes, both)]
    ppermute x7, waiting for transfers between devices: 0.91 us -> 0.02 us  [exchange(): found[mask] = lax.ppermute(blocks[mask], 'stack', pairs)]
where the time goes in v10:
time: 37.3 us; the launch traced here: 37.1 us
  starting transfers between devices  19.1 us (51%)
  Pallas kernels  11.2 us (30%)
  waiting for transfers between devices  6.64 us (18%)
    ppermute x7, starting transfers between devices, exchange(): found[mask] = lax.ppermute(blocks[mask], 'stack', pairs)  14.5 us
    ppermute x5, waiting for transfers between devices, swap(): return lax.ppermute(value, axes, both)  6.62 us
    ppermute x5, starting transfers between devices, swap(): return lax.ppermute(value, axes, both)  4.62 us
    pallas_call x1, Pallas kernels, prepare(): pl.pallas_call(functools.partial(prepare_kernel, order=order, col_total=c...  4.15 us
    pallas_call x1, Pallas kernels, invert(): pl.pallas_call(functools.partial(invert_kernel, row_local=row_local, date...  3.84 us
    pallas_call x1, Pallas kernels, cut(): pl.pallas_call(cut_kernel, out_shape=shapes, in_specs=[pl.BlockSpec(memor...  1.23 us
    pallas_call x1, Pallas kernels, deramp(): pl.pallas_call(functools.partial(deramp_kernel, row_local=row_local, date...  1.11 us
    pallas_call x2, Pallas kernels, early_fit(): pl.pallas_call(functools.partial(early_kernel, row_local=row_local, start...  0.9 us
  transfers between devices with their start and end apart: 12, of which 5 were waited for; matrix products, arithmetic and copies ran while one was open for 0% of the time, Pallas kernels for 14%

profile of v10, /device:TPU:0, one launch (start us, length us, event | category | flops | bytes accessed | tf_op | source)
XLA Modules:
  0.0 37.1 jit_solution(2585192792581442264)
XLA Ops:
  0.0 1.2 %cut.1 = (bf16[144,2,128]{2,1,0:T(2,128)(2,1)S(1)}, bf16[144,2,128]{2,1,0:T(2,128)(2,1)S(1)}, bf16[144,2,128]{2,1,0:T(2,128)(2,1)S(1)}, bf16[144,2,128]{2,1,0:T(...) custom-call(bf16[144,8,2,128]{3,2,1,0:T(2,128)(2,1)} %bitcast.21, ...), custom_call_target="tpu_custom_call" | custom-call | tf_op jit(solution)/shard_map/cut/pallas_call | solution.py:321
  1.2 6.1 %collective-permute-start.2 = (bf16[144,2,128]{2,1,0:T(2,128)(2,1)S(1)}, bf16[144,2,128]{2,1,0:T(2,128)(2,1)S(1)}, u32[]{:S(2)}, u32[]{:S(2)}) collective-permute-start(bf16[144,2,128]{2,1,0:T(2,128)(2,1)S(1)} %get-tuple-element.31), channel_id=1, source_target_pairs={{0,28},{4,24},{8,20},{12,16},{16,12},{20,8},{24,4},{28,0},{1,29},{... | collective-permute-start | bytes 221192 | tf_op jit(solution)/shard_map/ppermute | solution.py:345
  7.3 0.5 %collective-permute-start.3 = (bf16[144,2,128]{2,1,0:T(2,128)(2,1)S(1)}, bf16[144,2,128]{2,1,0:T(2,128)(2,1)S(1)}, u32[]{:S(2)}, u32[]{:S(2)}) collective-permute-start(bf16[144,2,128]{2,1,0:T(2,128)(2,1)S(1)} %get-tuple-element.32), channel_id=1, source_target_pairs={{0,4},{4,0},{8,12},{12,8},{16,20},{20,16},{24,28},{28,24},{1,5},{5... | collective-permute-start | bytes 221192 | tf_op jit(solution)/shard_map/ppermute | solution.py:345
  7.8 0.1 collective-permute-start.4
  8.0 0.0 collective-permute-start.5
  8.0 5.2 %collective-permute-start.6 = (bf16[144,2,128]{2,1,0:T(2,128)(2,1)S(1)}, bf16[144,2,128]{2,1,0:T(2,128)(2,1)S(1)}, u32[]{:S(2)}, u32[]{:S(2)}) collective-permute-start(bf16[144,2,128]{2,1,0:T(2,128)(2,1)S(1)} %get-tuple-element.41), channel_id=1, source_target_pairs={{0,20},{4,16},{8,28},{12,24},{16,4},{20,0},{24,12},{28,8},{1,21},{... | collective-permute-start | bytes 221192 | tf_op jit(solution)/shard_map/ppermute | solution.py:345
  13.2 0.0 collective-permute-done.2
  13.2 0.0 collective-permute-start
  13.2 0.0 collective-permute-done.3
  13.2 2.6 %collective-permute-start.1 = (bf16[144,2,128]{2,1,0:T(2,128)(2,1)S(1)}, bf16[144,2,128]{2,1,0:T(2,128)(2,1)S(1)}, u32[]{:S(2)}, u32[]{:S(2)}) collective-permute-start(bf16[144,2,128]{2,1,0:T(2,128)(2,1)S(1)} %get-tuple-element.29), channel_id=1, source_target_pairs={{0,16},{4,20},{8,24},{12,28},{16,0},{20,4},{24,8},{28,12},{1,17},{... | collective-permute-start | bytes 221192 | tf_op jit(solution)/shard_map/ppermute | solution.py:345
  15.7 4.2 %prepare.1 = (bf16[1152,1280]{1,0:T(8,128)(2,1)S(1)}, bf16[608,1152]{1,0:T(8,128)(2,1)S(1)}, bf16[608,1152]{1,0:T(8,128)(2,1)S(1)}, f32[16,256]{1,0:T(8,128)S(1)...) custom-call(f32[600,600]{1,0:T(8,128)} %prec_hbm.1, s32[2,1152]{1,0:T(2,128)S(1)} %get-tuple-element.34.pairs_ref, ...), custom_call_target="tpu_custom_call" | custom-call | tf_op jit(solution)/shard_map/prepare/pallas_call | solution.py:107
  19.9 0.0 collective-permute-done.4
  19.9 0.5 %early_fit.2 = (bf16[576,256]{1,0:T(8,128)(2,1)S(1)}, f32[608,256]{1,0:T(8,128)S(1)}) custom-call(bf16[288,128]{1,0:T(8,128)(2,1)S(1)} %bitcast.13, bf16[288,128]{1,0:T(8,128)(2,1)S(1)} %bitcast.14, bf16[288,128]{1,0:T(8,128)(2,1)S(1)} %bitcast.15, bf16[288,128]{1,0:T(8,128)(2,1)S(1)} %bitcast.16, bf16[608,1152]{1,0:T(8,128)(2,1)S(1)} %get-tuple-element.37.refs_4_.refs_6_, ...), custom_call_target="tpu_custom_call" | custom-call | tf_op jit(solution)/shard_map/early_fit/pallas_call | solution.py:163
  20.5 0.0 collective-permute-done.5
  20.5 0.0 collective-permute-done.6
  20.5 0.4 early_fit.3
  20.8 0.0 collective-permute-done
  20.8 0.0 collective-permute-done.1
  20.9 3.8 %invert.1 = (f32[608,256]{1,0:T(8,128)S(1)}, f32[16,608]{1,0:T(8,128)S(1)}) custom-call(bf16[288,128]{1,0:T(8,128)(2,1)S(1)} %bitcast.17, bf16[288,128]{1,0:T(8,128)(2,1)S(1)} %bitcast.20, bf16[576,256]{1,0:T(8,128)(2,1)S(1)} %get-tuple-element.39.refs_2_, bf16[288,256]{1,0:T(8,128)(2,1)S(1)} %get-tuple-element.43.refs_3_, ...), custom_call_target="tpu_custom_call" | custom-call | tf_op jit(solution)/shard_map/invert/pallas_call | solution.py:275
  24.7 0.5 %collective-permute-start.7 = (f32[8,608]{1,0:T(8,128)S(1)}, f32[8,608]{1,0:T(8,128)S(1)}, u32[]{:S(2)}, u32[]{:S(2)}) collective-permute-start(f32[8,608]{1,0:T(8,128)S(1)} %get-tuple-element.51), channel_id=1, source_target_pairs={{8,16},{12,20},{24,1},{28,5},{9,17},{13,21},{0,4},{25,29},{16,8},{... | collective-permute-start | bytes 58376 | tf_op jit(solution)/shard_map/ppermute | solution.py:440
  25.2 0.6 %collective-permute-start.8 = (f32[8,608]{1,0:T(8,128)S(1)}, f32[8,608]{1,0:T(8,128)S(1)}, u32[]{:S(2)}, u32[]{:S(2)}) collective-permute-start(f32[8,608]{1,0:T(8,128)S(1)} %get-tuple-element.52), channel_id=1, source_target_pairs={{0,8},{4,12},{16,24},{20,28},{1,9},{5,13},{17,25},{21,29},{8,0},{1... | collective-permute-start | bytes 58376 | tf_op jit(solution)/shard_map/ppermute | solution.py:440
  25.8 2.8 %collective-permute-done.7 = f32[8,608]{1,0:T(8,128)S(1)} collective-permute-done((f32[8,608]{1,0:T(8,128)S(1)}, f32[8,608]{1,0:T(8,128)S(1)}, u32[]{:S(2)}, u32[]{:S(2)}) %collective-permute-start.7) | collective-permute-done | bytes 19488 | tf_op jit(solution)/shard_map/ppermute | solution.py:440
  28.6 0.4 %collective-permute-done.8 = f32[8,608]{1,0:T(8,128)S(1)} collective-permute-done((f32[8,608]{1,0:T(8,128)S(1)}, f32[8,608]{1,0:T(8,128)S(1)}, u32[]{:S(2)}, u32[]{:S(2)}) %collective-permute-start.8) | collective-permute-done | bytes 19488 | tf_op jit(solution)/shard_map/ppermute | solution.py:440
  29.0 2.6 %collective-permute-start.9 = (f32[16,608]{1,0:T(8,128)S(1)}, f32[16,608]{1,0:T(8,128)S(1)}, u32[]{:S(2)}, u32[]{:S(2)}) collective-permute-start(f32[16,608]{1,0:T(8,128)S(1)} %maximum_add_fusion.first_ref), channel_id=1, source_target_pairs={{0,6},{2,4},{8,14},{10,12},{16,22},{18,20},{24,30},{26,28},{6,0},{... | collective-permute-start | bytes 116744 | tf_op jit(solution)/shard_map/ppermute | solution.py:440
  31.6 0.4 %collective-permute-start.10 = (f32[16,608]{1,0:T(8,128)S(1)}, f32[16,608]{1,0:T(8,128)S(1)}, u32[]{:S(2)}, u32[]{:S(2)}) collective-permute-start(f32[16,608]{1,0:T(8,128)S(1)} %maximum_add_fusion.first_ref), channel_id=1, source_target_pairs={{0,4},{8,12},{16,20},{24,28},{4,0},{12,8},{20,16},{28,24},{1,5},{9... | collective-permute-start | bytes 116744 | tf_op jit(solution)/shard_map/ppermute | solution.py:440
  32.0 0.5 %collective-permute-start.11 = (f32[16,608]{1,0:T(8,128)S(1)}, f32[16,608]{1,0:T(8,128)S(1)}, u32[]{:S(2)}, u32[]{:S(2)}) collective-permute-start(f32[16,608]{1,0:T(8,128)S(1)} %maximum_add_fusion.first_ref), channel_id=1, source_target_pairs={{0,2},{2,0},{1,3},{3,1},{4,6},{6,4},{5,7},{7,5},{8,10},{10,8},{9,1... | collective-permute-start | bytes 116744 | tf_op jit(solution)/shard_map/ppermute | solution.py:440
  32.5 1.4 %collective-permute-done.9.refs_0_ = f32[16,608]{1,0:T(8,128)S(1)} collective-permute-done((f32[16,608]{1,0:T(8,128)S(1)}, f32[16,608]{1,0:T(8,128)S(1)}, u32[]{:S(2)}, u32[]{:S(2)}) %collective-permute-start.9) | collective-permute-done | bytes 38944 | tf_op jit(solution)/shard_map/ppermute | solution.py:440
  33.9 1.7 %collective-permute-done.10.refs_1_ = f32[16,608]{1,0:T(8,128)S(1)} collective-permute-done((f32[16,608]{1,0:T(8,128)S(1)}, f32[16,608]{1,0:T(8,128)S(1)}, u32[]{:S(2)}, u32[]{:S(2)}) %collective-permute-start.10) | collective-permute-done | bytes 38944 | tf_op jit(solution)/shard_map/ppermute | solution.py:440
  35.6 0.4 %collective-permute-done.11.refs_2_ = f32[16,608]{1,0:T(8,128)S(1)} collective-permute-done((f32[16,608]{1,0:T(8,128)S(1)}, f32[16,608]{1,0:T(8,128)S(1)}, u32[]{:S(2)}, u32[]{:S(2)}) %collective-permute-start.11) | collective-permute-done | bytes 38944 | tf_op jit(solution)/shard_map/ppermute | solution.py:440
  36.0 1.1 %deramp.1 = f32[1200,128]{1,0:T(8,128)} custom-call(f32[16,608]{1,0:T(8,128)S(1)} %maximum_add_fusion.first_ref, f32[16,608]{1,0:T(8,128)S(1)} %collective-permute-done.9.refs_0_, f32[16,608]{1,0:T(8,128)S(1)} %collective-permute-done.10.refs_1_, f32[16,608]{1,0:T(8,128)S(1)} %collective-permute-done.11.refs_2_, f32[608,256]{1,0:T(8,128)S(1)} %get-tuple-element.49.refs_3_, ...), custom_call_target="tpu_custom_call" | custom-call | tf_op jit(solution)/shard_map/deramp/pallas_call | solution.py:427
  (3 shorter events, 0.0 us)
Async XLA Ops:
  1.2 11.9 %collective-permute-start.2 = (bf16[144,2,128]{2,1,0:T(2,128)(2,1)S(1)}, bf16[144,2,128]{2,1,0:T(2,128)(2,1)S(1)}, u32[]{:S(2)}, u32[]{:S(2)}) collective-permute-start(bf16[144,2,128]{2,1,0:T(2,128)(2,1)S(1)} %get-tuple-element.31), channel_id=1, source_target_pairs={{0,28},{4,24},{8,20},{12,16},{16,12},{20,8},{24,4},{28,0},{1,29},{... | collective-permute-start | bytes 221192 | tf_op jit(solution)/shard_map/ppermute | solution.py:345
  7.3 5.9 %collective-permute-start.3 = (bf16[144,2,128]{2,1,0:T(2,128)(2,1)S(1)}, bf16[144,2,128]{2,1,0:T(2,128)(2,1)S(1)}, u32[]{:S(2)}, u32[]{:S(2)}) collective-permute-start(bf16[144,2,128]{2,1,0:T(2,128)(2,1)S(1)} %get-tuple-element.32), channel_id=1, source_target_pairs={{0,4},{4,0},{8,12},{12,8},{16,20},{20,16},{24,28},{28,24},{1,5},{5... | collective-permute-start | bytes 221192 | tf_op jit(solution)/shard_map/ppermute | solution.py:345
  7.8 12.1 %collective-permute-start.4 = (bf16[144,2,128]{2,1,0:T(2,128)(2,1)S(1)}, bf16[144,2,128]{2,1,0:T(2,128)(2,1)S(1)}, u32[]{:S(2)}, u32[]{:S(2)}) collective-permute-start(bf16[144,2,128]{2,1,0:T(2,128)(2,1)S(1)} %get-tuple-element.33), channel_id=1, source_target_pairs={{0,24},{4,28},{8,16},{12,20},{16,8},{20,12},{24,0},{28,4},{1,25},{... | collective-permute-start | bytes 221192 | tf_op jit(solution)/shard_map/ppermute | solution.py:345
  8.0 12.5 %collective-permute-start.5 = (bf16[144,2,128]{2,1,0:T(2,128)(2,1)S(1)}, bf16[144,2,128]{2,1,0:T(2,128)(2,1)S(1)}, u32[]{:S(2)}, u32[]{:S(2)}) collective-permute-start(bf16[144,2,128]{2,1,0:T(2,128)(2,1)S(1)} %get-tuple-element.40), channel_id=1, source_target_pairs={{0,8},{4,12},{8,0},{12,4},{16,24},{20,28},{24,16},{28,20},{1,9},{5... | collective-permute-start | bytes 221192 | tf_op jit(solution)/shard_map/ppermute | solution.py:345
  8.0 12.5 %collective-permute-start.6 = (bf16[144,2,128]{2,1,0:T(2,128)(2,1)S(1)}, bf16[144,2,128]{2,1,0:T(2,128)(2,1)S(1)}, u32[]{:S(2)}, u32[]{:S(2)}) collective-permute-start(bf16[144,2,128]{2,1,0:T(2,128)(2,1)S(1)} %get-tuple-element.41), channel_id=1, source_target_pairs={{0,20},{4,16},{8,28},{12,24},{16,4},{20,0},{24,12},{28,8},{1,21},{... | collective-permute-start | bytes 221192 | tf_op jit(solution)/shard_map/ppermute | solution.py:345
  13.2 7.7 %collective-permute-start = (bf16[144,2,128]{2,1,0:T(2,128)(2,1)S(1)}, bf16[144,2,128]{2,1,0:T(2,128)(2,1)S(1)}, u32[]{:S(2)}, u32[]{:S(2)}) collective-permute-start(bf16[144,2,128]{2,1,0:T(2,128)(2,1)S(1)} %get-tuple-element.28), channel_id=1, source_target_pairs={{0,12},{4,8},{8,4},{12,0},{16,28},{20,24},{24,20},{28,16},{1,13},{... | collective-permute-start | bytes 221192 | tf_op jit(solution)/shard_map/ppermute | solution.py:345
  13.2 7.7 %collective-permute-start.1 = (bf16[144,2,128]{2,1,0:T(2,128)(2,1)S(1)}, bf16[144,2,128]{2,1,0:T(2,128)(2,1)S(1)}, u32[]{:S(2)}, u32[]{:S(2)}) collective-permute-start(bf16[144,2,128]{2,1,0:T(2,128)(2,1)S(1)} %get-tuple-element.29), channel_id=1, source_target_pairs={{0,16},{4,20},{8,24},{12,28},{16,0},{20,4},{24,8},{28,12},{1,17},{... | collective-permute-start | bytes 221192 | tf_op jit(solution)/shard_map/ppermute | solution.py:345
  24.7 3.8 %collective-permute-start.7 = (f32[8,608]{1,0:T(8,128)S(1)}, f32[8,608]{1,0:T(8,128)S(1)}, u32[]{:S(2)}, u32[]{:S(2)}) collective-permute-start(f32[8,608]{1,0:T(8,128)S(1)} %get-tuple-element.51), channel_id=1, source_target_pairs={{8,16},{12,20},{24,1},{28,5},{9,17},{13,21},{0,4},{25,29},{16,8},{... | collective-permute-start | bytes 58376 | tf_op jit(solution)/shard_map/ppermute | solution.py:440
  25.2 3.8 %collective-permute-start.8 = (f32[8,608]{1,0:T(8,128)S(1)}, f32[8,608]{1,0:T(8,128)S(1)}, u32[]{:S(2)}, u32[]{:S(2)}) collective-permute-start(f32[8,608]{1,0:T(8,128)S(1)} %get-tuple-element.52), channel_id=1, source_target_pairs={{0,8},{4,12},{16,24},{20,28},{1,9},{5,13},{17,25},{21,29},{8,0},{1... | collective-permute-start | bytes 58376 | tf_op jit(solution)/shard_map/ppermute | solution.py:440
  29.0 5.0 %collective-permute-start.9 = (f32[16,608]{1,0:T(8,128)S(1)}, f32[16,608]{1,0:T(8,128)S(1)}, u32[]{:S(2)}, u32[]{:S(2)}) collective-permute-start(f32[16,608]{1,0:T(8,128)S(1)} %maximum_add_fusion.first_ref), channel_id=1, source_target_pairs={{0,6},{2,4},{8,14},{10,12},{16,22},{18,20},{24,30},{26,28},{6,0},{... | collective-permute-start | bytes 116744 | tf_op jit(solution)/shard_map/ppermute | solution.py:440
  31.6 4.0 %collective-permute-start.10 = (f32[16,608]{1,0:T(8,128)S(1)}, f32[16,608]{1,0:T(8,128)S(1)}, u32[]{:S(2)}, u32[]{:S(2)}) collective-permute-start(f32[16,608]{1,0:T(8,128)S(1)} %maximum_add_fusion.first_ref), channel_id=1, source_target_pairs={{0,4},{8,12},{16,20},{24,28},{4,0},{12,8},{20,16},{28,24},{1,5},{9... | collective-permute-start | bytes 116744 | tf_op jit(solution)/shard_map/ppermute | solution.py:440
  32.0 4.0 %collective-permute-start.11 = (f32[16,608]{1,0:T(8,128)S(1)}, f32[16,608]{1,0:T(8,128)S(1)}, u32[]{:S(2)}, u32[]{:S(2)}) collective-permute-start(f32[16,608]{1,0:T(8,128)S(1)} %maximum_add_fusion.first_ref), channel_id=1, source_target_pairs={{0,2},{2,0},{1,3},{3,1},{4,6},{6,4},{5,7},{7,5},{8,10},{10,8},{9,1... | collective-permute-start | bytes 116744 | tf_op jit(solution)/shard_map/ppermute | solution.py:440

commit v11 on v10

--- a/solution.py
+++ b/solution.py
@@ -54,8 +54,13 @@
     prec = prec_ref[...]
     prec = prec - jnp.sum(prec, axis=1, keepdims=True) / date_total
     top, low = halves(prec)
-    used = incidence_t[:date_total]
-    gain_a, gain_b = halves(product(top, used) + product(low, used))
+    pad = jnp.zeros((date_total, date_pad - date_total), jnp.bfloat16)
+    gain_a, gain_b = halves(
+        product(
+            jnp.concatenate([top, pad, low, pad], axis=1),
+            jnp.concatenate([incidence_t, incidence_t], axis=0),
+        )
+    )
     zeros = jnp.zeros((gain_top.shape[0] - date_total, ifg_total), jnp.bfloat16)
     gain_top[...] = jnp.concatenate([gain_a, zeros], axis=0)
     gain_low[...] = jnp.concatenate([gain_b, zeros], axis=0)

time: 37.3 us -> 36.9 us (0.989)
  transfers between devices with their start and end apart: 12 -> 12, of which waited for: 5 -> 5; matrix products, arithmetic and copies ran while one was open for 0% -> 0% of each run, Pallas kernels for 14% -> 13%
where the time goes in v11:
time: 36.9 us; the launch traced here: 36.7 us
  starting transfers between devices  19.2 us (52%)
  Pallas kernels  10.9 us (30%)
  waiting for transfers between devices  6.51 us (18%)
    ppermute x7, starting transfers between devices, exchange(): found[mask] = lax.ppermute(blocks[mask], 'stack', pairs)  14.5 us
    ppermute x5, waiting for transfers between devices, swap(): return lax.ppermute(value, axes, both)  6.5 us
    ppermute x5, starting transfers between devices, swap(): return lax.ppermute(value, axes, both)  4.75 us
    pallas_call x1, Pallas kernels, invert(): pl.pallas_call(functools.partial(invert_kernel, row_local=row_local, date...  3.85 us
    pallas_call x1, Pallas kernels, prepare(): pl.pallas_call(functools.partial(prepare_kernel, order=order, col_total=c...  3.8 us
    pallas_call x1, Pallas kernels, cut(): pl.pallas_call(cut_kernel, out_shape=shapes, in_specs=[pl.BlockSpec(memor...  1.23 us
    pallas_call x1, Pallas kernels, deramp(): pl.pallas_call(functools.partial(deramp_kernel, row_local=row_local, date...  1.11 us
    pallas_call x2, Pallas kernels, early_fit(): pl.pallas_call(functools.partial(early_kernel, row_local=row_local, start...  0.9 us
  transfers between devices with their start and end apart: 12, of which 5 were waited for; matrix products, arithmetic and copies ran while one was open for 0% of the time, Pallas kernels for 13%

profile of v11, /device:TPU:0, one launch (start us, length us, event | category | flops | bytes accessed | tf_op | source)
XLA Modules:
  0.0 36.7 jit_solution(7963221392040764159)
XLA Ops:
  0.0 1.2 %cut.1 = (bf16[144,2,128]{2,1,0:T(2,128)(2,1)S(1)}, bf16[144,2,128]{2,1,0:T(2,128)(2,1)S(1)}, bf16[144,2,128]{2,1,0:T(2,128)(2,1)S(1)}, bf16[144,2,128]{2,1,0:T(...) custom-call(bf16[144,8,2,128]{3,2,1,0:T(2,128)(2,1)} %bitcast.21, ...), custom_call_target="tpu_custom_call" | custom-call | tf_op jit(solution)/shard_map/cut/pallas_call | solution.py:326
  1.2 6.1 %collective-permute-start.2 = (bf16[144,2,128]{2,1,0:T(2,128)(2,1)S(1)}, bf16[144,2,128]{2,1,0:T(2,128)(2,1)S(1)}, u32[]{:S(2)}, u32[]{:S(2)}) collective-permute-start(bf16[144,2,128]{2,1,0:T(2,128)(2,1)S(1)} %get-tuple-element.31), channel_id=1, source_target_pairs={{0,28},{4,24},{8,20},{12,16},{16,12},{20,8},{24,4},{28,0},{1,29},{... | collective-permute-start | bytes 221192 | tf_op jit(solution)/shard_map/ppermute | solution.py:350
  7.3 0.5 %collective-permute-start.3 = (bf16[144,2,128]{2,1,0:T(2,128)(2,1)S(1)}, bf16[144,2,128]{2,1,0:T(2,128)(2,1)S(1)}, u32[]{:S(2)}, u32[]{:S(2)}) collective-permute-start(bf16[144,2,128]{2,1,0:T(2,128)(2,1)S(1)} %get-tuple-element.32), channel_id=1, source_target_pairs={{0,4},{4,0},{8,12},{12,8},{16,20},{20,16},{24,28},{28,24},{1,5},{5... | collective-permute-start | bytes 221192 | tf_op jit(solution)/shard_map/ppermute | solution.py:350
  7.8 0.1 collective-permute-start.4
  8.0 0.0 collective-permute-start.5
  8.0 5.2 %collective-permute-start.6 = (bf16[144,2,128]{2,1,0:T(2,128)(2,1)S(1)}, bf16[144,2,128]{2,1,0:T(2,128)(2,1)S(1)}, u32[]{:S(2)}, u32[]{:S(2)}) collective-permute-start(bf16[144,2,128]{2,1,0:T(2,128)(2,1)S(1)} %get-tuple-element.41), channel_id=1, source_target_pairs={{0,20},{4,16},{8,28},{12,24},{16,4},{20,0},{24,12},{28,8},{1,21},{... | collective-permute-start | bytes 221192 | tf_op jit(solution)/shard_map/ppermute | solution.py:350
  13.2 0.0 collective-permute-done.2
  13.2 0.0 collective-permute-start
  13.2 0.0 collective-permute-done.3
  13.2 2.6 %collective-permute-start.1 = (bf16[144,2,128]{2,1,0:T(2,128)(2,1)S(1)}, bf16[144,2,128]{2,1,0:T(2,128)(2,1)S(1)}, u32[]{:S(2)}, u32[]{:S(2)}) collective-permute-start(bf16[144,2,128]{2,1,0:T(2,128)(2,1)S(1)} %get-tuple-element.29), channel_id=1, source_target_pairs={{0,16},{4,20},{8,24},{12,28},{16,0},{20,4},{24,8},{28,12},{1,17},{... | collective-permute-start | bytes 221192 | tf_op jit(solution)/shard_map/ppermute | solution.py:350
  15.7 3.8 %prepare.1 = (bf16[1152,1280]{1,0:T(8,128)(2,1)S(1)}, bf16[608,1152]{1,0:T(8,128)(2,1)S(1)}, bf16[608,1152]{1,0:T(8,128)(2,1)S(1)}, f32[16,256]{1,0:T(8,128)S(1)...) custom-call(f32[600,600]{1,0:T(8,128)} %prec_hbm.1, s32[2,1152]{1,0:T(2,128)S(1)} %get-tuple-element.34.pairs_ref, ...), custom_call_target="tpu_custom_call" | custom-call | tf_op jit(solution)/shard_map/prepare/pallas_call | solution.py:112
  19.5 0.0 collective-permute-done.4
  19.6 0.5 %early_fit.2 = (bf16[576,256]{1,0:T(8,128)(2,1)S(1)}, f32[608,256]{1,0:T(8,128)S(1)}) custom-call(bf16[288,128]{1,0:T(8,128)(2,1)S(1)} %bitcast.13, bf16[288,128]{1,0:T(8,128)(2,1)S(1)} %bitcast.14, bf16[288,128]{1,0:T(8,128)(2,1)S(1)} %bitcast.15, bf16[288,128]{1,0:T(8,128)(2,1)S(1)} %bitcast.16, bf16[608,1152]{1,0:T(8,128)(2,1)S(1)} %get-tuple-element.37.refs_4_.refs_6_, ...), custom_call_target="tpu_custom_call" | custom-call | tf_op jit(solution)/shard_map/early_fit/pallas_call | solution.py:168
  20.1 0.0 collective-permute-done.5
  20.1 0.0 collective-permute-done.6
  20.1 0.4 early_fit.3
  20.5 0.0 collective-permute-done
  20.5 0.0 collective-permute-done.1
  20.5 3.8 %invert.1 = (f32[608,256]{1,0:T(8,128)S(1)}, f32[16,608]{1,0:T(8,128)S(1)}) custom-call(bf16[288,128]{1,0:T(8,128)(2,1)S(1)} %bitcast.17, bf16[288,128]{1,0:T(8,128)(2,1)S(1)} %bitcast.20, bf16[576,256]{1,0:T(8,128)(2,1)S(1)} %get-tuple-element.39.refs_2_, bf16[288,256]{1,0:T(8,128)(2,1)S(1)} %get-tuple-element.43.refs_3_, ...), custom_call_target="tpu_custom_call" | custom-call | tf_op jit(solution)/shard_map/invert/pallas_call | solution.py:280
  24.4 0.4 %collective-permute-start.7 = (f32[8,608]{1,0:T(8,128)S(1)}, f32[8,608]{1,0:T(8,128)S(1)}, u32[]{:S(2)}, u32[]{:S(2)}) collective-permute-start(f32[8,608]{1,0:T(8,128)S(1)} %get-tuple-element.51), channel_id=1, source_target_pairs={{8,16},{12,20},{24,1},{28,5},{9,17},{13,21},{0,4},{25,29},{16,8},{... | collective-permute-start | bytes 58376 | tf_op jit(solution)/shard_map/ppermute | solution.py:445
  24.8 0.8 %collective-permute-start.8 = (f32[8,608]{1,0:T(8,128)S(1)}, f32[8,608]{1,0:T(8,128)S(1)}, u32[]{:S(2)}, u32[]{:S(2)}) collective-permute-start(f32[8,608]{1,0:T(8,128)S(1)} %get-tuple-element.52), channel_id=1, source_target_pairs={{0,8},{4,12},{16,24},{20,28},{1,9},{5,13},{17,25},{21,29},{8,0},{1... | collective-permute-start | bytes 58376 | tf_op jit(solution)/shard_map/ppermute | solution.py:445
  25.6 2.6 %collective-permute-done.7 = f32[8,608]{1,0:T(8,128)S(1)} collective-permute-done((f32[8,608]{1,0:T(8,128)S(1)}, f32[8,608]{1,0:T(8,128)S(1)}, u32[]{:S(2)}, u32[]{:S(2)}) %collective-permute-start.7) | collective-permute-done | bytes 19488 | tf_op jit(solution)/shard_map/ppermute | solution.py:445
  28.2 0.4 %collective-permute-done.8 = f32[8,608]{1,0:T(8,128)S(1)} collective-permute-done((f32[8,608]{1,0:T(8,128)S(1)}, f32[8,608]{1,0:T(8,128)S(1)}, u32[]{:S(2)}, u32[]{:S(2)}) %collective-permute-start.8) | collective-permute-done | bytes 19488 | tf_op jit(solution)/shard_map/ppermute | solution.py:445
  28.6 2.6 %collective-permute-start.9 = (f32[16,608]{1,0:T(8,128)S(1)}, f32[16,608]{1,0:T(8,128)S(1)}, u32[]{:S(2)}, u32[]{:S(2)}) collective-permute-start(f32[16,608]{1,0:T(8,128)S(1)} %maximum_add_fusion.first_ref), channel_id=1, source_target_pairs={{0,6},{2,4},{8,14},{10,12},{16,22},{18,20},{24,30},{26,28},{6,0},{... | collective-permute-start | bytes 116744 | tf_op jit(solution)/shard_map/ppermute | solution.py:445
  31.2 0.4 %collective-permute-start.10 = (f32[16,608]{1,0:T(8,128)S(1)}, f32[16,608]{1,0:T(8,128)S(1)}, u32[]{:S(2)}, u32[]{:S(2)}) collective-permute-start(f32[16,608]{1,0:T(8,128)S(1)} %maximum_add_fusion.first_ref), channel_id=1, source_target_pairs={{0,4},{8,12},{16,20},{24,28},{4,0},{12,8},{20,16},{28,24},{1,5},{9... | collective-permute-start | bytes 116744 | tf_op jit(solution)/shard_map/ppermute | solution.py:445
  31.6 0.5 %collective-permute-start.11 = (f32[16,608]{1,0:T(8,128)S(1)}, f32[16,608]{1,0:T(8,128)S(1)}, u32[]{:S(2)}, u32[]{:S(2)}) collective-permute-start(f32[16,608]{1,0:T(8,128)S(1)} %maximum_add_fusion.first_ref), channel_id=1, source_target_pairs={{0,2},{2,0},{1,3},{3,1},{4,6},{6,4},{5,7},{7,5},{8,10},{10,8},{9,1... | collective-permute-start | bytes 116744 | tf_op jit(solution)/shard_map/ppermute | solution.py:445
  32.2 1.4 %collective-permute-done.9.refs_0_ = f32[16,608]{1,0:T(8,128)S(1)} collective-permute-done((f32[16,608]{1,0:T(8,128)S(1)}, f32[16,608]{1,0:T(8,128)S(1)}, u32[]{:S(2)}, u32[]{:S(2)}) %collective-permute-start.9) | collective-permute-done | bytes 38944 | tf_op jit(solution)/shard_map/ppermute | solution.py:445
  33.6 1.7 %collective-permute-done.10.refs_1_ = f32[16,608]{1,0:T(8,128)S(1)} collective-permute-done((f32[16,608]{1,0:T(8,128)S(1)}, f32[16,608]{1,0:T(8,128)S(1)}, u32[]{:S(2)}, u32[]{:S(2)}) %collective-permute-start.10) | collective-permute-done | bytes 38944 | tf_op jit(solution)/shard_map/ppermute | solution.py:445
  35.2 0.4 %collective-permute-done.11.refs_2_ = f32[16,608]{1,0:T(8,128)S(1)} collective-permute-done((f32[16,608]{1,0:T(8,128)S(1)}, f32[16,608]{1,0:T(8,128)S(1)}, u32[]{:S(2)}, u32[]{:S(2)}) %collective-permute-start.11) | collective-permute-done | bytes 38944 | tf_op jit(solution)/shard_map/ppermute | solution.py:445
  35.6 1.1 %deramp.1 = f32[1200,128]{1,0:T(8,128)} custom-call(f32[16,608]{1,0:T(8,128)S(1)} %maximum_add_fusion.first_ref, f32[16,608]{1,0:T(8,128)S(1)} %collective-permute-done.9.refs_0_, f32[16,608]{1,0:T(8,128)S(1)} %collective-permute-done.10.refs_1_, f32[16,608]{1,0:T(8,128)S(1)} %collective-permute-done.11.refs_2_, f32[608,256]{1,0:T(8,128)S(1)} %get-tuple-element.49.refs_3_, ...), custom_call_target="tpu_custom_call" | custom-call | tf_op jit(solution)/shard_map/deramp/pallas_call | solution.py:432
  (3 shorter events, 0.0 us)
Async XLA Ops:
  1.2 11.9 %collective-permute-start.2 = (bf16[144,2,128]{2,1,0:T(2,128)(2,1)S(1)}, bf16[144,2,128]{2,1,0:T(2,128)(2,1)S(1)}, u32[]{:S(2)}, u32[]{:S(2)}) collective-permute-start(bf16[144,2,128]{2,1,0:T(2,128)(2,1)S(1)} %get-tuple-element.31), channel_id=1, source_target_pairs={{0,28},{4,24},{8,20},{12,16},{16,12},{20,8},{24,4},{28,0},{1,29},{... | collective-permute-start | bytes 221192 | tf_op jit(solution)/shard_map/ppermute | solution.py:350
  7.3 5.9 %collective-permute-start.3 = (bf16[144,2,128]{2,1,0:T(2,128)(2,1)S(1)}, bf16[144,2,128]{2,1,0:T(2,128)(2,1)S(1)}, u32[]{:S(2)}, u32[]{:S(2)}) collective-permute-start(bf16[144,2,128]{2,1,0:T(2,128)(2,1)S(1)} %get-tuple-element.32), channel_id=1, source_target_pairs={{0,4},{4,0},{8,12},{12,8},{16,20},{20,16},{24,28},{28,24},{1,5},{5... | collective-permute-start | bytes 221192 | tf_op jit(solution)/shard_map/ppermute | solution.py:350
  7.8 11.7 %collective-permute-start.4 = (bf16[144,2,128]{2,1,0:T(2,128)(2,1)S(1)}, bf16[144,2,128]{2,1,0:T(2,128)(2,1)S(1)}, u32[]{:S(2)}, u32[]{:S(2)}) collective-permute-start(bf16[144,2,128]{2,1,0:T(2,128)(2,1)S(1)} %get-tuple-element.33), channel_id=1, source_target_pairs={{0,24},{4,28},{8,16},{12,20},{16,8},{20,12},{24,0},{28,4},{1,25},{... | collective-permute-start | bytes 221192 | tf_op jit(solution)/shard_map/ppermute | solution.py:350
  8.0 12.2 %collective-permute-start.5 = (bf16[144,2,128]{2,1,0:T(2,128)(2,1)S(1)}, bf16[144,2,128]{2,1,0:T(2,128)(2,1)S(1)}, u32[]{:S(2)}, u32[]{:S(2)}) collective-permute-start(bf16[144,2,128]{2,1,0:T(2,128)(2,1)S(1)} %get-tuple-element.40), channel_id=1, source_target_pairs={{0,8},{4,12},{8,0},{12,4},{16,24},{20,28},{24,16},{28,20},{1,9},{5... | collective-permute-start | bytes 221192 | tf_op jit(solution)/shard_map/ppermute | solution.py:350
  8.0 12.2 %collective-permute-start.6 = (bf16[144,2,128]{2,1,0:T(2,128)(2,1)S(1)}, bf16[144,2,128]{2,1,0:T(2,128)(2,1)S(1)}, u32[]{:S(2)}, u32[]{:S(2)}) collective-permute-start(bf16[144,2,128]{2,1,0:T(2,128)(2,1)S(1)} %get-tuple-element.41), channel_id=1, source_target_pairs={{0,20},{4,16},{8,28},{12,24},{16,4},{20,0},{24,12},{28,8},{1,21},{... | collective-permute-start | bytes 221192 | tf_op jit(solution)/shard_map/ppermute | solution.py:350
  13.2 7.3 %collective-permute-start = (bf16[144,2,128]{2,1,0:T(2,128)(2,1)S(1)}, bf16[144,2,128]{2,1,0:T(2,128)(2,1)S(1)}, u32[]{:S(2)}, u32[]{:S(2)}) collective-permute-start(bf16[144,2,128]{2,1,0:T(2,128)(2,1)S(1)} %get-tuple-element.28), channel_id=1, source_target_pairs={{0,12},{4,8},{8,4},{12,0},{16,28},{20,24},{24,20},{28,16},{1,13},{... | collective-permute-start | bytes 221192 | tf_op jit(solution)/shard_map/ppermute | solution.py:350
  13.2 7.3 %collective-permute-start.1 = (bf16[144,2,128]{2,1,0:T(2,128)(2,1)S(1)}, bf16[144,2,128]{2,1,0:T(2,128)(2,1)S(1)}, u32[]{:S(2)}, u32[]{:S(2)}) collective-permute-start(bf16[144,2,128]{2,1,0:T(2,128)(2,1)S(1)} %get-tuple-element.29), channel_id=1, source_target_pairs={{0,16},{4,20},{8,24},{12,28},{16,0},{20,4},{24,8},{28,12},{1,17},{... | collective-permute-start | bytes 221192 | tf_op jit(solution)/shard_map/ppermute | solution.py:350
  24.4 3.8 %collective-permute-start.7 = (f32[8,608]{1,0:T(8,128)S(1)}, f32[8,608]{1,0:T(8,128)S(1)}, u32[]{:S(2)}, u32[]{:S(2)}) collective-permute-start(f32[8,608]{1,0:T(8,128)S(1)} %get-tuple-element.51), channel_id=1, source_target_pairs={{8,16},{12,20},{24,1},{28,5},{9,17},{13,21},{0,4},{25,29},{16,8},{... | collective-permute-start | bytes 58376 | tf_op jit(solution)/shard_map/ppermute | solution.py:445
  24.8 3.8 %collective-permute-start.8 = (f32[8,608]{1,0:T(8,128)S(1)}, f32[8,608]{1,0:T(8,128)S(1)}, u32[]{:S(2)}, u32[]{:S(2)}) collective-permute-start(f32[8,608]{1,0:T(8,128)S(1)} %get-tuple-element.52), channel_id=1, source_target_pairs={{0,8},{4,12},{16,24},{20,28},{1,9},{5,13},{17,25},{21,29},{8,0},{1... | collective-permute-start | bytes 58376 | tf_op jit(solution)/shard_map/ppermute | solution.py:445
  28.6 5.0 %collective-permute-start.9 = (f32[16,608]{1,0:T(8,128)S(1)}, f32[16,608]{1,0:T(8,128)S(1)}, u32[]{:S(2)}, u32[]{:S(2)}) collective-permute-start(f32[16,608]{1,0:T(8,128)S(1)} %maximum_add_fusion.first_ref), channel_id=1, source_target_pairs={{0,6},{2,4},{8,14},{10,12},{16,22},{18,20},{24,30},{26,28},{6,0},{... | collective-permute-start | bytes 116744 | tf_op jit(solution)/shard_map/ppermute | solution.py:445
  31.2 4.0 %collective-permute-start.10 = (f32[16,608]{1,0:T(8,128)S(1)}, f32[16,608]{1,0:T(8,128)S(1)}, u32[]{:S(2)}, u32[]{:S(2)}) collective-permute-start(f32[16,608]{1,0:T(8,128)S(1)} %maximum_add_fusion.first_ref), channel_id=1, source_target_pairs={{0,4},{8,12},{16,20},{24,28},{4,0},{12,8},{20,16},{28,24},{1,5},{9... | collective-permute-start | bytes 116744 | tf_op jit(solution)/shard_map/ppermute | solution.py:445
  31.6 4.0 %collective-permute-start.11 = (f32[16,608]{1,0:T(8,128)S(1)}, f32[16,608]{1,0:T(8,128)S(1)}, u32[]{:S(2)}, u32[]{:S(2)}) collective-permute-start(f32[16,608]{1,0:T(8,128)S(1)} %maximum_add_fusion.first_ref), channel_id=1, source_target_pairs={{0,2},{2,0},{1,3},{3,1},{4,6},{6,4},{5,7},{7,5},{8,10},{10,8},{9,1... | collective-permute-start | bytes 116744 | tf_op jit(solution)/shard_map/ppermute | solution.py:445

commit v12 on v11

--- a/solution.py
+++ b/solution.py
@@ -229,9 +229,11 @@
             moved[rows, :] = ((inverse * left) * (inverse * strength)).astype(jnp.bfloat16)
 
     left_columns = pl.ds(done, ifg_total - done)
+    twice = jnp.concatenate([data[...], data[...]], axis=0)
     tops, lows = [], []
     for rows in date_tiles:
-        part = gained(gain_top, gain_low, rows, left_columns, data[...])
+        parts = [gain_top[rows, left_columns], gain_low[rows, left_columns]]
+        part = product(jnp.concatenate(parts, axis=1), twice)
         if early_refs:
             part = part + early_series[rows, :]
         series_ref[rows, :] = part

time: 36.9 us -> 36.8 us (level)
  no operation moved by 1% of the time
where the time goes in v12:
time: 36.8 us; the launch traced here: 36.6 us
  starting transfers between devices  19.2 us (52%)
  Pallas kernels  10.8 us (29%)
  waiting for transfers between devices  6.51 us (18%)
    ppermute x7, starting transfers between devices, exchange(): found[mask] = lax.ppermute(blocks[mask], 'stack', pairs)  14.5 us
    ppermute x5, waiting for transfers between devices, swap(): return lax.ppermute(value, axes, both)  6.5 us
    ppermute x5, starting transfers between devices, swap(): return lax.ppermute(value, axes, both)  4.73 us
    pallas_call x1, Pallas kernels, prepare(): pl.pallas_call(functools.partial(prepare_kernel, order=order, col_total=c...  3.8 us
    pallas_call x1, Pallas kernels, invert(): pl.pallas_call(functools.partial(invert_kernel, row_local=row_local, date...  3.77 us
    pallas_call x1, Pallas kernels, cut(): pl.pallas_call(cut_kernel, out_shape=shapes, in_specs=[pl.BlockSpec(memor...  1.23 us
    pallas_call x1, Pallas kernels, deramp(): pl.pallas_call(functools.partial(deramp_kernel, row_local=row_local, date...  1.12 us
    pallas_call x2, Pallas kernels, early_fit(): pl.pallas_call(functools.partial(early_kernel, row_local=row_local, start...  0.9 us
  transfers between devices with their start and end apart: 12, of which 5 were waited for; matrix products, arithmetic and copies ran while one was open for 0% of the time, Pallas kernels for 13%

profile of v12, /device:TPU:0, one launch (start us, length us, event | category | flops | bytes accessed | tf_op | source)
XLA Modules:
  0.0 36.6 jit_solution(8457519645817279641)
XLA Ops:
  0.0 1.2 %cut.1 = (bf16[144,2,128]{2,1,0:T(2,128)(2,1)S(1)}, bf16[144,2,128]{2,1,0:T(2,128)(2,1)S(1)}, bf16[144,2,128]{2,1,0:T(2,128)(2,1)S(1)}, bf16[144,2,128]{2,1,0:T(...) custom-call(bf16[144,8,2,128]{3,2,1,0:T(2,128)(2,1)} %bitcast.21, ...), custom_call_target="tpu_custom_call" | custom-call | tf_op jit(solution)/shard_map/cut/pallas_call | solution.py:328
  1.2 6.1 %collective-permute-start.2 = (bf16[144,2,128]{2,1,0:T(2,128)(2,1)S(1)}, bf16[144,2,128]{2,1,0:T(2,128)(2,1)S(1)}, u32[]{:S(2)}, u32[]{:S(2)}) collective-permute-start(bf16[144,2,128]{2,1,0:T(2,128)(2,1)S(1)} %get-tuple-element.31), channel_id=1, source_target_pairs={{0,28},{4,24},{8,20},{12,16},{16,12},{20,8},{24,4},{28,0},{1,29},{... | collective-permute-start | bytes 221192 | tf_op jit(solution)/shard_map/ppermute | solution.py:352
  7.3 0.5 %collective-permute-start.3 = (bf16[144,2,128]{2,1,0:T(2,128)(2,1)S(1)}, bf16[144,2,128]{2,1,0:T(2,128)(2,1)S(1)}, u32[]{:S(2)}, u32[]{:S(2)}) collective-permute-start(bf16[144,2,128]{2,1,0:T(2,128)(2,1)S(1)} %get-tuple-element.32), channel_id=1, source_target_pairs={{0,4},{4,0},{8,12},{12,8},{16,20},{20,16},{24,28},{28,24},{1,5},{5... | collective-permute-start | bytes 221192 | tf_op jit(solution)/shard_map/ppermute | solution.py:352
  7.8 0.1 collective-permute-start.4
  8.0 0.0 collective-permute-start.5
  8.0 5.2 %collective-permute-start.6 = (bf16[144,2,128]{2,1,0:T(2,128)(2,1)S(1)}, bf16[144,2,128]{2,1,0:T(2,128)(2,1)S(1)}, u32[]{:S(2)}, u32[]{:S(2)}) collective-permute-start(bf16[144,2,128]{2,1,0:T(2,128)(2,1)S(1)} %get-tuple-element.41), channel_id=1, source_target_pairs={{0,20},{4,16},{8,28},{12,24},{16,4},{20,0},{24,12},{28,8},{1,21},{... | collective-permute-start | bytes 221192 | tf_op jit(solution)/shard_map/ppermute | solution.py:352
  13.2 0.0 collective-permute-done.2
  13.2 0.0 collective-permute-start
  13.2 0.0 collective-permute-done.3
  13.2 2.6 %collective-permute-start.1 = (bf16[144,2,128]{2,1,0:T(2,128)(2,1)S(1)}, bf16[144,2,128]{2,1,0:T(2,128)(2,1)S(1)}, u32[]{:S(2)}, u32[]{:S(2)}) collective-permute-start(bf16[144,2,128]{2,1,0:T(2,128)(2,1)S(1)} %get-tuple-element.29), channel_id=1, source_target_pairs={{0,16},{4,20},{8,24},{12,28},{16,0},{20,4},{24,8},{28,12},{1,17},{... | collective-permute-start | bytes 221192 | tf_op jit(solution)/shard_map/ppermute | solution.py:352
  15.7 3.8 %prepare.1 = (bf16[1152,1280]{1,0:T(8,128)(2,1)S(1)}, bf16[608,1152]{1,0:T(8,128)(2,1)S(1)}, bf16[608,1152]{1,0:T(8,128)(2,1)S(1)}, f32[16,256]{1,0:T(8,128)S(1)...) custom-call(f32[600,600]{1,0:T(8,128)} %prec_hbm.1, s32[2,1152]{1,0:T(2,128)S(1)} %get-tuple-element.34.pairs_ref, ...), custom_call_target="tpu_custom_call" | custom-call | tf_op jit(solution)/shard_map/prepare/pallas_call | solution.py:112
  19.5 0.0 collective-permute-done.4
  19.6 0.5 %early_fit.2 = (bf16[576,256]{1,0:T(8,128)(2,1)S(1)}, f32[608,256]{1,0:T(8,128)S(1)}) custom-call(bf16[288,128]{1,0:T(8,128)(2,1)S(1)} %bitcast.13, bf16[288,128]{1,0:T(8,128)(2,1)S(1)} %bitcast.14, bf16[288,128]{1,0:T(8,128)(2,1)S(1)} %bitcast.15, bf16[288,128]{1,0:T(8,128)(2,1)S(1)} %bitcast.16, bf16[608,1152]{1,0:T(8,128)(2,1)S(1)} %get-tuple-element.37.refs_4_.refs_6_, ...), custom_call_target="tpu_custom_call" | custom-call | tf_op jit(solution)/shard_map/early_fit/pallas_call | solution.py:168
  20.1 0.0 collective-permute-done.5
  20.1 0.0 collective-permute-done.6
  20.1 0.4 early_fit.3
  20.5 0.0 collective-permute-done
  20.5 0.0 collective-permute-done.1
  20.5 3.8 %invert.1 = (f32[608,256]{1,0:T(8,128)S(1)}, f32[16,608]{1,0:T(8,128)S(1)}) custom-call(bf16[288,128]{1,0:T(8,128)(2,1)S(1)} %bitcast.17, bf16[288,128]{1,0:T(8,128)(2,1)S(1)} %bitcast.20, bf16[576,256]{1,0:T(8,128)(2,1)S(1)} %get-tuple-element.39.refs_2_, bf16[288,256]{1,0:T(8,128)(2,1)S(1)} %get-tuple-element.43.refs_3_, ...), custom_call_target="tpu_custom_call" | custom-call | tf_op jit(solution)/shard_map/invert/pallas_call | solution.py:282
  24.3 0.4 %collective-permute-start.7 = (f32[8,608]{1,0:T(8,128)S(1)}, f32[8,608]{1,0:T(8,128)S(1)}, u32[]{:S(2)}, u32[]{:S(2)}) collective-permute-start(f32[8,608]{1,0:T(8,128)S(1)} %get-tuple-element.51), channel_id=1, source_target_pairs={{8,16},{12,20},{24,1},{28,5},{9,17},{13,21},{0,4},{25,29},{16,8},{... | collective-permute-start | bytes 58376 | tf_op jit(solution)/shard_map/ppermute | solution.py:447
  24.7 0.7 %collective-permute-start.8 = (f32[8,608]{1,0:T(8,128)S(1)}, f32[8,608]{1,0:T(8,128)S(1)}, u32[]{:S(2)}, u32[]{:S(2)}) collective-permute-start(f32[8,608]{1,0:T(8,128)S(1)} %get-tuple-element.52), channel_id=1, source_target_pairs={{0,8},{4,12},{16,24},{20,28},{1,9},{5,13},{17,25},{21,29},{8,0},{1... | collective-permute-start | bytes 58376 | tf_op jit(solution)/shard_map/ppermute | solution.py:447
  25.5 2.6 %collective-permute-done.7 = f32[8,608]{1,0:T(8,128)S(1)} collective-permute-done((f32[8,608]{1,0:T(8,128)S(1)}, f32[8,608]{1,0:T(8,128)S(1)}, u32[]{:S(2)}, u32[]{:S(2)}) %collective-permute-start.7) | collective-permute-done | bytes 19488 | tf_op jit(solution)/shard_map/ppermute | solution.py:447
  28.1 0.4 %collective-permute-done.8 = f32[8,608]{1,0:T(8,128)S(1)} collective-permute-done((f32[8,608]{1,0:T(8,128)S(1)}, f32[8,608]{1,0:T(8,128)S(1)}, u32[]{:S(2)}, u32[]{:S(2)}) %collective-permute-start.8) | collective-permute-done | bytes 19488 | tf_op jit(solution)/shard_map/ppermute | solution.py:447
  28.5 2.6 %collective-permute-start.9 = (f32[16,608]{1,0:T(8,128)S(1)}, f32[16,608]{1,0:T(8,128)S(1)}, u32[]{:S(2)}, u32[]{:S(2)}) collective-permute-start(f32[16,608]{1,0:T(8,128)S(1)} %maximum_add_fusion.first_ref), channel_id=1, source_target_pairs={{0,6},{2,4},{8,14},{10,12},{16,22},{18,20},{24,30},{26,28},{6,0},{... | collective-permute-start | bytes 116744 | tf_op jit(solution)/shard_map/ppermute | solution.py:447
  31.1 0.4 %collective-permute-start.10 = (f32[16,608]{1,0:T(8,128)S(1)}, f32[16,608]{1,0:T(8,128)S(1)}, u32[]{:S(2)}, u32[]{:S(2)}) collective-permute-start(f32[16,608]{1,0:T(8,128)S(1)} %maximum_add_fusion.first_ref), channel_id=1, source_target_pairs={{0,4},{8,12},{16,20},{24,28},{4,0},{12,8},{20,16},{28,24},{1,5},{9... | collective-permute-start | bytes 116744 | tf_op jit(solution)/shard_map/ppermute | solution.py:447
  31.5 0.5 %collective-permute-start.11 = (f32[16,608]{1,0:T(8,128)S(1)}, f32[16,608]{1,0:T(8,128)S(1)}, u32[]{:S(2)}, u32[]{:S(2)}) collective-permute-start(f32[16,608]{1,0:T(8,128)S(1)} %maximum_add_fusion.first_ref), channel_id=1, source_target_pairs={{0,2},{2,0},{1,3},{3,1},{4,6},{6,4},{5,7},{7,5},{8,10},{10,8},{9,1... | collective-permute-start | bytes 116744 | tf_op jit(solution)/shard_map/ppermute | solution.py:447
  32.1 1.4 %collective-permute-done.9.refs_0_ = f32[16,608]{1,0:T(8,128)S(1)} collective-permute-done((f32[16,608]{1,0:T(8,128)S(1)}, f32[16,608]{1,0:T(8,128)S(1)}, u32[]{:S(2)}, u32[]{:S(2)}) %collective-permute-start.9) | collective-permute-done | bytes 38944 | tf_op jit(solution)/shard_map/ppermute | solution.py:447
  33.5 1.7 %collective-permute-done.10.refs_1_ = f32[16,608]{1,0:T(8,128)S(1)} collective-permute-done((f32[16,608]{1,0:T(8,128)S(1)}, f32[16,608]{1,0:T(8,128)S(1)}, u32[]{:S(2)}, u32[]{:S(2)}) %collective-permute-start.10) | collective-permute-done | bytes 38944 | tf_op jit(solution)/shard_map/ppermute | solution.py:447
  35.1 0.4 %collective-permute-done.11.refs_2_ = f32[16,608]{1,0:T(8,128)S(1)} collective-permute-done((f32[16,608]{1,0:T(8,128)S(1)}, f32[16,608]{1,0:T(8,128)S(1)}, u32[]{:S(2)}, u32[]{:S(2)}) %collective-permute-start.11) | collective-permute-done | bytes 38944 | tf_op jit(solution)/shard_map/ppermute | solution.py:447
  35.5 1.1 %deramp.1 = f32[1200,128]{1,0:T(8,128)} custom-call(f32[16,608]{1,0:T(8,128)S(1)} %maximum_add_fusion.first_ref, f32[16,608]{1,0:T(8,128)S(1)} %collective-permute-done.9.refs_0_, f32[16,608]{1,0:T(8,128)S(1)} %collective-permute-done.10.refs_1_, f32[16,608]{1,0:T(8,128)S(1)} %collective-permute-done.11.refs_2_, f32[608,256]{1,0:T(8,128)S(1)} %get-tuple-element.49.refs_3_, ...), custom_call_target="tpu_custom_call" | custom-call | tf_op jit(solution)/shard_map/deramp/pallas_call | solution.py:434
  (3 shorter events, 0.0 us)
Async XLA Ops:
  1.2 11.9 %collective-permute-start.2 = (bf16[144,2,128]{2,1,0:T(2,128)(2,1)S(1)}, bf16[144,2,128]{2,1,0:T(2,128)(2,1)S(1)}, u32[]{:S(2)}, u32[]{:S(2)}) collective-permute-start(bf16[144,2,128]{2,1,0:T(2,128)(2,1)S(1)} %get-tuple-element.31), channel_id=1, source_target_pairs={{0,28},{4,24},{8,20},{12,16},{16,12},{20,8},{24,4},{28,0},{1,29},{... | collective-permute-start | bytes 221192 | tf_op jit(solution)/shard_map/ppermute | solution.py:352
  7.3 5.9 %collective-permute-start.3 = (bf16[144,2,128]{2,1,0:T(2,128)(2,1)S(1)}, bf16[144,2,128]{2,1,0:T(2,128)(2,1)S(1)}, u32[]{:S(2)}, u32[]{:S(2)}) collective-permute-start(bf16[144,2,128]{2,1,0:T(2,128)(2,1)S(1)} %get-tuple-element.32), channel_id=1, source_target_pairs={{0,4},{4,0},{8,12},{12,8},{16,20},{20,16},{24,28},{28,24},{1,5},{5... | collective-permute-start | bytes 221192 | tf_op jit(solution)/shard_map/ppermute | solution.py:352
  7.8 11.7 %collective-permute-start.4 = (bf16[144,2,128]{2,1,0:T(2,128)(2,1)S(1)}, bf16[144,2,128]{2,1,0:T(2,128)(2,1)S(1)}, u32[]{:S(2)}, u32[]{:S(2)}) collective-permute-start(bf16[144,2,128]{2,1,0:T(2,128)(2,1)S(1)} %get-tuple-element.33), channel_id=1, source_target_pairs={{0,24},{4,28},{8,16},{12,20},{16,8},{20,12},{24,0},{28,4},{1,25},{... | collective-permute-start | bytes 221192 | tf_op jit(solution)/shard_map/ppermute | solution.py:352
  8.0 12.2 %collective-permute-start.5 = (bf16[144,2,128]{2,1,0:T(2,128)(2,1)S(1)}, bf16[144,2,128]{2,1,0:T(2,128)(2,1)S(1)}, u32[]{:S(2)}, u32[]{:S(2)}) collective-permute-start(bf16[144,2,128]{2,1,0:T(2,128)(2,1)S(1)} %get-tuple-element.40), channel_id=1, source_target_pairs={{0,8},{4,12},{8,0},{12,4},{16,24},{20,28},{24,16},{28,20},{1,9},{5... | collective-permute-start | bytes 221192 | tf_op jit(solution)/shard_map/ppermute | solution.py:352
  8.0 12.2 %collective-permute-start.6 = (bf16[144,2,128]{2,1,0:T(2,128)(2,1)S(1)}, bf16[144,2,128]{2,1,0:T(2,128)(2,1)S(1)}, u32[]{:S(2)}, u32[]{:S(2)}) collective-permute-start(bf16[144,2,128]{2,1,0:T(2,128)(2,1)S(1)} %get-tuple-element.41), channel_id=1, source_target_pairs={{0,20},{4,16},{8,28},{12,24},{16,4},{20,0},{24,12},{28,8},{1,21},{... | collective-permute-start | bytes 221192 | tf_op jit(solution)/shard_map/ppermute | solution.py:352
  13.2 7.3 %collective-permute-start = (bf16[144,2,128]{2,1,0:T(2,128)(2,1)S(1)}, bf16[144,2,128]{2,1,0:T(2,128)(2,1)S(1)}, u32[]{:S(2)}, u32[]{:S(2)}) collective-permute-start(bf16[144,2,128]{2,1,0:T(2,128)(2,1)S(1)} %get-tuple-element.28), channel_id=1, source_target_pairs={{0,12},{4,8},{8,4},{12,0},{16,28},{20,24},{24,20},{28,16},{1,13},{... | collective-permute-start | bytes 221192 | tf_op jit(solution)/shard_map/ppermute | solution.py:352
  13.2 7.3 %collective-permute-start.1 = (bf16[144,2,128]{2,1,0:T(2,128)(2,1)S(1)}, bf16[144,2,128]{2,1,0:T(2,128)(2,1)S(1)}, u32[]{:S(2)}, u32[]{:S(2)}) collective-permute-start(bf16[144,2,128]{2,1,0:T(2,128)(2,1)S(1)} %get-tuple-element.29), channel_id=1, source_target_pairs={{0,16},{4,20},{8,24},{12,28},{16,0},{20,4},{24,8},{28,12},{1,17},{... | collective-permute-start | bytes 221192 | tf_op jit(solution)/shard_map/ppermute | solution.py:352
  24.3 3.8 %collective-permute-start.7 = (f32[8,608]{1,0:T(8,128)S(1)}, f32[8,608]{1,0:T(8,128)S(1)}, u32[]{:S(2)}, u32[]{:S(2)}) collective-permute-start(f32[8,608]{1,0:T(8,128)S(1)} %get-tuple-element.51), channel_id=1, source_target_pairs={{8,16},{12,20},{24,1},{28,5},{9,17},{13,21},{0,4},{25,29},{16,8},{... | collective-permute-start | bytes 58376 | tf_op jit(solution)/shard_map/ppermute | solution.py:447
  24.7 3.8 %collective-permute-start.8 = (f32[8,608]{1,0:T(8,128)S(1)}, f32[8,608]{1,0:T(8,128)S(1)}, u32[]{:S(2)}, u32[]{:S(2)}) collective-permute-start(f32[8,608]{1,0:T(8,128)S(1)} %get-tuple-element.52), channel_id=1, source_target_pairs={{0,8},{4,12},{16,24},{20,28},{1,9},{5,13},{17,25},{21,29},{8,0},{1... | collective-permute-start | bytes 58376 | tf_op jit(solution)/shard_map/ppermute | solution.py:447
  28.5 5.0 %collective-permute-start.9 = (f32[16,608]{1,0:T(8,128)S(1)}, f32[16,608]{1,0:T(8,128)S(1)}, u32[]{:S(2)}, u32[]{:S(2)}) collective-permute-start(f32[16,608]{1,0:T(8,128)S(1)} %maximum_add_fusion.first_ref), channel_id=1, source_target_pairs={{0,6},{2,4},{8,14},{10,12},{16,22},{18,20},{24,30},{26,28},{6,0},{... | collective-permute-start | bytes 116744 | tf_op jit(solution)/shard_map/ppermute | solution.py:447
  31.1 4.0 %collective-permute-start.10 = (f32[16,608]{1,0:T(8,128)S(1)}, f32[16,608]{1,0:T(8,128)S(1)}, u32[]{:S(2)}, u32[]{:S(2)}) collective-permute-start(f32[16,608]{1,0:T(8,128)S(1)} %maximum_add_fusion.first_ref), channel_id=1, source_target_pairs={{0,4},{8,12},{16,20},{24,28},{4,0},{12,8},{20,16},{28,24},{1,5},{9... | collective-permute-start | bytes 116744 | tf_op jit(solution)/shard_map/ppermute | solution.py:447
  31.5 4.0 %collective-permute-start.11 = (f32[16,608]{1,0:T(8,128)S(1)}, f32[16,608]{1,0:T(8,128)S(1)}, u32[]{:S(2)}, u32[]{:S(2)}) collective-permute-start(f32[16,608]{1,0:T(8,128)S(1)} %maximum_add_fusion.first_ref), channel_id=1, source_target_pairs={{0,2},{2,0},{1,3},{3,1},{4,6},{6,4},{5,7},{7,5},{8,10},{10,8},{9,1... | collective-permute-start | bytes 116744 | tf_op jit(solution)/shard_map/ppermute | solution.py:447

commit v13 on v12

--- a/solution.py
+++ b/solution.py
@@ -13,7 +13,7 @@
 ROWS_A = 192
 APPROX = False
 ARRIVAL = (0, 7, 1, 6, 2, 5, 3, 4)
-EARLY = (4, 6)
+EARLY = (4, 7)
 OUT_PARTS = 5
 
 

time: 36.8 us -> 36.9 us (level)
  no operation moved by 1% of the time
where the time goes in v13:
time: 36.9 us; the launch traced here: 36.7 us
  starting transfers between devices  19.1 us (52%)
  Pallas kernels  10.9 us (30%)
  waiting for transfers between devices  6.65 us (18%)
    ppermute x7, starting transfers between devices, exchange(): found[mask] = lax.ppermute(blocks[mask], 'stack', pairs)  14.5 us
    ppermute x5, waiting for transfers between devices, swap(): return lax.ppermute(value, axes, both)  6.63 us
    ppermute x5, starting transfers between devices, swap(): return lax.ppermute(value, axes, both)  4.57 us
    pallas_call x1, Pallas kernels, prepare(): pl.pallas_call(functools.partial(prepare_kernel, order=order, col_total=c...  3.8 us
    pallas_call x1, Pallas kernels, invert(): pl.pallas_call(functools.partial(invert_kernel, row_local=row_local, date...  3.69 us
    pallas_call x1, Pallas kernels, cut(): pl.pallas_call(cut_kernel, out_shape=shapes, in_specs=[pl.BlockSpec(memor...  1.23 us
    pallas_call x1, Pallas kernels, deramp(): pl.pallas_call(functools.partial(deramp_kernel, row_local=row_local, date...  1.12 us
    pallas_call x2, Pallas kernels, early_fit(): pl.pallas_call(functools.partial(early_kernel, row_local=row_local, start...  1.07 us
  transfers between devices with their start and end apart: 12, of which 5 were waited for; matrix products, arithmetic and copies ran while one was open for 0% of the time, Pallas kernels for 13%

profile of v13, /device:TPU:0, one launch (start us, length us, event | category | flops | bytes accessed | tf_op | source)
XLA Modules:
  0.0 36.7 jit_solution(5532929002553345858)
XLA Ops:
  0.0 1.2 %cut.1 = (bf16[144,2,128]{2,1,0:T(2,128)(2,1)S(1)}, bf16[144,2,128]{2,1,0:T(2,128)(2,1)S(1)}, bf16[144,2,128]{2,1,0:T(2,128)(2,1)S(1)}, bf16[144,2,128]{2,1,0:T(...) custom-call(bf16[144,8,2,128]{3,2,1,0:T(2,128)(2,1)} %bitcast.21, ...), custom_call_target="tpu_custom_call" | custom-call | tf_op jit(solution)/shard_map/cut/pallas_call | solution.py:328
  1.2 6.1 %collective-permute-start.1 = (bf16[144,2,128]{2,1,0:T(2,128)(2,1)S(1)}, bf16[144,2,128]{2,1,0:T(2,128)(2,1)S(1)}, u32[]{:S(2)}, u32[]{:S(2)}) collective-permute-start(bf16[144,2,128]{2,1,0:T(2,128)(2,1)S(1)} %get-tuple-element.30), channel_id=1, source_target_pairs={{0,28},{4,24},{8,20},{12,16},{16,12},{20,8},{24,4},{28,0},{1,29},{... | collective-permute-start | bytes 221192 | tf_op jit(solution)/shard_map/ppermute | solution.py:352
  7.3 0.5 %collective-permute-start.2 = (bf16[144,2,128]{2,1,0:T(2,128)(2,1)S(1)}, bf16[144,2,128]{2,1,0:T(2,128)(2,1)S(1)}, u32[]{:S(2)}, u32[]{:S(2)}) collective-permute-start(bf16[144,2,128]{2,1,0:T(2,128)(2,1)S(1)} %get-tuple-element.31), channel_id=1, source_target_pairs={{0,4},{4,0},{8,12},{12,8},{16,20},{20,16},{24,28},{28,24},{1,5},{5... | collective-permute-start | bytes 221192 | tf_op jit(solution)/shard_map/ppermute | solution.py:352
  7.8 0.1 collective-permute-start.3
  8.0 0.0 collective-permute-start.4
  8.0 5.2 %collective-permute-start.5 = (bf16[144,2,128]{2,1,0:T(2,128)(2,1)S(1)}, bf16[144,2,128]{2,1,0:T(2,128)(2,1)S(1)}, u32[]{:S(2)}, u32[]{:S(2)}) collective-permute-start(bf16[144,2,128]{2,1,0:T(2,128)(2,1)S(1)} %get-tuple-element.40), channel_id=1, source_target_pairs={{0,20},{4,16},{8,28},{12,24},{16,4},{20,0},{24,12},{28,8},{1,21},{... | collective-permute-start | bytes 221192 | tf_op jit(solution)/shard_map/ppermute | solution.py:352
  13.2 0.0 collective-permute-done.1
  13.2 0.0 collective-permute-start.6
  13.2 0.0 collective-permute-done.2
  13.2 2.6 %collective-permute-start = (bf16[144,2,128]{2,1,0:T(2,128)(2,1)S(1)}, bf16[144,2,128]{2,1,0:T(2,128)(2,1)S(1)}, u32[]{:S(2)}, u32[]{:S(2)}) collective-permute-start(bf16[144,2,128]{2,1,0:T(2,128)(2,1)S(1)} %get-tuple-element.28), channel_id=1, source_target_pairs={{0,16},{4,20},{8,24},{12,28},{16,0},{20,4},{24,8},{28,12},{1,17},{... | collective-permute-start | bytes 221192 | tf_op jit(solution)/shard_map/ppermute | solution.py:352
  15.7 3.8 %prepare.1 = (bf16[1152,1280]{1,0:T(8,128)(2,1)S(1)}, bf16[608,1152]{1,0:T(8,128)(2,1)S(1)}, bf16[608,1152]{1,0:T(8,128)(2,1)S(1)}, f32[16,256]{1,0:T(8,128)S(1)...) custom-call(f32[600,600]{1,0:T(8,128)} %prec_hbm.1, s32[2,1152]{1,0:T(2,128)S(1)} %get-tuple-element.33.pairs_ref, ...), custom_call_target="tpu_custom_call" | custom-call | tf_op jit(solution)/shard_map/prepare/pallas_call | solution.py:112
  19.5 0.0 collective-permute-done.3
  19.6 0.5 %early_fit.2 = (bf16[576,256]{1,0:T(8,128)(2,1)S(1)}, f32[608,256]{1,0:T(8,128)S(1)}) custom-call(bf16[288,128]{1,0:T(8,128)(2,1)S(1)} %bitcast.13, bf16[288,128]{1,0:T(8,128)(2,1)S(1)} %bitcast.14, bf16[288,128]{1,0:T(8,128)(2,1)S(1)} %bitcast.15, bf16[288,128]{1,0:T(8,128)(2,1)S(1)} %bitcast.16, bf16[608,1152]{1,0:T(8,128)(2,1)S(1)} %get-tuple-element.36.refs_4_.refs_5_, ...), custom_call_target="tpu_custom_call" | custom-call | tf_op jit(solution)/shard_map/early_fit/pallas_call | solution.py:168
  20.1 0.0 collective-permute-done.4
  20.1 0.0 collective-permute-done.5
  20.1 0.0 collective-permute-done.6
  20.1 0.5 %early_fit.3 = (bf16[432,256]{1,0:T(8,128)(2,1)S(1)}, f32[608,256]{1,0:T(8,128)S(1)}) custom-call(bf16[288,128]{1,0:T(8,128)(2,1)S(1)} %bitcast.17, bf16[288,128]{1,0:T(8,128)(2,1)S(1)} %bitcast.18, bf16[288,128]{1,0:T(8,128)(2,1)S(1)} %bitcast.20, bf16[576,256]{1,0:T(8,128)(2,1)S(1)} %get-tuple-element.38.refs_3_.refs_1_, ...), custom_call_target="tpu_custom_call" | custom-call | tf_op jit(solution)/shard_map/early_fit/pallas_call | solution.py:168
  20.7 0.0 collective-permute-done
  20.7 3.7 %invert.1 = (f32[608,256]{1,0:T(8,128)S(1)}, f32[16,608]{1,0:T(8,128)S(1)}) custom-call(bf16[288,128]{1,0:T(8,128)(2,1)S(1)} %bitcast.19, bf16[576,256]{1,0:T(8,128)(2,1)S(1)} %get-tuple-element.38.refs_3_.refs_1_, bf16[432,256]{1,0:T(8,128)(2,1)S(1)} %get-tuple-element.43.refs_2_, f32[608,256]{1,0:T(8,128)S(1)} %get-tuple-element.44.refs_3_, ...), custom_call_target="tpu_custom_call" | custom-call | tf_op jit(solution)/shard_map/invert/pallas_call | solution.py:282
  24.4 0.4 %collective-permute-start.7 = (f32[8,608]{1,0:T(8,128)S(1)}, f32[8,608]{1,0:T(8,128)S(1)}, u32[]{:S(2)}, u32[]{:S(2)}) collective-permute-start(f32[8,608]{1,0:T(8,128)S(1)} %get-tuple-element.51), channel_id=1, source_target_pairs={{8,16},{12,20},{24,1},{28,5},{9,17},{13,21},{0,4},{25,29},{16,8},{... | collective-permute-start | bytes 58376 | tf_op jit(solution)/shard_map/ppermute | solution.py:447
  24.8 0.6 %collective-permute-start.8 = (f32[8,608]{1,0:T(8,128)S(1)}, f32[8,608]{1,0:T(8,128)S(1)}, u32[]{:S(2)}, u32[]{:S(2)}) collective-permute-start(f32[8,608]{1,0:T(8,128)S(1)} %get-tuple-element.52), channel_id=1, source_target_pairs={{0,8},{4,12},{16,24},{20,28},{1,9},{5,13},{17,25},{21,29},{8,0},{1... | collective-permute-start | bytes 58376 | tf_op jit(solution)/shard_map/ppermute | solution.py:447
  25.4 2.8 %collective-permute-done.7 = f32[8,608]{1,0:T(8,128)S(1)} collective-permute-done((f32[8,608]{1,0:T(8,128)S(1)}, f32[8,608]{1,0:T(8,128)S(1)}, u32[]{:S(2)}, u32[]{:S(2)}) %collective-permute-start.7) | collective-permute-done | bytes 19488 | tf_op jit(solution)/shard_map/ppermute | solution.py:447
  28.2 0.4 %collective-permute-done.8 = f32[8,608]{1,0:T(8,128)S(1)} collective-permute-done((f32[8,608]{1,0:T(8,128)S(1)}, f32[8,608]{1,0:T(8,128)S(1)}, u32[]{:S(2)}, u32[]{:S(2)}) %collective-permute-start.8) | collective-permute-done | bytes 19488 | tf_op jit(solution)/shard_map/ppermute | solution.py:447
  28.6 2.6 %collective-permute-start.9 = (f32[16,608]{1,0:T(8,128)S(1)}, f32[16,608]{1,0:T(8,128)S(1)}, u32[]{:S(2)}, u32[]{:S(2)}) collective-permute-start(f32[16,608]{1,0:T(8,128)S(1)} %maximum_add_fusion.first_ref), channel_id=1, source_target_pairs={{0,6},{2,4},{8,14},{10,12},{16,22},{18,20},{24,30},{26,28},{6,0},{... | collective-permute-start | bytes 116744 | tf_op jit(solution)/shard_map/ppermute | solution.py:447
  31.2 0.4 %collective-permute-start.10 = (f32[16,608]{1,0:T(8,128)S(1)}, f32[16,608]{1,0:T(8,128)S(1)}, u32[]{:S(2)}, u32[]{:S(2)}) collective-permute-start(f32[16,608]{1,0:T(8,128)S(1)} %maximum_add_fusion.first_ref), channel_id=1, source_target_pairs={{0,4},{8,12},{16,20},{24,28},{4,0},{12,8},{20,16},{28,24},{1,5},{9... | collective-permute-start | bytes 116744 | tf_op jit(solution)/shard_map/ppermute | solution.py:447
  31.6 0.5 %collective-permute-start.11 = (f32[16,608]{1,0:T(8,128)S(1)}, f32[16,608]{1,0:T(8,128)S(1)}, u32[]{:S(2)}, u32[]{:S(2)}) collective-permute-start(f32[16,608]{1,0:T(8,128)S(1)} %maximum_add_fusion.first_ref), channel_id=1, source_target_pairs={{0,2},{2,0},{1,3},{3,1},{4,6},{6,4},{5,7},{7,5},{8,10},{10,8},{9,1... | collective-permute-start | bytes 116744 | tf_op jit(solution)/shard_map/ppermute | solution.py:447
  32.1 1.4 %collective-permute-done.9.refs_0_ = f32[16,608]{1,0:T(8,128)S(1)} collective-permute-done((f32[16,608]{1,0:T(8,128)S(1)}, f32[16,608]{1,0:T(8,128)S(1)}, u32[]{:S(2)}, u32[]{:S(2)}) %collective-permute-start.9) | collective-permute-done | bytes 38944 | tf_op jit(solution)/shard_map/ppermute | solution.py:447
  33.6 1.7 %collective-permute-done.10.refs_1_ = f32[16,608]{1,0:T(8,128)S(1)} collective-permute-done((f32[16,608]{1,0:T(8,128)S(1)}, f32[16,608]{1,0:T(8,128)S(1)}, u32[]{:S(2)}, u32[]{:S(2)}) %collective-permute-start.10) | collective-permute-done | bytes 38944 | tf_op jit(solution)/shard_map/ppermute | solution.py:447
  35.2 0.4 %collective-permute-done.11.refs_2_ = f32[16,608]{1,0:T(8,128)S(1)} collective-permute-done((f32[16,608]{1,0:T(8,128)S(1)}, f32[16,608]{1,0:T(8,128)S(1)}, u32[]{:S(2)}, u32[]{:S(2)}) %collective-permute-start.11) | collective-permute-done | bytes 38944 | tf_op jit(solution)/shard_map/ppermute | solution.py:447
  35.6 1.1 %deramp.1 = f32[1200,128]{1,0:T(8,128)} custom-call(f32[16,608]{1,0:T(8,128)S(1)} %maximum_add_fusion.first_ref, f32[16,608]{1,0:T(8,128)S(1)} %collective-permute-done.9.refs_0_, f32[16,608]{1,0:T(8,128)S(1)} %collective-permute-done.10.refs_1_, f32[16,608]{1,0:T(8,128)S(1)} %collective-permute-done.11.refs_2_, f32[608,256]{1,0:T(8,128)S(1)} %get-tuple-element.49.refs_3_, ...), custom_call_target="tpu_custom_call" | custom-call | tf_op jit(solution)/shard_map/deramp/pallas_call | solution.py:434
  (3 shorter events, 0.0 us)
Async XLA Ops:
  1.2 11.9 %collective-permute-start.1 = (bf16[144,2,128]{2,1,0:T(2,128)(2,1)S(1)}, bf16[144,2,128]{2,1,0:T(2,128)(2,1)S(1)}, u32[]{:S(2)}, u32[]{:S(2)}) collective-permute-start(bf16[144,2,128]{2,1,0:T(2,128)(2,1)S(1)} %get-tuple-element.30), channel_id=1, source_target_pairs={{0,28},{4,24},{8,20},{12,16},{16,12},{20,8},{24,4},{28,0},{1,29},{... | collective-permute-start | bytes 221192 | tf_op jit(solution)/shard_map/ppermute | solution.py:352
  7.3 5.9 %collective-permute-start.2 = (bf16[144,2,128]{2,1,0:T(2,128)(2,1)S(1)}, bf16[144,2,128]{2,1,0:T(2,128)(2,1)S(1)}, u32[]{:S(2)}, u32[]{:S(2)}) collective-permute-start(bf16[144,2,128]{2,1,0:T(2,128)(2,1)S(1)} %get-tuple-element.31), channel_id=1, source_target_pairs={{0,4},{4,0},{8,12},{12,8},{16,20},{20,16},{24,28},{28,24},{1,5},{5... | collective-permute-start | bytes 221192 | tf_op jit(solution)/shard_map/ppermute | solution.py:352
  7.8 11.7 %collective-permute-start.3 = (bf16[144,2,128]{2,1,0:T(2,128)(2,1)S(1)}, bf16[144,2,128]{2,1,0:T(2,128)(2,1)S(1)}, u32[]{:S(2)}, u32[]{:S(2)}) collective-permute-start(bf16[144,2,128]{2,1,0:T(2,128)(2,1)S(1)} %get-tuple-element.32), channel_id=1, source_target_pairs={{0,24},{4,28},{8,16},{12,20},{16,8},{20,12},{24,0},{28,4},{1,25},{... | collective-permute-start | bytes 221192 | tf_op jit(solution)/shard_map/ppermute | solution.py:352
  8.0 12.2 %collective-permute-start.4 = (bf16[144,2,128]{2,1,0:T(2,128)(2,1)S(1)}, bf16[144,2,128]{2,1,0:T(2,128)(2,1)S(1)}, u32[]{:S(2)}, u32[]{:S(2)}) collective-permute-start(bf16[144,2,128]{2,1,0:T(2,128)(2,1)S(1)} %get-tuple-element.39), channel_id=1, source_target_pairs={{0,8},{4,12},{8,0},{12,4},{16,24},{20,28},{24,16},{28,20},{1,9},{5... | collective-permute-start | bytes 221192 | tf_op jit(solution)/shard_map/ppermute | solution.py:352
  8.0 12.2 %collective-permute-start.5 = (bf16[144,2,128]{2,1,0:T(2,128)(2,1)S(1)}, bf16[144,2,128]{2,1,0:T(2,128)(2,1)S(1)}, u32[]{:S(2)}, u32[]{:S(2)}) collective-permute-start(bf16[144,2,128]{2,1,0:T(2,128)(2,1)S(1)} %get-tuple-element.40), channel_id=1, source_target_pairs={{0,20},{4,16},{8,28},{12,24},{16,4},{20,0},{24,12},{28,8},{1,21},{... | collective-permute-start | bytes 221192 | tf_op jit(solution)/shard_map/ppermute | solution.py:352
  13.2 7.0 %collective-permute-start.6 = (bf16[144,2,128]{2,1,0:T(2,128)(2,1)S(1)}, bf16[144,2,128]{2,1,0:T(2,128)(2,1)S(1)}, u32[]{:S(2)}, u32[]{:S(2)}) collective-permute-start(bf16[144,2,128]{2,1,0:T(2,128)(2,1)S(1)} %get-tuple-element.41), channel_id=1, source_target_pairs={{0,12},{4,8},{8,4},{12,0},{16,28},{20,24},{24,20},{28,16},{1,13},{... | collective-permute-start | bytes 221192 | tf_op jit(solution)/shard_map/ppermute | solution.py:352
  13.2 7.5 %collective-permute-start = (bf16[144,2,128]{2,1,0:T(2,128)(2,1)S(1)}, bf16[144,2,128]{2,1,0:T(2,128)(2,1)S(1)}, u32[]{:S(2)}, u32[]{:S(2)}) collective-permute-start(bf16[144,2,128]{2,1,0:T(2,128)(2,1)S(1)} %get-tuple-element.28), channel_id=1, source_target_pairs={{0,16},{4,20},{8,24},{12,28},{16,0},{20,4},{24,8},{28,12},{1,17},{... | collective-permute-start | bytes 221192 | tf_op jit(solution)/shard_map/ppermute | solution.py:352
  24.4 3.8 %collective-permute-start.7 = (f32[8,608]{1,0:T(8,128)S(1)}, f32[8,608]{1,0:T(8,128)S(1)}, u32[]{:S(2)}, u32[]{:S(2)}) collective-permute-start(f32[8,608]{1,0:T(8,128)S(1)} %get-tuple-element.51), channel_id=1, source_target_pairs={{8,16},{12,20},{24,1},{28,5},{9,17},{13,21},{0,4},{25,29},{16,8},{... | collective-permute-start | bytes 58376 | tf_op jit(solution)/shard_map/ppermute | solution.py:447
  24.8 3.8 %collective-permute-start.8 = (f32[8,608]{1,0:T(8,128)S(1)}, f32[8,608]{1,0:T(8,128)S(1)}, u32[]{:S(2)}, u32[]{:S(2)}) collective-permute-start(f32[8,608]{1,0:T(8,128)S(1)} %get-tuple-element.52), channel_id=1, source_target_pairs={{0,8},{4,12},{16,24},{20,28},{1,9},{5,13},{17,25},{21,29},{8,0},{1... | collective-permute-start | bytes 58376 | tf_op jit(solution)/shard_map/ppermute | solution.py:447
  28.6 5.0 %collective-permute-start.9 = (f32[16,608]{1,0:T(8,128)S(1)}, f32[16,608]{1,0:T(8,128)S(1)}, u32[]{:S(2)}, u32[]{:S(2)}) collective-permute-start(f32[16,608]{1,0:T(8,128)S(1)} %maximum_add_fusion.first_ref), channel_id=1, source_target_pairs={{0,6},{2,4},{8,14},{10,12},{16,22},{18,20},{24,30},{26,28},{6,0},{... | collective-permute-start | bytes 116744 | tf_op jit(solution)/shard_map/ppermute | solution.py:447
  31.2 4.0 %collective-permute-start.10 = (f32[16,608]{1,0:T(8,128)S(1)}, f32[16,608]{1,0:T(8,128)S(1)}, u32[]{:S(2)}, u32[]{:S(2)}) collective-permute-start(f32[16,608]{1,0:T(8,128)S(1)} %maximum_add_fusion.first_ref), channel_id=1, source_target_pairs={{0,4},{8,12},{16,20},{24,28},{4,0},{12,8},{20,16},{28,24},{1,5},{9... | collective-permute-start | bytes 116744 | tf_op jit(solution)/shard_map/ppermute | solution.py:447
  31.6 4.0 %collective-permute-start.11 = (f32[16,608]{1,0:T(8,128)S(1)}, f32[16,608]{1,0:T(8,128)S(1)}, u32[]{:S(2)}, u32[]{:S(2)}) collective-permute-start(f32[16,608]{1,0:T(8,128)S(1)} %maximum_add_fusion.first_ref), channel_id=1, source_target_pairs={{0,2},{2,0},{1,3},{3,1},{4,6},{6,4},{5,7},{7,5},{8,10},{10,8},{9,1... | collective-permute-start | bytes 116744 | tf_op jit(solution)/shard_map/ppermute | solution.py:447
